TPU v7x, 256 devices: a whole 4x4x8 slice. The times are simulated.
256 devices in a mesh: gx: 32 (over y, z_hi, core), gy: 8 (over z_lo, x).
Axes of the slice: x: 4, y: 4, z: 8 (z_hi: 4, z_lo: 2; z = z_hi * 2 + z_lo), core: 2. Of those that a mesh axis runs over, the one named last changes fastest.
Arguments:
- positions: float32 [3, 32768], P(None, ('gx', 'gy')), as said below
- species: int32 [32768], P(('gx', 'gy')), may hold values from 0 to 5
- neighbours: int32 [64, 32768], P(None, ('gx', 'gy')), may hold values from 0 to 512, as said below
- face_sends: int32 [4, 16384], P(None, ('gx', 'gy')), may hold values from 0 to 127, as said below
- corner_sends: int32 [4, 8192], P(None, ('gx', 'gy')), may hold values from 0 to 127, as said below
- embed: float32 [6, 128], replicated, may hold values from -6 to 6
- radial: float32 [2, 8, 128], replicated, may hold values from -6 to 6
- w_up: float32 [128, 128], replicated, may hold values from -0.5 to 0.5
- w_charge: float32 [128, 128], replicated, may hold values from -0.5 to 0.5
- kvec: float32 [3, 2048], replicated, may hold values from -4 to 4
- kfilter: float32 [2048, 128], replicated, may hold values from -6 to 6
- read: float32 [128], replicated, may hold values from -0.5 to 0.5
Outputs:
- atom_energy: float32 [32768], P(('gx', 'gy'))
- forces: float32 [3, 32768], P(None, ('gx', 'gy'))
- grad_embed: float32 [6, 128], replicated
- grad_radial: float32 [2, 8, 128], replicated
- grad_up: float32 [128, 128], replicated
- grad_charge: float32 [128, 128], replicated
- grad_filter: float32 [2048, 128], replicated
- grad_read: float32 [128], replicated
Inputs may be any that keep to these rules, and one draw needn't show every extreme that they name: `positions`: each domain is 8.8 wide along the first two dimensions; coordinates are relative to its corner. `neighbours`: entry [s, i] names a slot of atom i's device's extended list: 0 to 127 are its own atoms in order, then 64 atoms for each face direction and 32 for each corner direction, in the order of the steps; the value 128 + 6 * 64 marks an empty slot. An atom never names itself. `face_sends`: row f of a device lists 64 of its own atoms for face direction f; every own atom appears in some row. `corner_sends`: row f of a device lists 64 / 2 of its own atoms for corner direction f; every own atom appears in some row.
All inputs are finite; a program needn't handle non-finite values.
Results may differ from a plain program's by a relative error of at most 0.0003.
Values sent between devices are 32-bit elements; how exact they have to be, the bound alone decides.
No kernel may reach another device: no remote copies, remote signals or barrier semaphores. Data moves between devices by JAX's collectives and lax.ppermute only.
A program may use at most 64 MiB of HBM per device.

v0:
```python
import math

import jax
import jax.numpy as jnp
from jax import lax
from jax.sharding import PartitionSpec as P

CUTOFF = 5.0
SOFTEN = 0.01
WIDTH_GAUSS = 2.0
NORMALIZE = 4.0
DOMAIN = 8.8
slot_group = 16
HIGHEST = lax.Precision.HIGHEST
FACE_DIRS = ((1, 0), (-1, 0), (0, 1), (0, -1))
CORNER_DIRS = ((1, 1), (1, -1), (-1, 1), (-1, -1))


def shifted_2(value, axis, steps):
    count = lax.axis_size(axis)
    pairs = [(source, (source + steps) % count) for source in range(count)]
    return lax.ppermute(value, axis, pairs)


def product(left, right):
    return jnp.dot(left, right, precision=HIGHEST, preferred_element_type=jnp.float32)


def edge_block(coords, ext_pos, ext_feat, weights, centers, slots):
    limit = ext_pos.shape[1]
    valid = (slots < limit).astype(jnp.float32)
    index = jnp.minimum(slots, limit - 1)
    offset_vec = ext_pos[:, index] - coords[:, None, :]
    dist_sq = jnp.sum(offset_vec * offset_vec, axis=0)
    radius = jnp.sqrt(dist_sq + SOFTEN)
    envelope = jnp.square(jnp.maximum(1.0 - dist_sq / (CUTOFF * CUTOFF), 0.0)) * valid
    basis = (
        jnp.exp(-WIDTH_GAUSS * jnp.square(radius[None] - centers[:, None, None])) * envelope[None]
    )
    radial_zero = jnp.einsum("bc,bsa->csa", weights[0], basis, precision=HIGHEST)
    radial_one = jnp.einsum("bc,bsa->csa", weights[1], basis, precision=HIGHEST)
    gathered = ext_feat[:, index]
    scalar_part = jnp.sum(radial_zero * gathered, axis=1)
    vector_part = jnp.einsum("csa,dsa->dca", radial_one * gathered, offset_vec, precision=HIGHEST)
    return (scalar_part, vector_part)


def edge_features(coords, halo_pos, features, halo_feat, weights, neighbours):
    ext_pos = jnp.concatenate([coords, halo_pos], axis=1)
    ext_feat = jnp.concatenate([features, halo_feat], axis=1)
    basis_count = weights.shape[1]
    centers = jnp.arange(basis_count, dtype=jnp.float32) * (CUTOFF / (basis_count - 1))
    channels = features.shape[0]
    atoms = coords.shape[1]
    groups = neighbours.reshape(-1, slot_group, atoms)
    blocked = jax.checkpoint(edge_block)

    def step(carry, slots):
        first, second = blocked(coords, ext_pos, ext_feat, weights, centers, slots)
        return ((carry[0] + first, carry[1] + second), None)

    start = (
        jnp.zeros((channels, atoms), jnp.float32),
        jnp.zeros((3, channels, atoms), jnp.float32),
    )
    (scalar_msg, vector_msg), _ = lax.scan(step, start, groups)
    scalar_msg = scalar_msg / NORMALIZE
    vector_msg = vector_msg / (NORMALIZE * CUTOFF)
    return scalar_msg + jnp.sum(jnp.square(vector_msg), axis=0)


def phase_block(global_pos, k_block):
    phase_angle = (
        k_block[0][:, None] * global_pos[0][None, :]
        + k_block[1][:, None] * global_pos[1][None, :]
        + k_block[2][:, None] * global_pos[2][None, :]
    )
    return (jnp.cos(phase_angle), jnp.sin(phase_angle))


def silu_slope(values):
    logistic = jax.nn.sigmoid(values)
    return logistic * (1.0 + values * (1.0 - logistic))


def carry_direct(packet, direction):
    step_x, step_y = direction
    if step_x != 0:
        packet = shifted_2(packet, "gx", -step_x)
    if step_y != 0:
        packet = shifted_2(packet, "gy", -step_y)
    return packet


def return_direct(packet, direction):
    step_x, step_y = direction
    if step_y != 0:
        packet = shifted_2(packet, "gy", step_y)
    if step_x != 0:
        packet = shifted_2(packet, "gx", step_x)
    return packet


def halo_forward(faces, corners):
    got_faces = [carry_direct(faces[number], FACE_DIRS[number]) for number in range(4)]
    got_corners = [carry_direct(corners[number], CORNER_DIRS[number]) for number in range(4)]
    return (got_faces, got_corners)


def halo_reverse(faces, corners):
    out_faces = [return_direct(faces[number], FACE_DIRS[number]) for number in range(4)]
    out_corners = [return_direct(corners[number], CORNER_DIRS[number]) for number in range(4)]
    return (out_faces, out_corners)


def body(
    positions,
    species,
    neighbours,
    face_sends,
    corner_sends,
    embed,
    radial,
    w_up,
    w_charge,
    kvec,
    kfilter,
    read,
):
    atoms = positions.shape[1]
    kinds = embed.shape[0]
    channels = embed.shape[1]
    total_atoms = atoms * lax.axis_size("gx") * lax.axis_size("gy")
    onehot = (species[None, :] == jnp.arange(kinds, dtype=jnp.int32)[:, None]).astype(jnp.float32)
    initial = product(embed.T, onehot)
    source = jnp.concatenate([positions, initial], axis=0)
    face_pack = [source[:, face_sends[number]] for number in range(4)]
    corner_pack = [source[:, corner_sends[number]] for number in range(4)]
    got_faces, got_corners = halo_forward(face_pack, corner_pack)
    shifted = []
    for piece, (step_x, step_y) in zip(got_faces + got_corners, FACE_DIRS + CORNER_DIRS):
        shift_vec = jnp.array([step_x * DOMAIN, step_y * DOMAIN, 0.0], dtype=jnp.float32)[:, None]
        shifted.append(jnp.concatenate([piece[:3] + shift_vec, piece[3:]], axis=0))
    halo_rows = jnp.concatenate(shifted, axis=1)

    def short_range(coords, halo_pos, features, halo_feat, weights):
        return edge_features(coords, halo_pos, features, halo_feat, weights, neighbours)

    invariants, edge_back = jax.vjp(
        short_range, positions, halo_rows[:3], initial, halo_rows[3:], radial
    )
    activated = jax.nn.silu(invariants)
    updated = initial + product(w_up.T, activated)
    charges = product(w_charge.T, updated)
    row_index = lax.axis_index("gx").astype(jnp.float32)
    col_index = lax.axis_index("gy").astype(jnp.float32)
    anchor = jnp.stack([row_index * DOMAIN, col_index * DOMAIN, jnp.zeros((), jnp.float32)])
    global_pos = positions + anchor[:, None]
    wave_count = kvec.shape[1]
    block_size = min(512, wave_count)
    block_count = wave_count // block_size
    k_blocks = kvec.reshape(3, block_count, block_size).transpose(1, 0, 2)
    filter_blocks = kfilter.reshape(block_count, block_size, channels)
    scale = 1.0 / math.sqrt(total_atoms * wave_count)

    def structure_part(k_block):
        cosine, sine = phase_block(global_pos, k_block)
        return (product(cosine, charges.T), product(sine, charges.T))

    part_cos, part_sin = lax.map(structure_part, k_blocks)
    cos_factor, sin_factor = lax.psum((part_cos, part_sin), ("gx", "gy"))

    def potential_step(total, items):
        k_block, filter_blk, cos_blk, sin_blk = items
        cosine, sine = phase_block(global_pos, k_block)
        term = product((filter_blk * cos_blk).T, cosine) + product((filter_blk * sin_blk).T, sine)
        return (total + scale * term, None)

    potential, _ = lax.scan(
        potential_step,
        jnp.zeros((channels, atoms), jnp.float32),
        (k_blocks, filter_blocks, cos_factor, sin_factor),
    )
    combined = updated + potential
    activated_out = jax.nn.silu(combined)
    atom_energy = product(read[None, :], activated_out)[0]
    grad_combined = read[:, None] * silu_slope(combined)
    grad_read = jnp.sum(activated_out, axis=1)

    def projection_part(k_block):
        cosine, sine = phase_block(global_pos, k_block)
        return (product(cosine, grad_combined.T), product(sine, grad_combined.T))

    proj_cos, proj_sin = lax.map(projection_part, k_blocks)
    grad_cos, grad_sin = lax.psum(
        (scale * filter_blocks * proj_cos, scale * filter_blocks * proj_sin), ("gx", "gy")
    )
    filter_term = scale * (cos_factor * proj_cos + sin_factor * proj_sin)

    def backward_step(carry, items):
        grad_charges, grad_global = carry
        k_block, filter_blk, cos_blk, sin_blk, gcos_blk, gsin_blk = items
        cosine, sine = phase_block(global_pos, k_block)
        grad_charges = grad_charges + product(gcos_blk.T, cosine) + product(gsin_blk.T, sine)
        along_cos = product(scale * filter_blk * cos_blk, grad_combined) + product(
            gcos_blk, charges
        )
        along_sin = product(scale * filter_blk * sin_blk, grad_combined) + product(
            gsin_blk, charges
        )
        grad_phase = cosine * along_sin - sine * along_cos
        grad_global = grad_global + product(k_block, grad_phase)
        return ((grad_charges, grad_global), None)

    start = (jnp.zeros((channels, atoms), jnp.float32), jnp.zeros((3, atoms), jnp.float32))
    (grad_charges, grad_global), _ = lax.scan(
        backward_step, start, (k_blocks, filter_blocks, cos_factor, sin_factor, grad_cos, grad_sin)
    )
    grad_updated = grad_combined + product(w_charge, grad_charges)
    grad_wcharge = product(updated, grad_charges.T)
    grad_wup = product(activated, grad_updated.T)
    grad_inv = product(w_up, grad_updated) * silu_slope(invariants)
    grad_coords, grad_halo_pos, grad_initial, grad_halo_feat, grad_weights = edge_back(grad_inv)
    back_rows = jnp.concatenate([grad_halo_pos, grad_halo_feat], axis=1 - 1)
    face_width = face_sends.shape[1]
    corner_width = corner_sends.shape[1]
    back_faces = [
        back_rows[:, number * face_width : (number + 1) * face_width] for number in range(4)
    ]
    corner_base = 4 * face_width
    back_corners = [
        back_rows[
            :, corner_base + number * corner_width : corner_base + (number + 1) * corner_width
        ]
        for number in range(4)
    ]
    out_faces, out_corners = halo_reverse(back_faces, back_corners)
    all_index = jnp.concatenate([face_sends.reshape(-1), corner_sends.reshape(-1)])
    returned = (
        jnp.zeros((channels + 3, atoms), jnp.float32)
        .at[:, all_index]
        .add(jnp.concatenate(out_faces + out_corners, axis=1))
    )
    grad_features = grad_updated + grad_initial + returned[3:]
    grad_positions = grad_coords + returned[:3] + grad_global
    grad_table = product(onehot, grad_features.T)
    sum_table, sum_weights, sum_up, sum_charge, sum_filter, sum_read = lax.psum(
        (grad_table, grad_weights, grad_wup, grad_wcharge, filter_term, grad_read), ("gx", "gy")
    )
    mean_scale = 1.0 / total_atoms
    return (
        atom_energy,
        -grad_positions,
        sum_table * mean_scale,
        sum_weights * mean_scale,
        sum_up * mean_scale,
        sum_charge * mean_scale,
        sum_filter.reshape(wave_count, channels),
        sum_read * mean_scale,
    )


def solution(mesh):
    return jax.shard_map(
        body,
        mesh=mesh,
        in_specs=(
            P(None, ("gx", "gy")),
            P(("gx", "gy")),
            P(None, ("gx", "gy")),
            P(None, ("gx", "gy")),
            P(None, ("gx", "gy")),
            P(),
            P(),
            P(),
            P(),
            P(),
            P(),
            P(),
        ),
        out_specs=(P(("gx", "gy")), P(None, ("gx", "gy")), P(), P(), P(), P(), P(), P()),
        check_vma=False,
    )
```

profile of v0, /device:TPU:1, one launch (start us, length us, event | category | flops | bytes accessed | tf_op | source)
XLA Modules:
  0.0 1277.1 jit_solution(3592669035590173776)
XLA Ops:
  9.8 3.3 collective-permute-start.4
  13.7 6.5 collective-permute-start.6
  28.2 4.5 collective-permute-done.1
  32.8 2.9 collective-permute-start.2
  36.0 3.6 collective-permute-start.5
  39.6 3.6 collective-permute-start.9
  48.8 78.4 %while.84 = (s32[]{:T(128)}, f32[128,128]{0,1:T(8,128)S(1)}, f32[3,128,128]{1,0,2:T(4,128)S(1)}, s32[4,16,128]{2,1,0:T(8,128)}, f32[3,512]{0,1:T(8,128)S(1)}, /*...) while((s32[]{:T(128)}, f32[128,128]{0,1:T(8,128)S(1)}, ...), condition=%wide.region_3.4_spmd.clone, body=%wide.region_0.3_spmd.clone.sunk | while | flops 60848136 | bytes 7236840 | solution.py:66
  49.6 5.5 gather_fusion.1
  57.0 5.5 gather_fusion
  69.2 5.5 gather_fusion.1
  76.6 5.5 gather_fusion
  88.8 5.5 gather_fusion.1
  96.2 5.5 gather_fusion
  108.4 5.5 gather_fusion.1
  115.8 5.5 gather_fusion
  129.7 10.5 while.82
  142.1 262.4 %all-reduce.14.cloned.1.call-done = (f32[4,512,128]{2,1,0:T(8,128)}, f32[4,512,128]{2,1,0:T(8,128)}) async-done(((f32[4,512,128]{2,1,0:T(8,128)}, f32[4,512,128]{2,1,0:T(8,128)}), (f32[4,512,128]{2,1,0:T(8,128)}, f32[4,512,128]{2,1,0:T(8,128)})) %all-reduce.14.cloned.1.call-update) | async-done | bytes 2097168 | tf_op jit(solution)/shard_map/psum | solution.py:171
  404.5 19.8 %while.85 = (s32[]{:T(128)}, f32[128,128]{1,0:T(8,128)S(1)}, f32[4,512,128]{2,1,0:T(8,128)S(1)}, f32[4,512,128]{2,1,0:T(8,128)}, f32[4,3,512]{2,1,0:T(4,128)S(1)...) while((s32[]{:T(128)}, f32[128,128]{1,0:T(8,128)S(1)}, ...), condition=%wide.region_10.11_spmd.clone, body=%wide.region_9.10_spmd.clone.sunk | while | flops 202178560 | bytes 1341611 | solution.py:179
  404.5 2.4 fusion.330
  407.0 2.5 fusion.331
  409.5 2.4 fusion.330
  411.9 2.5 fusion.331
  414.4 2.4 fusion.330
  416.9 2.5 fusion.331
  419.4 2.4 fusion.330
  421.8 2.5 fusion.331
  428.2 15.9 %while.83 = (s32[]{:T(128)}, f32[4,512,128]{2,1,0:T(8,128)}, f32[4,512,128]{2,1,0:T(8,128)}, f32[4,3,512]{2,1,0:T(4,128)S(1)}, f32[3,128]{1,0:T(4,128)S(1)}, /*i...) while((s32[]{:T(128)}, f32[4,512,128]{2,1,0:T(8,128)}, f32[4,512,128]{2,1,0:T(8,128)}, ...), condition=%wide.region_12.13_spmd, body=%wide.region_11.12_spmd.sunk | while | flops 201981952 | bytes 686233 | solution.py:194
  444.1 3.7 add_multiply_fusion
  450.8 257.9 %all-reduce.12.cloned.1.call-done = (f32[4,512,128]{2,1,0:T(8,128)}, f32[4,512,128]{2,1,0:T(8,128)}) async-done(((f32[4,512,128]{2,1,0:T(8,128)}, f32[4,512,128]{2,1,0:T(8,128)}), (f32[4,512,128]{2,1,0:T(8,128)}, f32[4,512,128]{2,1,0:T(8,128)})) %all-reduce.12.cloned.1.call-update) | async-done | bytes 2097168 | tf_op jit(solution)/shard_map/psum | solution.py:195
  708.7 43.8 %while.86 = (s32[]{:T(128)}, f32[128,128]{1,0:T(8,128)S(1)}, f32[3,128]{1,0:T(4,128)S(1)}, f32[4,512,128]{2,1,0:T(8,128)}, f32[4,3,512]{2,1,0:T(4,128)S(1)}, /*i...) while((s32[]{:T(128)}, f32[128,128]{1,0:T(8,128)S(1)}, ...), condition=%wide.region_16.17_spmd.clone, body=%wide.region_15.16_spmd.clone.sunk | while | flops 608289536 | bytes 4776680 | solution.py:216
  708.7 2.4 convolution_add_fusion.10
  711.1 2.4 convolution_add_fusion.11
  719.6 2.4 convolution_add_fusion.10
  722.1 2.4 convolution_add_fusion.11
  730.6 2.4 convolution_add_fusion.10
  733.0 2.4 convolution_add_fusion.11
  741.6 2.4 convolution_add_fusion.10
  744.0 2.4 convolution_add_fusion.11
  755.7 242.8 %while.87 = (s32[]{:T(128)}, f32[3,128]{0,1:T(8,128)}, f32[3,512]{0,1:T(8,128)S(1)}, f32[128,512]{0,1:T(8,128)S(1)}, f32[2,8,128]{2,1,0:T(8,128)}, /*index=5*/s3...) while((s32[]{:T(128)}, f32[3,128]{0,1:T(8,128)}, ...), condition=%wide.region_24.25_spmd.clone, body=%wide.region_17.24_spmd.clone.sunk | while | flops 172808960 | bytes 28759172 | solution.py:66
  758.0 5.5 gather_fusion.3
  763.5 5.5 gather_fusion.2
  791.7 11.6 scatter_fusion.1
  804.4 11.6 scatter_fusion
  818.1 5.5 gather_fusion.3
  823.6 5.5 gather_fusion.2
  852.5 11.6 scatter_fusion.1
  865.1 11.6 scatter_fusion
  878.9 5.5 gather_fusion.3
  884.3 5.5 gather_fusion.2
  913.2 11.6 scatter_fusion.1
  925.9 11.6 scatter_fusion
  939.6 5.5 gather_fusion.3
  945.1 5.5 gather_fusion.2
  974.0 11.6 scatter_fusion.1
  986.7 11.6 scatter_fusion
  1001.2 4.4 collective-permute-start.22
  1005.7 3.6 collective-permute-start.18
  1009.8 4.9 collective-permute-done.13
  1014.7 4.2 collective-permute-start.15
  1019.0 2.5 collective-permute-start.17
  1021.6 3.0 collective-permute-start.21
  1027.3 2.8 scatter_custom_fusion.2
  1032.8 82.7 %all-reduce.2 = (f32[6,128]{1,0:T(8,128)S(1)}, f32[2,8,128]{2,1,0:T(8,128)S(1)}, f32[128]{0:T(128)S(1)}) all-reduce(f32[6,128]{1,0:T(8,128)S(1)} %fusion.198, f32[2,8,128]{2,1,0:T(8,128)} %get-tuple-element.505, f32[128]{0:T(128)S(1)} %copy-done.38), channel_id=1, replica_groups=mesh['gx'=32,'gy'=8] {'gx','gy'}, use_global_device_ids=true, to_apply=%region_26.27 | all-reduce | flops 2944 | bytes 23552 | tf_op jit(solution)/shard_map/psum | solution.py:247
  1117.2 148.6 %all-reduce.10.cloned.1.call-done = (f32[128,128]{1,0:T(8,128)}, f32[128,128]{1,0:T(8,128)}, f32[2048,128]{1,0:T(8,128)}) async-done(((f32[128,128]{1,0:T(8,128)}, f32[128,128]{1,0:T(8,128)}, f32[2048,128]{1,0:T(8,128)}), (f32[128,128]{1,0:T(8,128)}, f32[128,128]{1,0:T(8,128)}, f32[2048,128]{1,0:T(8,128)})) %all-reduce.10.cloned.1.call-update) | async-done | bytes 1179664 | tf_op jit(solution)/shard_map/psum | solution.py:247
  (575 shorter events, 235.8 us)
Async XLA Ops:
  7.2 120.5 %copy-start = (f32[128,128]{1,0:T(8,128)S(1)}, f32[128,128]{1,0:T(8,128)}, u32[]{:S(2)}) copy-start(f32[128,128]{1,0:T(8,128)} %param.39) | copy-start | bytes 196612
  7.2 397.3 %all-reduce.14.cloned.1.call-start = ((), (), s32[]{:S(2)}) async-start(), calls=%async_computation.2 | async-start | bytes 4194304 | tf_op jit(solution)/shard_map/psum | solution.py:171
  9.8 26.1 %collective-permute-start.4 = (f32[131,32]{0,1:T(8,128)S(1)}, f32[131,32]{0,1:T(8,128)S(1)}, u32[]{:S(2)}, u32[]{:S(2)}) collective-permute-start(f32[131,32]{0,1:T(8,128)S(1)} %bitcast.480), channel_id=1, source_target_pairs={{0,248},{8,0},{16,8},{24,16},{32,24},{40,32},{48,40},{56,48},{64,5... | collective-permute-start | bytes 50312 | tf_op jit(solution)/shard_map/ppermute | solution.py:22
  13.7 22.3 %collective-permute-start.6 = (f32[131,32]{0,1:T(8,128)S(1)}, f32[131,32]{0,1:T(8,128)S(1)}, u32[]{:S(2)}, u32[]{:S(2)}) collective-permute-start(f32[131,32]{0,1:T(8,128)S(1)} %bitcast.479), channel_id=1, source_target_pairs={{0,248},{8,0},{16,8},{24,16},{32,24},{40,32},{48,40},{56,48},{64,5... | collective-permute-start | bytes 50312 | tf_op jit(solution)/shard_map/ppermute | solution.py:22
  20.8 18.7 %collective-permute-start.8 = (f32[131,32]{0,1:T(8,128)S(1)}, f32[131,32]{0,1:T(8,128)S(1)}, u32[]{:S(2)}, u32[]{:S(2)}) collective-permute-start(f32[131,32]{0,1:T(8,128)S(1)} %bitcast.482), channel_id=1, source_target_pairs={{0,8},{8,16},{16,24},{24,32},{32,40},{40,48},{48,56},{56,64},{64,7... | collective-permute-start | bytes 50312 | tf_op jit(solution)/shard_map/ppermute | solution.py:22
  21.5 18.0 %collective-permute-start.10 = (f32[131,32]{0,1:T(8,128)S(1)}, f32[131,32]{0,1:T(8,128)S(1)}, u32[]{:S(2)}, u32[]{:S(2)}) collective-permute-start(f32[131,32]{0,1:T(8,128)S(1)} %bitcast.481), channel_id=1, source_target_pairs={{0,8},{8,16},{16,24},{24,32},{32,40},{40,48},{48,56},{56,64},{64,7... | collective-permute-start | bytes 50312 | tf_op jit(solution)/shard_map/ppermute | solution.py:22
  22.3 5.0 collective-permute-start
  27.3 5.5 collective-permute-start.1
  32.8 3.0 copy-start.45
  32.8 10.4 collective-permute-start.2
  35.9 7.5 copy-start.44
  35.9 7.6 collective-permute-start.3
  36.0 8.3 collective-permute-start.5
  39.6 5.5 collective-permute-start.7
  39.6 6.2 collective-permute-start.9
  43.1 5.1 collective-permute-start.11
  46.5 1.8 copy-start.39
  141.2 263.3 %copy-start.2 = (f32[2048,128]{1,0:T(8,128)S(1)}, f32[2048,128]{1,0:T(8,128)}, u32[]{:S(2)}) copy-start(f32[2048,128]{1,0:T(8,128)} %param.42) | copy-start | bytes 3145732
  141.6 567.1 %all-reduce.12.cloned.1.call-start = ((), (), s32[]{:S(2)}) async-start(), calls=%async_computation.1 | async-start | bytes 4194304 | tf_op jit(solution)/shard_map/psum | solution.py:195
  428.2 15.9 %copy-start.11 = (f32[4,512,128]{2,1,0:T(8,128)S(1)}, f32[4,512,128]{2,1,0:T(8,128)}, u32[]{:S(2)}) copy-start(f32[4,512,128]{2,1,0:T(8,128)} %get-tuple-element.1751) | copy-start | bytes 3145732
  447.8 818.0 %all-reduce.10.cloned.1.call-start = ((), (), s32[]{:S(2)}) async-start(), calls=%async_computation | async-start | bytes 2359296 | tf_op jit(solution)/shard_map/psum | solution.py:247
  755.9 7.6 copy-start.3
  772.8 2.0 copy-start.24
  785.0 1.9 copy-start.7
  788.7 2.3 copy-start.16
  788.7 2.4 copy-start.1
  791.1 12.3 copy-start.17
  804.4 11.6 copy-start.4
  816.0 7.6 copy-start.3
  833.0 2.0 copy-start.24
  835.9 1.3 copy-start.20
  845.8 1.9 copy-start.7
  849.4 2.3 copy-start.16
  849.4 2.4 copy-start.1
  851.8 12.3 copy-start.17
  865.1 11.6 copy-start.4
  876.8 7.6 copy-start.3
  893.7 2.0 copy-start.24
  896.7 1.3 copy-start.20
  906.5 1.9 copy-start.7
  910.2 2.3 copy-start.16
  910.2 2.4 copy-start.1
  912.6 12.3 copy-start.17
  925.9 11.6 copy-start.4
  937.5 7.6 copy-start.3
  954.5 2.0 copy-start.24
  967.3 1.9 copy-start.7
  970.9 2.3 copy-start.16
  970.9 2.4 copy-start.1
  973.3 12.3 copy-start.17
  986.6 11.6 copy-start.4
  999.5 9.8 collective-permute-start.12
  1001.2 13.5 %collective-permute-start.22 = (f32[131,32]{0,1:T(8,128)S(1)}, f32[131,32]{0,1:T(8,128)S(1)}, u32[]{:S(2)}, u32[]{:S(2)}) collective-permute-start(f32[131,32]{0,1:T(8,128)S(1)} %get-tuple-element.1075), channel_id=1, source_target_pairs={{0,7},{1,0},{2,1},{3,2},{4,3},{5,4},{6,5},{7,6},{8,15},{9,8},{10,9... | collective-permute-start | bytes 50312 | tf_op jit(solution)/shard_map/ppermute | solution.py:22
  1005.7 13.2 %collective-permute-start.16 = (f32[131,32]{0,1:T(8,128)S(1)}, f32[131,32]{0,1:T(8,128)S(1)}, u32[]{:S(2)}, u32[]{:S(2)}) collective-permute-start(f32[131,32]{0,1:T(8,128)S(1)} %get-tuple-element.1076), channel_id=1, source_target_pairs={{0,1},{1,2},{2,3},{3,4},{4,5},{5,6},{6,7},{7,0},{8,9},{9,10},{10,1... | collective-permute-start | bytes 50312 | tf_op jit(solution)/shard_map/ppermute | solution.py:22
  1005.7 13.4 %collective-permute-start.18 = (f32[131,32]{0,1:T(8,128)S(1)}, f32[131,32]{0,1:T(8,128)S(1)}, u32[]{:S(2)}, u32[]{:S(2)}) collective-permute-start(f32[131,32]{0,1:T(8,128)S(1)} %get-tuple-element.1077), channel_id=1, source_target_pairs={{0,7},{1,0},{2,1},{3,2},{4,3},{5,4},{6,5},{7,6},{8,15},{9,8},{10,9... | collective-permute-start | bytes 50312 | tf_op jit(solution)/shard_map/ppermute | solution.py:22
  1009.2 12.3 collective-permute-start.20
  1009.3 5.4 collective-permute-start.13
  1014.7 6.9 collective-permute-start.14
  1014.7 9.9 collective-permute-start.15
  1018.9 8.4 collective-permute-start.23
  1019.0 6.2 collective-permute-start.17
  1021.5 3.7 collective-permute-start.19
  1021.6 5.7 collective-permute-start.21
  1265.8 1.5 copy-start.31
  (64 other events, 52.7 us)
Sparse Core Ops, SparseCore 0:
  141.7 262.7 all-reduce.13
  447.9 260.6 all-reduce.11
  1009.4 256.3 all-reduce.9
where the time goes:
time: 1290 us; the launch traced here: 1280 us
  waiting for transfers between devices  684 us (53%)
  matrix products  168 us (13%)
  local copies, waits for them, and re-layouts  147 us (11%)
  other arithmetic  135 us (10%)
  blocking collectives  82.7 us (6%)
  starting transfers between devices  42.3 us (3%)
  between operations  14.9 us (1%)
    psum x1, waiting for transfers between devices, body(): cos_factor, sin_factor = lax.psum((part_cos, part_sin), ('gx', 'gy'))  262 us
    psum x1, waiting for transfers between devices, body(): lax.psum((scale * filter_blocks * proj_cos, scale * filter_blocks * proj_...  258 us
    psum x1, waiting for transfers between devices, body(): lax.psum((grad_table, grad_weights, grad_wup, grad_wcharge, filter_term,...  149 us
    dot_general x61, matrix products, product(): jnp.dot(left, right, precision=HIGHEST, preferred_element_type=jnp.float32)  94.5 us
    psum x1, blocking collectives, body(): lax.psum((grad_table, grad_weights, grad_wup, grad_wcharge, filter_term,...  82.7 us
    gather x16, local copies, waits for them, and re-layouts, edge_block(): offset_vec = ext_pos[:, index] - coords[:, None, :]  50.9 us
    scatter-add x4, other arithmetic, edge_block(): offset_vec = ext_pos[:, index] - coords[:, None, :]  46.4 us
    scatter-add x4, other arithmetic, edge_block(): gathered = ext_feat[:, index]  46.3 us
  transfers between devices with their start and end apart: 27, of which 10 were waited for; matrix products, arithmetic and copies ran while one was open for 1% of the time, Pallas kernels for 0%

commit v1 on v0

v1 whole, which is shorter than its diff:
```python
import functools
import math

import jax
import jax.numpy as jnp
from jax import lax
from jax.experimental import pallas as pl
from jax.experimental.pallas import tpu as pltpu
from jax.sharding import Mesh
from jax.sharding import PartitionSpec as P

CUTOFF = 5.0
SOFTEN = 0.01
WIDTH_GAUSS = 2.0
DOMAIN = 8.8
N = 128
SLOTS = 64
KINDS = 6
BASIS = 8
WAVES = 2048
ATOMS = 32768
SHARD = 256
HIGHEST = lax.Precision.HIGHEST
SCALE = 1.0 / math.sqrt(ATOMS * WAVES)

GX = ("y", "zh", "c")
GY = ("zl", "x")
ALL = GX + GY
GROUP = ("c", "x")
CROSS = ("y", "zh", "zl")
MEMBERS = 8
CROSSES = 32

COS_POLY = None
SIN_POLY = None


def _fit():
    import numpy as np

    count = 9
    points = (1.0 + np.cos(np.pi * (np.arange(200) + 0.5) / 200)) / 8.0
    root = np.sqrt(points)
    matrix = np.vander(points * 4.0, count, increasing=True)
    cosine = np.linalg.lstsq(matrix, np.cos(2 * np.pi * root), rcond=None)[0]
    sine = np.linalg.lstsq(matrix, np.sin(2 * np.pi * root) / root, rcond=None)[0]
    powers = 4.0 ** np.arange(count)
    return ([float(v) for v in cosine * powers], [float(v) for v in sine * powers])


COS_POLY, SIN_POLY = _fit()


def dims(left, right):
    return (((left,), (right,)), ((), ()))


def dot(left, right, left_dim=1, right_dim=0, precision=HIGHEST):
    return lax.dot_general(
        left,
        right,
        dims(left_dim, right_dim),
        precision=precision,
        preferred_element_type=jnp.float32,
    )


def half_dot(left, right, left_dim=1, right_dim=0):
    return lax.dot_general(
        left, right, dims(left_dim, right_dim), preferred_element_type=jnp.float32
    )


def split(value):
    high = value.astype(jnp.bfloat16)
    return high, (value - high.astype(jnp.float32)).astype(jnp.bfloat16)


def dot_three(left, right, left_dim=1, right_dim=0):
    left_high, left_low = left
    right_high, right_low = right
    return (
        half_dot(left_high, right_high, left_dim, right_dim)
        + half_dot(left_high, right_low, left_dim, right_dim)
        + half_dot(left_low, right_high, left_dim, right_dim)
    )


def sigmoid(value):
    return 1.0 / (1.0 + jnp.exp(-value))


def lane(shape):
    return lax.broadcasted_iota(jnp.int32, shape, 1)


def row_of(shape):
    return lax.broadcasted_iota(jnp.int32, shape, 0)


def call(kernel, out_shape, *args, scratch=(), vmem=32):
    return pl.pallas_call(
        kernel,
        out_shape=out_shape,
        scratch_shapes=list(scratch),
        compiler_params=pltpu.CompilerParams(vmem_limit_bytes=vmem * 1024 * 1024),
    )(*args)


def f32(*shape):
    return jax.ShapeDtypeStruct(shape, jnp.float32)


def take(row, index):
    return jnp.take_along_axis(
        jnp.broadcast_to(row, index.shape), index, axis=1, mode="promise_in_bounds"
    )


def pack_kernel(pos, species, index, to_minus, to_plus, own):
    rows = [pos[0:1, :], pos[1:2, :], pos[2:3, :], species[...].astype(jnp.float32)]
    where_from = index[...]
    for number, row in enumerate(rows):
        got = take(row, where_from)
        to_minus[number : number + 1, :] = got[0:1, :]
        to_plus[number : number + 1, :] = got[1:2, :]
        own[number : number + 1, :] = got[2:3, :]
    zero = jnp.zeros((4, N), jnp.float32)
    to_minus[4:8, :] = zero
    to_plus[4:8, :] = zero
    own[4:8, :] = zero


def relay_kernel(own, first, second, one, two):
    at = lane((8, N))
    a, b, d = own[...], first[...], second[...]
    one[...] = jnp.where(at < 64, a, jnp.where(at < 96, b, pltpu.roll(d, 32, 1)))
    two[...] = jnp.where(at < 64, pltpu.roll(a, 64, 1), jnp.where(at < 96, pltpu.roll(b, 96, 1), d))


def relay(own, first, second):
    return call(relay_kernel, (f32(8, N), f32(8, N)), own, first, second)


def moved(value, axes, steps):
    count = 1
    for axis in axes:
        count *= lax.axis_size(axis)
    return lax.ppermute(value, axes, [(s, (s + steps) % count) for s in range(count)])


def pair_weights(embed, radial):
    scalar, vector = [], []
    for kind in range(KINDS):
        row = embed[kind : kind + 1, :]
        scalar.append(radial[0] * row * 0.25)
        vector.append(radial[1] * row * 0.05)
    return jnp.concatenate(scalar, axis=0), jnp.concatenate(vector, axis=0)


def basis_centers():
    return row_of((BASIS, N)).astype(jnp.float32) * (CUTOFF / (BASIS - 1))


def edge_kernel(
    pos, species, nbr, from_plus_x, from_minus_x, from_plus_y, from_minus_y, embed, radial,
    shared, active, invariants, vectors, sums, edges, places,
):
    at = lane((8, N))
    own = [pos[0:1, :], pos[1:2, :], pos[2:3, :], species[...].astype(jnp.float32)]
    first, second = from_plus_x[...], from_minus_x[...]
    third = jnp.where(at < 64, from_plus_y[...], pltpu.roll(from_minus_y[...], 64, 1))
    line = lane((1, N))
    corner_y = jnp.where(line < 64, 0.0, jnp.where(line < 96, DOMAIN, -DOMAIN))
    tables = [
        own,
        [first[0:1] + DOMAIN, first[1:2] + corner_y, first[2:3], first[3:4]],
        [second[0:1] - DOMAIN, second[1:2] + corner_y, second[2:3], second[3:4]],
        [third[0:1], third[1:2] + jnp.where(line < 64, DOMAIN, -DOMAIN), third[2:3], third[3:4]],
    ]
    for group in range(SLOTS // 8):
        rows = slice(8 * group, 8 * group + 8)
        slot = nbr[rows, :]
        block = lax.shift_right_logical(slot, 6)
        table = jnp.where(
            block < 2,
            0,
            jnp.where(
                (block == 4) | (block == 5), 3, jnp.where((block & 1) == 0, 1, 2)
            ),
        )
        table = jnp.where(block == 8, 4, table)
        half = jnp.where((block == 1) | ((block >= 5) & (block < 8)), 64, 0)
        place = (slot & 63) + half
        found = []
        for number in range(4):
            value = take(tables[0][number], place)
            for other in range(1, 4):
                value = jnp.where(table == other, take(tables[other][number], place), value)
            found.append(value)
        offset = [found[d] - own[d] for d in range(3)]
        dist_sq = offset[0] * offset[0] + offset[1] * offset[1] + offset[2] * offset[2]
        valid = (table < 4).astype(jnp.float32)
        ramp = jnp.maximum(1.0 - dist_sq / (CUTOFF * CUTOFF), 0.0)
        edges[0, rows, :] = offset[0]
        edges[1, rows, :] = offset[1]
        edges[2, rows, :] = offset[2]
        edges[3, rows, :] = found[3]
        edges[4, rows, :] = jnp.sqrt(dist_sq + SOFTEN)
        edges[5, rows, :] = ramp * ramp * valid
        edges[6, rows, :] = (-2.0 / (CUTOFF * CUTOFF)) * ramp * valid
        places[0, rows, :] = table
        places[1, rows, :] = place
    centers = basis_centers()

    def step(slot, carry):
        row = pl.ds(slot, 1)
        away = edges[4, row, :] - centers
        basis = jnp.exp(-WIDTH_GAUSS * away * away) * edges[5, row, :]
        parts = [basis] + [basis * edges[d, row, :] for d in range(3)]
        kind_row = jnp.broadcast_to(edges[3, row, :], (BASIS, N))
        out = []
        for kind in range(KINDS):
            mask = kind_row == float(kind)
            for number in range(4):
                out.append(carry[4 * kind + number] + jnp.where(mask, parts[number], 0.0))
        return tuple(out)

    zero = jnp.zeros((BASIS, N), jnp.float32)
    total = lax.fori_loop(0, SLOTS, step, (zero,) * (4 * KINDS), unroll=4)
    for number in range(4):
        sums[number, :, :] = jnp.concatenate(
            [total[4 * kind + number] for kind in range(KINDS)], axis=0
        )
    scalar_w, vector_w = pair_weights(embed, radial)
    value = dot(sums[0], scalar_w, 0, 0)
    for d in range(3):
        vector = dot(sums[1 + d], vector_w, 0, 0)
        vectors[d, :, :] = vector
        value = value + vector * vector
    invariants[...] = value
    result = value * sigmoid(value)
    active[...] = result
    anchor_x = lax.convert_element_type(lax.axis_index(GX), jnp.float32) * DOMAIN
    anchor_y = lax.convert_element_type(lax.axis_index(GY), jnp.float32) * DOMAIN
    zero_row = jnp.zeros((1, N), jnp.float32)
    tail = jnp.concatenate(
        [own[0] + anchor_x, own[1] + anchor_y, own[2], own[3]] + [zero_row] * 4, axis=0
    )
    for member in range(MEMBERS):
        shared[member, 0:N, :] = result
        shared[member, N : N + 8, :] = tail


def edge_back_kernel(
    tiles, common, active, invariants, vectors, sums, edges, places, embed, radial, w_up, w_charge,
    species, grad_out, read_row,
    payload, charge_piece, own_grad, to_one, to_two, to_three,
):
    total = tiles[0]
    for member in range(1, MEMBERS):
        total = total + tiles[member]
    grad_charges = jnp.transpose(total[0:N, :])
    updated = grad_out[...] + dot(grad_charges, w_charge[...], 1, 1)
    value = invariants[...]
    logistic = sigmoid(value)
    slope = logistic * (1.0 + value * (1.0 - logistic))
    grad_inv = dot(updated, w_up[...], 1, 1) * slope
    scalar_w, vector_w = pair_weights(embed, radial)
    pulls = [dot(scalar_w, grad_inv, 1, 1)]
    grad_scalar = dot(sums[0], grad_inv)
    grad_vector = jnp.zeros((KINDS * BASIS, N), jnp.float32)
    for d in range(3):
        along = 2.0 * vectors[d] * grad_inv
        pulls.append(dot(vector_w, along, 1, 1))
        grad_vector = grad_vector + dot(sums[1 + d], along)
    onehot = (row_of((8, N)) == species[...]).astype(jnp.float32)
    grad_table = dot(onehot, updated)
    radial_zero = jnp.zeros((BASIS, N), jnp.float32)
    radial_one = jnp.zeros((BASIS, N), jnp.float32)
    table_rows = []
    for kind in range(KINDS):
        rows = slice(kind * BASIS, (kind + 1) * BASIS)
        row = embed[kind : kind + 1, :]
        part_zero, part_one = grad_scalar[rows] * 0.25, grad_vector[rows] * 0.05
        radial_zero = radial_zero + part_zero * row
        radial_one = radial_one + part_one * row
        table_rows.append(
            grad_table[kind : kind + 1]
            + jnp.sum(radial[0] * part_zero + radial[1] * part_one, axis=0, keepdims=True)
        )
    rest = jnp.concatenate(
        [radial_zero, radial_one] + table_rows + [read_row[...], jnp.zeros((1, N), jnp.float32)],
        axis=0,
    )
    up_piece = total[N + 24 : N + 40, :]
    charge_piece[...] = total[N + 8 : N + 24, :]
    for other in range(CROSSES):
        payload[other, 0:16, :] = up_piece
        payload[other, 16:40, :] = rest
    centers = basis_centers()
    sub = row_of((8, N))
    sub_table = sub & 3
    high_rows = sub < 4
    lane_rows = row_of((N, N))
    pull = [
        [pulls[number][kind * BASIS : (kind + 1) * BASIS] for number in range(4)]
        for kind in range(KINDS)
    ]

    def step(slot, carry):
        row = pl.ds(slot, 1)
        kind_row = jnp.broadcast_to(edges[3, row, :], (BASIS, N))
        own_pull = list(pull[KINDS - 1])
        for kind in range(KINDS - 1):
            mask = kind_row == float(kind)
            own_pull = [jnp.where(mask, pull[kind][n], own_pull[n]) for n in range(4)]
        radius = edges[4, row, :]
        envelope = edges[5, row, :]
        away = radius - centers
        bell = jnp.exp(-WIDTH_GAUSS * away * away)
        offset = [jnp.broadcast_to(edges[d, row, :], (BASIS, N)) for d in range(3)]
        by_basis = own_pull[0]
        for d in range(3):
            by_basis = by_basis + offset[d] * own_pull[1 + d]
        by_square = by_basis * bell * (edges[6, row, :] - (2.0 * envelope / radius) * away)
        basis = bell * envelope
        table = jnp.broadcast_to(places[0, row, :], (8, N)) == sub_table
        place = lane_rows == places[1, row, :]
        onehot = jnp.where(place, 1.0, 0.0).astype(jnp.bfloat16)
        centre, pieces = [], []
        for d in range(3):
            part = basis * own_pull[1 + d] + 2.0 * offset[d] * by_square
            centre.append(carry[d] + part)
            whole = jnp.broadcast_to(jnp.sum(part, axis=0, keepdims=True), (8, N))
            high = whole.astype(jnp.bfloat16).astype(jnp.float32)
            pieces.append(jnp.where(table, jnp.where(high_rows, high, whole - high), 0.0))
        rows = jnp.concatenate(pieces, axis=0).astype(jnp.bfloat16)
        return (*centre, carry[3] + half_dot(rows, onehot, 1, 1))

    zero = jnp.zeros((8, N), jnp.float32)
    out = lax.fori_loop(
        0, SLOTS, step, (zero, zero, zero, jnp.zeros((24, N), jnp.float32)), unroll=4
    )
    scattered = out[3]
    waves = total[N : N + 8, :]
    own_rows, one_rows, two_rows, three_rows = [], [], [], []
    for d in range(3):
        both = scattered[8 * d : 8 * d + 4] + scattered[8 * d + 4 : 8 * d + 8]
        centre = jnp.sum(out[d], axis=0, keepdims=True)
        own_rows.append(both[0:1] - centre + waves[d : d + 1])
        one_rows.append(both[1:2])
        two_rows.append(both[2:3])
        three_rows.append(both[3:4])
    pad = [jnp.zeros((5, N), jnp.float32)]
    own_grad[...] = jnp.concatenate(own_rows + pad, axis=0)
    to_one[...] = jnp.concatenate(one_rows + pad, axis=0)
    to_two[...] = jnp.concatenate(two_rows + pad, axis=0)
    to_three[...] = jnp.concatenate(three_rows + pad, axis=0)


def force_kernel(own_grad, from_minus_x, from_plus_x, from_minus_y, from_plus_y, index, forces):
    at = lane((8, N))
    faces = jnp.where(at < 64, from_minus_x[...], pltpu.roll(from_plus_x[...], 64, 1))
    total = own_grad[...]
    lane_rows = row_of((N, N))
    for number, piece in enumerate((from_minus_y[...], from_plus_y[...], faces)):
        onehot = jnp.where(lane_rows == index[number : number + 1, :], 1.0, 0.0)
        total = total + dot(piece, onehot, 1, 1)
    forces[...] = -total[0:3, :]


def structure_kernel(shared, kvec, embed, w_up, w_charge, factor, wave_high, wave_low, charges,
                     feature_high, feature_low):
    me = lax.axis_index(GROUP)
    at = pl.multiple_of(me * SHARD, SHARD)
    rows = jnp.concatenate(
        [kvec[:, pl.ds(at, SHARD)], jnp.zeros((5, SHARD), jnp.float32)], axis=0
    )
    turns = jnp.transpose(rows * (1.0 / (2.0 * math.pi)))
    table = jnp.concatenate([embed[...], jnp.zeros((2, N), jnp.float32)], axis=0)
    up = split(w_up[...])
    charge_w = split(w_charge[...])
    for member in range(MEMBERS):
        part = slice(member * N, (member + 1) * N)
        tail = shared[member, N : N + 8, :]
        onehot = (row_of((8, N)).astype(jnp.float32) == tail[3:4, :]).astype(jnp.float32)
        feature = dot(onehot, table, 0, 0) + dot_three(split(shared[member, 0:N, :]), up)
        high, low = split(feature)
        feature_high[part, :] = high
        feature_low[part, :] = low
        charges[part, :] = dot_three((high, low), charge_w)
        for chunk in range(SHARD // 64):
            waves = slice(chunk * 64, chunk * 64 + 64)
            angle = (
                turns[waves, 0:1] * tail[0:1, :]
                + turns[waves, 1:2] * tail[1:2, :]
                + turns[waves, 2:3] * tail[2:3, :]
            )
            angle = angle - jnp.round(angle)
            square = angle * angle
            cosine = jnp.full(square.shape, COS_POLY[-1], jnp.float32)
            for value in COS_POLY[-2::-1]:
                cosine = cosine * square + value
            sine = jnp.full(square.shape, SIN_POLY[-1], jnp.float32)
            for value in SIN_POLY[-2::-1]:
                sine = sine * square + value
            sine = sine * angle
            high, low = split(cosine)
            wave_high[waves, part] = high
            wave_low[waves, part] = low
            high, low = split(sine)
            waves = slice(SHARD + chunk * 64, SHARD + chunk * 64 + 64)
            wave_high[waves, part] = high
            wave_low[waves, part] = low
    project(wave_high, wave_low, feature_high[...], feature_low[...], factor)


def project(wave_high, wave_low, high, low, out):
    both = jnp.concatenate([high, low], axis=1)
    wide = half_dot(wave_high[...], both)
    total = wide[:, 0:N] + wide[:, N:] + half_dot(wave_low[...], high)
    out[...] = total.reshape(CROSSES, 16, N)


def projection_kernel(gathered, wave_high, wave_low, out):
    high, low = split(gathered[...].reshape(MEMBERS * N, N))
    project(wave_high, wave_low, high, low, out)


def sum_kernel(tiles, out):
    total = jnp.sum(tiles[...], axis=0)
    for other in range(out.shape[0]):
        out[other, :, :] = total


def filter_of(kfilter):
    me = lax.axis_index(GROUP)
    return kfilter[pl.ds(pl.multiple_of(me * SHARD, SHARD), SHARD), :] * SCALE


def waves_to_atoms(field, wave_high, wave_low):
    high, low = split(jnp.transpose(field))
    wide = half_dot(jnp.concatenate([high, low], axis=0), wave_high[...])
    return wide[0:N] + wide[N:] + half_dot(high, wave_low[...])


def potential_kernel(factor, w_charge, kfilter, wave_high, wave_low, out, weighted, charge_factor):
    scaled = filter_of(kfilter)
    charged = dot(factor[...], w_charge[...])
    charge_factor[...] = charged
    field = charged * jnp.concatenate([scaled, scaled], axis=0)
    weighted[...] = field
    total = waves_to_atoms(field, wave_high, wave_low)
    for member in range(MEMBERS):
        out[member, :, :] = total[:, member * N : (member + 1) * N]


def energy_kernel(tiles, active, species, embed, w_up, read,
                  shared, grad_out, energy, read_row, up_part):
    total = tiles[0]
    for member in range(1, MEMBERS):
        total = total + tiles[member]
    table = jnp.concatenate([embed[...], jnp.zeros((2, N), jnp.float32)], axis=0)
    onehot = (row_of((8, N)) == species[...]).astype(jnp.float32)
    act = active[...]
    combined = dot(onehot, table, 0, 0) + dot(act, w_up[...]) + jnp.transpose(total)
    logistic = sigmoid(combined)
    result = combined * logistic
    weights = read[...]
    energy[...] = dot(jnp.broadcast_to(weights, (8, N)), result, 1, 1)[0:1, :]
    read_row[...] = jnp.sum(result, axis=0, keepdims=True)
    grad = weights * (logistic * (1.0 + combined * (1.0 - logistic)))
    grad_out[...] = grad
    up_part[...] = dot(act, grad, 0, 0)
    for member in range(MEMBERS):
        shared[member, :, :] = grad


def wave_back_kernel(projected, factor, charge_factor, weighted, kfilter, kvec, wave_high, wave_low,
                     gathered, charges, shared, w_charge, up_part, out, grad_filter, phase):
    me = lax.axis_index(GROUP)
    at = pl.multiple_of(me * SHARD, SHARD)
    scaled = filter_of(kfilter)
    proj = projected[...]
    mixed = charge_factor[...] * proj
    grad_filter[...] = SCALE * (mixed[0:SHARD] + mixed[SHARD:])
    field = proj * jnp.concatenate([scaled, scaled], axis=0)
    by_charge = waves_to_atoms(field, wave_high, wave_low)
    charge_grad = dot(factor[...], field, 0, 0)
    active = jnp.concatenate([shared[member, 0:N, :] for member in range(MEMBERS)], axis=0)
    mix = dot_three(split(by_charge), split(active))
    up_grad = dot(mix, w_charge[...], 0, 1) + up_part[...]
    left = split(jnp.concatenate([weighted[...], field], axis=1))
    right = split(
        jnp.concatenate([gathered[...].reshape(MEMBERS * N, N), charges[...]], axis=1)
    )
    along = dot_three(left, right, 1, 1)
    cosine = wave_high[0:SHARD, :].astype(jnp.float32) + wave_low[0:SHARD, :].astype(jnp.float32)
    sine = wave_high[SHARD:, :].astype(jnp.float32) + wave_low[SHARD:, :].astype(jnp.float32)
    phase[...] = cosine * along[SHARD:] - sine * along[0:SHARD]
    rows = jnp.concatenate(
        [kvec[:, pl.ds(at, SHARD)], jnp.zeros((5, SHARD), jnp.float32)], axis=0
    )
    by_pos = dot(rows, phase[...])
    for member in range(MEMBERS):
        part = slice(member * N, (member + 1) * N)
        piece = slice(member * 16, (member + 1) * 16)
        out[member, 0:N, :] = by_charge[:, part]
        out[member, N : N + 8, :] = by_pos[:, part]
        out[member, N + 8 : N + 24, :] = charge_grad[piece]
        out[member, N + 24 : N + 40, :] = up_grad[piece]


def gather_sum_kernel(tiles, charge_piece, out):
    total = jnp.sum(tiles[...], axis=0)
    piece = charge_piece[...]
    for member in range(MEMBERS):
        out[member, 0:40, :] = total
        out[member, 40:56, :] = piece


def finish_kernel(tiles, grad_embed, grad_radial, grad_up, grad_charge, grad_read):
    mean = 1.0 / ATOMS
    total = tiles[0, 16:40, :]
    for member in range(1, MEMBERS):
        total = total + tiles[member, 16:40, :]
    total = total * mean
    for member in range(MEMBERS):
        grad_up[16 * member : 16 * member + 16, :] = tiles[member, 0:16, :] * mean
        grad_charge[16 * member : 16 * member + 16, :] = tiles[member, 40:56, :] * mean
    grad_radial[0, :, :] = total[0:8]
    grad_radial[1, :, :] = total[8:16]
    grad_embed[...] = total[16:22]
    grad_read[...] = total[22:23]


def body(
    positions, species, neighbours, face_sends, corner_sends,
    embed, radial, w_up, w_charge, kvec, kfilter, read,
):
    species = species.reshape(1, N)
    read = read.reshape(1, N)
    index = jnp.concatenate(
        [
            jnp.concatenate([face_sends[2], corner_sends[0], corner_sends[2]])[None],
            jnp.concatenate([face_sends[3], corner_sends[1], corner_sends[3]])[None],
            jnp.concatenate([face_sends[0], face_sends[1]])[None],
            jnp.zeros((5, N), jnp.int32),
        ],
        axis=0,
    )
    to_minus, to_plus, own_x = call(pack_kernel, (f32(8, N),) * 3, positions, species, index)
    from_plus_y = moved(to_minus, GY, -1)
    from_minus_y = moved(to_plus, GY, 1)
    to_minus, to_plus = relay(own_x, from_plus_y, from_minus_y)
    from_plus_x = moved(to_minus, GX, -1)
    from_minus_x = moved(to_plus, GX, 1)
    shared, active, invariants, vectors, sums, edges, places = call(
        edge_kernel,
        (
            f32(MEMBERS, N + 8, N), f32(N, N), f32(N, N), f32(3, N, N), f32(4, KINDS * BASIS, N),
            f32(7, SLOTS, N), jax.ShapeDtypeStruct((2, SLOTS, N), jnp.int32),
        ),
        positions, species, neighbours, from_plus_x, from_minus_x, from_plus_y, from_minus_y,
        embed, radial,
    )
    shared = lax.all_to_all(shared, GROUP, 0, 0)
    half = jax.ShapeDtypeStruct((2 * SHARD, MEMBERS * N), jnp.bfloat16)
    scratch = pltpu.VMEM((MEMBERS * N, N), jnp.bfloat16)
    factor, wave_high, wave_low, charges = call(
        structure_kernel,
        (f32(CROSSES, 16, N), half, half, f32(MEMBERS * N, N)),
        shared, kvec, embed, w_up, w_charge,
        scratch=(scratch, scratch),
    )

    def cross_sum(tiles):
        tiles = lax.all_to_all(tiles, CROSS, 0, 0)
        tiles = call(sum_kernel, f32(CROSSES, 16, N), tiles)
        return lax.all_to_all(tiles, CROSS, 0, 0).reshape(2 * SHARD, N)

    factor = cross_sum(factor)
    potential, weighted, charge_factor = call(
        potential_kernel,
        (f32(MEMBERS, N, N), f32(2 * SHARD, N), f32(2 * SHARD, N)),
        factor, w_charge, kfilter, wave_high, wave_low,
    )
    potential = lax.all_to_all(potential, GROUP, 0, 0)
    gathered, grad_out, energy, read_row, up_part = call(
        energy_kernel,
        (f32(MEMBERS, N, N), f32(N, N), f32(1, N), f32(1, N), f32(N, N)),
        potential, active, species, embed, w_up, read,
    )
    gathered = lax.all_to_all(gathered, GROUP, 0, 0)
    projected = cross_sum(
        call(projection_kernel, f32(CROSSES, 16, N), gathered, wave_high, wave_low)
    )
    tiles, grad_filter = call(
        wave_back_kernel,
        (f32(MEMBERS, N + 40, N), f32(SHARD, N)),
        projected, factor, charge_factor, weighted, kfilter, kvec, wave_high, wave_low,
        gathered, charges, shared, w_charge, up_part,
        scratch=(pltpu.VMEM((SHARD, MEMBERS * N), jnp.float32),),
    )
    grad_filter = lax.all_gather(grad_filter, GROUP, axis=0, tiled=True)
    tiles = lax.all_to_all(tiles, GROUP, 0, 0)
    payload, charge_piece, own_grad, to_one, to_two, to_three = call(
        edge_back_kernel,
        (f32(CROSSES, 40, N), f32(16, N)) + (f32(8, N),) * 4,
        tiles, shared, active, invariants, vectors, sums, edges, places, embed, radial, w_up,
        w_charge, species, grad_out, read_row,
    )
    back_minus_x = moved(to_one, GX, 1)
    back_plus_x = moved(to_two, GX, -1)
    to_plus, to_minus = relay(to_three, back_minus_x, back_plus_x)
    back_minus_y = moved(to_plus, GY, 1)
    back_plus_y = moved(to_minus, GY, -1)
    forces = call(
        force_kernel, f32(3, N),
        own_grad, back_minus_x, back_plus_x, back_minus_y, back_plus_y, index,
    )
    payload = lax.all_to_all(payload, CROSS, 0, 0)
    payload = call(gather_sum_kernel, f32(MEMBERS, 56, N), payload, charge_piece)
    payload = lax.all_to_all(payload, GROUP, 0, 0)
    grad_embed, grad_radial, grad_up, grad_charge, grad_read = call(
        finish_kernel,
        (f32(KINDS, N), f32(2, BASIS, N), f32(N, N), f32(N, N), f32(1, N)),
        payload,
    )
    return (
        energy.reshape(N), forces, grad_embed, grad_radial, grad_up, grad_charge, grad_filter,
        grad_read.reshape(N),
    )


def solution(mesh):
    fine = Mesh(mesh.devices.reshape(4, 4, 2, 2, 4), ALL)
    atoms = P(ALL)
    rows = P(None, ALL)
    return jax.shard_map(
        body,
        mesh=fine,
        in_specs=(rows, atoms, rows, rows, rows) + (P(),) * 7,
        out_specs=(atoms, rows) + (P(),) * 6,
        check_vma=False,
    )
```

time: 1290 us -> 224 us (0.17)
  waiting for transfers between devices: 684 us -> 24.5 us
  matrix products: 168 us -> 0 us
  local copies, waits for them, and re-layouts: 147 us -> 4.96 us
  other arithmetic: 135 us -> 0.22 us
  blocking collectives: 82.7 us -> 127 us
  Pallas kernels: 0 us -> 19.8 us
    psum x3 -> x0, waiting for transfers between devices: 669 us -> none  [the longest x1 262 us: body(): cos_factor, sin_factor = lax.psum((part_cos, part_sin), ('gx', 'gy'))]
    dot_general x97 -> x0, matrix products: 153 us -> none  [the longest x61 94.5 us: product(): jnp.dot(left, right, precision=HIGHEST, preferred_element_type=jnp.float32)]
    all_to_all x0 -> x8, blocking collectives: none -> 127 us  [the longest x2 32.2 us: cross_sum(): return lax.all_to_all(tiles, CROSS, 0, 0).reshape(2 * SHARD, N)]
    gather x32 -> x0, local copies, waits for them, and re-layouts: 99.6 us -> none  [the longest x16 50.9 us: edge_block(): offset_vec = ext_pos[:, index] - coords[:, None, :]]
    scatter-add x9 -> x0, other arithmetic: 95.5 us -> none  [the longest x4 46.4 us: edge_block(): offset_vec = ext_pos[:, index] - coords[:, None, :]]
    psum x1 -> x0, blocking collectives: 82.7 us -> none  [body(): lax.psum((grad_table, grad_weights, grad_wup, grad_wcharge, filter_term,...]
    ppermute x24 -> x8, starting transfers between devices: 41.7 us -> 15.1 us  [moved(): lax.ppermute(value, axes, [(s, (s + steps) % count) for s in range(count)])]
    pallas_call x0 -> x15, Pallas kernels: none -> 19.8 us  [call(): pl.pallas_call(kernel, out_shape=out_shape, scratch_shapes=list(scratch),...]
  transfers between devices with their start and end apart: 27 -> 11, of which waited for: 10 -> 8; matrix products, arithmetic and copies ran while one was open for 1% -> 0% of each run, Pallas kernels for 0% -> 3%
where the time goes in v1:
time: 224 us; the launch traced here: 220 us
  blocking collectives  127 us (57%)
  starting transfers between devices  29.4 us (13%)
  waiting for transfers between devices  24.5 us (11%)
  Pallas kernels  19.8 us (9%)
  between operations  14.1 us (6%)
  local copies, waits for them, and re-layouts  4.96 us (2%)
    all_to_all x2, blocking collectives, cross_sum(): return lax.all_to_all(tiles, CROSS, 0, 0).reshape(2 * SHARD, N)  32.2 us
    all_to_all x2, blocking collectives, cross_sum(): tiles = lax.all_to_all(tiles, CROSS, 0, 0)  26.8 us
    all_to_all x1, blocking collectives, body(): payload = lax.all_to_all(payload, CROSS, 0, 0)  20.9 us
    pallas_call x15, Pallas kernels, call(): pl.pallas_call(kernel, out_shape=out_shape, scratch_shapes=list(scratch),...  19.8 us
    all_to_all x1, blocking collectives, body(): shared = lax.all_to_all(shared, GROUP, 0, 0)  19.3 us
    all_to_all x1, blocking collectives, body(): potential = lax.all_to_all(potential, GROUP, 0, 0)  15.4 us
    ppermute x8, starting transfers between devices, moved(): lax.ppermute(value, axes, [(s, (s + steps) % count) for s in range(count)])  15.1 us
    ppermute x8, waiting for transfers between devices, moved(): lax.ppermute(value, axes, [(s, (s + steps) % count) for s in range(count)])  13.3 us
  transfers between devices with their start and end apart: 11, of which 8 were waited for; matrix products, arithmetic and copies ran while one was open for 0% of the time, Pallas kernels for 3%

profile of v1, /device:TPU:1, one launch (start us, length us, event | category | flops | bytes accessed | tf_op | source)
XLA Modules:
  0.0 220.2 jit_solution(17697240931066043484)
XLA Ops:
  7.2 0.0 copy-start.10
  7.2 0.1 pad.3.clone
  7.3 0.6 copy-done.10
  7.9 0.7 copy-done.11
  8.5 0.1 add_bitcast_fusion.2
  8.6 0.1 add_bitcast_fusion
  8.7 0.1 add_add_fusion.index
  8.8 0.6 copy-done.7
  9.4 0.0 copy-done.8
  9.4 0.1 shard_map.179
  9.5 4.7 %collective-permute-start = (f32[8,128]{1,0:T(8,128)S(1)}, f32[8,128]{1,0:T(8,128)S(1)}, u32[]{:S(2)}, u32[]{:S(2)}) collective-permute-start(f32[8,128]{1,0:T(8,128)S(1)} %get-tuple-element.48), channel_id=1, source_target_pairs={{0,7},{1,0},{2,1},{3,2},{4,3},{5,4},{6,5},{7,6},{8,15},{9,8},{10,9... | collective-permute-start | bytes 12296 | tf_op jit(solution)/shard_map/ppermute | solution.py:149
  14.2 0.0 collective-permute-start.1
  14.2 0.8 collective-permute-done.first.from_plus_y
  14.9 3.8 %collective-permute-done.1.second.from_minus_y = f32[8,128]{1,0:T(8,128)S(1)} collective-permute-done((f32[8,128]{1,0:T(8,128)S(1)}, f32[8,128]{1,0:T(8,128)S(1)}, u32[]{:S(2)}, u32[]{:S(2)}) %collective-permute-start.1) | collective-permute-done | bytes 4128 | tf_op jit(solution)/shard_map/ppermute | solution.py:149
  18.7 0.1 shard_map.180
  18.8 2.1 collective-permute-start.2
  20.9 3.0 %collective-permute-start.3 = (f32[8,128]{1,0:T(8,128)S(1)}, f32[8,128]{1,0:T(8,128)S(1)}, u32[]{:S(2)}, u32[]{:S(2)}) collective-permute-start(f32[8,128]{1,0:T(8,128)S(1)} %get-tuple-element.51), channel_id=1, source_target_pairs={{0,8},{8,16},{16,24},{24,32},{32,40},{40,48},{48,56},{56,64},{64,7... | collective-permute-start | bytes 12296 | tf_op jit(solution)/shard_map/ppermute | solution.py:149
  23.9 1.2 collective-permute-done.2.from_plus_x
  25.1 2.4 %collective-permute-done.3.from_minus_x = f32[8,128]{1,0:T(8,128)S(1)} collective-permute-done((f32[8,128]{1,0:T(8,128)S(1)}, f32[8,128]{1,0:T(8,128)S(1)}, u32[]{:S(2)}, u32[]{:S(2)}) %collective-permute-start.3) | collective-permute-done | bytes 4128 | tf_op jit(solution)/shard_map/ppermute | solution.py:149
  27.5 0.0 copy-done.6
  27.5 0.0 copy-done.4
  27.5 0.0 copy-done.5
  27.5 1.4 shard_map.181
  28.9 0.0 copy-start.1
  28.9 0.0 copy-start.2
  28.9 0.0 copy-start.3
  29.0 19.3 %all_to_all.50.shared.common = f32[8,136,128]{2,1,0:T(8,128)S(1)} all-to-all(f32[8,136,128]{2,1,0:T(8,128)S(1)} %get-tuple-element.52), channel_id=1, replica_groups=mesh['y'=4,'zh'=4,'c'=2,'zl'=2,'x'=4] {'c','x'}, dimensions={0} | all-to-all | bytes 1114112 | tf_op jit(solution)/shard_map/all_to_all | solution.py:568
  48.2 0.0 copy-done.1
  48.2 0.0 copy-done.2
  48.2 0.0 copy-start
  48.3 3.8 %shard_map.182 = (f32[32,16,128]{2,1,0:T(8,128)S(1)}, bf16[512,1024]{1,0:T(8,128)(2,1)S(1)}, bf16[512,1024]{1,0:T(8,128)(2,1)S(1)}, f32[1024,128]{1,0:T(8,128)S(1)}) custom-call(f32[8,136,128]{2,1,0:T(8,128)S(1)} %all_to_all.50.shared.common, f32[3,2048]{1,0:T(4,128)S(1)} %copy-done.3, f32[6,128]{1,0:T(8,128)S(1)} %copy-done.4, f32[128,128]{1,0:T(8,128)S(1)} %copy-done.2, ...), custom_call_target="tpu_custom_call" | custom-call | tf_op jit(solution)/shard_map/pallas_call | solution.py:102
  52.1 13.2 %all_to_all.51.tiles = f32[32,16,128]{2,1,0:T(8,128)S(1)} all-to-all(f32[32,16,128]{2,1,0:T(8,128)S(1)} %get-tuple-element.53), channel_id=1, replica_groups=mesh['y'=4,'zh'=4,'c'=2,'zl'=2,'x'=4] {'y','zh','zl'}, dimensions={0} | all-to-all | bytes 524288 | tf_op jit(solution)/shard_map/all_to_all | solution.py:579
  65.2 0.1 shard_map.183
  65.3 16.0 %all_to_all.52 = f32[32,16,128]{2,1,0:T(8,128)S(1)} all-to-all(f32[32,16,128]{2,1,0:T(8,128)S(1)} %shard_map.183), channel_id=1, replica_groups=mesh['y'=4,'zh'=4,'c'=2,'zl'=2,'x'=4] {'y','zh','zl'}, dimensions={0} | all-to-all | bytes 524288 | tf_op jit(solution)/shard_map/all_to_all | solution.py:581
  81.3 1.3 shard_map.184
  82.6 15.4 %all_to_all.53.tiles = f32[8,128,128]{2,1,0:T(8,128)S(1)} all-to-all(f32[8,128,128]{2,1,0:T(8,128)S(1)} %get-tuple-element.56), channel_id=1, replica_groups=mesh['y'=4,'zh'=4,'c'=2,'zl'=2,'x'=4] {'c','x'}, dimensions={0} | all-to-all | bytes 1048576 | tf_op jit(solution)/shard_map/all_to_all | solution.py:589
  98.0 0.7 copy-done.9
  98.6 1.2 shard_map.185
  99.8 12.6 %all_to_all.54.gathered = f32[8,128,128]{2,1,0:T(8,128)S(1)} all-to-all(f32[8,128,128]{2,1,0:T(8,128)S(1)} %get-tuple-element.59), channel_id=1, replica_groups=mesh['y'=4,'zh'=4,'c'=2,'zl'=2,'x'=4] {'c','x'}, dimensions={0} | all-to-all | bytes 1048576 | tf_op jit(solution)/shard_map/all_to_all | solution.py:595
  112.4 0.7 shard_map.186
  113.1 13.7 %all_to_all.55.tiles = f32[32,16,128]{2,1,0:T(8,128)S(1)} all-to-all(f32[32,16,128]{2,1,0:T(8,128)S(1)} %shard_map.186), channel_id=1, replica_groups=mesh['y'=4,'zh'=4,'c'=2,'zl'=2,'x'=4] {'y','zh','zl'}, dimensions={0} | all-to-all | bytes 524288 | tf_op jit(solution)/shard_map/all_to_all | solution.py:579
  126.8 0.1 shard_map.187
  126.8 16.2 %all_to_all.56 = f32[32,16,128]{2,1,0:T(8,128)S(1)} all-to-all(f32[32,16,128]{2,1,0:T(8,128)S(1)} %shard_map.187), channel_id=1, replica_groups=mesh['y'=4,'zh'=4,'c'=2,'zl'=2,'x'=4] {'y','zh','zl'}, dimensions={0} | all-to-all | bytes 524288 | tf_op jit(solution)/shard_map/all_to_all | solution.py:581
  143.0 3.9 %shard_map.188 = (f32[8,168,128]{2,1,0:T(8,128)}, f32[256,128]{1,0:T(8,128)}) custom-call(f32[512,128]{1,0:T(8,128)S(1)} %bitcast.30, f32[512,128]{1,0:T(8,128)S(1)} %bitcast.29, f32[512,128]{1,0:T(8,128)S(1)} %get-tuple-element.60.charge_factor, f32[512,128]{1,0:T(8,128)S(1)} %get-tuple-element.61.weighted, f32[2048,128]{1,0:T(8,128)S(1)} %copy-done, ...), custom_call_target="tpu_custom_call" | custom-call | tf_op jit(solution)/shard_map/pallas_call | solution.py:102
  147.0 7.1 %all-to-all-start.7 = ((f32[8,168,128]{2,1,0:T(8,128)}), f32[8,168,128]{2,1,0:T(8,128)S(1)}, u32[]{:S(2)}, u32[]{:S(2)}) async-start(f32[8,168,128]{2,1,0:T(8,128)} %get-tuple-element.64), calls=%async_computation.7 | async-start | bytes 1376256 | tf_op jit(solution)/shard_map/all_to_all | solution.py:607
  154.0 0.7 all-gather.2.cloned.1.call-update
  154.7 10.4 %all-to-all-done.7.tiles = f32[8,168,128]{2,1,0:T(8,128)S(1)} async-done(((f32[8,168,128]{2,1,0:T(8,128)}), f32[8,168,128]{2,1,0:T(8,128)S(1)}, u32[]{:S(2)}, u32[]{:S(2)}) %all-to-all-start.7) | async-done | bytes 688160 | tf_op jit(solution)/shard_map/all_to_all | solution.py:607
  165.1 4.7 %shard_map.189 = (f32[32,40,128]{2,1,0:T(8,128)S(1)}, f32[16,128]{1,0:T(8,128)S(1)}, f32[8,128]{1,0:T(8,128)S(1)}, f32[8,128]{1,0:T(8,128)S(1)}, f32[8,128]{1,0:T(8,128)S(1)}, /*index=5*/f32[8,128]{1,0:T(8,128)S(1)}) custom-call(f32[8,168,128]{2,1,0:T(8,128)S(1)} %all-to-all-done.7.tiles, f32[8,136,128]{2,1,0:T(8,128)S(1)} %all_to_all.50.shared.common, ...), custom_call_target="tpu_custom_call" | custom-call | tf_op jit(solution)/shard_map/pallas_call | solution.py:102
  169.8 20.9 %all_to_all.57.tiles = f32[32,40,128]{2,1,0:T(8,128)S(1)} all-to-all(f32[32,40,128]{2,1,0:T(8,128)S(1)} %get-tuple-element.78), channel_id=1, replica_groups=mesh['y'=4,'zh'=4,'c'=2,'zl'=2,'x'=4] {'y','zh','zl'}, dimensions={0} | all-to-all | bytes 1310720 | tf_op jit(solution)/shard_map/all_to_all | solution.py:623
  190.8 0.7 shard_map.192
  191.5 7.2 %all-to-all-start.9 = ((f32[8,56,128]{2,1,0:T(8,128)}), f32[8,56,128]{2,1,0:T(8,128)S(1)}, u32[]{:S(2)}, u32[]{:S(2)}) async-start(f32[8,56,128]{2,1,0:T(8,128)} %shard_map.192), calls=%async_computation.9 | async-start | bytes 458752 | tf_op jit(solution)/shard_map/all_to_all | solution.py:625
  198.8 1.8 collective-permute-start.4
  200.5 0.0 collective-permute-start.5
  200.5 0.8 collective-permute-done.4.first.from_minus_x
  201.3 3.5 %collective-permute-done.5.second.from_plus_x = f32[8,128]{1,0:T(8,128)S(1)} collective-permute-done((f32[8,128]{1,0:T(8,128)S(1)}, f32[8,128]{1,0:T(8,128)S(1)}, u32[]{:S(2)}, u32[]{:S(2)}) %collective-permute-start.5) | collective-permute-done | bytes 4128 | tf_op jit(solution)/shard_map/ppermute | solution.py:149
  204.8 0.1 shard_map.190
  204.8 1.6 collective-permute-start.6
  206.4 2.0 collective-permute-start.7
  208.4 1.0 collective-permute-done.6.from_minus_y
  209.4 0.0 collective-permute-done.7.from_plus_y
  209.4 1.0 shard_map.191
  210.4 0.0 all-to-all-done.9.tiles
  210.4 0.7 shard_map.193
  211.1 2.3 %copy.21 = f32[2048,128]{1,0:T(8,128)} copy(f32[2048,128]{1,0:T(8,128)} %all-gather.2.cloned.1.call-done) | data formatting | bytes 2097152
  (14 shorter events, 0.0 us)
Async XLA Ops:
  7.2 0.7 copy-start.10
  7.8 0.7 copy-start.11
  8.5 18.9 %copy-start.6 = (s32[64,128]{1,0:T(8,128)S(1)}, s32[64,128]{1,0:T(8,128)}, u32[]{:S(2)}) copy-start(s32[64,128]{1,0:T(8,128)} %nbr.1) | copy-start | bytes 98308
  8.7 0.7 copy-start.7
  8.8 0.7 copy-start.8
  9.5 5.4 %collective-permute-start = (f32[8,128]{1,0:T(8,128)S(1)}, f32[8,128]{1,0:T(8,128)S(1)}, u32[]{:S(2)}, u32[]{:S(2)}) collective-permute-start(f32[8,128]{1,0:T(8,128)S(1)} %get-tuple-element.48), channel_id=1, source_target_pairs={{0,7},{1,0},{2,1},{3,2},{4,3},{5,4},{6,5},{7,6},{8,15},{9,8},{10,9... | collective-permute-start | bytes 12296 | tf_op jit(solution)/shard_map/ppermute | solution.py:149
  14.2 4.6 %collective-permute-start.1 = (f32[8,128]{1,0:T(8,128)S(1)}, f32[8,128]{1,0:T(8,128)S(1)}, u32[]{:S(2)}, u32[]{:S(2)}) collective-permute-start(f32[8,128]{1,0:T(8,128)S(1)} %get-tuple-element.49), channel_id=1, source_target_pairs={{0,1},{1,2},{2,3},{3,4},{4,5},{5,6},{6,7},{7,0},{8,9},{9,10},{10,1... | collective-permute-start | bytes 12296 | tf_op jit(solution)/shard_map/ppermute | solution.py:149
  18.7 8.7 %copy-start.4 = (f32[6,128]{1,0:T(8,128)S(1)}, f32[6,128]{1,0:T(8,128)}, u32[]{:S(2)}) copy-start(f32[6,128]{1,0:T(8,128)} %embed.7) | copy-start | bytes 9220
  18.7 8.7 %copy-start.5 = (f32[2,8,128]{2,1,0:T(8,128)S(1)}, f32[2,8,128]{2,1,0:T(8,128)}, u32[]{:S(2)}) copy-start(f32[2,8,128]{2,1,0:T(8,128)} %radial.3) | copy-start | bytes 24580
  18.8 6.3 %collective-permute-start.2 = (f32[8,128]{1,0:T(8,128)S(1)}, f32[8,128]{1,0:T(8,128)S(1)}, u32[]{:S(2)}, u32[]{:S(2)}) collective-permute-start(f32[8,128]{1,0:T(8,128)S(1)} %get-tuple-element.50), channel_id=1, source_target_pairs={{0,248},{8,0},{16,8},{24,16},{32,24},{40,32},{48,40},{56,48},{64,5... | collective-permute-start | bytes 12296 | tf_op jit(solution)/shard_map/ppermute | solution.py:149
  20.9 6.5 %collective-permute-start.3 = (f32[8,128]{1,0:T(8,128)S(1)}, f32[8,128]{1,0:T(8,128)S(1)}, u32[]{:S(2)}, u32[]{:S(2)}) collective-permute-start(f32[8,128]{1,0:T(8,128)S(1)} %get-tuple-element.51), channel_id=1, source_target_pairs={{0,8},{8,16},{16,24},{24,32},{32,40},{40,48},{48,56},{56,64},{64,7... | collective-permute-start | bytes 12296 | tf_op jit(solution)/shard_map/ppermute | solution.py:149
  28.9 19.3 %copy-start.1 = (f32[128,128]{1,0:T(8,128)S(1)}, f32[128,128]{1,0:T(8,128)}, u32[]{:S(2)}) copy-start(f32[128,128]{1,0:T(8,128)} %w_charge.7) | copy-start | bytes 196612
  28.9 19.3 %copy-start.2 = (f32[128,128]{1,0:T(8,128)S(1)}, f32[128,128]{1,0:T(8,128)}, u32[]{:S(2)}) copy-start(f32[128,128]{1,0:T(8,128)} %w_up.5) | copy-start | bytes 196612
  28.9 19.3 %copy-start.3 = (f32[3,2048]{1,0:T(4,128)S(1)}, f32[3,2048]{1,0:T(4,128)}, u32[]{:S(2)}) copy-start(f32[3,2048]{1,0:T(4,128)} %kvec.3) | copy-start | bytes 73732
  48.2 33.0 %copy-start = (f32[2048,128]{1,0:T(8,128)S(1)}, f32[2048,128]{1,0:T(8,128)}, u32[]{:S(2)}) copy-start(f32[2048,128]{1,0:T(8,128)} %kfilter.3) | copy-start | bytes 3145732
  98.0 0.7 copy-start.9
  147.0 18.2 %all-to-all-start.7 = ((f32[8,168,128]{2,1,0:T(8,128)}), f32[8,168,128]{2,1,0:T(8,128)S(1)}, u32[]{:S(2)}, u32[]{:S(2)}) async-start(f32[8,168,128]{2,1,0:T(8,128)} %get-tuple-element.64), calls=%async_computation.7 | async-start | bytes 1376256 | tf_op jit(solution)/shard_map/all_to_all | solution.py:607
  154.0 56.4 %all-gather.2.cloned.1.call-start = ((), (), s32[]{:S(2)}) async-start(), calls=%async_computation.10 | async-start | bytes 1179648 | tf_op jit(solution)/shard_map/all_gather | solution.py:606
  191.5 18.9 %all-to-all-start.9 = ((f32[8,56,128]{2,1,0:T(8,128)}), f32[8,56,128]{2,1,0:T(8,128)S(1)}, u32[]{:S(2)}, u32[]{:S(2)}) async-start(f32[8,56,128]{2,1,0:T(8,128)} %shard_map.192), calls=%async_computation.9 | async-start | bytes 458752 | tf_op jit(solution)/shard_map/all_to_all | solution.py:625
  198.8 2.5 %collective-permute-start.4 = (f32[8,128]{1,0:T(8,128)S(1)}, f32[8,128]{1,0:T(8,128)S(1)}, u32[]{:S(2)}, u32[]{:S(2)}) collective-permute-start(f32[8,128]{1,0:T(8,128)S(1)} %get-tuple-element.73), channel_id=1, source_target_pairs={{0,8},{8,16},{16,24},{24,32},{32,40},{40,48},{48,56},{56,64},{64,7... | collective-permute-start | bytes 12296 | tf_op jit(solution)/shard_map/ppermute | solution.py:149
  200.5 4.2 %collective-permute-start.5 = (f32[8,128]{1,0:T(8,128)S(1)}, f32[8,128]{1,0:T(8,128)S(1)}, u32[]{:S(2)}, u32[]{:S(2)}) collective-permute-start(f32[8,128]{1,0:T(8,128)S(1)} %get-tuple-element.74), channel_id=1, source_target_pairs={{0,248},{8,0},{16,8},{24,16},{32,24},{40,32},{48,40},{56,48},{64,5... | collective-permute-start | bytes 12296 | tf_op jit(solution)/shard_map/ppermute | solution.py:149
  204.8 4.6 %collective-permute-start.6 = (f32[8,128]{1,0:T(8,128)S(1)}, f32[8,128]{1,0:T(8,128)S(1)}, u32[]{:S(2)}, u32[]{:S(2)}) collective-permute-start(f32[8,128]{1,0:T(8,128)S(1)} %get-tuple-element.76), channel_id=1, source_target_pairs={{0,1},{1,2},{2,3},{3,4},{4,5},{5,6},{6,7},{7,0},{8,9},{9,10},{10,1... | collective-permute-start | bytes 12296 | tf_op jit(solution)/shard_map/ppermute | solution.py:149
  206.4 3.0 %collective-permute-start.7 = (f32[8,128]{1,0:T(8,128)S(1)}, f32[8,128]{1,0:T(8,128)S(1)}, u32[]{:S(2)}, u32[]{:S(2)}) collective-permute-start(f32[8,128]{1,0:T(8,128)S(1)} %get-tuple-element.77), channel_id=1, source_target_pairs={{0,7},{1,0},{2,1},{3,2},{4,3},{5,4},{6,5},{7,6},{8,15},{9,8},{10,9... | collective-permute-start | bytes 12296 | tf_op jit(solution)/shard_map/ppermute | solution.py:149
Sparse Core Ops, SparseCore 0:
  156.7 22.1 all-gather.1

commit v2 on v1

--- a/solution.py
+++ b/solution.py
@@ -30,6 +30,8 @@
 CROSS = ("y", "zh", "zl")
 MEMBERS = 8
 CROSSES = 32
+DEPTH = ("zh", "zl")
+PLANE = ("y", "x")
 
 COS_POLY = None
 SIN_POLY = None
@@ -38,14 +40,14 @@
 def _fit():
     import numpy as np
 
-    count = 9
     points = (1.0 + np.cos(np.pi * (np.arange(200) + 0.5) / 200)) / 8.0
     root = np.sqrt(points)
-    matrix = np.vander(points * 4.0, count, increasing=True)
-    cosine = np.linalg.lstsq(matrix, np.cos(2 * np.pi * root), rcond=None)[0]
-    sine = np.linalg.lstsq(matrix, np.sin(2 * np.pi * root) / root, rcond=None)[0]
-    powers = 4.0 ** np.arange(count)
-    return ([float(v) for v in cosine * powers], [float(v) for v in sine * powers])
+    found = []
+    for count, value in ((7, np.cos(2 * np.pi * root)), (6, np.sin(2 * np.pi * root) / root)):
+        matrix = np.vander(points * 4.0, count, increasing=True)
+        terms = np.linalg.lstsq(matrix, value, rcond=None)[0] * 4.0 ** np.arange(count)
+        found.append([float(term) for term in terms])
+    return found
 
 
 COS_POLY, SIN_POLY = _fit()
@@ -117,36 +119,54 @@
     )
 
 
-def pack_kernel(pos, species, index, to_minus, to_plus, own):
+def joined(face, corner, faces, corners):
+    return jnp.concatenate(
+        [face[f : f + 1, :] for f in faces] + [corner[f : f + 1, :] for f in corners], axis=1
+    )
+
+
+def pack_kernel(pos, species, face, corner, near, far, own):
+    even = lax.axis_index("x") % 2 == 0
     rows = [pos[0:1, :], pos[1:2, :], pos[2:3, :], species[...].astype(jnp.float32)]
-    where_from = index[...]
+    where_from = jnp.concatenate(
+        [
+            joined(face, corner, (2,), (0, 2)),
+            joined(face, corner, (3,), (1, 3)),
+            joined(face, corner, (0, 1), ()),
+            jnp.zeros((5, N), jnp.int32),
+        ],
+        axis=0,
+    )
     for number, row in enumerate(rows):
         got = take(row, where_from)
-        to_minus[number : number + 1, :] = got[0:1, :]
-        to_plus[number : number + 1, :] = got[1:2, :]
+        near[number : number + 1, :] = jnp.where(even, got[1:2, :], got[0:1, :])
+        far[number : number + 1, :] = jnp.where(even, got[0:1, :], got[1:2, :])
         own[number : number + 1, :] = got[2:3, :]
     zero = jnp.zeros((4, N), jnp.float32)
-    to_minus[4:8, :] = zero
-    to_plus[4:8, :] = zero
+    near[4:8, :] = zero
+    far[4:8, :] = zero
     own[4:8, :] = zero
 
 
-def relay_kernel(own, first, second, one, two):
+def swapped(value, axes, odd):
+    count = math.prod(lax.axis_size(axis) for axis in axes)
+    places = [(at, ((((at + odd) % count) ^ 1) - odd) % count) for at in range(count)]
+    return lax.ppermute(value, axes, places)
+
+
+def relay_kernel(own, near, far, one, two):
     at = lane((8, N))
-    a, b, d = own[...], first[...], second[...]
-    one[...] = jnp.where(at < 64, a, jnp.where(at < 96, b, pltpu.roll(d, 32, 1)))
-    two[...] = jnp.where(at < 64, pltpu.roll(a, 64, 1), jnp.where(at < 96, pltpu.roll(b, 96, 1), d))
-
-
-def relay(own, first, second):
-    return call(relay_kernel, (f32(8, N), f32(8, N)), own, first, second)
-
-
-def moved(value, axes, steps):
-    count = 1
-    for axis in axes:
-        count *= lax.axis_size(axis)
-    return lax.ppermute(value, axes, [(s, (s + steps) % count) for s in range(count)])
+    even = lax.axis_index("x") % 2 == 0
+    a = own[...]
+    b = jnp.where(even, near[...], far[...])
+    d = jnp.where(even, far[...], near[...])
+    to_minus = jnp.where(at < 64, a, jnp.where(at < 96, b, pltpu.roll(d, 32, 1)))
+    to_plus = jnp.where(
+        at < 64, pltpu.roll(a, 64, 1), jnp.where(at < 96, pltpu.roll(b, 96, 1), d)
+    )
+    first = lax.axis_index("c") == 0
+    one[...] = jnp.where(first, to_plus, to_minus)
+    two[...] = jnp.where(first, to_minus, to_plus)
 
 
 def pair_weights(embed, radial):
@@ -163,13 +183,18 @@
 
 
 def edge_kernel(
-    pos, species, nbr, from_plus_x, from_minus_x, from_plus_y, from_minus_y, embed, radial,
+    pos, species, nbr, near_x, far_x, near_y, far_y, embed, radial,
     shared, active, invariants, vectors, sums, edges, places,
 ):
     at = lane((8, N))
     own = [pos[0:1, :], pos[1:2, :], pos[2:3, :], species[...].astype(jnp.float32)]
-    first, second = from_plus_x[...], from_minus_x[...]
-    third = jnp.where(at < 64, from_plus_y[...], pltpu.roll(from_minus_y[...], 64, 1))
+    core_zero = lax.axis_index("c") == 0
+    even = lax.axis_index("x") % 2 == 0
+    first = jnp.where(core_zero, near_x[...], far_x[...])
+    second = jnp.where(core_zero, far_x[...], near_x[...])
+    plus_y = jnp.where(even, near_y[...], far_y[...])
+    minus_y = jnp.where(even, far_y[...], near_y[...])
+    third = jnp.where(at < 64, plus_y, pltpu.roll(minus_y, 64, 1))
     line = lane((1, N))
     corner_y = jnp.where(line < 64, 0.0, jnp.where(line < 96, DOMAIN, -DOMAIN))
     tables = [
@@ -253,9 +278,9 @@
 
 
 def edge_back_kernel(
-    tiles, common, active, invariants, vectors, sums, edges, places, embed, radial, w_up, w_charge,
+    tiles, active, invariants, vectors, sums, edges, places, embed, radial, w_up, w_charge,
     species, grad_out, read_row,
-    payload, charge_piece, own_grad, to_one, to_two, to_three,
+    payload, own_grad, charge_piece,
 ):
     total = tiles[0]
     for member in range(1, MEMBERS):
@@ -293,11 +318,8 @@
         [radial_zero, radial_one] + table_rows + [read_row[...], jnp.zeros((1, N), jnp.float32)],
         axis=0,
     )
-    up_piece = total[N + 24 : N + 40, :]
-    charge_piece[...] = total[N + 8 : N + 24, :]
-    for other in range(CROSSES):
-        payload[other, 0:16, :] = up_piece
-        payload[other, 16:40, :] = rest
+    up_piece = total[N + 8 : N + 24, :]
+    charge_piece[...] = total[N + 24 : N + 40, :]
     centers = basis_centers()
     sub = row_of((8, N))
     sub_table = sub & 3
@@ -354,20 +376,129 @@
         three_rows.append(both[3:4])
     pad = [jnp.zeros((5, N), jnp.float32)]
     own_grad[...] = jnp.concatenate(own_rows + pad, axis=0)
-    to_one[...] = jnp.concatenate(one_rows + pad, axis=0)
-    to_two[...] = jnp.concatenate(two_rows + pad, axis=0)
-    to_three[...] = jnp.concatenate(three_rows + pad, axis=0)
-
-
-def force_kernel(own_grad, from_minus_x, from_plus_x, from_minus_y, from_plus_y, index, forces):
-    at = lane((8, N))
-    faces = jnp.where(at < 64, from_minus_x[...], pltpu.roll(from_plus_x[...], 64, 1))
-    total = own_grad[...]
+    depth_of = [depth_after(step_x, step_y) for step_x, step_y in TABLE_DIRS]
+    line = lane((8, N))
+    ones = jnp.concatenate(one_rows + pad, axis=0)
+    twos = jnp.concatenate(two_rows + pad, axis=0)
+    threes = jnp.concatenate(three_rows + pad, axis=0)
+    home_one = segments(line, depth_of[0:3])
+    home_two = segments(line, depth_of[3:6])
+    home_three = jnp.where(line < 64, depth_of[6], depth_of[7])
+    for other in range(8):
+        payload[other, 0:16, :] = up_piece
+        payload[other, 16:40, :] = rest
+        payload[other, 40:48, :] = pack_six(
+            jnp.where(home_one == other, ones, 0.0), jnp.where(home_two == other, twos, 0.0)
+        )
+        payload[other, 48:56, :] = jnp.where(home_three == other, threes, 0.0)
+
+
+TABLE_DIRS = ((1, 0), (1, 1), (1, -1), (-1, 0), (-1, 1), (-1, -1), (0, 1), (0, -1))
+
+
+def segments(line, values):
+    return jnp.where(line < 64, values[0], jnp.where(line < 96, values[1], values[2]))
+
+
+def pack_six(one, two):
+    return jnp.where(row_of((8, N)) < 4, one, pltpu.roll(two, 4, 0))
+
+
+def depth_after(step_x, step_y):
+    core, high = lax.axis_index("c"), lax.axis_index("zh")
+    low, column = lax.axis_index("zl"), lax.axis_index("x")
+    if step_x == 1:
+        high = jnp.where(core == 1, (high + 1) % 4, high)
+    if step_x == -1:
+        high = jnp.where(core == 0, (high + 3) % 4, high)
+    if step_y == 1:
+        low = jnp.where(column == 3, 1 - low, low)
+    if step_y == -1:
+        low = jnp.where(column == 0, 1 - low, low)
+    return high * 2 + low
+
+
+def plane_after(step_x, step_y):
+    core, high = lax.axis_index("c"), lax.axis_index("zh")
+    row, column = lax.axis_index("y"), lax.axis_index("x")
+    if step_x == 1:
+        row = jnp.where((core == 1) & (high == 0), (row + 1) % 4, row)
+    if step_x == -1:
+        row = jnp.where((core == 0) & (high == 3), (row + 3) % 4, row)
+    return row * 4 + (column + step_y + 4) % 4
+
+
+def depth_sum_kernel(tiles, charge_piece, out):
+    total = jnp.sum(tiles[...], axis=0)
+    place_of = [plane_after(step_x, step_y) for step_x, step_y in TABLE_DIRS]
+    line = lane((8, N))
+    home = jnp.where(
+        row_of((8, N)) < 4, segments(line, place_of[0:3]), segments(line, place_of[3:6])
+    )
+    home_three = jnp.where(line < 64, place_of[6], place_of[7])
+    sixes, threes = total[40:48], total[48:56]
+    row = lax.axis_index("y")
+    quarter = charge_piece[0:4, :]
+    for number in range(1, 4):
+        quarter = jnp.where(row == number, charge_piece[4 * number : 4 * number + 4, :], quarter)
+    for other in range(16):
+        out[other, 0:40, :] = total[0:40]
+        out[other, 40:48, :] = jnp.where(home == other, sixes, 0.0)
+        out[other, 48:56, :] = jnp.where(home_three == other, threes, 0.0)
+        out[other, 52:56, :] = quarter
+
+
+def plane_sum_kernel(tiles, swap, threes):
+    for column in range(4):
+        total = tiles[column, 0:16, :]
+        for row in range(1, 4):
+            total = total + tiles[4 * row + column, 0:16, :]
+        swap[16 * column : 16 * column + 16, :] = total
+        for row in range(4):
+            at = 96 + 16 * column + 4 * row
+            swap[at : at + 4, :] = tiles[4 * row + column, 52:56, :]
+    rest = tiles[0, 16:56, :]
+    for other in range(1, 16):
+        rest = rest + tiles[other, 16:56, :]
+    swap[64:96, :] = rest[0:32]
+    threes[...] = jnp.where(row_of((8, N)) < 4, rest[32:40], 0.0)
+
+
+def finish_kernel(own, other, threes, own_grad, face, corner, forces, grad_embed, grad_radial, grad_up,
+                  grad_charge, grad_read):
+    mean = 1.0 / ATOMS
+    core = lax.axis_index("c")
+    mine = pl.ds(pl.multiple_of(core * 64, 64), 64)
+    theirs = pl.ds(pl.multiple_of((1 - core) * 64, 64), 64)
+    grad_up[mine, :] = own[0:64, :] * mean
+    grad_up[theirs, :] = other[0:64, :] * mean
+    grad_charge[mine, :] = own[96:160, :] * mean
+    grad_charge[theirs, :] = other[96:160, :] * mean
+    total = (own[64:88, :] + other[64:88, :]) * mean
+    grad_radial[0, :, :] = total[0:8]
+    grad_radial[1, :, :] = total[8:16]
+    grad_embed[...] = total[16:22]
+    grad_read[...] = total[22:23]
+    sixes = other[88:96, :]
+    grad = own_grad[...]
     lane_rows = row_of((N, N))
-    for number, piece in enumerate((from_minus_y[...], from_plus_y[...], faces)):
-        onehot = jnp.where(lane_rows == index[number : number + 1, :], 1.0, 0.0)
-        total = total + dot(piece, onehot, 1, 1)
-    forces[...] = -total[0:3, :]
+    for piece, faces, corners in (
+        (sixes, (0,), (0, 1)),
+        (pltpu.roll(sixes, 4, 0), (1,), (2, 3)),
+        (threes[...], (2, 3), ()),
+    ):
+        onehot = jnp.where(lane_rows == joined(face, corner, faces, corners), 1.0, 0.0)
+        grad = grad + dot(piece, onehot, 1, 1)
+    forces[...] = -grad[0:3, :]
+
+
+def spread_kernel(*refs):
+    out = refs[-1]
+    core, column = lax.axis_index("c"), lax.axis_index("x")
+    for number, shard in enumerate(refs[:-1]):
+        source = (column + 4 - number % 4) % 4
+        member = jnp.where(number < 4, core, 1 - core) * 4 + source
+        out[pl.ds(pl.multiple_of(member * SHARD, SHARD), SHARD), :] = shard[...]
 
 
 def structure_kernel(shared, kvec, embed, w_up, w_charge, factor, wave_high, wave_low, charges,
@@ -477,62 +608,50 @@
         shared[member, :, :] = grad
 
 
+def wave_trig(wave_high, wave_low):
+    cosine = wave_high[0:SHARD, :].astype(jnp.float32) + wave_low[0:SHARD, :].astype(jnp.float32)
+    sine = wave_high[SHARD:, :].astype(jnp.float32) + wave_low[SHARD:, :].astype(jnp.float32)
+    return cosine, sine
+
+
+def by_position(fields, atoms, kvec, wave_high, wave_low):
+    along = dot_three(split(fields), split(atoms), 1, 1)
+    cosine, sine = wave_trig(wave_high, wave_low)
+    phase = cosine * along[SHARD:] - sine * along[0:SHARD]
+    me = lax.axis_index(GROUP)
+    rows = jnp.concatenate(
+        [
+            kvec[:, pl.ds(pl.multiple_of(me * SHARD, SHARD), SHARD)],
+            jnp.zeros((5, SHARD), jnp.float32),
+        ],
+        axis=0,
+    )
+    return dot_three(split(rows), split(phase))
+
+
 def wave_back_kernel(projected, factor, charge_factor, weighted, kfilter, kvec, wave_high, wave_low,
-                     gathered, charges, shared, w_charge, up_part, out, grad_filter, phase):
-    me = lax.axis_index(GROUP)
-    at = pl.multiple_of(me * SHARD, SHARD)
+                     gathered, charges, shared, w_charge, up_part, out, grad_filter):
     scaled = filter_of(kfilter)
     proj = projected[...]
     mixed = charge_factor[...] * proj
     grad_filter[...] = SCALE * (mixed[0:SHARD] + mixed[SHARD:])
     field = proj * jnp.concatenate([scaled, scaled], axis=0)
+    charge_grad = dot_three(split(factor[...]), split(field), 0, 0)
     by_charge = waves_to_atoms(field, wave_high, wave_low)
-    charge_grad = dot(factor[...], field, 0, 0)
     active = jnp.concatenate([shared[member, 0:N, :] for member in range(MEMBERS)], axis=0)
     mix = dot_three(split(by_charge), split(active))
     up_grad = dot(mix, w_charge[...], 0, 1) + up_part[...]
-    left = split(jnp.concatenate([weighted[...], field], axis=1))
-    right = split(
-        jnp.concatenate([gathered[...].reshape(MEMBERS * N, N), charges[...]], axis=1)
-    )
-    along = dot_three(left, right, 1, 1)
-    cosine = wave_high[0:SHARD, :].astype(jnp.float32) + wave_low[0:SHARD, :].astype(jnp.float32)
-    sine = wave_high[SHARD:, :].astype(jnp.float32) + wave_low[SHARD:, :].astype(jnp.float32)
-    phase[...] = cosine * along[SHARD:] - sine * along[0:SHARD]
-    rows = jnp.concatenate(
-        [kvec[:, pl.ds(at, SHARD)], jnp.zeros((5, SHARD), jnp.float32)], axis=0
-    )
-    by_pos = dot(rows, phase[...])
+    by_pos = by_position(
+        jnp.concatenate([weighted[...], field], axis=1),
+        jnp.concatenate([gathered[...].reshape(MEMBERS * N, N), charges[...]], axis=1),
+        kvec, wave_high, wave_low,
+    )
     for member in range(MEMBERS):
         part = slice(member * N, (member + 1) * N)
-        piece = slice(member * 16, (member + 1) * 16)
         out[member, 0:N, :] = by_charge[:, part]
         out[member, N : N + 8, :] = by_pos[:, part]
-        out[member, N + 8 : N + 24, :] = charge_grad[piece]
-        out[member, N + 24 : N + 40, :] = up_grad[piece]
-
-
-def gather_sum_kernel(tiles, charge_piece, out):
-    total = jnp.sum(tiles[...], axis=0)
-    piece = charge_piece[...]
-    for member in range(MEMBERS):
-        out[member, 0:40, :] = total
-        out[member, 40:56, :] = piece
-
-
-def finish_kernel(tiles, grad_embed, grad_radial, grad_up, grad_charge, grad_read):
-    mean = 1.0 / ATOMS
-    total = tiles[0, 16:40, :]
-    for member in range(1, MEMBERS):
-        total = total + tiles[member, 16:40, :]
-    total = total * mean
-    for member in range(MEMBERS):
-        grad_up[16 * member : 16 * member + 16, :] = tiles[member, 0:16, :] * mean
-        grad_charge[16 * member : 16 * member + 16, :] = tiles[member, 40:56, :] * mean
-    grad_radial[0, :, :] = total[0:8]
-    grad_radial[1, :, :] = total[8:16]
-    grad_embed[...] = total[16:22]
-    grad_read[...] = total[22:23]
+        out[member, N + 8 : N + 24, :] = up_grad[member * 16 : (member + 1) * 16]
+        out[member, N + 24 : N + 40, :] = charge_grad[member * 16 : (member + 1) * 16]
 
 
 def body(
@@ -541,29 +660,19 @@
 ):
     species = species.reshape(1, N)
     read = read.reshape(1, N)
-    index = jnp.concatenate(
-        [
-            jnp.concatenate([face_sends[2], corner_sends[0], corner_sends[2]])[None],
-            jnp.concatenate([face_sends[3], corner_sends[1], corner_sends[3]])[None],
-            jnp.concatenate([face_sends[0], face_sends[1]])[None],
-            jnp.zeros((5, N), jnp.int32),
-        ],
-        axis=0,
-    )
-    to_minus, to_plus, own_x = call(pack_kernel, (f32(8, N),) * 3, positions, species, index)
-    from_plus_y = moved(to_minus, GY, -1)
-    from_minus_y = moved(to_plus, GY, 1)
-    to_minus, to_plus = relay(own_x, from_plus_y, from_minus_y)
-    from_plus_x = moved(to_minus, GX, -1)
-    from_minus_x = moved(to_plus, GX, 1)
+    near, far, own_x = call(
+        pack_kernel, (f32(8, N),) * 3, positions, species, face_sends, corner_sends
+    )
+    near_y, far_y = swapped(near, GY, 0), swapped(far, GY, 1)
+    near, far = call(relay_kernel, (f32(8, N),) * 2, own_x, near_y, far_y)
+    near_x, far_x = swapped(near, GX, 0), swapped(far, GX, 1)
     shared, active, invariants, vectors, sums, edges, places = call(
         edge_kernel,
         (
             f32(MEMBERS, N + 8, N), f32(N, N), f32(N, N), f32(3, N, N), f32(4, KINDS * BASIS, N),
             f32(7, SLOTS, N), jax.ShapeDtypeStruct((2, SLOTS, N), jnp.int32),
         ),
-        positions, species, neighbours, from_plus_x, from_minus_x, from_plus_y, from_minus_y,
-        embed, radial,
+        positions, species, neighbours, near_x, far_x, near_y, far_y, embed, radial,
     )
     shared = lax.all_to_all(shared, GROUP, 0, 0)
     half = jax.ShapeDtypeStruct((2 * SHARD, MEMBERS * N), jnp.bfloat16)
@@ -593,40 +702,36 @@
         potential, active, species, embed, w_up, read,
     )
     gathered = lax.all_to_all(gathered, GROUP, 0, 0)
-    projected = cross_sum(
-        call(projection_kernel, f32(CROSSES, 16, N), gathered, wave_high, wave_low)
-    )
-    tiles, grad_filter = call(
+    projected = call(projection_kernel, f32(CROSSES, 16, N), gathered, wave_high, wave_low)
+    projected = cross_sum(projected)
+    tiles, shard = call(
         wave_back_kernel,
         (f32(MEMBERS, N + 40, N), f32(SHARD, N)),
         projected, factor, charge_factor, weighted, kfilter, kvec, wave_high, wave_low,
         gathered, charges, shared, w_charge, up_part,
-        scratch=(pltpu.VMEM((SHARD, MEMBERS * N), jnp.float32),),
-    )
-    grad_filter = lax.all_gather(grad_filter, GROUP, axis=0, tiled=True)
+    )
+    swap = [(0, 1), (1, 0)]
+    shards = [shard] + [
+        lax.ppermute(shard, "x", [(at, (at + step) % 4) for at in range(4)]) for step in (1, 2, 3)
+    ]
+    shards += [lax.ppermute(value, "c", swap) for value in shards]
     tiles = lax.all_to_all(tiles, GROUP, 0, 0)
-    payload, charge_piece, own_grad, to_one, to_two, to_three = call(
+    payload, own_grad, charge_piece = call(
         edge_back_kernel,
-        (f32(CROSSES, 40, N), f32(16, N)) + (f32(8, N),) * 4,
-        tiles, shared, active, invariants, vectors, sums, edges, places, embed, radial, w_up,
+        (f32(8, 56, N), f32(8, N), f32(16, N)),
+        tiles, active, invariants, vectors, sums, edges, places, embed, radial, w_up,
         w_charge, species, grad_out, read_row,
     )
-    back_minus_x = moved(to_one, GX, 1)
-    back_plus_x = moved(to_two, GX, -1)
-    to_plus, to_minus = relay(to_three, back_minus_x, back_plus_x)
-    back_minus_y = moved(to_plus, GY, 1)
-    back_plus_y = moved(to_minus, GY, -1)
-    forces = call(
-        force_kernel, f32(3, N),
-        own_grad, back_minus_x, back_plus_x, back_minus_y, back_plus_y, index,
-    )
-    payload = lax.all_to_all(payload, CROSS, 0, 0)
-    payload = call(gather_sum_kernel, f32(MEMBERS, 56, N), payload, charge_piece)
-    payload = lax.all_to_all(payload, GROUP, 0, 0)
-    grad_embed, grad_radial, grad_up, grad_charge, grad_read = call(
+    payload = lax.all_to_all(payload, DEPTH, 0, 0)
+    payload = call(depth_sum_kernel, f32(16, 56, N), payload, charge_piece)
+    payload = lax.all_to_all(payload, PLANE, 0, 0)
+    payload, threes = call(plane_sum_kernel, (f32(160, N), f32(8, N)), payload)
+    other = lax.ppermute(payload, "c", swap)
+    grad_filter = call(spread_kernel, f32(WAVES, N), *shards)
+    forces, grad_embed, grad_radial, grad_up, grad_charge, grad_read = call(
         finish_kernel,
-        (f32(KINDS, N), f32(2, BASIS, N), f32(N, N), f32(N, N), f32(1, N)),
-        payload,
+        (f32(3, N), f32(KINDS, N), f32(2, BASIS, N), f32(N, N), f32(N, N), f32(1, N)),
+        payload, other, threes, own_grad, face_sends, corner_sends,
     )
     return (
         energy.reshape(N), forces, grad_embed, grad_radial, grad_up, grad_charge, grad_filter,

time: 224 us -> 198 us (0.88); the launches traced: 220 us -> 197 us
  waiting for transfers between devices: 24.5 us -> 4.8 us
  between operations: 14.1 us -> 0.8 us
  blocking collectives: 127 us -> 140 us
    all_to_all x2 -> x1, starting transfers between devices: 14.3 us -> 3.56 us  [body(): payload = lax.all_to_all(payload, PLANE, 0, 0)]
    all_to_all x2 -> x1, waiting for transfers between devices: 10.4 us -> 0.01 us  [body(): payload = lax.all_to_all(payload, PLANE, 0, 0)]
    all_to_all x1 -> x2, blocking collectives: 20.9 us -> 30.2 us  [the longest x1 17.1 us: body(): tiles = lax.all_to_all(tiles, GROUP, 0, 0)]
    ppermute x8 -> x12, starting transfers between devices: 15.1 us -> 24.3 us  [the longest x4 10.4 us: swapped(): return lax.ppermute(value, axes, places)]
    ppermute x8 -> x12, waiting for transfers between devices: 13.3 us -> 4.79 us  [the longest x4 2.7 us: swapped(): return lax.ppermute(value, axes, places)]
    all_to_all x2, blocking collectives: 26.8 us -> 30.5 us  [cross_sum(): tiles = lax.all_to_all(tiles, CROSS, 0, 0)]
    unnamed x25 -> x30, local copies, waits for them, and re-layouts: 4.88 us -> 4.82 us
  transfers between devices with their start and end apart: 11 -> 13, of which waited for: 8 -> 4; matrix products, arithmetic and copies ran while one was open for 0% -> 0% of each run, Pallas kernels for 3% -> 1%
where the time goes in v2:
time: 198 us; the launch traced here: 197 us
  blocking collectives  140 us (71%)
  starting transfers between devices  27.8 us (14%)
  Pallas kernels  18.8 us (9%)
  local copies, waits for them, and re-layouts  4.82 us (2%)
  waiting for transfers between devices  4.8 us (2%)
    all_to_all x2, blocking collectives, cross_sum(): return lax.all_to_all(tiles, CROSS, 0, 0).reshape(2 * SHARD, N)  32.2 us
    all_to_all x2, blocking collectives, cross_sum(): tiles = lax.all_to_all(tiles, CROSS, 0, 0)  30.5 us
    all_to_all x1, blocking collectives, body(): shared = lax.all_to_all(shared, GROUP, 0, 0)  19.4 us
    pallas_call x15, Pallas kernels, call(): pl.pallas_call(kernel, out_shape=out_shape, scratch_shapes=list(scratch),...  18.8 us
    all_to_all x1, blocking collectives, body(): tiles = lax.all_to_all(tiles, GROUP, 0, 0)  17.1 us
    all_to_all x1, blocking collectives, body(): potential = lax.all_to_all(potential, GROUP, 0, 0)  15.4 us
    all_to_all x1, blocking collectives, body(): payload = lax.all_to_all(payload, DEPTH, 0, 0)  13.1 us
    all_to_all x1, blocking collectives, body(): gathered = lax.all_to_all(gathered, GROUP, 0, 0)  12.6 us
  transfers between devices with their start and end apart: 13, of which 4 were waited for; matrix products, arithmetic and copies ran while one was open for 0% of the time, Pallas kernels for 1%

profile of v2, /device:TPU:1, one launch (start us, length us, event | category | flops | bytes accessed | tf_op | source)
XLA Modules:
  0.0 197.3 jit_solution(12327152707046338)
XLA Ops:
  0.6 0.0 copy-start.7
  0.6 0.6 copy-done.7
  1.3 0.7 copy-done.8
  2.0 0.7 copy-done.10
  2.7 0.7 copy-done.12
  3.3 0.1 shard_map.179
  3.5 2.1 %collective-permute-start = (f32[8,128]{1,0:T(8,128)S(1)}, f32[8,128]{1,0:T(8,128)S(1)}, u32[]{:S(2)}, u32[]{:S(2)}) collective-permute-start(f32[8,128]{1,0:T(8,128)S(1)} %get-tuple-element.46), channel_id=1, source_target_pairs={{0,1},{1,0},{2,3},{3,2},{4,5},{5,4},{6,7},{7,6},{8,9},{9,8},{10,11... | collective-permute-start | bytes 12296 | tf_op jit(solution)/shard_map/ppermute | solution.py:154
  5.6 3.2 %collective-permute-start.1 = (f32[8,128]{1,0:T(8,128)S(1)}, f32[8,128]{1,0:T(8,128)S(1)}, u32[]{:S(2)}, u32[]{:S(2)}) collective-permute-start(f32[8,128]{1,0:T(8,128)S(1)} %get-tuple-element.47), channel_id=1, source_target_pairs={{0,7},{1,2},{2,1},{3,4},{4,3},{5,6},{6,5},{7,0},{8,15},{9,10},{10,... | collective-permute-start | bytes 12296 | tf_op jit(solution)/shard_map/ppermute | solution.py:154
  8.7 0.0 collective-permute-done.near.near_y
  8.7 1.4 collective-permute-done.1.far.far_y
  10.1 0.1 shard_map.180
  10.2 2.5 %collective-permute-start.2 = (f32[8,128]{1,0:T(8,128)S(1)}, f32[8,128]{1,0:T(8,128)S(1)}, u32[]{:S(2)}, u32[]{:S(2)}) collective-permute-start(f32[8,128]{1,0:T(8,128)S(1)} %get-tuple-element.48), channel_id=1, source_target_pairs={{0,8},{8,0},{16,24},{24,16},{32,40},{40,32},{48,56},{56,48},{64,72... | collective-permute-start | bytes 12296 | tf_op jit(solution)/shard_map/ppermute | solution.py:154
  12.7 2.6 %collective-permute-start.3 = (f32[8,128]{1,0:T(8,128)S(1)}, f32[8,128]{1,0:T(8,128)S(1)}, u32[]{:S(2)}, u32[]{:S(2)}) collective-permute-start(f32[8,128]{1,0:T(8,128)S(1)} %get-tuple-element.49), channel_id=1, source_target_pairs={{0,248},{8,16},{16,8},{24,32},{32,24},{40,48},{48,40},{56,64},{64,... | collective-permute-start | bytes 12296 | tf_op jit(solution)/shard_map/ppermute | solution.py:154
  15.3 0.0 collective-permute-done.2.near_x
  15.3 1.3 collective-permute-done.3.far_x
  16.6 0.0 copy-done.13
  16.6 0.0 copy-start.6
  16.6 0.7 copy-done.6
  17.4 1.4 shard_map.181
  18.8 0.0 copy-start.1
  18.9 0.0 copy-start.2
  18.9 0.0 copy-start.3
  18.9 19.4 %all_to_all.50.shared = f32[8,136,128]{2,1,0:T(8,128)S(1)} all-to-all(f32[8,136,128]{2,1,0:T(8,128)S(1)} %get-tuple-element.50), channel_id=1, replica_groups=mesh['y'=4,'zh'=4,'c'=2,'zl'=2,'x'=4] {'c','x'}, dimensions={0} | all-to-all | bytes 1114112 | tf_op jit(solution)/shard_map/all_to_all | solution.py:677
  38.3 0.0 copy-done.2
  38.3 0.0 copy-start
  38.3 3.5 %shard_map.182 = (f32[32,16,128]{2,1,0:T(8,128)S(1)}, bf16[512,1024]{1,0:T(8,128)(2,1)S(1)}, bf16[512,1024]{1,0:T(8,128)(2,1)S(1)}, f32[1024,128]{1,0:T(8,128)S(1)}) custom-call(f32[8,136,128]{2,1,0:T(8,128)S(1)} %all_to_all.50.shared, f32[3,2048]{1,0:T(4,128)S(1)} %copy-done.3, f32[6,128]{1,0:T(8,128)S(1)} %copy-done.4, f32[128,128]{1,0:T(8,128)S(1)} %copy-done.2, ...), custom_call_target="tpu_custom_call" | custom-call | tf_op jit(solution)/shard_map/pallas_call | solution.py:104
  41.8 16.8 %all_to_all.51.tiles = f32[32,16,128]{2,1,0:T(8,128)S(1)} all-to-all(f32[32,16,128]{2,1,0:T(8,128)S(1)} %get-tuple-element.51), channel_id=1, replica_groups=mesh['y'=4,'zh'=4,'c'=2,'zl'=2,'x'=4] {'y','zh','zl'}, dimensions={0} | all-to-all | bytes 524288 | tf_op jit(solution)/shard_map/all_to_all | solution.py:688
  58.6 0.1 shard_map.183
  58.7 16.0 %all_to_all.52 = f32[32,16,128]{2,1,0:T(8,128)S(1)} all-to-all(f32[32,16,128]{2,1,0:T(8,128)S(1)} %shard_map.183), channel_id=1, replica_groups=mesh['y'=4,'zh'=4,'c'=2,'zl'=2,'x'=4] {'y','zh','zl'}, dimensions={0} | all-to-all | bytes 524288 | tf_op jit(solution)/shard_map/all_to_all | solution.py:690
  74.6 1.3 shard_map.184
  75.9 15.4 %all_to_all.53.tiles = f32[8,128,128]{2,1,0:T(8,128)S(1)} all-to-all(f32[8,128,128]{2,1,0:T(8,128)S(1)} %get-tuple-element.54), channel_id=1, replica_groups=mesh['y'=4,'zh'=4,'c'=2,'zl'=2,'x'=4] {'c','x'}, dimensions={0} | all-to-all | bytes 1048576 | tf_op jit(solution)/shard_map/all_to_all | solution.py:698
  91.4 0.7 copy-done.14
  92.0 1.2 shard_map.185
  93.2 12.6 %all_to_all.54.gathered = f32[8,128,128]{2,1,0:T(8,128)S(1)} all-to-all(f32[8,128,128]{2,1,0:T(8,128)S(1)} %get-tuple-element.57), channel_id=1, replica_groups=mesh['y'=4,'zh'=4,'c'=2,'zl'=2,'x'=4] {'c','x'}, dimensions={0} | all-to-all | bytes 1048576 | tf_op jit(solution)/shard_map/all_to_all | solution.py:704
  105.8 0.7 shard_map.186
  106.5 13.7 %all_to_all.55.tiles = f32[32,16,128]{2,1,0:T(8,128)S(1)} all-to-all(f32[32,16,128]{2,1,0:T(8,128)S(1)} %shard_map.186), channel_id=1, replica_groups=mesh['y'=4,'zh'=4,'c'=2,'zl'=2,'x'=4] {'y','zh','zl'}, dimensions={0} | all-to-all | bytes 524288 | tf_op jit(solution)/shard_map/all_to_all | solution.py:688
  120.2 0.1 shard_map.187
  120.2 16.2 %all_to_all.56 = f32[32,16,128]{2,1,0:T(8,128)S(1)} all-to-all(f32[32,16,128]{2,1,0:T(8,128)S(1)} %shard_map.187), channel_id=1, replica_groups=mesh['y'=4,'zh'=4,'c'=2,'zl'=2,'x'=4] {'y','zh','zl'}, dimensions={0} | all-to-all | bytes 524288 | tf_op jit(solution)/shard_map/all_to_all | solution.py:690
  136.4 2.6 %shard_map.188 = (f32[8,168,128]{2,1,0:T(8,128)S(1)}, f32[256,128]{1,0:T(8,128)S(1)}) custom-call(f32[512,128]{1,0:T(8,128)S(1)} %bitcast.8, f32[512,128]{1,0:T(8,128)S(1)} %bitcast.7, f32[512,128]{1,0:T(8,128)S(1)} %get-tuple-element.58.charge_factor, f32[512,128]{1,0:T(8,128)S(1)} %get-tuple-element.59.weighted, f32[2048,128]{1,0:T(8,128)S(1)} %copy-done, ...), custom_call_target="tpu_custom_call" | custom-call | tf_op jit(solution)/shard_map/pallas_call | solution.py:104
  139.0 17.1 %all_to_all.57.tiles = f32[8,168,128]{2,1,0:T(8,128)S(1)} all-to-all(f32[8,168,128]{2,1,0:T(8,128)S(1)} %get-tuple-element.62), channel_id=1, replica_groups=mesh['y'=4,'zh'=4,'c'=2,'zl'=2,'x'=4] {'c','x'}, dimensions={0} | all-to-all | bytes 1376256 | tf_op jit(solution)/shard_map/all_to_all | solution.py:718
  156.1 4.7 %shard_map.189 = (f32[8,56,128]{2,1,0:T(8,128)S(1)}, f32[8,128]{1,0:T(8,128)S(1)}, f32[16,128]{1,0:T(8,128)S(1)}) custom-call(f32[8,168,128]{2,1,0:T(8,128)S(1)} %all_to_all.57.tiles, f32[128,128]{1,0:T(8,128)S(1)} %get-tuple-element.55.active, f32[128,128]{1,0:T(8,128)S(1)} %get-tuple-element.63.invariants, f32[3,128,128]{2,1,0:T(8,128)S(1)} %get-tuple-element.64.vectors, ...), custom_call_target="tpu_custom_call" | custom-call | tf_op jit(solution)/shard_map/pallas_call | solution.py:104
  160.9 13.1 %all_to_all.58.tiles = f32[8,56,128]{2,1,0:T(8,128)S(1)} all-to-all(f32[8,56,128]{2,1,0:T(8,128)S(1)} %get-tuple-element.70), channel_id=1, replica_groups=mesh['y'=4,'zh'=4,'c'=2,'zl'=2,'x'=4] {'zh','zl'}, dimensions={0} | all-to-all | bytes 458752 | tf_op jit(solution)/shard_map/all_to_all | solution.py:725
  174.0 0.8 shard_map.190
  174.8 3.6 %all-to-all-start.9 = ((f32[16,56,128]{2,1,0:T(8,128)}), f32[16,56,128]{2,1,0:T(8,128)S(1)}, u32[]{:S(2)}, u32[]{:S(2)}) async-start(f32[16,56,128]{2,1,0:T(8,128)} %shard_map.190), calls=%async_computation.9 | async-start | bytes 917504 | tf_op jit(solution)/shard_map/all_to_all | solution.py:727
  178.4 2.5 %collective-permute-start.7 = (f32[256,128]{1,0:T(8,128)S(1)}, f32[256,128]{1,0:T(8,128)S(1)}, u32[]{:S(2)}, u32[]{:S(2)}) collective-permute-start(f32[256,128]{1,0:T(8,128)S(1)} %get-tuple-element.80.refs_0_), channel_id=1, source_target_pairs={{0,3},{1,0},{2,1},{3,2},{4,7},{5,4},{6,5},{7,6},{8,11},{9,8},{10,9... | collective-permute-start | bytes 393224 | tf_op jit(solution)/shard_map/ppermute | solution.py:715
  180.8 0.6 collective-permute-start.6
  181.4 0.6 collective-permute-start.5
  182.0 3.1 %collective-permute-start.8 = (f32[256,128]{1,0:T(8,128)S(1)}, f32[256,128]{1,0:T(8,128)S(1)}, u32[]{:S(2)}, u32[]{:S(2)}) collective-permute-start(f32[256,128]{1,0:T(8,128)S(1)} %get-tuple-element.80.refs_0_), channel_id=1, source_target_pairs={{0,8},{8,0},{1,9},{9,1},{2,10},{10,2},{3,11},{11,3},{4,12},{12,4},... | collective-permute-start | bytes 393224 | tf_op jit(solution)/shard_map/ppermute | solution.py:717
  185.0 1.3 collective-permute-done.7.refs_3_
  186.3 4.3 %collective-permute-start.11 = (f32[256,128]{1,0:T(8,128)S(1)}, f32[256,128]{1,0:T(8,128)S(1)}, u32[]{:S(2)}, u32[]{:S(2)}) collective-permute-start(f32[256,128]{1,0:T(8,128)S(1)} %collective-permute-done.7.refs_3_), channel_id=1, source_target_pairs={{0,8},{8,0},{1,9},{9,1},{2,10},{10,2},{3,11},{11,3},{4,12},{12,4},... | collective-permute-start | bytes 393224 | tf_op jit(solution)/shard_map/ppermute | solution.py:717
  190.6 0.0 collective-permute-done.6.refs_2_
  190.6 1.7 collective-permute-start.10
  192.2 0.0 collective-permute-done.5.refs_1_
  192.3 1.2 collective-permute-start.9
  193.5 0.0 all-to-all-done.9.tiles
  193.5 0.1 collective-permute-start.4
  193.6 0.0 collective-permute-done.8.refs_4_
  193.6 0.0 collective-permute-done.11.refs_7_
  193.6 0.0 collective-permute-done.10.refs_6_
  193.6 0.8 collective-permute-done.9.refs_5_
  194.5 1.0 shard_map.193
  195.5 0.0 collective-permute-done.4.other
  195.5 0.7 copy-done.9
  196.2 1.1 shard_map.192
  (16 shorter events, 0.1 us)
Async XLA Ops:
  0.6 0.7 copy-start.7
  1.3 0.7 copy-start.8
  2.0 0.7 copy-start.10
  2.7 0.7 copy-start.12
  3.5 5.2 %collective-permute-start = (f32[8,128]{1,0:T(8,128)S(1)}, f32[8,128]{1,0:T(8,128)S(1)}, u32[]{:S(2)}, u32[]{:S(2)}) collective-permute-start(f32[8,128]{1,0:T(8,128)S(1)} %get-tuple-element.46), channel_id=1, source_target_pairs={{0,1},{1,0},{2,3},{3,2},{4,5},{5,4},{6,7},{7,6},{8,9},{9,8},{10,11... | collective-permute-start | bytes 12296 | tf_op jit(solution)/shard_map/ppermute | solution.py:154
  5.6 4.6 %collective-permute-start.1 = (f32[8,128]{1,0:T(8,128)S(1)}, f32[8,128]{1,0:T(8,128)S(1)}, u32[]{:S(2)}, u32[]{:S(2)}) collective-permute-start(f32[8,128]{1,0:T(8,128)S(1)} %get-tuple-element.47), channel_id=1, source_target_pairs={{0,7},{1,2},{2,1},{3,4},{4,3},{5,6},{6,5},{7,0},{8,15},{9,10},{10,... | collective-permute-start | bytes 12296 | tf_op jit(solution)/shard_map/ppermute | solution.py:154
  10.1 6.5 %copy-start.4 = (f32[6,128]{1,0:T(8,128)S(1)}, f32[6,128]{1,0:T(8,128)}, u32[]{:S(2)}) copy-start(f32[6,128]{1,0:T(8,128)} %embed.7) | copy-start | bytes 9220
  10.1 6.5 %copy-start.5 = (f32[2,8,128]{2,1,0:T(8,128)S(1)}, f32[2,8,128]{2,1,0:T(8,128)}, u32[]{:S(2)}) copy-start(f32[2,8,128]{2,1,0:T(8,128)} %radial.3) | copy-start | bytes 24580
  10.2 6.4 %copy-start.13 = (f32[3,128]{1,0:T(4,128)S(1)}, f32[3,128]{1,0:T(4,128)}, u32[]{:S(2)}) copy-start(f32[3,128]{1,0:T(4,128)} %pos.3) | copy-start | bytes 4612
  10.2 5.1 %collective-permute-start.2 = (f32[8,128]{1,0:T(8,128)S(1)}, f32[8,128]{1,0:T(8,128)S(1)}, u32[]{:S(2)}, u32[]{:S(2)}) collective-permute-start(f32[8,128]{1,0:T(8,128)S(1)} %get-tuple-element.48), channel_id=1, source_target_pairs={{0,8},{8,0},{16,24},{24,16},{32,40},{40,32},{48,56},{56,48},{64,72... | collective-permute-start | bytes 12296 | tf_op jit(solution)/shard_map/ppermute | solution.py:154
  12.7 3.9 %collective-permute-start.3 = (f32[8,128]{1,0:T(8,128)S(1)}, f32[8,128]{1,0:T(8,128)S(1)}, u32[]{:S(2)}, u32[]{:S(2)}) collective-permute-start(f32[8,128]{1,0:T(8,128)S(1)} %get-tuple-element.49), channel_id=1, source_target_pairs={{0,248},{8,16},{16,8},{24,32},{32,24},{40,48},{48,40},{56,64},{64,... | collective-permute-start | bytes 12296 | tf_op jit(solution)/shard_map/ppermute | solution.py:154
  16.6 0.8 copy-start.6
  18.8 19.4 %copy-start.1 = (f32[128,128]{1,0:T(8,128)S(1)}, f32[128,128]{1,0:T(8,128)}, u32[]{:S(2)}) copy-start(f32[128,128]{1,0:T(8,128)} %w_charge.7) | copy-start | bytes 196612
  18.9 19.4 %copy-start.2 = (f32[128,128]{1,0:T(8,128)S(1)}, f32[128,128]{1,0:T(8,128)}, u32[]{:S(2)}) copy-start(f32[128,128]{1,0:T(8,128)} %w_up.5) | copy-start | bytes 196612
  18.9 19.4 %copy-start.3 = (f32[3,2048]{1,0:T(4,128)S(1)}, f32[3,2048]{1,0:T(4,128)}, u32[]{:S(2)}) copy-start(f32[3,2048]{1,0:T(4,128)} %kvec.3) | copy-start | bytes 73732
  38.3 36.3 %copy-start = (f32[2048,128]{1,0:T(8,128)S(1)}, f32[2048,128]{1,0:T(8,128)}, u32[]{:S(2)}) copy-start(f32[2048,128]{1,0:T(8,128)} %kfilter.3) | copy-start | bytes 3145732
  91.4 0.7 copy-start.14
  174.8 18.7 %all-to-all-start.9 = ((f32[16,56,128]{2,1,0:T(8,128)}), f32[16,56,128]{2,1,0:T(8,128)S(1)}, u32[]{:S(2)}, u32[]{:S(2)}) async-start(f32[16,56,128]{2,1,0:T(8,128)} %shard_map.190), calls=%async_computation.9 | async-start | bytes 917504 | tf_op jit(solution)/shard_map/all_to_all | solution.py:727
  178.4 7.9 %collective-permute-start.7 = (f32[256,128]{1,0:T(8,128)S(1)}, f32[256,128]{1,0:T(8,128)S(1)}, u32[]{:S(2)}, u32[]{:S(2)}) collective-permute-start(f32[256,128]{1,0:T(8,128)S(1)} %get-tuple-element.80.refs_0_), channel_id=1, source_target_pairs={{0,3},{1,0},{2,1},{3,2},{4,7},{5,4},{6,5},{7,6},{8,11},{9,8},{10,9... | collective-permute-start | bytes 393224 | tf_op jit(solution)/shard_map/ppermute | solution.py:715
  180.8 9.7 %collective-permute-start.6 = (f32[256,128]{1,0:T(8,128)S(1)}, f32[256,128]{1,0:T(8,128)S(1)}, u32[]{:S(2)}, u32[]{:S(2)}) collective-permute-start(f32[256,128]{1,0:T(8,128)S(1)} %get-tuple-element.80.refs_0_), channel_id=1, source_target_pairs={{0,2},{1,3},{2,0},{3,1},{4,6},{5,7},{6,4},{7,5},{8,10},{9,11},{10,... | collective-permute-start | bytes 393224 | tf_op jit(solution)/shard_map/ppermute | solution.py:715
  181.4 10.8 %collective-permute-start.5 = (f32[256,128]{1,0:T(8,128)S(1)}, f32[256,128]{1,0:T(8,128)S(1)}, u32[]{:S(2)}, u32[]{:S(2)}) collective-permute-start(f32[256,128]{1,0:T(8,128)S(1)} %get-tuple-element.80.refs_0_), channel_id=1, source_target_pairs={{0,1},{1,2},{2,3},{3,0},{4,5},{5,6},{6,7},{7,4},{8,9},{9,10},{10,1... | collective-permute-start | bytes 393224 | tf_op jit(solution)/shard_map/ppermute | solution.py:715
  182.0 11.6 %collective-permute-start.8 = (f32[256,128]{1,0:T(8,128)S(1)}, f32[256,128]{1,0:T(8,128)S(1)}, u32[]{:S(2)}, u32[]{:S(2)}) collective-permute-start(f32[256,128]{1,0:T(8,128)S(1)} %get-tuple-element.80.refs_0_), channel_id=1, source_target_pairs={{0,8},{8,0},{1,9},{9,1},{2,10},{10,2},{3,11},{11,3},{4,12},{12,4},... | collective-permute-start | bytes 393224 | tf_op jit(solution)/shard_map/ppermute | solution.py:717
  186.3 7.3 %collective-permute-start.11 = (f32[256,128]{1,0:T(8,128)S(1)}, f32[256,128]{1,0:T(8,128)S(1)}, u32[]{:S(2)}, u32[]{:S(2)}) collective-permute-start(f32[256,128]{1,0:T(8,128)S(1)} %collective-permute-done.7.refs_3_), channel_id=1, source_target_pairs={{0,8},{8,0},{1,9},{9,1},{2,10},{10,2},{3,11},{11,3},{4,12},{12,4},... | collective-permute-start | bytes 393224 | tf_op jit(solution)/shard_map/ppermute | solution.py:717
  190.6 3.0 %collective-permute-start.10 = (f32[256,128]{1,0:T(8,128)S(1)}, f32[256,128]{1,0:T(8,128)S(1)}, u32[]{:S(2)}, u32[]{:S(2)}) collective-permute-start(f32[256,128]{1,0:T(8,128)S(1)} %collective-permute-done.6.refs_2_), channel_id=1, source_target_pairs={{0,8},{8,0},{1,9},{9,1},{2,10},{10,2},{3,11},{11,3},{4,12},{12,4},... | collective-permute-start | bytes 393224 | tf_op jit(solution)/shard_map/ppermute | solution.py:717
  192.3 2.2 %collective-permute-start.9 = (f32[256,128]{1,0:T(8,128)S(1)}, f32[256,128]{1,0:T(8,128)S(1)}, u32[]{:S(2)}, u32[]{:S(2)}) collective-permute-start(f32[256,128]{1,0:T(8,128)S(1)} %collective-permute-done.5.refs_1_), channel_id=1, source_target_pairs={{0,8},{8,0},{1,9},{9,1},{2,10},{10,2},{3,11},{11,3},{4,12},{12,4},... | collective-permute-start | bytes 393224 | tf_op jit(solution)/shard_map/ppermute | solution.py:717
  193.5 2.0 %collective-permute-start.4 = (f32[160,128]{1,0:T(8,128)S(1)}, f32[160,128]{1,0:T(8,128)S(1)}, u32[]{:S(2)}, u32[]{:S(2)}) collective-permute-start(f32[160,128]{1,0:T(8,128)S(1)} %get-tuple-element.72.own), channel_id=1, source_target_pairs={{0,8},{8,0},{1,9},{9,1},{2,10},{10,2},{3,11},{11,3},{4,12},{12,4},... | collective-permute-start | bytes 245768 | tf_op jit(solution)/shard_map/ppermute | solution.py:729
  194.5 1.1 copy-start.11
  195.5 0.7 copy-start.9

commit v3 on v2

--- a/solution.py
+++ b/solution.py
@@ -100,17 +100,24 @@
     return lax.broadcasted_iota(jnp.int32, shape, 0)
 
 
-def call(kernel, out_shape, *args, scratch=(), vmem=32):
+def call(kernel, out_shape, *args, scratch=(), vmem=32, far=False, cost=None):
+    more = {"in_specs": [pl.BlockSpec(memory_space=pltpu.HBM)] * len(args)} if far else {}
     return pl.pallas_call(
         kernel,
         out_shape=out_shape,
         scratch_shapes=list(scratch),
+        cost_estimate=cost,
+        **more,
         compiler_params=pltpu.CompilerParams(vmem_limit_bytes=vmem * 1024 * 1024),
     )(*args)
 
 
 def f32(*shape):
     return jax.ShapeDtypeStruct(shape, jnp.float32)
+
+
+def i32(*shape):
+    return jax.ShapeDtypeStruct(shape, jnp.int32)
 
 
 def take(row, index):
@@ -125,15 +132,38 @@
     )
 
 
-def pack_kernel(pos, species, face, corner, near, far, own):
+def pack_kernel(pos_in, species_in, face_in, corner_in, nbr_in, embed_in, radial_in, read_in,
+                near, far, own, home, pos, species, nbr, embed, radial, read, face, corner, sems):
+    pairs = (
+        (pos_in, pos), (species_in, species), (face_in, face), (corner_in, corner),
+        (nbr_in, nbr), (embed_in, embed), (radial_in, radial), (read_in, read),
+    )
+    copies = [
+        pltpu.make_async_copy(source, target, sems.at[number])
+        for number, (source, target) in enumerate(pairs)
+    ]
+    for copy in copies:
+        copy.start()
+    for copy in copies:
+        copy.wait()
     even = lax.axis_index("x") % 2 == 0
     rows = [pos[0:1, :], pos[1:2, :], pos[2:3, :], species[...].astype(jnp.float32)]
+    padding = jnp.zeros((5, N), jnp.int32)
     where_from = jnp.concatenate(
         [
             joined(face, corner, (2,), (0, 2)),
             joined(face, corner, (3,), (1, 3)),
             joined(face, corner, (0, 1), ()),
-            jnp.zeros((5, N), jnp.int32),
+            padding,
+        ],
+        axis=0,
+    )
+    home[...] = jnp.concatenate(
+        [
+            joined(face, corner, (0,), (0, 1)),
+            joined(face, corner, (1,), (2, 3)),
+            joined(face, corner, (2, 3), ()),
+            padding,
         ],
         axis=0,
     )
@@ -272,7 +302,7 @@
     tail = jnp.concatenate(
         [own[0] + anchor_x, own[1] + anchor_y, own[2], own[3]] + [zero_row] * 4, axis=0
     )
-    for member in range(MEMBERS):
+    for member in range(4):
         shared[member, 0:N, :] = result
         shared[member, N : N + 8, :] = tail
 
@@ -283,7 +313,7 @@
     payload, own_grad, charge_piece,
 ):
     total = tiles[0]
-    for member in range(1, MEMBERS):
+    for member in range(1, 4):
         total = total + tiles[member]
     grad_charges = jnp.transpose(total[0:N, :])
     updated = grad_out[...] + dot(grad_charges, w_charge[...], 1, 1)
@@ -464,7 +494,7 @@
     threes[...] = jnp.where(row_of((8, N)) < 4, rest[32:40], 0.0)
 
 
-def finish_kernel(own, other, threes, own_grad, face, corner, forces, grad_embed, grad_radial, grad_up,
+def finish_kernel(own, other, threes, own_grad, home, forces, grad_embed, grad_radial, grad_up,
                   grad_charge, grad_read):
     mean = 1.0 / ATOMS
     core = lax.axis_index("c")
@@ -482,12 +512,8 @@
     sixes = other[88:96, :]
     grad = own_grad[...]
     lane_rows = row_of((N, N))
-    for piece, faces, corners in (
-        (sixes, (0,), (0, 1)),
-        (pltpu.roll(sixes, 4, 0), (1,), (2, 3)),
-        (threes[...], (2, 3), ()),
-    ):
-        onehot = jnp.where(lane_rows == joined(face, corner, faces, corners), 1.0, 0.0)
+    for number, piece in enumerate((sixes, pltpu.roll(sixes, 4, 0), threes[...])):
+        onehot = jnp.where(lane_rows == home[number : number + 1, :], 1.0, 0.0)
         grad = grad + dot(piece, onehot, 1, 1)
     forces[...] = -grad[0:3, :]
 
@@ -501,7 +527,7 @@
         out[pl.ds(pl.multiple_of(member * SHARD, SHARD), SHARD), :] = shard[...]
 
 
-def structure_kernel(shared, kvec, embed, w_up, w_charge, factor, wave_high, wave_low, charges,
+def structure_kernel(mine, other, kvec, embed, w_up, factor, wave_high, wave_low,
                      feature_high, feature_low):
     me = lax.axis_index(GROUP)
     at = pl.multiple_of(me * SHARD, SHARD)
@@ -511,16 +537,15 @@
     turns = jnp.transpose(rows * (1.0 / (2.0 * math.pi)))
     table = jnp.concatenate([embed[...], jnp.zeros((2, N), jnp.float32)], axis=0)
     up = split(w_up[...])
-    charge_w = split(w_charge[...])
     for member in range(MEMBERS):
         part = slice(member * N, (member + 1) * N)
-        tail = shared[member, N : N + 8, :]
+        tile = (mine, other)[member // 4].at[member % 4]
+        tail = tile[N : N + 8, :]
         onehot = (row_of((8, N)).astype(jnp.float32) == tail[3:4, :]).astype(jnp.float32)
-        feature = dot(onehot, table, 0, 0) + dot_three(split(shared[member, 0:N, :]), up)
+        feature = dot(onehot, table, 0, 0) + dot_three(split(tile[0:N, :]), up)
         high, low = split(feature)
         feature_high[part, :] = high
         feature_low[part, :] = low
-        charges[part, :] = dot_three((high, low), charge_w)
         for chunk in range(SHARD // 64):
             waves = slice(chunk * 64, chunk * 64 + 64)
             angle = (
@@ -547,6 +572,10 @@
     project(wave_high, wave_low, feature_high[...], feature_low[...], factor)
 
 
+def whole(mine, other):
+    return jnp.concatenate([mine[...].reshape(4 * N, N), other[...].reshape(4 * N, N)], axis=0)
+
+
 def project(wave_high, wave_low, high, low, out):
     both = jnp.concatenate([high, low], axis=1)
     wide = half_dot(wave_high[...], both)
@@ -554,8 +583,8 @@
     out[...] = total.reshape(CROSSES, 16, N)
 
 
-def projection_kernel(gathered, wave_high, wave_low, out):
-    high, low = split(gathered[...].reshape(MEMBERS * N, N))
+def projection_kernel(mine, other, wave_high, wave_low, out):
+    high, low = split(whole(mine, other))
     project(wave_high, wave_low, high, low, out)
 
 
@@ -576,7 +605,8 @@
     return wide[0:N] + wide[N:] + half_dot(high, wave_low[...])
 
 
-def potential_kernel(factor, w_charge, kfilter, wave_high, wave_low, out, weighted, charge_factor):
+def potential_kernel(factor, w_charge, kfilter, wave_high, wave_low,
+                     mine, other, weighted, charge_factor):
     scaled = filter_of(kfilter)
     charged = dot(factor[...], w_charge[...])
     charge_factor[...] = charged
@@ -584,13 +614,13 @@
     weighted[...] = field
     total = waves_to_atoms(field, wave_high, wave_low)
     for member in range(MEMBERS):
-        out[member, :, :] = total[:, member * N : (member + 1) * N]
+        (mine, other)[member // 4][member % 4] = total[:, member * N : (member + 1) * N]
 
 
 def energy_kernel(tiles, active, species, embed, w_up, read,
                   shared, grad_out, energy, read_row, up_part):
     total = tiles[0]
-    for member in range(1, MEMBERS):
+    for member in range(1, 4):
         total = total + tiles[member]
     table = jnp.concatenate([embed[...], jnp.zeros((2, N), jnp.float32)], axis=0)
     onehot = (row_of((8, N)) == species[...]).astype(jnp.float32)
@@ -604,7 +634,7 @@
     grad = weights * (logistic * (1.0 + combined * (1.0 - logistic)))
     grad_out[...] = grad
     up_part[...] = dot(act, grad, 0, 0)
-    for member in range(MEMBERS):
+    for member in range(4):
         shared[member, :, :] = grad
 
 
@@ -614,8 +644,31 @@
     return cosine, sine
 
 
-def by_position(fields, atoms, kvec, wave_high, wave_low):
-    along = dot_three(split(fields), split(atoms), 1, 1)
+def wave_back_kernel(projected, factor, charge_factor, weighted, kfilter, kvec, wave_high, wave_low,
+                     grad_mine, grad_other, feature_high, feature_low, shared_mine, shared_other,
+                     w_charge, up_part, mine, other, grad_filter, up_grad, charge_grad):
+    scaled = filter_of(kfilter)
+    proj = projected[...]
+    mixed = charge_factor[...] * proj
+    grad_filter[...] = SCALE * (mixed[0:SHARD] + mixed[SHARD:])
+    field = proj * jnp.concatenate([scaled, scaled], axis=0)
+    pieces = split(field)
+    by_charge = waves_to_atoms(field, wave_high, wave_low)
+    charge_grad[...] = dot_three(split(factor[...]), pieces, 0, 0)
+    active = whole(shared_mine.at[:, 0:N, :], shared_other.at[:, 0:N, :])
+    mix = dot_three(split(by_charge), split(active))
+    weights = split(w_charge[...])
+    up_grad[...] = dot_three(split(mix), weights, 0, 1) + up_part[...]
+    by_feature = dot_three(pieces, weights, 1, 1)
+    grad_high, grad_low = split(whole(grad_mine, grad_other))
+    along = dot_three(
+        split(jnp.concatenate([weighted[...], by_feature], axis=1)),
+        (
+            jnp.concatenate([grad_high, feature_high[...]], axis=1),
+            jnp.concatenate([grad_low, feature_low[...]], axis=1),
+        ),
+        1, 1,
+    )
     cosine, sine = wave_trig(wave_high, wave_low)
     phase = cosine * along[SHARD:] - sine * along[0:SHARD]
     me = lax.axis_index(GROUP)
@@ -626,42 +679,38 @@
         ],
         axis=0,
     )
-    return dot_three(split(rows), split(phase))
-
-
-def wave_back_kernel(projected, factor, charge_factor, weighted, kfilter, kvec, wave_high, wave_low,
-                     gathered, charges, shared, w_charge, up_part, out, grad_filter):
-    scaled = filter_of(kfilter)
-    proj = projected[...]
-    mixed = charge_factor[...] * proj
-    grad_filter[...] = SCALE * (mixed[0:SHARD] + mixed[SHARD:])
-    field = proj * jnp.concatenate([scaled, scaled], axis=0)
-    charge_grad = dot_three(split(factor[...]), split(field), 0, 0)
-    by_charge = waves_to_atoms(field, wave_high, wave_low)
-    active = jnp.concatenate([shared[member, 0:N, :] for member in range(MEMBERS)], axis=0)
-    mix = dot_three(split(by_charge), split(active))
-    up_grad = dot(mix, w_charge[...], 0, 1) + up_part[...]
-    by_pos = by_position(
-        jnp.concatenate([weighted[...], field], axis=1),
-        jnp.concatenate([gathered[...].reshape(MEMBERS * N, N), charges[...]], axis=1),
-        kvec, wave_high, wave_low,
-    )
+    by_pos = dot_three(split(rows), split(phase))
+    core = lax.axis_index("c")
     for member in range(MEMBERS):
         part = slice(member * N, (member + 1) * N)
-        out[member, 0:N, :] = by_charge[:, part]
-        out[member, N : N + 8, :] = by_pos[:, part]
-        out[member, N + 8 : N + 24, :] = up_grad[member * 16 : (member + 1) * 16]
-        out[member, N + 24 : N + 40, :] = charge_grad[member * 16 : (member + 1) * 16]
+        out = (mine, other)[member // 4].at[member % 4]
+        place = jnp.where(core == member // 4, member % 4, 4 + member % 4) * 16
+        piece = pl.ds(pl.multiple_of(place, 16), 16)
+        out[0:N, :] = by_charge[:, part]
+        out[N : N + 8, :] = by_pos[:, part]
+        out[N + 8 : N + 24, :] = up_grad[piece, :]
+        out[N + 24 : N + 40, :] = charge_grad[piece, :]
 
 
 def body(
     positions, species, neighbours, face_sends, corner_sends,
     embed, radial, w_up, w_charge, kvec, kfilter, read,
 ):
-    species = species.reshape(1, N)
-    read = read.reshape(1, N)
-    near, far, own_x = call(
-        pack_kernel, (f32(8, N),) * 3, positions, species, face_sends, corner_sends
+    near, far, own_x, home, positions, species, neighbours, embed, radial, read = call(
+        pack_kernel,
+        (f32(8, N),) * 3
+        + (
+            i32(8, N), f32(3, N), i32(1, N), i32(SLOTS, N), f32(KINDS, N), f32(2, BASIS, N),
+            f32(1, N),
+        ),
+        positions, species.reshape(1, N), face_sends, corner_sends, neighbours, embed, radial,
+        read.reshape(1, N),
+        scratch=(
+            pltpu.VMEM((4, N // 2), jnp.int32),
+            pltpu.VMEM((4, N // 4), jnp.int32),
+            pltpu.SemaphoreType.DMA((8,)),
+        ),
+        far=True,
     )
     near_y, far_y = swapped(near, GY, 0), swapped(far, GY, 1)
     near, far = call(relay_kernel, (f32(8, N),) * 2, own_x, near_y, far_y)
@@ -669,19 +718,27 @@
     shared, active, invariants, vectors, sums, edges, places = call(
         edge_kernel,
         (
-            f32(MEMBERS, N + 8, N), f32(N, N), f32(N, N), f32(3, N, N), f32(4, KINDS * BASIS, N),
-            f32(7, SLOTS, N), jax.ShapeDtypeStruct((2, SLOTS, N), jnp.int32),
+            f32(4, N + 8, N), f32(N, N), f32(N, N), f32(3, N, N), f32(4, KINDS * BASIS, N),
+            f32(7, SLOTS, N), i32(2, SLOTS, N),
         ),
         positions, species, neighbours, near_x, far_x, near_y, far_y, embed, radial,
     )
-    shared = lax.all_to_all(shared, GROUP, 0, 0)
+    swap = [(0, 1), (1, 0)]
+
+    def other_core(value):
+        return lax.ppermute(value, "c", swap)
+
+    def row_exchange(tiles):
+        return lax.all_to_all(tiles, "x", 0, 0)
+
+    shared = row_exchange(shared)
+    shared_other = other_core(shared)
     half = jax.ShapeDtypeStruct((2 * SHARD, MEMBERS * N), jnp.bfloat16)
-    scratch = pltpu.VMEM((MEMBERS * N, N), jnp.bfloat16)
-    factor, wave_high, wave_low, charges = call(
+    feature = jax.ShapeDtypeStruct((MEMBERS * N, N), jnp.bfloat16)
+    factor, wave_high, wave_low, feature_high, feature_low = call(
         structure_kernel,
-        (f32(CROSSES, 16, N), half, half, f32(MEMBERS * N, N)),
-        shared, kvec, embed, w_up, w_charge,
-        scratch=(scratch, scratch),
+        (f32(CROSSES, 16, N), half, half, feature, feature),
+        shared, shared_other, kvec, embed, w_up,
     )
 
     def cross_sum(tiles):
@@ -690,48 +747,53 @@
         return lax.all_to_all(tiles, CROSS, 0, 0).reshape(2 * SHARD, N)
 
     factor = cross_sum(factor)
-    potential, weighted, charge_factor = call(
+    mine, other, weighted, charge_factor = call(
         potential_kernel,
-        (f32(MEMBERS, N, N), f32(2 * SHARD, N), f32(2 * SHARD, N)),
+        (f32(4, N, N), f32(4, N, N), f32(2 * SHARD, N), f32(2 * SHARD, N)),
         factor, w_charge, kfilter, wave_high, wave_low,
     )
-    potential = lax.all_to_all(potential, GROUP, 0, 0)
-    gathered, grad_out, energy, read_row, up_part = call(
+    potential = row_exchange(mine + other_core(other))
+    grads, grad_out, energy, read_row, up_part = call(
         energy_kernel,
-        (f32(MEMBERS, N, N), f32(N, N), f32(1, N), f32(1, N), f32(N, N)),
+        (f32(4, N, N), f32(N, N), f32(1, N), f32(1, N), f32(N, N)),
         potential, active, species, embed, w_up, read,
     )
-    gathered = lax.all_to_all(gathered, GROUP, 0, 0)
-    projected = call(projection_kernel, f32(CROSSES, 16, N), gathered, wave_high, wave_low)
-    projected = cross_sum(projected)
-    tiles, shard = call(
+    grads = row_exchange(grads)
+    grads_other = other_core(grads)
+    projected = cross_sum(
+        call(projection_kernel, f32(CROSSES, 16, N), grads, grads_other, wave_high, wave_low)
+    )
+    square = pltpu.VMEM((N, N), jnp.float32)
+    mine, other, shard = call(
         wave_back_kernel,
-        (f32(MEMBERS, N + 40, N), f32(SHARD, N)),
+        (f32(4, N + 40, N), f32(4, N + 40, N), f32(SHARD, N)),
         projected, factor, charge_factor, weighted, kfilter, kvec, wave_high, wave_low,
-        gathered, charges, shared, w_charge, up_part,
-    )
-    swap = [(0, 1), (1, 0)]
+        grads, grads_other, feature_high, feature_low, shared, shared_other, w_charge, up_part,
+        scratch=(square, square),
+    )
+    tiles = row_exchange(mine + other_core(other))
     shards = [shard] + [
         lax.ppermute(shard, "x", [(at, (at + step) % 4) for at in range(4)]) for step in (1, 2, 3)
     ]
-    shards += [lax.ppermute(value, "c", swap) for value in shards]
-    tiles = lax.all_to_all(tiles, GROUP, 0, 0)
     payload, own_grad, charge_piece = call(
         edge_back_kernel,
         (f32(8, 56, N), f32(8, N), f32(16, N)),
         tiles, active, invariants, vectors, sums, edges, places, embed, radial, w_up,
         w_charge, species, grad_out, read_row,
-    )
+        cost=pl.CostEstimate(flops=10**9, bytes_accessed=10**7, transcendentals=10**5),
+    )
+    payload, *shards = lax.optimization_barrier((payload, *shards))
     payload = lax.all_to_all(payload, DEPTH, 0, 0)
     payload = call(depth_sum_kernel, f32(16, 56, N), payload, charge_piece)
     payload = lax.all_to_all(payload, PLANE, 0, 0)
     payload, threes = call(plane_sum_kernel, (f32(160, N), f32(8, N)), payload)
-    other = lax.ppermute(payload, "c", swap)
+    shards += [other_core(value) for value in shards]
+    payload_other = other_core(payload)
     grad_filter = call(spread_kernel, f32(WAVES, N), *shards)
     forces, grad_embed, grad_radial, grad_up, grad_charge, grad_read = call(
         finish_kernel,
         (f32(3, N), f32(KINDS, N), f32(2, BASIS, N), f32(N, N), f32(N, N), f32(1, N)),
-        payload, other, threes, own_grad, face_sends, corner_sends,
+        payload, payload_other, threes, own_grad, home,
     )
     return (
         energy.reshape(N), forces, grad_embed, grad_radial, grad_up, grad_charge, grad_filter,

time: 198 us -> 187 us (0.944)
  blocking collectives: 140 us -> 100 us
  starting transfers between devices: 27.8 us -> 44.3 us
  waiting for transfers between devices: 4.8 us -> 18.5 us
    all_to_all x4 -> x3, blocking collectives: 64.5 us -> 25.3 us  [row_exchange(): return lax.all_to_all(tiles, 'x', 0, 0)]
    ppermute x5 -> x9, starting transfers between devices: 10.3 us -> 23.1 us  [other_core(): return lax.ppermute(value, 'c', swap)]
    all_to_all x1, waiting for transfers between devices: 0.01 us -> 5.89 us  [body(): payload = lax.all_to_all(payload, PLANE, 0, 0)]
    ppermute x5 -> x9, waiting for transfers between devices: 0.82 us -> 4.8 us  [other_core(): return lax.ppermute(value, 'c', swap)]
    all_to_all x0 -> x1, waiting for transfers between devices: none -> 3.47 us  [row_exchange(): return lax.all_to_all(tiles, 'x', 0, 0)]
    all_to_all x0 -> x1, starting transfers between devices: none -> 3.46 us  [row_exchange(): return lax.all_to_all(tiles, 'x', 0, 0)]
    unnamed x30 -> x24, local copies, waits for them, and re-layouts: 4.82 us -> 4.19 us
  transfers between devices with their start and end apart: 13 -> 18, of which waited for: 4 -> 9; matrix products, arithmetic and copies ran while one was open for 0% -> 0% of each run, Pallas kernels for 1% -> 3%
where the time goes in v3:
time: 187 us; the launch traced here: 186 us
  blocking collectives  100 us (53%)
  starting transfers between devices  44.3 us (24%)
  waiting for transfers between devices  18.5 us (10%)
  Pallas kernels  17.8 us (10%)
  local copies, waits for them, and re-layouts  4.19 us (2%)
    all_to_all x2, blocking collectives, cross_sum(): return lax.all_to_all(tiles, CROSS, 0, 0).reshape(2 * SHARD, N)  32.5 us
    all_to_all x2, blocking collectives, cross_sum(): tiles = lax.all_to_all(tiles, CROSS, 0, 0)  29.5 us
    all_to_all x3, blocking collectives, row_exchange(): return lax.all_to_all(tiles, 'x', 0, 0)  25.3 us
    ppermute x9, starting transfers between devices, other_core(): return lax.ppermute(value, 'c', swap)  23.1 us
    pallas_call x15, Pallas kernels, call(): pl.pallas_call(kernel, out_shape=out_shape, scratch_shapes=list(scratch),...  17.8 us
    all_to_all x1, blocking collectives, body(): payload = lax.all_to_all(payload, DEPTH, 0, 0)  12.8 us
    ppermute x4, starting transfers between devices, swapped(): return lax.ppermute(value, axes, places)  10.4 us
    all_to_all x1, waiting for transfers between devices, body(): payload = lax.all_to_all(payload, PLANE, 0, 0)  5.89 us
  transfers between devices with their start and end apart: 18, of which 9 were waited for; matrix products, arithmetic and copies ran while one was open for 0% of the time, Pallas kernels for 3%

profile of v3, /device:TPU:1, one launch (start us, length us, event | category | flops | bytes accessed | tf_op | source)
XLA Modules:
  0.0 186.5 jit_solution(558782016400071456)
XLA Ops:
  0.7 0.7 copy-done.7
  1.3 0.8 copy-done.4
  2.1 0.7 copy-done.5
  2.8 0.7 copy-done.6
  3.5 0.7 copy-done.8
  4.2 0.7 copy-done.9
  4.8 0.3 shard_map.179
  5.1 2.1 %collective-permute-start = (f32[8,128]{1,0:T(8,128)S(1)}, f32[8,128]{1,0:T(8,128)S(1)}, u32[]{:S(2)}, u32[]{:S(2)}) collective-permute-start(f32[8,128]{1,0:T(8,128)S(1)} %get-tuple-element.64), channel_id=1, source_target_pairs={{0,1},{1,0},{2,3},{3,2},{4,5},{5,4},{6,7},{7,6},{8,9},{9,8},{10,11... | collective-permute-start | bytes 12296 | tf_op jit(solution)/shard_map/ppermute | solution.py:184
  7.2 3.2 %collective-permute-start.1 = (f32[8,128]{1,0:T(8,128)S(1)}, f32[8,128]{1,0:T(8,128)S(1)}, u32[]{:S(2)}, u32[]{:S(2)}) collective-permute-start(f32[8,128]{1,0:T(8,128)S(1)} %get-tuple-element.65), channel_id=1, source_target_pairs={{0,7},{1,2},{2,1},{3,4},{4,3},{5,6},{6,5},{7,0},{8,15},{9,10},{10,... | collective-permute-start | bytes 12296 | tf_op jit(solution)/shard_map/ppermute | solution.py:184
  10.4 1.4 collective-permute-done.1.far.far_y
  11.8 0.1 shard_map.180
  11.9 2.5 %collective-permute-start.2 = (f32[8,128]{1,0:T(8,128)S(1)}, f32[8,128]{1,0:T(8,128)S(1)}, u32[]{:S(2)}, u32[]{:S(2)}) collective-permute-start(f32[8,128]{1,0:T(8,128)S(1)} %get-tuple-element.66), channel_id=1, source_target_pairs={{0,8},{8,0},{16,24},{24,16},{32,40},{40,32},{48,56},{56,48},{64,72... | collective-permute-start | bytes 12296 | tf_op jit(solution)/shard_map/ppermute | solution.py:184
  14.4 2.6 %collective-permute-start.3 = (f32[8,128]{1,0:T(8,128)S(1)}, f32[8,128]{1,0:T(8,128)S(1)}, u32[]{:S(2)}, u32[]{:S(2)}) collective-permute-start(f32[8,128]{1,0:T(8,128)S(1)} %get-tuple-element.67), channel_id=1, source_target_pairs={{0,248},{8,16},{16,8},{24,32},{32,24},{40,48},{48,40},{56,64},{64,... | collective-permute-start | bytes 12296 | tf_op jit(solution)/shard_map/ppermute | solution.py:184
  17.0 0.0 collective-permute-done.2.near_x
  17.0 1.3 collective-permute-done.3.far_x
  18.3 1.4 shard_map.181
  19.7 0.0 copy-start.2
  19.8 0.0 copy-start.3
  19.8 8.6 %all_to_all.50.mine.shared_mine = f32[4,136,128]{2,1,0:T(8,128)S(1)} all-to-all(f32[4,136,128]{2,1,0:T(8,128)S(1)} %get-tuple-element.70), channel_id=1, replica_groups=mesh['y'=4,'zh'=4,'c'=2,'zl'=2,'x'=4] {'x'}, dimensions={0} | all-to-all | bytes 557056 | tf_op jit(solution)/shard_map/all_to_all | solution.py:732
  28.4 7.4 %collective-permute-start.4 = (f32[4,136,128]{2,1,0:T(8,128)S(1)}, f32[4,136,128]{2,1,0:T(8,128)S(1)}, u32[]{:S(2)}, u32[]{:S(2)}) collective-permute-start(f32[4,136,128]{2,1,0:T(8,128)S(1)} %all_to_all.50.mine.shared_mine), channel_id=1, source_target_pairs={{0,8},{8,0},{1,9},{9,1},{2,10},{10,2},{3,11},{11,3},{4,12},{12,4},... | collective-permute-start | bytes 835592 | tf_op jit(solution)/shard_map/ppermute | solution.py:729
  35.8 1.2 collective-permute-done.4.other.shared_other
  36.9 2.6 %shard_map.182 = (f32[32,16,128]{2,1,0:T(8,128)S(1)}, bf16[512,1024]{1,0:T(8,128)(2,1)S(1)}, bf16[512,1024]{1,0:T(8,128)(2,1)S(1)}, bf16[1024,128]{1,0:T(8,128)(2,1)S(1)}, bf16[1024,128]{1,0:T(8,128)(2,1)S(1)}) custom-call(f32[4,136,128]{2,1,0:T(8,128)S(1)} %all_to_all.50.mine.shared_mine, f32[4,136,128]{2,1,0:T(8,128)S(1)} %collective-permute-done.4.other.shared_other, ...), custom_call_target="tpu_custom_call" | custom-call | tf_op jit(solution)/shard_map/pallas_call | solution.py:105
  39.5 15.7 %all_to_all.51.tiles = f32[32,16,128]{2,1,0:T(8,128)S(1)} all-to-all(f32[32,16,128]{2,1,0:T(8,128)S(1)} %get-tuple-element.71), channel_id=1, replica_groups=mesh['y'=4,'zh'=4,'c'=2,'zl'=2,'x'=4] {'y','zh','zl'}, dimensions={0} | all-to-all | bytes 524288 | tf_op jit(solution)/shard_map/all_to_all | solution.py:745
  55.3 0.1 shard_map.183
  55.3 0.0 copy-start.1
  55.3 16.3 %all_to_all.52 = f32[32,16,128]{2,1,0:T(8,128)S(1)} all-to-all(f32[32,16,128]{2,1,0:T(8,128)S(1)} %shard_map.183), channel_id=1, replica_groups=mesh['y'=4,'zh'=4,'c'=2,'zl'=2,'x'=4] {'y','zh','zl'}, dimensions={0} | all-to-all | bytes 524288 | tf_op jit(solution)/shard_map/all_to_all | solution.py:747
  71.6 1.3 shard_map.184
  72.9 3.7 %collective-permute-start.5 = (f32[4,128,128]{2,1,0:T(8,128)S(1)}, f32[4,128,128]{2,1,0:T(8,128)S(1)}, u32[]{:S(2)}, u32[]{:S(2)}) collective-permute-start(f32[4,128,128]{2,1,0:T(8,128)S(1)} %get-tuple-element.75), channel_id=1, source_target_pairs={{0,8},{8,0},{1,9},{9,1},{2,10},{10,2},{3,11},{11,3},{4,12},{12,4},... | collective-permute-start | bytes 786440 | tf_op jit(solution)/shard_map/ppermute | solution.py:729
  76.6 1.2 collective-permute-done.5
  77.8 8.8 %all_to_all.53.tiles = f32[4,128,128]{2,1,0:T(8,128)S(1)} all-to-all(f32[4,128,128]{2,1,0:T(8,128)S(1)} %add.6), channel_id=1, replica_groups=mesh['y'=4,'zh'=4,'c'=2,'zl'=2,'x'=4] {'x'}, dimensions={0} | all-to-all | bytes 524288 | tf_op jit(solution)/shard_map/all_to_all | solution.py:732
  86.6 1.2 shard_map.185
  87.8 7.9 %all_to_all.54.mine.grad_mine = f32[4,128,128]{2,1,0:T(8,128)S(1)} all-to-all(f32[4,128,128]{2,1,0:T(8,128)S(1)} %get-tuple-element.79), channel_id=1, replica_groups=mesh['y'=4,'zh'=4,'c'=2,'zl'=2,'x'=4] {'x'}, dimensions={0} | all-to-all | bytes 524288 | tf_op jit(solution)/shard_map/all_to_all | solution.py:732
  95.7 2.4 %collective-permute-start.6 = (f32[4,128,128]{2,1,0:T(8,128)S(1)}, f32[4,128,128]{2,1,0:T(8,128)S(1)}, u32[]{:S(2)}, u32[]{:S(2)}) collective-permute-start(f32[4,128,128]{2,1,0:T(8,128)S(1)} %all_to_all.54.mine.grad_mine), channel_id=1, source_target_pairs={{0,8},{8,0},{1,9},{9,1},{2,10},{10,2},{3,11},{11,3},{4,12},{12,4},... | collective-permute-start | bytes 786440 | tf_op jit(solution)/shard_map/ppermute | solution.py:729
  98.0 1.2 collective-permute-done.6.other.grad_other
  99.2 0.7 shard_map.186
  99.9 13.7 %all_to_all.55.tiles = f32[32,16,128]{2,1,0:T(8,128)S(1)} all-to-all(f32[32,16,128]{2,1,0:T(8,128)S(1)} %shard_map.186), channel_id=1, replica_groups=mesh['y'=4,'zh'=4,'c'=2,'zl'=2,'x'=4] {'y','zh','zl'}, dimensions={0} | all-to-all | bytes 524288 | tf_op jit(solution)/shard_map/all_to_all | solution.py:745
  113.7 0.1 shard_map.187
  113.7 16.2 %all_to_all.56 = f32[32,16,128]{2,1,0:T(8,128)S(1)} all-to-all(f32[32,16,128]{2,1,0:T(8,128)S(1)} %shard_map.187), channel_id=1, replica_groups=mesh['y'=4,'zh'=4,'c'=2,'zl'=2,'x'=4] {'y','zh','zl'}, dimensions={0} | all-to-all | bytes 524288 | tf_op jit(solution)/shard_map/all_to_all | solution.py:747
  129.9 2.5 %shard_map.188 = (f32[4,168,128]{2,1,0:T(8,128)S(1)}, f32[4,168,128]{2,1,0:T(8,128)S(1)}, f32[256,128]{1,0:T(8,128)S(1)}) custom-call(f32[512,128]{1,0:T(8,128)S(1)} %bitcast.8, f32[512,128]{1,0:T(8,128)S(1)} %bitcast.7, f32[512,128]{1,0:T(8,128)S(1)} %get-tuple-element.80.charge_factor, f32[512,128]{1,0:T(8,128)S(1)} %get-tuple-element.81.weighted, ...), custom_call_target="tpu_custom_call" | custom-call | tf_op jit(solution)/shard_map/pallas_call | solution.py:105
  132.4 3.6 %collective-permute-start.7 = (f32[4,168,128]{2,1,0:T(8,128)S(1)}, f32[4,168,128]{2,1,0:T(8,128)S(1)}, u32[]{:S(2)}, u32[]{:S(2)}) collective-permute-start(f32[4,168,128]{2,1,0:T(8,128)S(1)} %get-tuple-element.86), channel_id=1, source_target_pairs={{0,8},{8,0},{1,9},{9,1},{2,10},{10,2},{3,11},{11,3},{4,12},{12,4},... | collective-permute-start | bytes 1032200 | tf_op jit(solution)/shard_map/ppermute | solution.py:729
  136.1 1.3 collective-permute-done.7
  137.3 0.8 add.7
  138.1 3.5 %all-to-all-start.7 = ((f32[4,168,128]{2,1,0:T(8,128)}), f32[4,168,128]{2,1,0:T(8,128)S(1)}, u32[]{:S(2)}, u32[]{:S(2)}) async-start(f32[4,168,128]{2,1,0:T(8,128)} %add.7), calls=%async_computation.7 | async-start | bytes 688128 | tf_op jit(solution)/shard_map/all_to_all | solution.py:732
  141.6 2.6 %collective-permute-start.10 = (f32[256,128]{1,0:T(8,128)S(1)}, f32[256,128]{1,0:T(8,128)S(1)}, u32[]{:S(2)}, u32[]{:S(2)}) collective-permute-start(f32[256,128]{1,0:T(8,128)S(1)} %get-tuple-element.107.refs_0_), channel_id=1, source_target_pairs={{0,3},{1,0},{2,1},{3,2},{4,7},{5,4},{6,5},{7,6},{8,11},{9,8},{10,9... | collective-permute-start | bytes 393224 | tf_op jit(solution)/shard_map/ppermute | solution.py:776
  144.2 0.6 collective-permute-start.9
  144.8 0.6 collective-permute-start.8
  145.4 3.5 %all-to-all-done.7.tiles = f32[4,168,128]{2,1,0:T(8,128)S(1)} async-done(((f32[4,168,128]{2,1,0:T(8,128)}), f32[4,168,128]{2,1,0:T(8,128)S(1)}, u32[]{:S(2)}, u32[]{:S(2)}) %all-to-all-start.7) | async-done | bytes 344096 | tf_op jit(solution)/shard_map/all_to_all | solution.py:732
  148.8 4.7 %shard_map.189 = (f32[8,56,128]{2,1,0:T(8,128)S(1)}, f32[8,128]{1,0:T(8,128)S(1)}, f32[16,128]{1,0:T(8,128)S(1)}) custom-call(f32[4,168,128]{2,1,0:T(8,128)S(1)} %all-to-all-done.7.tiles, f32[128,128]{1,0:T(8,128)S(1)} %get-tuple-element.76.active, f32[128,128]{1,0:T(8,128)S(1)} %get-tuple-element.87.invariants, ...), custom_call_target="tpu_custom_call" | custom-call | flops 1000000000 | bytes 10000000 | tf_op jit(solution)/shard_map/pallas_call | solution.py:105
  153.5 0.0 collective-permute-done.9.refs_2_
  153.6 1.6 collective-permute-done.8.refs_1_
  155.1 12.8 %all_to_all.57.tiles = f32[8,56,128]{2,1,0:T(8,128)S(1)} all-to-all(f32[8,56,128]{2,1,0:T(8,128)S(1)} %get-tuple-element.96), channel_id=1, replica_groups=mesh['y'=4,'zh'=4,'c'=2,'zl'=2,'x'=4] {'zh','zl'}, dimensions={0} | all-to-all | bytes 458752 | tf_op jit(solution)/shard_map/all_to_all | solution.py:786
  168.0 0.8 shard_map.190
  168.8 3.6 %all-to-all-start.9 = ((f32[16,56,128]{2,1,0:T(8,128)}), f32[16,56,128]{2,1,0:T(8,128)S(1)}, u32[]{:S(2)}, u32[]{:S(2)}) async-start(f32[16,56,128]{2,1,0:T(8,128)} %shard_map.190), calls=%async_computation.9 | async-start | bytes 917504 | tf_op jit(solution)/shard_map/all_to_all | solution.py:788
  172.4 2.3 %collective-permute-start.12 = (f32[256,128]{1,0:T(8,128)S(1)}, f32[256,128]{1,0:T(8,128)S(1)}, u32[]{:S(2)}, u32[]{:S(2)}) collective-permute-start(f32[256,128]{1,0:T(8,128)S(1)} %get-tuple-element.107.refs_0_), channel_id=1, source_target_pairs={{0,8},{8,0},{1,9},{9,1},{2,10},{10,2},{3,11},{11,3},{4,12},{12,4},... | collective-permute-start | bytes 393224 | tf_op jit(solution)/shard_map/ppermute | solution.py:729
  174.7 0.1 collective-permute-start.13
  174.8 0.4 collective-permute-start.14
  175.2 0.1 collective-permute-start.15
  175.3 5.9 %all-to-all-done.9.tiles = f32[16,56,128]{2,1,0:T(8,128)S(1)} async-done(((f32[16,56,128]{2,1,0:T(8,128)}), f32[16,56,128]{2,1,0:T(8,128)S(1)}, u32[]{:S(2)}, u32[]{:S(2)}) %all-to-all-start.9) | async-done | bytes 458784 | tf_op jit(solution)/shard_map/all_to_all | solution.py:788
  181.2 3.2 %collective-permute-start.11 = (f32[160,128]{1,0:T(8,128)S(1)}, f32[160,128]{1,0:T(8,128)S(1)}, u32[]{:S(2)}, u32[]{:S(2)}) collective-permute-start(f32[160,128]{1,0:T(8,128)S(1)} %get-tuple-element.98.own), channel_id=1, source_target_pairs={{0,8},{8,0},{1,9},{9,1},{2,10},{10,2},{3,11},{11,3},{4,12},{12,4},... | collective-permute-start | bytes 245768 | tf_op jit(solution)/shard_map/ppermute | solution.py:729
  184.4 0.0 collective-permute-done.12.refs_4_
  184.4 0.0 collective-permute-done.13.refs_5_
  184.4 0.0 collective-permute-done.14.refs_6_
  184.4 1.1 shard_map.193
  185.5 1.0 shard_map.192
  (21 shorter events, 0.1 us)
Async XLA Ops:
  0.6 0.7 copy-start.7
  0.6 0.7 copy-start.10
  0.7 0.7 copy-start.11
  1.3 0.8 copy-start.4
  2.1 0.7 copy-start.5
  2.8 0.7 copy-start.6
  3.5 0.7 copy-start.8
  4.2 0.7 copy-start.9
  5.1 5.3 %collective-permute-start = (f32[8,128]{1,0:T(8,128)S(1)}, f32[8,128]{1,0:T(8,128)S(1)}, u32[]{:S(2)}, u32[]{:S(2)}) collective-permute-start(f32[8,128]{1,0:T(8,128)S(1)} %get-tuple-element.64), channel_id=1, source_target_pairs={{0,1},{1,0},{2,3},{3,2},{4,5},{5,4},{6,7},{7,6},{8,9},{9,8},{10,11... | collective-permute-start | bytes 12296 | tf_op jit(solution)/shard_map/ppermute | solution.py:184
  7.2 4.6 %collective-permute-start.1 = (f32[8,128]{1,0:T(8,128)S(1)}, f32[8,128]{1,0:T(8,128)S(1)}, u32[]{:S(2)}, u32[]{:S(2)}) collective-permute-start(f32[8,128]{1,0:T(8,128)S(1)} %get-tuple-element.65), channel_id=1, source_target_pairs={{0,7},{1,2},{2,1},{3,4},{4,3},{5,6},{6,5},{7,0},{8,15},{9,10},{10,... | collective-permute-start | bytes 12296 | tf_op jit(solution)/shard_map/ppermute | solution.py:184
  11.9 5.1 %collective-permute-start.2 = (f32[8,128]{1,0:T(8,128)S(1)}, f32[8,128]{1,0:T(8,128)S(1)}, u32[]{:S(2)}, u32[]{:S(2)}) collective-permute-start(f32[8,128]{1,0:T(8,128)S(1)} %get-tuple-element.66), channel_id=1, source_target_pairs={{0,8},{8,0},{16,24},{24,16},{32,40},{40,32},{48,56},{56,48},{64,72... | collective-permute-start | bytes 12296 | tf_op jit(solution)/shard_map/ppermute | solution.py:184
  14.4 3.9 %collective-permute-start.3 = (f32[8,128]{1,0:T(8,128)S(1)}, f32[8,128]{1,0:T(8,128)S(1)}, u32[]{:S(2)}, u32[]{:S(2)}) collective-permute-start(f32[8,128]{1,0:T(8,128)S(1)} %get-tuple-element.67), channel_id=1, source_target_pairs={{0,248},{8,16},{16,8},{24,32},{32,24},{40,48},{48,40},{56,64},{64,... | collective-permute-start | bytes 12296 | tf_op jit(solution)/shard_map/ppermute | solution.py:184
  19.7 17.2 %copy-start.2 = (f32[128,128]{1,0:T(8,128)S(1)}, f32[128,128]{1,0:T(8,128)}, u32[]{:S(2)}) copy-start(f32[128,128]{1,0:T(8,128)} %w_up.5) | copy-start | bytes 196612
  19.8 17.2 %copy-start.3 = (f32[3,2048]{1,0:T(4,128)S(1)}, f32[3,2048]{1,0:T(4,128)}, u32[]{:S(2)}) copy-start(f32[3,2048]{1,0:T(4,128)} %kvec.3) | copy-start | bytes 73732
  28.4 43.2 %copy-start = (f32[2048,128]{1,0:T(8,128)S(1)}, f32[2048,128]{1,0:T(8,128)}, u32[]{:S(2)}) copy-start(f32[2048,128]{1,0:T(8,128)} %kfilter.3) | copy-start | bytes 3145732
  28.4 8.5 %collective-permute-start.4 = (f32[4,136,128]{2,1,0:T(8,128)S(1)}, f32[4,136,128]{2,1,0:T(8,128)S(1)}, u32[]{:S(2)}, u32[]{:S(2)}) collective-permute-start(f32[4,136,128]{2,1,0:T(8,128)S(1)} %all_to_all.50.mine.shared_mine), channel_id=1, source_target_pairs={{0,8},{8,0},{1,9},{9,1},{2,10},{10,2},{3,11},{11,3},{4,12},{12,4},... | collective-permute-start | bytes 835592 | tf_op jit(solution)/shard_map/ppermute | solution.py:729
  55.3 16.3 %copy-start.1 = (f32[128,128]{1,0:T(8,128)S(1)}, f32[128,128]{1,0:T(8,128)}, u32[]{:S(2)}) copy-start(f32[128,128]{1,0:T(8,128)} %w_charge.5) | copy-start | bytes 196612
  72.9 4.9 %collective-permute-start.5 = (f32[4,128,128]{2,1,0:T(8,128)S(1)}, f32[4,128,128]{2,1,0:T(8,128)S(1)}, u32[]{:S(2)}, u32[]{:S(2)}) collective-permute-start(f32[4,128,128]{2,1,0:T(8,128)S(1)} %get-tuple-element.75), channel_id=1, source_target_pairs={{0,8},{8,0},{1,9},{9,1},{2,10},{10,2},{3,11},{11,3},{4,12},{12,4},... | collective-permute-start | bytes 786440 | tf_op jit(solution)/shard_map/ppermute | solution.py:729
  95.7 3.5 %collective-permute-start.6 = (f32[4,128,128]{2,1,0:T(8,128)S(1)}, f32[4,128,128]{2,1,0:T(8,128)S(1)}, u32[]{:S(2)}, u32[]{:S(2)}) collective-permute-start(f32[4,128,128]{2,1,0:T(8,128)S(1)} %all_to_all.54.mine.grad_mine), channel_id=1, source_target_pairs={{0,8},{8,0},{1,9},{9,1},{2,10},{10,2},{3,11},{11,3},{4,12},{12,4},... | collective-permute-start | bytes 786440 | tf_op jit(solution)/shard_map/ppermute | solution.py:729
  132.4 4.9 %collective-permute-start.7 = (f32[4,168,128]{2,1,0:T(8,128)S(1)}, f32[4,168,128]{2,1,0:T(8,128)S(1)}, u32[]{:S(2)}, u32[]{:S(2)}) collective-permute-start(f32[4,168,128]{2,1,0:T(8,128)S(1)} %get-tuple-element.86), channel_id=1, source_target_pairs={{0,8},{8,0},{1,9},{9,1},{2,10},{10,2},{3,11},{11,3},{4,12},{12,4},... | collective-permute-start | bytes 1032200 | tf_op jit(solution)/shard_map/ppermute | solution.py:729
  138.1 10.7 %all-to-all-start.7 = ((f32[4,168,128]{2,1,0:T(8,128)}), f32[4,168,128]{2,1,0:T(8,128)S(1)}, u32[]{:S(2)}, u32[]{:S(2)}) async-start(f32[4,168,128]{2,1,0:T(8,128)} %add.7), calls=%async_computation.7 | async-start | bytes 688128 | tf_op jit(solution)/shard_map/all_to_all | solution.py:732
  141.6 12.0 %collective-permute-start.10 = (f32[256,128]{1,0:T(8,128)S(1)}, f32[256,128]{1,0:T(8,128)S(1)}, u32[]{:S(2)}, u32[]{:S(2)}) collective-permute-start(f32[256,128]{1,0:T(8,128)S(1)} %get-tuple-element.107.refs_0_), channel_id=1, source_target_pairs={{0,3},{1,0},{2,1},{3,2},{4,7},{5,4},{6,5},{7,6},{8,11},{9,8},{10,9... | collective-permute-start | bytes 393224 | tf_op jit(solution)/shard_map/ppermute | solution.py:776
  144.2 9.3 %collective-permute-start.9 = (f32[256,128]{1,0:T(8,128)S(1)}, f32[256,128]{1,0:T(8,128)S(1)}, u32[]{:S(2)}, u32[]{:S(2)}) collective-permute-start(f32[256,128]{1,0:T(8,128)S(1)} %get-tuple-element.107.refs_0_), channel_id=1, source_target_pairs={{0,2},{1,3},{2,0},{3,1},{4,6},{5,7},{6,4},{7,5},{8,10},{9,11},{10,... | collective-permute-start | bytes 393224 | tf_op jit(solution)/shard_map/ppermute | solution.py:776
  144.8 10.4 %collective-permute-start.8 = (f32[256,128]{1,0:T(8,128)S(1)}, f32[256,128]{1,0:T(8,128)S(1)}, u32[]{:S(2)}, u32[]{:S(2)}) collective-permute-start(f32[256,128]{1,0:T(8,128)S(1)} %get-tuple-element.107.refs_0_), channel_id=1, source_target_pairs={{0,1},{1,2},{2,3},{3,0},{4,5},{5,6},{6,7},{7,4},{8,9},{9,10},{10,1... | collective-permute-start | bytes 393224 | tf_op jit(solution)/shard_map/ppermute | solution.py:776
  168.8 12.3 %all-to-all-start.9 = ((f32[16,56,128]{2,1,0:T(8,128)}), f32[16,56,128]{2,1,0:T(8,128)S(1)}, u32[]{:S(2)}, u32[]{:S(2)}) async-start(f32[16,56,128]{2,1,0:T(8,128)} %shard_map.190), calls=%async_computation.9 | async-start | bytes 917504 | tf_op jit(solution)/shard_map/all_to_all | solution.py:788
  172.4 12.0 %collective-permute-start.12 = (f32[256,128]{1,0:T(8,128)S(1)}, f32[256,128]{1,0:T(8,128)S(1)}, u32[]{:S(2)}, u32[]{:S(2)}) collective-permute-start(f32[256,128]{1,0:T(8,128)S(1)} %get-tuple-element.107.refs_0_), channel_id=1, source_target_pairs={{0,8},{8,0},{1,9},{9,1},{2,10},{10,2},{3,11},{11,3},{4,12},{12,4},... | collective-permute-start | bytes 393224 | tf_op jit(solution)/shard_map/ppermute | solution.py:729
  174.7 9.8 %collective-permute-start.13 = (f32[256,128]{1,0:T(8,128)S(1)}, f32[256,128]{1,0:T(8,128)S(1)}, u32[]{:S(2)}, u32[]{:S(2)}) collective-permute-start(f32[256,128]{1,0:T(8,128)S(1)} %collective-permute-done.8.refs_1_), channel_id=1, source_target_pairs={{0,8},{8,0},{1,9},{9,1},{2,10},{10,2},{3,11},{11,3},{4,12},{12,4},... | collective-permute-start | bytes 393224 | tf_op jit(solution)/shard_map/ppermute | solution.py:729
  174.8 9.7 %collective-permute-start.14 = (f32[256,128]{1,0:T(8,128)S(1)}, f32[256,128]{1,0:T(8,128)S(1)}, u32[]{:S(2)}, u32[]{:S(2)}) collective-permute-start(f32[256,128]{1,0:T(8,128)S(1)} %collective-permute-done.9.refs_2_), channel_id=1, source_target_pairs={{0,8},{8,0},{1,9},{9,1},{2,10},{10,2},{3,11},{11,3},{4,12},{12,4},... | collective-permute-start | bytes 393224 | tf_op jit(solution)/shard_map/ppermute | solution.py:729
  175.2 9.2 %collective-permute-start.15 = (f32[256,128]{1,0:T(8,128)S(1)}, f32[256,128]{1,0:T(8,128)S(1)}, u32[]{:S(2)}, u32[]{:S(2)}) collective-permute-start(f32[256,128]{1,0:T(8,128)S(1)} %collective-permute-done.10.refs_3_), channel_id=1, source_target_pairs={{0,8},{8,0},{1,9},{9,1},{2,10},{10,2},{3,11},{11,3},{4,12},{12,4},... | collective-permute-start | bytes 393224 | tf_op jit(solution)/shard_map/ppermute | solution.py:729
  181.2 4.3 %collective-permute-start.11 = (f32[160,128]{1,0:T(8,128)S(1)}, f32[160,128]{1,0:T(8,128)S(1)}, u32[]{:S(2)}, u32[]{:S(2)}) collective-permute-start(f32[160,128]{1,0:T(8,128)S(1)} %get-tuple-element.98.own), channel_id=1, source_target_pairs={{0,8},{8,0},{1,9},{9,1},{2,10},{10,2},{3,11},{11,3},{4,12},{12,4},... | collective-permute-start | bytes 245768 | tf_op jit(solution)/shard_map/ppermute | solution.py:729

commit v4 on v3

--- a/solution.py
+++ b/solution.py
@@ -101,7 +101,10 @@
 
 
 def call(kernel, out_shape, *args, scratch=(), vmem=32, far=False, cost=None):
-    more = {"in_specs": [pl.BlockSpec(memory_space=pltpu.HBM)] * len(args)} if far else {}
+    more = {}
+    if far:
+        more["in_specs"] = [pl.BlockSpec(memory_space=pltpu.HBM)] * len(args)
+        args = [pltpu.with_memory_space_constraint(value, pltpu.HBM) for value in args]
     return pl.pallas_call(
         kernel,
         out_shape=out_shape,
@@ -302,19 +305,16 @@
     tail = jnp.concatenate(
         [own[0] + anchor_x, own[1] + anchor_y, own[2], own[3]] + [zero_row] * 4, axis=0
     )
-    for member in range(4):
-        shared[member, 0:N, :] = result
-        shared[member, N : N + 8, :] = tail
+    shared[0:N, :] = result
+    shared[N : N + 8, :] = tail
 
 
 def edge_back_kernel(
-    tiles, active, invariants, vectors, sums, edges, places, embed, radial, w_up, w_charge,
+    tile_0, tile_1, tile_2, tile_3, active, invariants, vectors, sums, edges, places, embed, radial, w_up, w_charge,
     species, grad_out, read_row,
     payload, own_grad, charge_piece,
 ):
-    total = tiles[0]
-    for member in range(1, 4):
-        total = total + tiles[member]
+    total = tile_0[...] + tile_1[...] + tile_2[...] + tile_3[...]
     grad_charges = jnp.transpose(total[0:N, :])
     updated = grad_out[...] + dot(grad_charges, w_charge[...], 1, 1)
     value = invariants[...]
@@ -527,8 +527,9 @@
         out[pl.ds(pl.multiple_of(member * SHARD, SHARD), SHARD), :] = shard[...]
 
 
-def structure_kernel(mine, other, kvec, embed, w_up, factor, wave_high, wave_low,
-                     feature_high, feature_low):
+def structure_kernel(*refs):
+    tiles = refs[:MEMBERS]
+    kvec, embed, w_up, factor, wave_high, wave_low, feature_high, feature_low = refs[MEMBERS:]
     me = lax.axis_index(GROUP)
     at = pl.multiple_of(me * SHARD, SHARD)
     rows = jnp.concatenate(
@@ -539,7 +540,7 @@
     up = split(w_up[...])
     for member in range(MEMBERS):
         part = slice(member * N, (member + 1) * N)
-        tile = (mine, other)[member // 4].at[member % 4]
+        tile = tiles[member]
         tail = tile[N : N + 8, :]
         onehot = (row_of((8, N)).astype(jnp.float32) == tail[3:4, :]).astype(jnp.float32)
         feature = dot(onehot, table, 0, 0) + dot_three(split(tile[0:N, :]), up)
@@ -572,8 +573,8 @@
     project(wave_high, wave_low, feature_high[...], feature_low[...], factor)
 
 
-def whole(mine, other):
-    return jnp.concatenate([mine[...].reshape(4 * N, N), other[...].reshape(4 * N, N)], axis=0)
+def whole(tiles):
+    return jnp.concatenate([tile[0:N, :] for tile in tiles], axis=0)
 
 
 def project(wave_high, wave_low, high, low, out):
@@ -583,8 +584,9 @@
     out[...] = total.reshape(CROSSES, 16, N)
 
 
-def projection_kernel(mine, other, wave_high, wave_low, out):
-    high, low = split(whole(mine, other))
+def projection_kernel(*refs):
+    wave_high, wave_low, out = refs[MEMBERS:]
+    high, low = split(whole(refs[:MEMBERS]))
     project(wave_high, wave_low, high, low, out)
 
 
@@ -597,6 +599,11 @@
 def filter_of(kfilter):
     me = lax.axis_index(GROUP)
     return kfilter[pl.ds(pl.multiple_of(me * SHARD, SHARD), SHARD), :] * SCALE
+
+
+def core_sum_kernel(mine, other, *out):
+    for number, ref in enumerate(out):
+        ref[...] = mine[number] + other[number]
 
 
 def waves_to_atoms(field, wave_high, wave_low):
@@ -617,11 +624,9 @@
         (mine, other)[member // 4][member % 4] = total[:, member * N : (member + 1) * N]
 
 
-def energy_kernel(tiles, active, species, embed, w_up, read,
-                  shared, grad_out, energy, read_row, up_part):
-    total = tiles[0]
-    for member in range(1, 4):
-        total = total + tiles[member]
+def energy_kernel(tile_0, tile_1, tile_2, tile_3, active, species, embed, w_up, read,
+                  grad_out, energy, read_row, up_part):
+    total = tile_0[...] + tile_1[...] + tile_2[...] + tile_3[...]
     table = jnp.concatenate([embed[...], jnp.zeros((2, N), jnp.float32)], axis=0)
     onehot = (row_of((8, N)) == species[...]).astype(jnp.float32)
     act = active[...]
@@ -634,8 +639,6 @@
     grad = weights * (logistic * (1.0 + combined * (1.0 - logistic)))
     grad_out[...] = grad
     up_part[...] = dot(act, grad, 0, 0)
-    for member in range(4):
-        shared[member, :, :] = grad
 
 
 def wave_trig(wave_high, wave_low):
@@ -644,9 +647,13 @@
     return cosine, sine
 
 
-def wave_back_kernel(projected, factor, charge_factor, weighted, kfilter, kvec, wave_high, wave_low,
-                     grad_mine, grad_other, feature_high, feature_low, shared_mine, shared_other,
-                     w_charge, up_part, mine, other, grad_filter, up_grad, charge_grad):
+def wave_back_kernel(*refs):
+    grads, shared = refs[:MEMBERS], refs[MEMBERS : 2 * MEMBERS]
+    (
+        projected, factor, charge_factor, weighted, kfilter, kvec, wave_high, wave_low,
+        feature_high, feature_low, w_charge, up_part,
+        mine, other, grad_filter, up_grad, charge_grad,
+    ) = refs[2 * MEMBERS :]
     scaled = filter_of(kfilter)
     proj = projected[...]
     mixed = charge_factor[...] * proj
@@ -655,12 +662,12 @@
     pieces = split(field)
     by_charge = waves_to_atoms(field, wave_high, wave_low)
     charge_grad[...] = dot_three(split(factor[...]), pieces, 0, 0)
-    active = whole(shared_mine.at[:, 0:N, :], shared_other.at[:, 0:N, :])
+    active = whole(shared)
     mix = dot_three(split(by_charge), split(active))
     weights = split(w_charge[...])
     up_grad[...] = dot_three(split(mix), weights, 0, 1) + up_part[...]
     by_feature = dot_three(pieces, weights, 1, 1)
-    grad_high, grad_low = split(whole(grad_mine, grad_other))
+    grad_high, grad_low = split(whole(grads))
     along = dot_three(
         split(jnp.concatenate([weighted[...], by_feature], axis=1)),
         (
@@ -680,11 +687,12 @@
         axis=0,
     )
     by_pos = dot_three(split(rows), split(phase))
-    core = lax.axis_index("c")
+    core, column = lax.axis_index("c"), lax.axis_index("x")
     for member in range(MEMBERS):
         part = slice(member * N, (member + 1) * N)
         out = (mine, other)[member // 4].at[member % 4]
-        place = jnp.where(core == member // 4, member % 4, 4 + member % 4) * 16
+        place = jnp.where(core == member // 4, 0, 4) + (column + 4 - member % 4) % 4
+        place = place * 16
         piece = pl.ds(pl.multiple_of(place, 16), 16)
         out[0:N, :] = by_charge[:, part]
         out[N : N + 8, :] = by_pos[:, part]
@@ -718,7 +726,7 @@
     shared, active, invariants, vectors, sums, edges, places = call(
         edge_kernel,
         (
-            f32(4, N + 8, N), f32(N, N), f32(N, N), f32(3, N, N), f32(4, KINDS * BASIS, N),
+            f32(N + 8, N), f32(N, N), f32(N, N), f32(3, N, N), f32(4, KINDS * BASIS, N),
             f32(7, SLOTS, N), i32(2, SLOTS, N),
         ),
         positions, species, neighbours, near_x, far_x, near_y, far_y, embed, radial,
@@ -728,17 +736,24 @@
     def other_core(value):
         return lax.ppermute(value, "c", swap)
 
-    def row_exchange(tiles):
-        return lax.all_to_all(tiles, "x", 0, 0)
-
-    shared = row_exchange(shared)
-    shared_other = other_core(shared)
+    def step_x(value, step):
+        return lax.ppermute(value, "x", [(at, (at + step) % 4) for at in range(4)])
+
+    def gather(value):
+        values = [value] + [step_x(value, step) for step in (1, 2, 3)]
+        return values + [other_core(item) for item in values]
+
+    def scatter(mine, other):
+        tiles = call(core_sum_kernel, (f32(*mine.shape[1:]),) * 4, mine, other_core(other))
+        return [tiles[0]] + [step_x(tiles[step], -step) for step in (1, 2, 3)]
+
+    shared = gather(shared)
     half = jax.ShapeDtypeStruct((2 * SHARD, MEMBERS * N), jnp.bfloat16)
     feature = jax.ShapeDtypeStruct((MEMBERS * N, N), jnp.bfloat16)
     factor, wave_high, wave_low, feature_high, feature_low = call(
         structure_kernel,
         (f32(CROSSES, 16, N), half, half, feature, feature),
-        shared, shared_other, kvec, embed, w_up,
+        *shared, kvec, embed, w_up,
     )
 
     def cross_sum(tiles):
@@ -752,33 +767,30 @@
         (f32(4, N, N), f32(4, N, N), f32(2 * SHARD, N), f32(2 * SHARD, N)),
         factor, w_charge, kfilter, wave_high, wave_low,
     )
-    potential = row_exchange(mine + other_core(other))
-    grads, grad_out, energy, read_row, up_part = call(
+    grad_out, energy, read_row, up_part = call(
         energy_kernel,
-        (f32(4, N, N), f32(N, N), f32(1, N), f32(1, N), f32(N, N)),
-        potential, active, species, embed, w_up, read,
-    )
-    grads = row_exchange(grads)
-    grads_other = other_core(grads)
+        (f32(N, N), f32(1, N), f32(1, N), f32(N, N)),
+        *scatter(mine, other), active, species, embed, w_up, read,
+    )
+    grads = gather(grad_out)
     projected = cross_sum(
-        call(projection_kernel, f32(CROSSES, 16, N), grads, grads_other, wave_high, wave_low)
+        call(projection_kernel, f32(CROSSES, 16, N), *grads, wave_high, wave_low)
     )
     square = pltpu.VMEM((N, N), jnp.float32)
     mine, other, shard = call(
         wave_back_kernel,
         (f32(4, N + 40, N), f32(4, N + 40, N), f32(SHARD, N)),
-        projected, factor, charge_factor, weighted, kfilter, kvec, wave_high, wave_low,
-        grads, grads_other, feature_high, feature_low, shared, shared_other, w_charge, up_part,
+        *grads, *shared, projected, factor, charge_factor, weighted, kfilter, kvec,
+        wave_high, wave_low, feature_high, feature_low, w_charge, up_part,
         scratch=(square, square),
     )
-    tiles = row_exchange(mine + other_core(other))
-    shards = [shard] + [
-        lax.ppermute(shard, "x", [(at, (at + step) % 4) for at in range(4)]) for step in (1, 2, 3)
-    ]
+    tiles = scatter(mine, other)
+    shard, *tiles = lax.optimization_barrier((shard, *tiles))
+    shards = [shard] + [step_x(shard, step) for step in (1, 2, 3)]
     payload, own_grad, charge_piece = call(
         edge_back_kernel,
         (f32(8, 56, N), f32(8, N), f32(16, N)),
-        tiles, active, invariants, vectors, sums, edges, places, embed, radial, w_up,
+        *tiles, active, invariants, vectors, sums, edges, places, embed, radial, w_up,
         w_charge, species, grad_out, read_row,
         cost=pl.CostEstimate(flops=10**9, bytes_accessed=10**7, transcendentals=10**5),
     )

time: 187 us -> 178 us (0.952)
  blocking collectives: 100 us -> 74.3 us
  starting transfers between devices: 44.3 us -> 60.1 us
  waiting for transfers between devices: 18.5 us -> 23.8 us
  local copies, waits for them, and re-layouts: 4.19 us -> 0.02 us
    all_to_all x3 -> x0, blocking collectives: 25.3 us -> none  [row_exchange(): return lax.all_to_all(tiles, 'x', 0, 0)]
    ppermute x9 -> x15, starting transfers between devices: 23.1 us -> 35 us  [other_core(): return lax.ppermute(value, 'c', swap)]
    ppermute x3 -> x15, waiting for transfers between devices: 1.6 us -> 12.1 us  [step_x(): return lax.ppermute(value, 'x', [(at, (at + step) % 4) for at in range(4)])]
    ppermute x3 -> x15, starting transfers between devices: 3.79 us -> 11.1 us  [step_x(): return lax.ppermute(value, 'x', [(at, (at + step) % 4) for at in range(4)])]
    unnamed x24 -> x8, local copies, waits for them, and re-layouts: 4.19 us -> 0.02 us
    all_to_all x1 -> x0, waiting for transfers between devices: 3.47 us -> none  [row_exchange(): return lax.all_to_all(tiles, 'x', 0, 0)]
    all_to_all x1 -> x0, starting transfers between devices: 3.46 us -> none  [row_exchange(): return lax.all_to_all(tiles, 'x', 0, 0)]
    pallas_call x15 -> x17, Pallas kernels: 17.8 us -> 18.7 us  [call(): pl.pallas_call(kernel, out_shape=out_shape, scratch_shapes=list(scratch),...]
  transfers between devices with their start and end apart: 18 -> 35, of which waited for: 9 -> 16; matrix products, arithmetic and copies ran while one was open for 0% -> 0% of each run, Pallas kernels for 3% -> 3%
where the time goes in v4:
time: 178 us
  blocking collectives  74.3 us (42%)
  starting transfers between devices  60.1 us (34%)
  waiting for transfers between devices  23.8 us (13%)
  Pallas kernels  18.7 us (11%)
    ppermute x15, starting transfers between devices, other_core(): return lax.ppermute(value, 'c', swap)  35 us
    all_to_all x2, blocking collectives, cross_sum(): return lax.all_to_all(tiles, CROSS, 0, 0).reshape(2 * SHARD, N)  32.5 us
    all_to_all x2, blocking collectives, cross_sum(): tiles = lax.all_to_all(tiles, CROSS, 0, 0)  29.5 us
    pallas_call x17, Pallas kernels, call(): pl.pallas_call(kernel, out_shape=out_shape, scratch_shapes=list(scratch),...  18.7 us
    all_to_all x1, blocking collectives, body(): payload = lax.all_to_all(payload, DEPTH, 0, 0)  12.3 us
    ppermute x15, waiting for transfers between devices, step_x(): return lax.ppermute(value, 'x', [(at, (at + step) % 4) for at in range(4)])  12.1 us
    ppermute x15, starting transfers between devices, step_x(): return lax.ppermute(value, 'x', [(at, (at + step) % 4) for at in range(4)])  11.1 us
    ppermute x4, starting transfers between devices, swapped(): return lax.ppermute(value, axes, places)  10.4 us
  transfers between devices with their start and end apart: 35, of which 16 were waited for; matrix products, arithmetic and copies ran while one was open for 0% of the time, Pallas kernels for 3%

profile of v4, /device:TPU:1, one launch (start us, length us, event | category | flops | bytes accessed | tf_op | source)
XLA Modules:
  0.0 177.6 jit_solution(6530305180300096243)
XLA Ops:
  0.6 1.1 shard_map.179
  1.7 2.1 %collective-permute-start = (f32[8,128]{1,0:T(8,128)S(1)}, f32[8,128]{1,0:T(8,128)S(1)}, u32[]{:S(2)}, u32[]{:S(2)}) collective-permute-start(f32[8,128]{1,0:T(8,128)S(1)} %get-tuple-element.76), channel_id=1, source_target_pairs={{0,1},{1,0},{2,3},{3,2},{4,5},{5,4},{6,7},{7,6},{8,9},{9,8},{10,11... | collective-permute-start | bytes 12296 | tf_op jit(solution)/shard_map/ppermute | solution.py:187
  3.9 3.2 %collective-permute-start.1 = (f32[8,128]{1,0:T(8,128)S(1)}, f32[8,128]{1,0:T(8,128)S(1)}, u32[]{:S(2)}, u32[]{:S(2)}) collective-permute-start(f32[8,128]{1,0:T(8,128)S(1)} %get-tuple-element.77), channel_id=1, source_target_pairs={{0,7},{1,2},{2,1},{3,4},{4,3},{5,6},{6,5},{7,0},{8,15},{9,10},{10,... | collective-permute-start | bytes 12296 | tf_op jit(solution)/shard_map/ppermute | solution.py:187
  7.0 1.4 collective-permute-done.1.far.far_y
  8.5 2.5 %collective-permute-start.2 = (f32[8,128]{1,0:T(8,128)S(1)}, f32[8,128]{1,0:T(8,128)S(1)}, u32[]{:S(2)}, u32[]{:S(2)}) collective-permute-start(f32[8,128]{1,0:T(8,128)S(1)} %get-tuple-element.78), channel_id=1, source_target_pairs={{0,8},{8,0},{16,24},{24,16},{32,40},{40,32},{48,56},{56,48},{64,72... | collective-permute-start | bytes 12296 | tf_op jit(solution)/shard_map/ppermute | solution.py:187
  11.0 2.6 %collective-permute-start.3 = (f32[8,128]{1,0:T(8,128)S(1)}, f32[8,128]{1,0:T(8,128)S(1)}, u32[]{:S(2)}, u32[]{:S(2)}) collective-permute-start(f32[8,128]{1,0:T(8,128)S(1)} %get-tuple-element.79), channel_id=1, source_target_pairs={{0,248},{8,16},{16,8},{24,32},{32,24},{40,48},{48,40},{56,64},{64,... | collective-permute-start | bytes 12296 | tf_op jit(solution)/shard_map/ppermute | solution.py:187
  13.6 1.3 collective-permute-done.3.far_x
  14.9 1.4 shard_map.181
  16.4 1.9 %collective-permute-start.6 = (f32[136,128]{1,0:T(8,128)S(1)}, f32[136,128]{1,0:T(8,128)S(1)}, u32[]{:S(2)}, u32[]{:S(2)}) collective-permute-start(f32[136,128]{1,0:T(8,128)S(1)} %get-tuple-element.82.refs_0_.refs_8_), channel_id=1, source_target_pairs={{0,3},{1,0},{2,1},{3,2},{4,7},{5,4},{6,5},{7,6},{8,11},{9,8},{10,9... | collective-permute-start | bytes 208904 | tf_op jit(solution)/shard_map/ppermute | solution.py:740
  18.3 0.7 collective-permute-start.4
  18.9 6.5 %collective-permute-start.7 = (f32[136,128]{1,0:T(8,128)S(1)}, f32[136,128]{1,0:T(8,128)S(1)}, u32[]{:S(2)}, u32[]{:S(2)}) collective-permute-start(f32[136,128]{1,0:T(8,128)S(1)} %get-tuple-element.82.refs_0_.refs_8_), channel_id=1, source_target_pairs={{0,8},{8,0},{1,9},{9,1},{2,10},{10,2},{3,11},{11,3},{4,12},{12,4},... | collective-permute-start | bytes 208904 | tf_op jit(solution)/shard_map/ppermute | solution.py:737
  25.4 1.6 collective-permute-start.10
  27.1 3.3 %collective-permute-start.9 = (f32[136,128]{1,0:T(8,128)S(1)}, f32[136,128]{1,0:T(8,128)S(1)}, u32[]{:S(2)}, u32[]{:S(2)}) collective-permute-start(f32[136,128]{1,0:T(8,128)S(1)} %collective-permute-done.5.refs_2_.refs_10_), channel_id=1, source_target_pairs={{0,8},{8,0},{1,9},{9,1},{2,10},{10,2},{3,11},{11,3},{4,12},{12,4},... | collective-permute-start | bytes 208904 | tf_op jit(solution)/shard_map/ppermute | solution.py:737
  30.4 0.3 collective-permute-start.8
  30.7 0.6 collective-permute-done.9.refs_6_.refs_14_
  31.3 0.4 collective-permute-done.8.refs_5_.refs_13_
  31.6 2.6 %shard_map.182 = (f32[32,16,128]{2,1,0:T(8,128)S(1)}, bf16[512,1024]{1,0:T(8,128)(2,1)S(1)}, bf16[512,1024]{1,0:T(8,128)(2,1)S(1)}, bf16[1024,128]{1,0:T(8,128)(2,1)S(1)}, bf16[1024,128]{1,0:T(8,128)(2,1)S(1)}) custom-call(f32[136,128]{1,0:T(8,128)S(1)} %get-tuple-element.82.refs_0_.refs_8_, f32[136,128]{1,0:T(8,128)S(1)} %collective-permute-done.4.refs_1_.refs_9_, ...), custom_call_target="tpu_custom_call" | custom-call | tf_op jit(solution)/shard_map/pallas_call | solution.py:108
  34.2 15.7 %all_to_all.30.tiles = f32[32,16,128]{2,1,0:T(8,128)S(1)} all-to-all(f32[32,16,128]{2,1,0:T(8,128)S(1)} %get-tuple-element.83), channel_id=1, replica_groups=mesh['y'=4,'zh'=4,'c'=2,'zl'=2,'x'=4] {'y','zh','zl'}, dimensions={0} | all-to-all | bytes 524288 | tf_op jit(solution)/shard_map/all_to_all | solution.py:760
  50.0 16.3 %all_to_all.31 = f32[32,16,128]{2,1,0:T(8,128)S(1)} all-to-all(f32[32,16,128]{2,1,0:T(8,128)S(1)} %shard_map.183), channel_id=1, replica_groups=mesh['y'=4,'zh'=4,'c'=2,'zl'=2,'x'=4] {'y','zh','zl'}, dimensions={0} | all-to-all | bytes 524288 | tf_op jit(solution)/shard_map/all_to_all | solution.py:762
  66.4 1.3 shard_map.184
  67.7 3.7 %collective-permute-start.11 = (f32[4,128,128]{2,1,0:T(8,128)S(1)}, f32[4,128,128]{2,1,0:T(8,128)S(1)}, u32[]{:S(2)}, u32[]{:S(2)}) collective-permute-start(f32[4,128,128]{2,1,0:T(8,128)S(1)} %get-tuple-element.87), channel_id=1, source_target_pairs={{0,8},{8,0},{1,9},{9,1},{2,10},{10,2},{3,11},{11,3},{4,12},{12,4},... | collective-permute-start | bytes 786440 | tf_op jit(solution)/shard_map/ppermute | solution.py:737
  71.4 1.2 collective-permute-done.11.other
  72.6 0.8 collective-permute-start.12
  73.4 1.1 collective-permute-start.13
  74.5 0.5 collective-permute-start.14
  74.9 1.0 collective-permute-done.12.tile_1
  75.9 2.1 %collective-permute-done.13.tile_2 = f32[128,128]{1,0:T(8,128)S(1)} collective-permute-done((f32[128,128]{1,0:T(8,128)S(1)}, f32[128,128]{1,0:T(8,128)S(1)}, u32[]{:S(2)}, u32[]{:S(2)}) %collective-permute-start.13) | collective-permute-done | bytes 65568 | tf_op jit(solution)/shard_map/ppermute | solution.py:740
  78.0 1.8 collective-permute-done.14.tile_3
  79.8 1.2 shard_map.186
  80.9 0.6 collective-permute-start.17
  81.5 0.3 collective-permute-start.16
  81.8 0.5 collective-permute-start.15
  82.4 2.3 %collective-permute-start.18 = (f32[128,128]{1,0:T(8,128)S(1)}, f32[128,128]{1,0:T(8,128)S(1)}, u32[]{:S(2)}, u32[]{:S(2)}) collective-permute-start(f32[128,128]{1,0:T(8,128)S(1)} %get-tuple-element.95.refs_0_.grad_out), channel_id=1, source_target_pairs={{0,8},{8,0},{1,9},{9,1},{2,10},{10,2},{3,11},{11,3},{4,12},{12,4},... | collective-permute-start | bytes 196616 | tf_op jit(solution)/shard_map/ppermute | solution.py:737
  84.7 1.6 collective-permute-start.21
  86.3 2.8 %collective-permute-start.20 = (f32[128,128]{1,0:T(8,128)S(1)}, f32[128,128]{1,0:T(8,128)S(1)}, u32[]{:S(2)}, u32[]{:S(2)}) collective-permute-start(f32[128,128]{1,0:T(8,128)S(1)} %collective-permute-done.16.refs_2_), channel_id=1, source_target_pairs={{0,8},{8,0},{1,9},{9,1},{2,10},{10,2},{3,11},{11,3},{4,12},{12,4},... | collective-permute-start | bytes 196616 | tf_op jit(solution)/shard_map/ppermute | solution.py:737
  89.1 0.7 collective-permute-start.19
  89.8 0.2 collective-permute-done.20.refs_6_
  90.0 0.7 collective-permute-done.19.refs_5_
  90.7 0.7 shard_map.187
  91.4 13.8 %all_to_all.32.tiles = f32[32,16,128]{2,1,0:T(8,128)S(1)} all-to-all(f32[32,16,128]{2,1,0:T(8,128)S(1)} %shard_map.187), channel_id=1, replica_groups=mesh['y'=4,'zh'=4,'c'=2,'zl'=2,'x'=4] {'y','zh','zl'}, dimensions={0} | all-to-all | bytes 524288 | tf_op jit(solution)/shard_map/all_to_all | solution.py:760
  105.2 16.2 %all_to_all.33 = f32[32,16,128]{2,1,0:T(8,128)S(1)} all-to-all(f32[32,16,128]{2,1,0:T(8,128)S(1)} %shard_map.188), channel_id=1, replica_groups=mesh['y'=4,'zh'=4,'c'=2,'zl'=2,'x'=4] {'y','zh','zl'}, dimensions={0} | all-to-all | bytes 524288 | tf_op jit(solution)/shard_map/all_to_all | solution.py:762
  121.4 2.5 %shard_map.189 = (f32[4,168,128]{2,1,0:T(8,128)S(1)}, f32[4,168,128]{2,1,0:T(8,128)S(1)}, f32[256,128]{1,0:T(8,128)S(1)}) custom-call(f32[128,128]{1,0:T(8,128)S(1)} %get-tuple-element.95.refs_0_.grad_out, f32[128,128]{1,0:T(8,128)S(1)} %collective-permute-done.15.refs_1_, f32[128,128]{1,0:T(8,128)S(1)} %collective-permute-done.16.refs_2_, ...), custom_call_target="tpu_custom_call" | custom-call | tf_op jit(solution)/shard_map/pallas_call | solution.py:108
  123.9 3.6 %collective-permute-start.22 = (f32[4,168,128]{2,1,0:T(8,128)S(1)}, f32[4,168,128]{2,1,0:T(8,128)S(1)}, u32[]{:S(2)}, u32[]{:S(2)}) collective-permute-start(f32[4,168,128]{2,1,0:T(8,128)S(1)} %get-tuple-element.103), channel_id=1, source_target_pairs={{0,8},{8,0},{1,9},{9,1},{2,10},{10,2},{3,11},{11,3},{4,12},{12,4},... | collective-permute-start | bytes 1032200 | tf_op jit(solution)/shard_map/ppermute | solution.py:737
  127.5 1.3 collective-permute-done.22.other
  128.9 1.0 collective-permute-start.23
  129.9 1.3 collective-permute-start.24
  131.1 1.5 collective-permute-done.23.tile_1
  132.7 2.0 %collective-permute-done.24.tile_2 = f32[168,128]{1,0:T(8,128)S(1)} collective-permute-done((f32[168,128]{1,0:T(8,128)S(1)}, f32[168,128]{1,0:T(8,128)S(1)}, u32[]{:S(2)}, u32[]{:S(2)}) %collective-permute-start.24) | collective-permute-done | bytes 86048 | tf_op jit(solution)/shard_map/ppermute | solution.py:740
  134.7 2.3 %collective-permute-done.25.tile_3 = f32[168,128]{1,0:T(8,128)S(1)} collective-permute-done((f32[168,128]{1,0:T(8,128)S(1)}, f32[168,128]{1,0:T(8,128)S(1)}, u32[]{:S(2)}, u32[]{:S(2)}) %collective-permute-start.25) | collective-permute-done | bytes 86048 | tf_op jit(solution)/shard_map/ppermute | solution.py:740
  137.0 0.3 collective-permute-start.28
  137.4 1.2 collective-permute-start.27
  138.6 0.9 collective-permute-start.26
  139.4 4.7 %shard_map.191 = (f32[8,56,128]{2,1,0:T(8,128)S(1)}, f32[8,128]{1,0:T(8,128)S(1)}, f32[16,128]{1,0:T(8,128)S(1)}) custom-call(f32[168,128]{1,0:T(8,128)S(1)} %get-tuple-element.108.tile_0, f32[168,128]{1,0:T(8,128)S(1)} %collective-permute-done.23.tile_1, f32[168,128]{1,0:T(8,128)S(1)} %collective-permute-done.24.tile_2, ...), custom_call_target="tpu_custom_call" | custom-call | flops 1000000000 | bytes 10000000 | tf_op jit(solution)/shard_map/pallas_call | solution.py:108
  144.2 1.4 collective-permute-done.26.refs_1_
  145.5 12.3 %all_to_all.34.tiles = f32[8,56,128]{2,1,0:T(8,128)S(1)} all-to-all(f32[8,56,128]{2,1,0:T(8,128)S(1)} %get-tuple-element.120), channel_id=1, replica_groups=mesh['y'=4,'zh'=4,'c'=2,'zl'=2,'x'=4] {'zh','zl'}, dimensions={0} | all-to-all | bytes 458752 | tf_op jit(solution)/shard_map/all_to_all | solution.py:798
  157.8 0.8 shard_map.192
  158.7 3.6 %all-to-all-start.5 = ((f32[16,56,128]{2,1,0:T(8,128)}), f32[16,56,128]{2,1,0:T(8,128)S(1)}, u32[]{:S(2)}, u32[]{:S(2)}) async-start(f32[16,56,128]{2,1,0:T(8,128)} %shard_map.192), calls=%async_computation.5 | async-start | bytes 917504 | tf_op jit(solution)/shard_map/all_to_all | solution.py:800
  162.2 3.5 %collective-permute-start.30 = (f32[256,128]{1,0:T(8,128)S(1)}, f32[256,128]{1,0:T(8,128)S(1)}, u32[]{:S(2)}, u32[]{:S(2)}) collective-permute-start(f32[256,128]{1,0:T(8,128)S(1)} %get-tuple-element.131.refs_0_), channel_id=1, source_target_pairs={{0,8},{8,0},{1,9},{9,1},{2,10},{10,2},{3,11},{11,3},{4,12},{12,4},... | collective-permute-start | bytes 393224 | tf_op jit(solution)/shard_map/ppermute | solution.py:737
  165.7 0.1 collective-permute-start.31
  165.8 0.4 collective-permute-start.32
  166.4 4.7 %all-to-all-done.5.tiles = f32[16,56,128]{2,1,0:T(8,128)S(1)} async-done(((f32[16,56,128]{2,1,0:T(8,128)}), f32[16,56,128]{2,1,0:T(8,128)S(1)}, u32[]{:S(2)}, u32[]{:S(2)}) %all-to-all-start.5) | async-done | bytes 458784 | tf_op jit(solution)/shard_map/all_to_all | solution.py:800
  171.1 4.4 %collective-permute-start.29 = (f32[160,128]{1,0:T(8,128)S(1)}, f32[160,128]{1,0:T(8,128)S(1)}, u32[]{:S(2)}, u32[]{:S(2)}) collective-permute-start(f32[160,128]{1,0:T(8,128)S(1)} %get-tuple-element.122.own), channel_id=1, source_target_pairs={{0,8},{8,0},{1,9},{9,1},{2,10},{10,2},{3,11},{11,3},{4,12},{12,4},... | collective-permute-start | bytes 245768 | tf_op jit(solution)/shard_map/ppermute | solution.py:737
  175.5 1.1 shard_map.195
  176.6 1.0 shard_map.194
  (36 shorter events, 0.5 us)
Async XLA Ops:
  0.6 31.0 %copy-start.2 = (f32[128,128]{1,0:T(8,128)S(1)}, f32[128,128]{1,0:T(8,128)}, u32[]{:S(2)}) copy-start(f32[128,128]{1,0:T(8,128)} %w_up.3) | copy-start | bytes 196612
  1.7 5.3 %collective-permute-start = (f32[8,128]{1,0:T(8,128)S(1)}, f32[8,128]{1,0:T(8,128)S(1)}, u32[]{:S(2)}, u32[]{:S(2)}) collective-permute-start(f32[8,128]{1,0:T(8,128)S(1)} %get-tuple-element.76), channel_id=1, source_target_pairs={{0,1},{1,0},{2,3},{3,2},{4,5},{5,4},{6,7},{7,6},{8,9},{9,8},{10,11... | collective-permute-start | bytes 12296 | tf_op jit(solution)/shard_map/ppermute | solution.py:187
  3.9 4.6 %collective-permute-start.1 = (f32[8,128]{1,0:T(8,128)S(1)}, f32[8,128]{1,0:T(8,128)S(1)}, u32[]{:S(2)}, u32[]{:S(2)}) collective-permute-start(f32[8,128]{1,0:T(8,128)S(1)} %get-tuple-element.77), channel_id=1, source_target_pairs={{0,7},{1,2},{2,1},{3,4},{4,3},{5,6},{6,5},{7,0},{8,15},{9,10},{10,... | collective-permute-start | bytes 12296 | tf_op jit(solution)/shard_map/ppermute | solution.py:187
  8.5 5.1 %collective-permute-start.2 = (f32[8,128]{1,0:T(8,128)S(1)}, f32[8,128]{1,0:T(8,128)S(1)}, u32[]{:S(2)}, u32[]{:S(2)}) collective-permute-start(f32[8,128]{1,0:T(8,128)S(1)} %get-tuple-element.78), channel_id=1, source_target_pairs={{0,8},{8,0},{16,24},{24,16},{32,40},{40,32},{48,56},{56,48},{64,72... | collective-permute-start | bytes 12296 | tf_op jit(solution)/shard_map/ppermute | solution.py:187
  11.0 3.9 %collective-permute-start.3 = (f32[8,128]{1,0:T(8,128)S(1)}, f32[8,128]{1,0:T(8,128)S(1)}, u32[]{:S(2)}, u32[]{:S(2)}) collective-permute-start(f32[8,128]{1,0:T(8,128)S(1)} %get-tuple-element.79), channel_id=1, source_target_pairs={{0,248},{8,16},{16,8},{24,32},{32,24},{40,48},{48,40},{56,64},{64,... | collective-permute-start | bytes 12296 | tf_op jit(solution)/shard_map/ppermute | solution.py:187
  14.9 16.7 %copy-start.3 = (f32[3,2048]{1,0:T(4,128)S(1)}, f32[3,2048]{1,0:T(4,128)}, u32[]{:S(2)}) copy-start(f32[3,2048]{1,0:T(4,128)} %refs_21_.1) | copy-start | bytes 73732
  16.4 50.0 %copy-start = (f32[2048,128]{1,0:T(8,128)S(1)}, f32[2048,128]{1,0:T(8,128)}, u32[]{:S(2)}) copy-start(f32[2048,128]{1,0:T(8,128)} %refs_20_.1) | copy-start | bytes 3145732
  16.4 9.1 %collective-permute-start.6 = (f32[136,128]{1,0:T(8,128)S(1)}, f32[136,128]{1,0:T(8,128)S(1)}, u32[]{:S(2)}, u32[]{:S(2)}) collective-permute-start(f32[136,128]{1,0:T(8,128)S(1)} %get-tuple-element.82.refs_0_.refs_8_), channel_id=1, source_target_pairs={{0,3},{1,0},{2,1},{3,2},{4,7},{5,4},{6,5},{7,6},{8,11},{9,8},{10,9... | collective-permute-start | bytes 208904 | tf_op jit(solution)/shard_map/ppermute | solution.py:740
  18.3 8.8 %collective-permute-start.5 = (f32[136,128]{1,0:T(8,128)S(1)}, f32[136,128]{1,0:T(8,128)S(1)}, u32[]{:S(2)}, u32[]{:S(2)}) collective-permute-start(f32[136,128]{1,0:T(8,128)S(1)} %get-tuple-element.82.refs_0_.refs_8_), channel_id=1, source_target_pairs={{0,2},{1,3},{2,0},{3,1},{4,6},{5,7},{6,4},{7,5},{8,10},{9,11},{10,... | collective-permute-start | bytes 208904 | tf_op jit(solution)/shard_map/ppermute | solution.py:740
  18.3 12.1 %collective-permute-start.4 = (f32[136,128]{1,0:T(8,128)S(1)}, f32[136,128]{1,0:T(8,128)S(1)}, u32[]{:S(2)}, u32[]{:S(2)}) collective-permute-start(f32[136,128]{1,0:T(8,128)S(1)} %get-tuple-element.82.refs_0_.refs_8_), channel_id=1, source_target_pairs={{0,1},{1,2},{2,3},{3,0},{4,5},{5,6},{6,7},{7,4},{8,9},{9,10},{10,1... | collective-permute-start | bytes 208904 | tf_op jit(solution)/shard_map/ppermute | solution.py:740
  18.9 11.8 %collective-permute-start.7 = (f32[136,128]{1,0:T(8,128)S(1)}, f32[136,128]{1,0:T(8,128)S(1)}, u32[]{:S(2)}, u32[]{:S(2)}) collective-permute-start(f32[136,128]{1,0:T(8,128)S(1)} %get-tuple-element.82.refs_0_.refs_8_), channel_id=1, source_target_pairs={{0,8},{8,0},{1,9},{9,1},{2,10},{10,2},{3,11},{11,3},{4,12},{12,4},... | collective-permute-start | bytes 208904 | tf_op jit(solution)/shard_map/ppermute | solution.py:737
  25.4 5.3 %collective-permute-start.10 = (f32[136,128]{1,0:T(8,128)S(1)}, f32[136,128]{1,0:T(8,128)S(1)}, u32[]{:S(2)}, u32[]{:S(2)}) collective-permute-start(f32[136,128]{1,0:T(8,128)S(1)} %collective-permute-done.6.refs_3_.refs_11_), channel_id=1, source_target_pairs={{0,8},{8,0},{1,9},{9,1},{2,10},{10,2},{3,11},{11,3},{4,12},{12,4},... | collective-permute-start | bytes 208904 | tf_op jit(solution)/shard_map/ppermute | solution.py:737
  27.1 4.2 %collective-permute-start.9 = (f32[136,128]{1,0:T(8,128)S(1)}, f32[136,128]{1,0:T(8,128)S(1)}, u32[]{:S(2)}, u32[]{:S(2)}) collective-permute-start(f32[136,128]{1,0:T(8,128)S(1)} %collective-permute-done.5.refs_2_.refs_10_), channel_id=1, source_target_pairs={{0,8},{8,0},{1,9},{9,1},{2,10},{10,2},{3,11},{11,3},{4,12},{12,4},... | collective-permute-start | bytes 208904 | tf_op jit(solution)/shard_map/ppermute | solution.py:737
  30.4 1.3 collective-permute-start.8
  50.0 16.3 %copy-start.1 = (f32[128,128]{1,0:T(8,128)S(1)}, f32[128,128]{1,0:T(8,128)}, u32[]{:S(2)}) copy-start(f32[128,128]{1,0:T(8,128)} %w_charge.3) | copy-start | bytes 196612
  67.7 4.8 %collective-permute-start.11 = (f32[4,128,128]{2,1,0:T(8,128)S(1)}, f32[4,128,128]{2,1,0:T(8,128)S(1)}, u32[]{:S(2)}, u32[]{:S(2)}) collective-permute-start(f32[4,128,128]{2,1,0:T(8,128)S(1)} %get-tuple-element.87), channel_id=1, source_target_pairs={{0,8},{8,0},{1,9},{9,1},{2,10},{10,2},{3,11},{11,3},{4,12},{12,4},... | collective-permute-start | bytes 786440 | tf_op jit(solution)/shard_map/ppermute | solution.py:737
  72.6 3.4 %collective-permute-start.12 = (f32[128,128]{1,0:T(8,128)S(1)}, f32[128,128]{1,0:T(8,128)S(1)}, u32[]{:S(2)}, u32[]{:S(2)}) collective-permute-start(f32[128,128]{1,0:T(8,128)S(1)} %get-tuple-element.89), channel_id=1, source_target_pairs={{0,3},{1,0},{2,1},{3,2},{4,7},{5,4},{6,5},{7,6},{8,11},{9,8},{10,9... | collective-permute-start | bytes 196616 | tf_op jit(solution)/shard_map/ppermute | solution.py:740
  73.4 4.6 %collective-permute-start.13 = (f32[128,128]{1,0:T(8,128)S(1)}, f32[128,128]{1,0:T(8,128)S(1)}, u32[]{:S(2)}, u32[]{:S(2)}) collective-permute-start(f32[128,128]{1,0:T(8,128)S(1)} %get-tuple-element.90), channel_id=1, source_target_pairs={{0,2},{1,3},{2,0},{3,1},{4,6},{5,7},{6,4},{7,5},{8,10},{9,11},{10,... | collective-permute-start | bytes 196616 | tf_op jit(solution)/shard_map/ppermute | solution.py:740
  74.5 5.3 %collective-permute-start.14 = (f32[128,128]{1,0:T(8,128)S(1)}, f32[128,128]{1,0:T(8,128)S(1)}, u32[]{:S(2)}, u32[]{:S(2)}) collective-permute-start(f32[128,128]{1,0:T(8,128)S(1)} %get-tuple-element.91), channel_id=1, source_target_pairs={{0,1},{1,2},{2,3},{3,0},{4,5},{5,6},{6,7},{7,4},{8,9},{9,10},{10,1... | collective-permute-start | bytes 196616 | tf_op jit(solution)/shard_map/ppermute | solution.py:740
  80.9 3.8 %collective-permute-start.17 = (f32[128,128]{1,0:T(8,128)S(1)}, f32[128,128]{1,0:T(8,128)S(1)}, u32[]{:S(2)}, u32[]{:S(2)}) collective-permute-start(f32[128,128]{1,0:T(8,128)S(1)} %get-tuple-element.95.refs_0_.grad_out), channel_id=1, source_target_pairs={{0,3},{1,0},{2,1},{3,2},{4,7},{5,4},{6,5},{7,6},{8,11},{9,8},{10,9... | collective-permute-start | bytes 196616 | tf_op jit(solution)/shard_map/ppermute | solution.py:740
  81.5 4.8 %collective-permute-start.16 = (f32[128,128]{1,0:T(8,128)S(1)}, f32[128,128]{1,0:T(8,128)S(1)}, u32[]{:S(2)}, u32[]{:S(2)}) collective-permute-start(f32[128,128]{1,0:T(8,128)S(1)} %get-tuple-element.95.refs_0_.grad_out), channel_id=1, source_target_pairs={{0,2},{1,3},{2,0},{3,1},{4,6},{5,7},{6,4},{7,5},{8,10},{9,11},{10,... | collective-permute-start | bytes 196616 | tf_op jit(solution)/shard_map/ppermute | solution.py:740
  81.8 7.2 %collective-permute-start.15 = (f32[128,128]{1,0:T(8,128)S(1)}, f32[128,128]{1,0:T(8,128)S(1)}, u32[]{:S(2)}, u32[]{:S(2)}) collective-permute-start(f32[128,128]{1,0:T(8,128)S(1)} %get-tuple-element.95.refs_0_.grad_out), channel_id=1, source_target_pairs={{0,1},{1,2},{2,3},{3,0},{4,5},{5,6},{6,7},{7,4},{8,9},{9,10},{10,1... | collective-permute-start | bytes 196616 | tf_op jit(solution)/shard_map/ppermute | solution.py:740
  82.4 7.4 %collective-permute-start.18 = (f32[128,128]{1,0:T(8,128)S(1)}, f32[128,128]{1,0:T(8,128)S(1)}, u32[]{:S(2)}, u32[]{:S(2)}) collective-permute-start(f32[128,128]{1,0:T(8,128)S(1)} %get-tuple-element.95.refs_0_.grad_out), channel_id=1, source_target_pairs={{0,8},{8,0},{1,9},{9,1},{2,10},{10,2},{3,11},{11,3},{4,12},{12,4},... | collective-permute-start | bytes 196616 | tf_op jit(solution)/shard_map/ppermute | solution.py:737
  84.7 5.0 %collective-permute-start.21 = (f32[128,128]{1,0:T(8,128)S(1)}, f32[128,128]{1,0:T(8,128)S(1)}, u32[]{:S(2)}, u32[]{:S(2)}) collective-permute-start(f32[128,128]{1,0:T(8,128)S(1)} %collective-permute-done.17.refs_3_), channel_id=1, source_target_pairs={{0,8},{8,0},{1,9},{9,1},{2,10},{10,2},{3,11},{11,3},{4,12},{12,4},... | collective-permute-start | bytes 196616 | tf_op jit(solution)/shard_map/ppermute | solution.py:737
  86.3 3.7 %collective-permute-start.20 = (f32[128,128]{1,0:T(8,128)S(1)}, f32[128,128]{1,0:T(8,128)S(1)}, u32[]{:S(2)}, u32[]{:S(2)}) collective-permute-start(f32[128,128]{1,0:T(8,128)S(1)} %collective-permute-done.16.refs_2_), channel_id=1, source_target_pairs={{0,8},{8,0},{1,9},{9,1},{2,10},{10,2},{3,11},{11,3},{4,12},{12,4},... | collective-permute-start | bytes 196616 | tf_op jit(solution)/shard_map/ppermute | solution.py:737
  89.1 1.6 collective-permute-start.19
  123.9 4.9 %collective-permute-start.22 = (f32[4,168,128]{2,1,0:T(8,128)S(1)}, f32[4,168,128]{2,1,0:T(8,128)S(1)}, u32[]{:S(2)}, u32[]{:S(2)}) collective-permute-start(f32[4,168,128]{2,1,0:T(8,128)S(1)} %get-tuple-element.103), channel_id=1, source_target_pairs={{0,8},{8,0},{1,9},{9,1},{2,10},{10,2},{3,11},{11,3},{4,12},{12,4},... | collective-permute-start | bytes 1032200 | tf_op jit(solution)/shard_map/ppermute | solution.py:737
  128.9 3.8 %collective-permute-start.23 = (f32[168,128]{1,0:T(8,128)S(1)}, f32[168,128]{1,0:T(8,128)S(1)}, u32[]{:S(2)}, u32[]{:S(2)}) collective-permute-start(f32[168,128]{1,0:T(8,128)S(1)} %get-tuple-element.105), channel_id=1, source_target_pairs={{0,3},{1,0},{2,1},{3,2},{4,7},{5,4},{6,5},{7,6},{8,11},{9,8},{10,9... | collective-permute-start | bytes 258056 | tf_op jit(solution)/shard_map/ppermute | solution.py:740
  129.9 4.8 %collective-permute-start.24 = (f32[168,128]{1,0:T(8,128)S(1)}, f32[168,128]{1,0:T(8,128)S(1)}, u32[]{:S(2)}, u32[]{:S(2)}) collective-permute-start(f32[168,128]{1,0:T(8,128)S(1)} %get-tuple-element.106), channel_id=1, source_target_pairs={{0,2},{1,3},{2,0},{3,1},{4,6},{5,7},{6,4},{7,5},{8,10},{9,11},{10,... | collective-permute-start | bytes 258056 | tf_op jit(solution)/shard_map/ppermute | solution.py:740
  131.1 5.9 %collective-permute-start.25 = (f32[168,128]{1,0:T(8,128)S(1)}, f32[168,128]{1,0:T(8,128)S(1)}, u32[]{:S(2)}, u32[]{:S(2)}) collective-permute-start(f32[168,128]{1,0:T(8,128)S(1)} %get-tuple-element.107), channel_id=1, source_target_pairs={{0,1},{1,2},{2,3},{3,0},{4,5},{5,6},{6,7},{7,4},{8,9},{9,10},{10,1... | collective-permute-start | bytes 258056 | tf_op jit(solution)/shard_map/ppermute | solution.py:740
  137.0 7.1 %collective-permute-start.28 = (f32[256,128]{1,0:T(8,128)S(1)}, f32[256,128]{1,0:T(8,128)S(1)}, u32[]{:S(2)}, u32[]{:S(2)}) collective-permute-start(f32[256,128]{1,0:T(8,128)S(1)} %get-tuple-element.131.refs_0_), channel_id=1, source_target_pairs={{0,3},{1,0},{2,1},{3,2},{4,7},{5,4},{6,5},{7,6},{8,11},{9,8},{10,9... | collective-permute-start | bytes 393224 | tf_op jit(solution)/shard_map/ppermute | solution.py:740
  137.4 6.8 %collective-permute-start.27 = (f32[256,128]{1,0:T(8,128)S(1)}, f32[256,128]{1,0:T(8,128)S(1)}, u32[]{:S(2)}, u32[]{:S(2)}) collective-permute-start(f32[256,128]{1,0:T(8,128)S(1)} %get-tuple-element.131.refs_0_), channel_id=1, source_target_pairs={{0,2},{1,3},{2,0},{3,1},{4,6},{5,7},{6,4},{7,5},{8,10},{9,11},{10,... | collective-permute-start | bytes 393224 | tf_op jit(solution)/shard_map/ppermute | solution.py:740
  138.6 7.0 %collective-permute-start.26 = (f32[256,128]{1,0:T(8,128)S(1)}, f32[256,128]{1,0:T(8,128)S(1)}, u32[]{:S(2)}, u32[]{:S(2)}) collective-permute-start(f32[256,128]{1,0:T(8,128)S(1)} %get-tuple-element.131.refs_0_), channel_id=1, source_target_pairs={{0,1},{1,2},{2,3},{3,0},{4,5},{5,6},{6,7},{7,4},{8,9},{9,10},{10,1... | collective-permute-start | bytes 393224 | tf_op jit(solution)/shard_map/ppermute | solution.py:740
  158.7 12.4 %all-to-all-start.5 = ((f32[16,56,128]{2,1,0:T(8,128)}), f32[16,56,128]{2,1,0:T(8,128)S(1)}, u32[]{:S(2)}, u32[]{:S(2)}) async-start(f32[16,56,128]{2,1,0:T(8,128)} %shard_map.192), calls=%async_computation.5 | async-start | bytes 917504 | tf_op jit(solution)/shard_map/all_to_all | solution.py:800
  162.2 13.3 %collective-permute-start.30 = (f32[256,128]{1,0:T(8,128)S(1)}, f32[256,128]{1,0:T(8,128)S(1)}, u32[]{:S(2)}, u32[]{:S(2)}) collective-permute-start(f32[256,128]{1,0:T(8,128)S(1)} %get-tuple-element.131.refs_0_), channel_id=1, source_target_pairs={{0,8},{8,0},{1,9},{9,1},{2,10},{10,2},{3,11},{11,3},{4,12},{12,4},... | collective-permute-start | bytes 393224 | tf_op jit(solution)/shard_map/ppermute | solution.py:737
  165.7 9.8 %collective-permute-start.31 = (f32[256,128]{1,0:T(8,128)S(1)}, f32[256,128]{1,0:T(8,128)S(1)}, u32[]{:S(2)}, u32[]{:S(2)}) collective-permute-start(f32[256,128]{1,0:T(8,128)S(1)} %collective-permute-done.26.refs_1_), channel_id=1, source_target_pairs={{0,8},{8,0},{1,9},{9,1},{2,10},{10,2},{3,11},{11,3},{4,12},{12,4},... | collective-permute-start | bytes 393224 | tf_op jit(solution)/shard_map/ppermute | solution.py:737
  165.8 9.7 %collective-permute-start.32 = (f32[256,128]{1,0:T(8,128)S(1)}, f32[256,128]{1,0:T(8,128)S(1)}, u32[]{:S(2)}, u32[]{:S(2)}) collective-permute-start(f32[256,128]{1,0:T(8,128)S(1)} %collective-permute-done.27.refs_2_), channel_id=1, source_target_pairs={{0,8},{8,0},{1,9},{9,1},{2,10},{10,2},{3,11},{11,3},{4,12},{12,4},... | collective-permute-start | bytes 393224 | tf_op jit(solution)/shard_map/ppermute | solution.py:737
  166.3 9.3 %collective-permute-start.33 = (f32[256,128]{1,0:T(8,128)S(1)}, f32[256,128]{1,0:T(8,128)S(1)}, u32[]{:S(2)}, u32[]{:S(2)}) collective-permute-start(f32[256,128]{1,0:T(8,128)S(1)} %collective-permute-done.28.refs_3_), channel_id=1, source_target_pairs={{0,8},{8,0},{1,9},{9,1},{2,10},{10,2},{3,11},{11,3},{4,12},{12,4},... | collective-permute-start | bytes 393224 | tf_op jit(solution)/shard_map/ppermute | solution.py:737
  171.1 5.5 %collective-permute-start.29 = (f32[160,128]{1,0:T(8,128)S(1)}, f32[160,128]{1,0:T(8,128)S(1)}, u32[]{:S(2)}, u32[]{:S(2)}) collective-permute-start(f32[160,128]{1,0:T(8,128)S(1)} %get-tuple-element.122.own), channel_id=1, source_target_pairs={{0,8},{8,0},{1,9},{9,1},{2,10},{10,2},{3,11},{11,3},{4,12},{12,4},... | collective-permute-start | bytes 245768 | tf_op jit(solution)/shard_map/ppermute | solution.py:737

commit v5 on v4

--- a/solution.py
+++ b/solution.py
@@ -57,12 +57,12 @@
     return (((left,), (right,)), ((), ()))
 
 
-def dot(left, right, left_dim=1, right_dim=0, precision=HIGHEST):
+def exact_dot(left, right, left_dim=1, right_dim=0):
     return lax.dot_general(
         left,
         right,
         dims(left_dim, right_dim),
-        precision=precision,
+        precision=HIGHEST,
         preferred_element_type=jnp.float32,
     )
 
@@ -86,6 +86,10 @@
         + half_dot(left_high, right_low, left_dim, right_dim)
         + half_dot(left_low, right_high, left_dim, right_dim)
     )
+
+
+def dot(left, right, left_dim=1, right_dim=0):
+    return dot_three(split(left), split(right), left_dim, right_dim)
 
 
 def sigmoid(value):
@@ -285,7 +289,7 @@
         return tuple(out)
 
     zero = jnp.zeros((BASIS, N), jnp.float32)
-    total = lax.fori_loop(0, SLOTS, step, (zero,) * (4 * KINDS), unroll=4)
+    total = lax.fori_loop(0, SLOTS, step, (zero,) * (4 * KINDS), unroll=16)
     for number in range(4):
         sums[number, :, :] = jnp.concatenate(
             [total[4 * kind + number] for kind in range(KINDS)], axis=0
@@ -392,7 +396,7 @@
 
     zero = jnp.zeros((8, N), jnp.float32)
     out = lax.fori_loop(
-        0, SLOTS, step, (zero, zero, zero, jnp.zeros((24, N), jnp.float32)), unroll=4
+        0, SLOTS, step, (zero, zero, zero, jnp.zeros((24, N), jnp.float32)), unroll=16
     )
     scattered = out[3]
     waves = total[N : N + 8, :]
@@ -521,10 +525,12 @@
 def spread_kernel(*refs):
     out = refs[-1]
     core, column = lax.axis_index("c"), lax.axis_index("x")
-    for number, shard in enumerate(refs[:-1]):
-        source = (column + 4 - number % 4) % 4
-        member = jnp.where(number < 4, core, 1 - core) * 4 + source
-        out[pl.ds(pl.multiple_of(member * SHARD, SHARD), SHARD), :] = shard[...]
+    for number, pair in enumerate(refs[:-1]):
+        for half in range(2):
+            source = column ^ (2 * (number % 2) + half)
+            member = jnp.where(number < 2, core, 1 - core) * 4 + source
+            place = pl.ds(pl.multiple_of(member * SHARD, SHARD), SHARD)
+            out[place, :] = pair[half * SHARD : (half + 1) * SHARD, :]
 
 
 def structure_kernel(*refs):
@@ -543,7 +549,7 @@
         tile = tiles[member]
         tail = tile[N : N + 8, :]
         onehot = (row_of((8, N)).astype(jnp.float32) == tail[3:4, :]).astype(jnp.float32)
-        feature = dot(onehot, table, 0, 0) + dot_three(split(tile[0:N, :]), up)
+        feature = exact_dot(onehot, table, 0, 0) + dot_three(split(tile[0:N, :]), up)
         high, low = split(feature)
         feature_high[part, :] = high
         feature_low[part, :] = low
@@ -624,21 +630,21 @@
         (mine, other)[member // 4][member % 4] = total[:, member * N : (member + 1) * N]
 
 
-def energy_kernel(tile_0, tile_1, tile_2, tile_3, active, species, embed, w_up, read,
-                  grad_out, energy, read_row, up_part):
+def energy_kernel(tile_0, tile_1, tile_2, tile_3, feature_high, feature_low, read,
+                  grad_out, result_out):
     total = tile_0[...] + tile_1[...] + tile_2[...] + tile_3[...]
-    table = jnp.concatenate([embed[...], jnp.zeros((2, N), jnp.float32)], axis=0)
-    onehot = (row_of((8, N)) == species[...]).astype(jnp.float32)
-    act = active[...]
-    combined = dot(onehot, table, 0, 0) + dot(act, w_up[...]) + jnp.transpose(total)
+    feature = feature_high[0:N, :].astype(jnp.float32) + feature_low[0:N, :].astype(jnp.float32)
+    combined = feature + jnp.transpose(total)
     logistic = sigmoid(combined)
-    result = combined * logistic
-    weights = read[...]
-    energy[...] = dot(jnp.broadcast_to(weights, (8, N)), result, 1, 1)[0:1, :]
-    read_row[...] = jnp.sum(result, axis=0, keepdims=True)
-    grad = weights * (logistic * (1.0 + combined * (1.0 - logistic)))
-    grad_out[...] = grad
-    up_part[...] = dot(act, grad, 0, 0)
+    result_out[...] = combined * logistic
+    grad_out[...] = read[...] * (logistic * (1.0 + combined * (1.0 - logistic)))
+
+
+def read_kernel(result, grad, active, read, energy, read_row, up_part):
+    value = result[...]
+    energy[...] = dot(jnp.broadcast_to(read[...], (8, N)), value, 1, 1)[0:1, :]
+    read_row[...] = jnp.sum(value, axis=0, keepdims=True)
+    up_part[...] = dot(active[...], grad[...], 0, 0)
 
 
 def wave_trig(wave_high, wave_low):
@@ -767,12 +773,16 @@
         (f32(4, N, N), f32(4, N, N), f32(2 * SHARD, N), f32(2 * SHARD, N)),
         factor, w_charge, kfilter, wave_high, wave_low,
     )
-    grad_out, energy, read_row, up_part = call(
-        energy_kernel,
-        (f32(N, N), f32(1, N), f32(1, N), f32(N, N)),
-        *scatter(mine, other), active, species, embed, w_up, read,
+    grad_out, result = call(
+        energy_kernel, (f32(N, N),) * 2, *scatter(mine, other), feature_high, feature_low, read
     )
     grads = gather(grad_out)
+    energy, read_row, up_part = call(
+        read_kernel, (f32(1, N), f32(1, N), f32(N, N)), result, grad_out, active, read
+    )
+    *grads, energy, read_row, up_part = lax.optimization_barrier(
+        (*grads, energy, read_row, up_part)
+    )
     projected = cross_sum(
         call(projection_kernel, f32(CROSSES, 16, N), *grads, wave_high, wave_low)
     )
@@ -786,7 +796,7 @@
     )
     tiles = scatter(mine, other)
     shard, *tiles = lax.optimization_barrier((shard, *tiles))
-    shards = [shard] + [step_x(shard, step) for step in (1, 2, 3)]
+    next_shard = lax.ppermute(shard, "x", [(at, at ^ 1) for at in range(4)])
     payload, own_grad, charge_piece = call(
         edge_back_kernel,
         (f32(8, 56, N), f32(8, N), f32(16, N)),
@@ -794,12 +804,14 @@
         w_charge, species, grad_out, read_row,
         cost=pl.CostEstimate(flops=10**9, bytes_accessed=10**7, transcendentals=10**5),
     )
-    payload, *shards = lax.optimization_barrier((payload, *shards))
+    payload, next_shard = lax.optimization_barrier((payload, next_shard))
+    near_shards = jnp.concatenate([shard, next_shard], axis=0)
+    far_shards = lax.ppermute(near_shards, "x", [(at, at ^ 2) for at in range(4)])
     payload = lax.all_to_all(payload, DEPTH, 0, 0)
     payload = call(depth_sum_kernel, f32(16, 56, N), payload, charge_piece)
     payload = lax.all_to_all(payload, PLANE, 0, 0)
     payload, threes = call(plane_sum_kernel, (f32(160, N), f32(8, N)), payload)
-    shards += [other_core(value) for value in shards]
+    shards = [near_shards, far_shards, other_core(near_shards), other_core(far_shards)]
     payload_other = other_core(payload)
     grad_filter = call(spread_kernel, f32(WAVES, N), *shards)
     forces, grad_embed, grad_radial, grad_up, grad_charge, grad_read = call(

time: 178 us -> 172 us (0.966)
  blocking collectives: 74.3 us -> 62 us
  waiting for transfers between devices: 23.8 us -> 29.5 us
  starting transfers between devices: 60.1 us -> 62.8 us
  Pallas kernels: 18.7 us -> 16.5 us
    all_to_all x1 -> x0, blocking collectives: 12.3 us -> none  [body(): payload = lax.all_to_all(payload, DEPTH, 0, 0)]
    all_to_all x0 -> x1, waiting for transfers between devices: none -> 6.99 us  [body(): payload = lax.all_to_all(payload, DEPTH, 0, 0)]
    all_to_all x0 -> x1, starting transfers between devices: none -> 3.4 us  [body(): payload = lax.all_to_all(payload, DEPTH, 0, 0)]
    ppermute x15 -> x12, starting transfers between devices: 11.1 us -> 8.78 us  [step_x(): return lax.ppermute(value, 'x', [(at, (at + step) % 4) for at in range(4)])]
    pallas_call x17 -> x18, Pallas kernels: 18.7 us -> 16.5 us  [call(): pl.pallas_call(kernel, out_shape=out_shape, scratch_shapes=list(scratch),...]
    ppermute x0 -> x2, starting transfers between devices: none -> 1.92 us  [the longest x1 1.92 us: body(): lax.ppermute(near_shards, 'x', [(at, at ^ 2) for at in range(4)])]
    ppermute x15 -> x12, waiting for transfers between devices: 12.1 us -> 10.7 us  [step_x(): return lax.ppermute(value, 'x', [(at, (at + step) % 4) for at in range(4)])]
    ppermute x15 -> x13, starting transfers between devices: 35 us -> 34.1 us  [other_core(): return lax.ppermute(value, 'c', swap)]
  transfers between devices with their start and end apart: 35 -> 33, of which waited for: 16 -> 16; matrix products, arithmetic and copies ran while one was open for 0% -> 0% of each run, Pallas kernels for 3% -> 4%
where the time goes in v5:
time: 172 us
  starting transfers between devices  62.8 us (37%)
  blocking collectives  62 us (36%)
  waiting for transfers between devices  29.5 us (17%)
  Pallas kernels  16.5 us (10%)
    ppermute x13, starting transfers between devices, other_core(): return lax.ppermute(value, 'c', swap)  34.1 us
    all_to_all x2, blocking collectives, cross_sum(): return lax.all_to_all(tiles, CROSS, 0, 0).reshape(2 * SHARD, N)  32.5 us
    all_to_all x2, blocking collectives, cross_sum(): tiles = lax.all_to_all(tiles, CROSS, 0, 0)  29.5 us
    pallas_call x18, Pallas kernels, call(): pl.pallas_call(kernel, out_shape=out_shape, scratch_shapes=list(scratch),...  16.5 us
    ppermute x12, waiting for transfers between devices, step_x(): return lax.ppermute(value, 'x', [(at, (at + step) % 4) for at in range(4)])  10.7 us
    ppermute x4, starting transfers between devices, swapped(): return lax.ppermute(value, axes, places)  10.4 us
    ppermute x12, starting transfers between devices, step_x(): return lax.ppermute(value, 'x', [(at, (at + step) % 4) for at in range(4)])  8.78 us
    all_to_all x1, waiting for transfers between devices, body(): payload = lax.all_to_all(payload, DEPTH, 0, 0)  6.99 us
  transfers between devices with their start and end apart: 33, of which 16 were waited for; matrix products, arithmetic and copies ran while one was open for 0% of the time, Pallas kernels for 4%

profile of v5, /device:TPU:1, one launch (start us, length us, event | category | flops | bytes accessed | tf_op | source)
XLA Modules:
  0.0 171.6 jit_solution(16790670312363972277)
XLA Ops:
  0.6 1.1 shard_map.179
  1.7 2.1 %collective-permute-start = (f32[8,128]{1,0:T(8,128)S(1)}, f32[8,128]{1,0:T(8,128)S(1)}, u32[]{:S(2)}, u32[]{:S(2)}) collective-permute-start(f32[8,128]{1,0:T(8,128)S(1)} %get-tuple-element.85), channel_id=1, source_target_pairs={{0,1},{1,0},{2,3},{3,2},{4,5},{5,4},{6,7},{7,6},{8,9},{9,8},{10,11... | collective-permute-start | bytes 12296 | tf_op jit(solution)/shard_map/ppermute | solution.py:191
  3.9 3.2 %collective-permute-start.1 = (f32[8,128]{1,0:T(8,128)S(1)}, f32[8,128]{1,0:T(8,128)S(1)}, u32[]{:S(2)}, u32[]{:S(2)}) collective-permute-start(f32[8,128]{1,0:T(8,128)S(1)} %get-tuple-element.86), channel_id=1, source_target_pairs={{0,7},{1,2},{2,1},{3,4},{4,3},{5,6},{6,5},{7,0},{8,15},{9,10},{10,... | collective-permute-start | bytes 12296 | tf_op jit(solution)/shard_map/ppermute | solution.py:191
  7.0 1.4 collective-permute-done.1.far.far_y
  8.4 0.1 shard_map.180
  8.5 2.5 %collective-permute-start.2 = (f32[8,128]{1,0:T(8,128)S(1)}, f32[8,128]{1,0:T(8,128)S(1)}, u32[]{:S(2)}, u32[]{:S(2)}) collective-permute-start(f32[8,128]{1,0:T(8,128)S(1)} %get-tuple-element.87), channel_id=1, source_target_pairs={{0,8},{8,0},{16,24},{24,16},{32,40},{40,32},{48,56},{56,48},{64,72... | collective-permute-start | bytes 12296 | tf_op jit(solution)/shard_map/ppermute | solution.py:191
  11.0 2.6 %collective-permute-start.3 = (f32[8,128]{1,0:T(8,128)S(1)}, f32[8,128]{1,0:T(8,128)S(1)}, u32[]{:S(2)}, u32[]{:S(2)}) collective-permute-start(f32[8,128]{1,0:T(8,128)S(1)} %get-tuple-element.88), channel_id=1, source_target_pairs={{0,248},{8,16},{16,8},{24,32},{32,24},{40,48},{48,40},{56,64},{64,... | collective-permute-start | bytes 12296 | tf_op jit(solution)/shard_map/ppermute | solution.py:191
  13.6 1.3 collective-permute-done.3.far_x
  14.9 1.2 shard_map.181
  16.1 1.9 %collective-permute-start.6 = (f32[136,128]{1,0:T(8,128)S(1)}, f32[136,128]{1,0:T(8,128)S(1)}, u32[]{:S(2)}, u32[]{:S(2)}) collective-permute-start(f32[136,128]{1,0:T(8,128)S(1)} %get-tuple-element.91.refs_0_.refs_8_), channel_id=1, source_target_pairs={{0,3},{1,0},{2,1},{3,2},{4,7},{5,4},{6,5},{7,6},{8,11},{9,8},{10,9... | collective-permute-start | bytes 208904 | tf_op jit(solution)/shard_map/ppermute | solution.py:746
  18.0 0.7 collective-permute-start.4
  18.7 6.5 %collective-permute-start.7 = (f32[136,128]{1,0:T(8,128)S(1)}, f32[136,128]{1,0:T(8,128)S(1)}, u32[]{:S(2)}, u32[]{:S(2)}) collective-permute-start(f32[136,128]{1,0:T(8,128)S(1)} %get-tuple-element.91.refs_0_.refs_8_), channel_id=1, source_target_pairs={{0,8},{8,0},{1,9},{9,1},{2,10},{10,2},{3,11},{11,3},{4,12},{12,4},... | collective-permute-start | bytes 208904 | tf_op jit(solution)/shard_map/ppermute | solution.py:743
  25.1 1.6 collective-permute-start.10
  26.8 3.3 %collective-permute-start.9 = (f32[136,128]{1,0:T(8,128)S(1)}, f32[136,128]{1,0:T(8,128)S(1)}, u32[]{:S(2)}, u32[]{:S(2)}) collective-permute-start(f32[136,128]{1,0:T(8,128)S(1)} %collective-permute-done.5.refs_2_.refs_10_), channel_id=1, source_target_pairs={{0,8},{8,0},{1,9},{9,1},{2,10},{10,2},{3,11},{11,3},{4,12},{12,4},... | collective-permute-start | bytes 208904 | tf_op jit(solution)/shard_map/ppermute | solution.py:743
  30.1 0.3 collective-permute-start.8
  30.5 0.6 collective-permute-done.9.refs_6_.refs_14_
  31.0 0.4 collective-permute-done.8.refs_5_.refs_13_
  31.4 2.6 %shard_map.182 = (f32[32,16,128]{2,1,0:T(8,128)S(1)}, bf16[512,1024]{1,0:T(8,128)(2,1)S(1)}, bf16[512,1024]{1,0:T(8,128)(2,1)S(1)}, bf16[1024,128]{1,0:T(8,128)(2,1)S(1)}, bf16[1024,128]{1,0:T(8,128)(2,1)S(1)}) custom-call(f32[136,128]{1,0:T(8,128)S(1)} %get-tuple-element.91.refs_0_.refs_8_, f32[136,128]{1,0:T(8,128)S(1)} %collective-permute-done.4.refs_1_.refs_9_, ...), custom_call_target="tpu_custom_call" | custom-call | tf_op jit(solution)/shard_map/pallas_call | solution.py:112
  34.0 15.7 %all_to_all.30.tiles = f32[32,16,128]{2,1,0:T(8,128)S(1)} all-to-all(f32[32,16,128]{2,1,0:T(8,128)S(1)} %get-tuple-element.92), channel_id=1, replica_groups=mesh['y'=4,'zh'=4,'c'=2,'zl'=2,'x'=4] {'y','zh','zl'}, dimensions={0} | all-to-all | bytes 524288 | tf_op jit(solution)/shard_map/all_to_all | solution.py:766
  49.7 0.1 shard_map.183
  49.8 16.3 %all_to_all.31 = f32[32,16,128]{2,1,0:T(8,128)S(1)} all-to-all(f32[32,16,128]{2,1,0:T(8,128)S(1)} %shard_map.183), channel_id=1, replica_groups=mesh['y'=4,'zh'=4,'c'=2,'zl'=2,'x'=4] {'y','zh','zl'}, dimensions={0} | all-to-all | bytes 524288 | tf_op jit(solution)/shard_map/all_to_all | solution.py:768
  66.1 1.0 shard_map.184
  67.1 3.7 %collective-permute-start.11 = (f32[4,128,128]{2,1,0:T(8,128)S(1)}, f32[4,128,128]{2,1,0:T(8,128)S(1)}, u32[]{:S(2)}, u32[]{:S(2)}) collective-permute-start(f32[4,128,128]{2,1,0:T(8,128)S(1)} %get-tuple-element.96), channel_id=1, source_target_pairs={{0,8},{8,0},{1,9},{9,1},{2,10},{10,2},{3,11},{11,3},{4,12},{12,4},... | collective-permute-start | bytes 786440 | tf_op jit(solution)/shard_map/ppermute | solution.py:743
  70.8 1.2 collective-permute-done.11.other
  72.0 0.8 collective-permute-start.12
  72.8 1.1 collective-permute-start.13
  73.9 0.5 collective-permute-start.14
  74.4 1.0 collective-permute-done.12.tile_1
  75.4 2.1 %collective-permute-done.13.tile_2 = f32[128,128]{1,0:T(8,128)S(1)} collective-permute-done((f32[128,128]{1,0:T(8,128)S(1)}, f32[128,128]{1,0:T(8,128)S(1)}, u32[]{:S(2)}, u32[]{:S(2)}) %collective-permute-start.13) | collective-permute-done | bytes 65568 | tf_op jit(solution)/shard_map/ppermute | solution.py:746
  77.4 1.7 %collective-permute-done.14.tile_3 = f32[128,128]{1,0:T(8,128)S(1)} collective-permute-done((f32[128,128]{1,0:T(8,128)S(1)}, f32[128,128]{1,0:T(8,128)S(1)}, u32[]{:S(2)}, u32[]{:S(2)}) %collective-permute-start.14) | collective-permute-done | bytes 65568 | tf_op jit(solution)/shard_map/ppermute | solution.py:746
  79.2 0.1 shard_map.186
  79.3 0.7 collective-permute-start.17
  80.0 0.3 collective-permute-start.16
  80.3 0.5 collective-permute-start.15
  80.9 2.4 %collective-permute-start.18 = (f32[128,128]{1,0:T(8,128)S(1)}, f32[128,128]{1,0:T(8,128)S(1)}, u32[]{:S(2)}, u32[]{:S(2)}) collective-permute-start(f32[128,128]{1,0:T(8,128)S(1)} %get-tuple-element.111.grad.refs_0_.grad_out), channel_id=1, source_target_pairs={{0,8},{8,0},{1,9},{9,1},{2,10},{10,2},{3,11},{11,3},{4,12},{12,4},... | collective-permute-start | bytes 196616 | tf_op jit(solution)/shard_map/ppermute | solution.py:743
  83.2 1.6 collective-permute-start.21
  84.8 2.8 %collective-permute-start.20 = (f32[128,128]{1,0:T(8,128)S(1)}, f32[128,128]{1,0:T(8,128)S(1)}, u32[]{:S(2)}, u32[]{:S(2)}) collective-permute-start(f32[128,128]{1,0:T(8,128)S(1)} %collective-permute-done.16.refs_2_), channel_id=1, source_target_pairs={{0,8},{8,0},{1,9},{9,1},{2,10},{10,2},{3,11},{11,3},{4,12},{12,4},... | collective-permute-start | bytes 196616 | tf_op jit(solution)/shard_map/ppermute | solution.py:743
  87.6 0.7 collective-permute-start.19
  88.3 0.7 shard_map.187
  89.0 0.2 collective-permute-done.19.refs_5_
  89.2 0.7 shard_map.188
  89.9 13.8 %all_to_all.32.tiles = f32[32,16,128]{2,1,0:T(8,128)S(1)} all-to-all(f32[32,16,128]{2,1,0:T(8,128)S(1)} %shard_map.188), channel_id=1, replica_groups=mesh['y'=4,'zh'=4,'c'=2,'zl'=2,'x'=4] {'y','zh','zl'}, dimensions={0} | all-to-all | bytes 524288 | tf_op jit(solution)/shard_map/all_to_all | solution.py:766
  103.7 16.2 %all_to_all.33 = f32[32,16,128]{2,1,0:T(8,128)S(1)} all-to-all(f32[32,16,128]{2,1,0:T(8,128)S(1)} %shard_map.189), channel_id=1, replica_groups=mesh['y'=4,'zh'=4,'c'=2,'zl'=2,'x'=4] {'y','zh','zl'}, dimensions={0} | all-to-all | bytes 524288 | tf_op jit(solution)/shard_map/all_to_all | solution.py:768
  119.9 2.5 %shard_map.190 = (f32[4,168,128]{2,1,0:T(8,128)S(1)}, f32[4,168,128]{2,1,0:T(8,128)S(1)}, f32[256,128]{1,0:T(8,128)S(1)}) custom-call(f32[128,128]{1,0:T(8,128)S(1)} %get-tuple-element.111.grad.refs_0_.grad_out, f32[128,128]{1,0:T(8,128)S(1)} %collective-permute-done.15.refs_1_, f32[128,128]{1,0:T(8,128)S(1)} %collective-permute-done.16.refs_2_, ...), custom_call_target="tpu_custom_call" | custom-call | tf_op jit(solution)/shard_map/pallas_call | solution.py:112
  122.4 3.6 %collective-permute-start.22 = (f32[4,168,128]{2,1,0:T(8,128)S(1)}, f32[4,168,128]{2,1,0:T(8,128)S(1)}, u32[]{:S(2)}, u32[]{:S(2)}) collective-permute-start(f32[4,168,128]{2,1,0:T(8,128)S(1)} %get-tuple-element.124), channel_id=1, source_target_pairs={{0,8},{8,0},{1,9},{9,1},{2,10},{10,2},{3,11},{11,3},{4,12},{12,4},... | collective-permute-start | bytes 1032200 | tf_op jit(solution)/shard_map/ppermute | solution.py:743
  126.0 1.3 collective-permute-done.22.other
  127.4 1.0 collective-permute-start.23
  128.3 1.3 collective-permute-start.24
  129.6 1.5 collective-permute-done.23.tile_1
  131.2 2.0 %collective-permute-done.24.tile_2 = f32[168,128]{1,0:T(8,128)S(1)} collective-permute-done((f32[168,128]{1,0:T(8,128)S(1)}, f32[168,128]{1,0:T(8,128)S(1)}, u32[]{:S(2)}, u32[]{:S(2)}) %collective-permute-start.24) | collective-permute-done | bytes 86048 | tf_op jit(solution)/shard_map/ppermute | solution.py:746
  133.2 2.4 %collective-permute-done.25.tile_3 = f32[168,128]{1,0:T(8,128)S(1)} collective-permute-done((f32[168,128]{1,0:T(8,128)S(1)}, f32[168,128]{1,0:T(8,128)S(1)}, u32[]{:S(2)}, u32[]{:S(2)}) %collective-permute-start.25) | collective-permute-done | bytes 86048 | tf_op jit(solution)/shard_map/ppermute | solution.py:746
  135.5 3.5 %shard_map.192 = (f32[8,56,128]{2,1,0:T(8,128)}, f32[8,128]{1,0:T(8,128)S(1)}, f32[16,128]{1,0:T(8,128)S(1)}) custom-call(f32[168,128]{1,0:T(8,128)S(1)} %get-tuple-element.129.tile_0, f32[168,128]{1,0:T(8,128)S(1)} %collective-permute-done.23.tile_1, f32[168,128]{1,0:T(8,128)S(1)} %collective-permute-done.24.tile_2, ...), custom_call_target="tpu_custom_call" | custom-call | flops 1000000000 | bytes 10000000 | tf_op jit(solution)/shard_map/pallas_call | solution.py:112
  139.1 0.3 collective-permute-done.26
  139.4 3.4 %all-to-all-start.4 = ((f32[8,56,128]{2,1,0:T(8,128)}), f32[8,56,128]{2,1,0:T(8,128)S(1)}, u32[]{:S(2)}, u32[]{:S(2)}) async-start(f32[8,56,128]{2,1,0:T(8,128)} %get-tuple-element.141), calls=%async_computation.4 | async-start | bytes 458752 | tf_op jit(solution)/shard_map/all_to_all | solution.py:810
  142.8 1.9 %collective-permute-start.28 = (f32[512,128]{1,0:T(8,128)S(1)}, f32[512,128]{1,0:T(8,128)S(1)}, u32[]{:S(2)}, u32[]{:S(2)}) collective-permute-start(f32[512,128]{1,0:T(8,128)S(1)} %constant_dynamic-update-slice_fusion.refs_0_), channel_id=1, source_target_pairs={{0,2},{1,3},{2,0},{3,1},{4,6},{5,7},{6,4},{7,5},{8,10},{9,11},{10,... | collective-permute-start | bytes 786440 | tf_op jit(solution)/shard_map/ppermute | solution.py:809
  144.7 7.0 %all-to-all-done.4.tiles = f32[8,56,128]{2,1,0:T(8,128)S(1)} async-done(((f32[8,56,128]{2,1,0:T(8,128)}), f32[8,56,128]{2,1,0:T(8,128)S(1)}, u32[]{:S(2)}, u32[]{:S(2)}) %all-to-all-start.4) | async-done | bytes 229408 | tf_op jit(solution)/shard_map/all_to_all | solution.py:810
  151.7 0.8 shard_map.193
  152.5 4.2 %all-to-all-start.5 = ((f32[16,56,128]{2,1,0:T(8,128)}), f32[16,56,128]{2,1,0:T(8,128)S(1)}, u32[]{:S(2)}, u32[]{:S(2)}) async-start(f32[16,56,128]{2,1,0:T(8,128)} %shard_map.193), calls=%async_computation.5 | async-start | bytes 917504 | tf_op jit(solution)/shard_map/all_to_all | solution.py:812
  156.7 3.2 %collective-permute-start.29 = (f32[512,128]{1,0:T(8,128)S(1)}, f32[512,128]{1,0:T(8,128)S(1)}, u32[]{:S(2)}, u32[]{:S(2)}) collective-permute-start(f32[512,128]{1,0:T(8,128)S(1)} %constant_dynamic-update-slice_fusion.refs_0_), channel_id=1, source_target_pairs={{0,8},{8,0},{1,9},{9,1},{2,10},{10,2},{3,11},{11,3},{4,12},{12,4},... | collective-permute-start | bytes 786440 | tf_op jit(solution)/shard_map/ppermute | solution.py:743
  159.9 0.1 collective-permute-start.30
  160.0 5.3 %all-to-all-done.5.tiles = f32[16,56,128]{2,1,0:T(8,128)S(1)} async-done(((f32[16,56,128]{2,1,0:T(8,128)}), f32[16,56,128]{2,1,0:T(8,128)S(1)}, u32[]{:S(2)}, u32[]{:S(2)}) %all-to-all-start.5) | async-done | bytes 458784 | tf_op jit(solution)/shard_map/all_to_all | solution.py:812
  165.3 4.3 %collective-permute-start.27 = (f32[160,128]{1,0:T(8,128)S(1)}, f32[160,128]{1,0:T(8,128)S(1)}, u32[]{:S(2)}, u32[]{:S(2)}) collective-permute-start(f32[160,128]{1,0:T(8,128)S(1)} %get-tuple-element.143.own), channel_id=1, source_target_pairs={{0,8},{8,0},{1,9},{9,1},{2,10},{10,2},{3,11},{11,3},{4,12},{12,4},... | collective-permute-start | bytes 245768 | tf_op jit(solution)/shard_map/ppermute | solution.py:743
  169.7 1.1 shard_map.196
  170.7 0.9 shard_map.195
  (34 shorter events, 0.3 us)
Async XLA Ops:
  0.6 30.7 %copy-start.3 = (f32[128,128]{1,0:T(8,128)S(1)}, f32[128,128]{1,0:T(8,128)}, u32[]{:S(2)}) copy-start(f32[128,128]{1,0:T(8,128)} %w_up.1) | copy-start | bytes 196612
  1.7 5.3 %collective-permute-start = (f32[8,128]{1,0:T(8,128)S(1)}, f32[8,128]{1,0:T(8,128)S(1)}, u32[]{:S(2)}, u32[]{:S(2)}) collective-permute-start(f32[8,128]{1,0:T(8,128)S(1)} %get-tuple-element.85), channel_id=1, source_target_pairs={{0,1},{1,0},{2,3},{3,2},{4,5},{5,4},{6,7},{7,6},{8,9},{9,8},{10,11... | collective-permute-start | bytes 12296 | tf_op jit(solution)/shard_map/ppermute | solution.py:191
  3.9 4.6 %collective-permute-start.1 = (f32[8,128]{1,0:T(8,128)S(1)}, f32[8,128]{1,0:T(8,128)S(1)}, u32[]{:S(2)}, u32[]{:S(2)}) collective-permute-start(f32[8,128]{1,0:T(8,128)S(1)} %get-tuple-element.86), channel_id=1, source_target_pairs={{0,7},{1,2},{2,1},{3,4},{4,3},{5,6},{6,5},{7,0},{8,15},{9,10},{10,... | collective-permute-start | bytes 12296 | tf_op jit(solution)/shard_map/ppermute | solution.py:191
  8.5 5.1 %collective-permute-start.2 = (f32[8,128]{1,0:T(8,128)S(1)}, f32[8,128]{1,0:T(8,128)S(1)}, u32[]{:S(2)}, u32[]{:S(2)}) collective-permute-start(f32[8,128]{1,0:T(8,128)S(1)} %get-tuple-element.87), channel_id=1, source_target_pairs={{0,8},{8,0},{16,24},{24,16},{32,40},{40,32},{48,56},{56,48},{64,72... | collective-permute-start | bytes 12296 | tf_op jit(solution)/shard_map/ppermute | solution.py:191
  11.0 3.9 %collective-permute-start.3 = (f32[8,128]{1,0:T(8,128)S(1)}, f32[8,128]{1,0:T(8,128)S(1)}, u32[]{:S(2)}, u32[]{:S(2)}) collective-permute-start(f32[8,128]{1,0:T(8,128)S(1)} %get-tuple-element.88), channel_id=1, source_target_pairs={{0,248},{8,16},{16,8},{24,32},{32,24},{40,48},{48,40},{56,64},{64,... | collective-permute-start | bytes 12296 | tf_op jit(solution)/shard_map/ppermute | solution.py:191
  14.9 16.5 %copy-start.2 = (f32[3,2048]{1,0:T(4,128)S(1)}, f32[3,2048]{1,0:T(4,128)}, u32[]{:S(2)}) copy-start(f32[3,2048]{1,0:T(4,128)} %refs_21_.1) | copy-start | bytes 73732
  16.1 50.0 %copy-start = (f32[2048,128]{1,0:T(8,128)S(1)}, f32[2048,128]{1,0:T(8,128)}, u32[]{:S(2)}) copy-start(f32[2048,128]{1,0:T(8,128)} %refs_20_.1) | copy-start | bytes 3145732
  16.1 9.1 %collective-permute-start.6 = (f32[136,128]{1,0:T(8,128)S(1)}, f32[136,128]{1,0:T(8,128)S(1)}, u32[]{:S(2)}, u32[]{:S(2)}) collective-permute-start(f32[136,128]{1,0:T(8,128)S(1)} %get-tuple-element.91.refs_0_.refs_8_), channel_id=1, source_target_pairs={{0,3},{1,0},{2,1},{3,2},{4,7},{5,4},{6,5},{7,6},{8,11},{9,8},{10,9... | collective-permute-start | bytes 208904 | tf_op jit(solution)/shard_map/ppermute | solution.py:746
  18.0 8.8 %collective-permute-start.5 = (f32[136,128]{1,0:T(8,128)S(1)}, f32[136,128]{1,0:T(8,128)S(1)}, u32[]{:S(2)}, u32[]{:S(2)}) collective-permute-start(f32[136,128]{1,0:T(8,128)S(1)} %get-tuple-element.91.refs_0_.refs_8_), channel_id=1, source_target_pairs={{0,2},{1,3},{2,0},{3,1},{4,6},{5,7},{6,4},{7,5},{8,10},{9,11},{10,... | collective-permute-start | bytes 208904 | tf_op jit(solution)/shard_map/ppermute | solution.py:746
  18.0 12.1 %collective-permute-start.4 = (f32[136,128]{1,0:T(8,128)S(1)}, f32[136,128]{1,0:T(8,128)S(1)}, u32[]{:S(2)}, u32[]{:S(2)}) collective-permute-start(f32[136,128]{1,0:T(8,128)S(1)} %get-tuple-element.91.refs_0_.refs_8_), channel_id=1, source_target_pairs={{0,1},{1,2},{2,3},{3,0},{4,5},{5,6},{6,7},{7,4},{8,9},{9,10},{10,1... | collective-permute-start | bytes 208904 | tf_op jit(solution)/shard_map/ppermute | solution.py:746
  18.7 11.8 %collective-permute-start.7 = (f32[136,128]{1,0:T(8,128)S(1)}, f32[136,128]{1,0:T(8,128)S(1)}, u32[]{:S(2)}, u32[]{:S(2)}) collective-permute-start(f32[136,128]{1,0:T(8,128)S(1)} %get-tuple-element.91.refs_0_.refs_8_), channel_id=1, source_target_pairs={{0,8},{8,0},{1,9},{9,1},{2,10},{10,2},{3,11},{11,3},{4,12},{12,4},... | collective-permute-start | bytes 208904 | tf_op jit(solution)/shard_map/ppermute | solution.py:743
  25.1 5.3 %collective-permute-start.10 = (f32[136,128]{1,0:T(8,128)S(1)}, f32[136,128]{1,0:T(8,128)S(1)}, u32[]{:S(2)}, u32[]{:S(2)}) collective-permute-start(f32[136,128]{1,0:T(8,128)S(1)} %collective-permute-done.6.refs_3_.refs_11_), channel_id=1, source_target_pairs={{0,8},{8,0},{1,9},{9,1},{2,10},{10,2},{3,11},{11,3},{4,12},{12,4},... | collective-permute-start | bytes 208904 | tf_op jit(solution)/shard_map/ppermute | solution.py:743
  26.8 4.2 %collective-permute-start.9 = (f32[136,128]{1,0:T(8,128)S(1)}, f32[136,128]{1,0:T(8,128)S(1)}, u32[]{:S(2)}, u32[]{:S(2)}) collective-permute-start(f32[136,128]{1,0:T(8,128)S(1)} %collective-permute-done.5.refs_2_.refs_10_), channel_id=1, source_target_pairs={{0,8},{8,0},{1,9},{9,1},{2,10},{10,2},{3,11},{11,3},{4,12},{12,4},... | collective-permute-start | bytes 208904 | tf_op jit(solution)/shard_map/ppermute | solution.py:743
  30.1 1.3 collective-permute-start.8
  49.8 16.3 %copy-start.1 = (f32[128,128]{1,0:T(8,128)S(1)}, f32[128,128]{1,0:T(8,128)}, u32[]{:S(2)}) copy-start(f32[128,128]{1,0:T(8,128)} %w_charge.3) | copy-start | bytes 196612
  67.1 4.8 %collective-permute-start.11 = (f32[4,128,128]{2,1,0:T(8,128)S(1)}, f32[4,128,128]{2,1,0:T(8,128)S(1)}, u32[]{:S(2)}, u32[]{:S(2)}) collective-permute-start(f32[4,128,128]{2,1,0:T(8,128)S(1)} %get-tuple-element.96), channel_id=1, source_target_pairs={{0,8},{8,0},{1,9},{9,1},{2,10},{10,2},{3,11},{11,3},{4,12},{12,4},... | collective-permute-start | bytes 786440 | tf_op jit(solution)/shard_map/ppermute | solution.py:743
  72.0 3.4 %collective-permute-start.12 = (f32[128,128]{1,0:T(8,128)S(1)}, f32[128,128]{1,0:T(8,128)S(1)}, u32[]{:S(2)}, u32[]{:S(2)}) collective-permute-start(f32[128,128]{1,0:T(8,128)S(1)} %get-tuple-element.98), channel_id=1, source_target_pairs={{0,3},{1,0},{2,1},{3,2},{4,7},{5,4},{6,5},{7,6},{8,11},{9,8},{10,9... | collective-permute-start | bytes 196616 | tf_op jit(solution)/shard_map/ppermute | solution.py:746
  72.8 4.6 %collective-permute-start.13 = (f32[128,128]{1,0:T(8,128)S(1)}, f32[128,128]{1,0:T(8,128)S(1)}, u32[]{:S(2)}, u32[]{:S(2)}) collective-permute-start(f32[128,128]{1,0:T(8,128)S(1)} %get-tuple-element.99), channel_id=1, source_target_pairs={{0,2},{1,3},{2,0},{3,1},{4,6},{5,7},{6,4},{7,5},{8,10},{9,11},{10,... | collective-permute-start | bytes 196616 | tf_op jit(solution)/shard_map/ppermute | solution.py:746
  73.9 5.3 %collective-permute-start.14 = (f32[128,128]{1,0:T(8,128)S(1)}, f32[128,128]{1,0:T(8,128)S(1)}, u32[]{:S(2)}, u32[]{:S(2)}) collective-permute-start(f32[128,128]{1,0:T(8,128)S(1)} %get-tuple-element.100), channel_id=1, source_target_pairs={{0,1},{1,2},{2,3},{3,0},{4,5},{5,6},{6,7},{7,4},{8,9},{9,10},{10,1... | collective-permute-start | bytes 196616 | tf_op jit(solution)/shard_map/ppermute | solution.py:746
  79.3 3.9 %collective-permute-start.17 = (f32[128,128]{1,0:T(8,128)S(1)}, f32[128,128]{1,0:T(8,128)S(1)}, u32[]{:S(2)}, u32[]{:S(2)}) collective-permute-start(f32[128,128]{1,0:T(8,128)S(1)} %get-tuple-element.111.grad.refs_0_.grad_out), channel_id=1, source_target_pairs={{0,3},{1,0},{2,1},{3,2},{4,7},{5,4},{6,5},{7,6},{8,11},{9,8},{10,9... | collective-permute-start | bytes 196616 | tf_op jit(solution)/shard_map/ppermute | solution.py:746
  80.0 4.8 %collective-permute-start.16 = (f32[128,128]{1,0:T(8,128)S(1)}, f32[128,128]{1,0:T(8,128)S(1)}, u32[]{:S(2)}, u32[]{:S(2)}) collective-permute-start(f32[128,128]{1,0:T(8,128)S(1)} %get-tuple-element.111.grad.refs_0_.grad_out), channel_id=1, source_target_pairs={{0,2},{1,3},{2,0},{3,1},{4,6},{5,7},{6,4},{7,5},{8,10},{9,11},{10,... | collective-permute-start | bytes 196616 | tf_op jit(solution)/shard_map/ppermute | solution.py:746
  80.3 7.2 %collective-permute-start.15 = (f32[128,128]{1,0:T(8,128)S(1)}, f32[128,128]{1,0:T(8,128)S(1)}, u32[]{:S(2)}, u32[]{:S(2)}) collective-permute-start(f32[128,128]{1,0:T(8,128)S(1)} %get-tuple-element.111.grad.refs_0_.grad_out), channel_id=1, source_target_pairs={{0,1},{1,2},{2,3},{3,0},{4,5},{5,6},{6,7},{7,4},{8,9},{9,10},{10,1... | collective-permute-start | bytes 196616 | tf_op jit(solution)/shard_map/ppermute | solution.py:746
  80.9 8.1 %collective-permute-start.18 = (f32[128,128]{1,0:T(8,128)S(1)}, f32[128,128]{1,0:T(8,128)S(1)}, u32[]{:S(2)}, u32[]{:S(2)}) collective-permute-start(f32[128,128]{1,0:T(8,128)S(1)} %get-tuple-element.111.grad.refs_0_.grad_out), channel_id=1, source_target_pairs={{0,8},{8,0},{1,9},{9,1},{2,10},{10,2},{3,11},{11,3},{4,12},{12,4},... | collective-permute-start | bytes 196616 | tf_op jit(solution)/shard_map/ppermute | solution.py:743
  83.2 5.8 %collective-permute-start.21 = (f32[128,128]{1,0:T(8,128)S(1)}, f32[128,128]{1,0:T(8,128)S(1)}, u32[]{:S(2)}, u32[]{:S(2)}) collective-permute-start(f32[128,128]{1,0:T(8,128)S(1)} %collective-permute-done.17.refs_3_), channel_id=1, source_target_pairs={{0,8},{8,0},{1,9},{9,1},{2,10},{10,2},{3,11},{11,3},{4,12},{12,4},... | collective-permute-start | bytes 196616 | tf_op jit(solution)/shard_map/ppermute | solution.py:743
  84.8 4.2 %collective-permute-start.20 = (f32[128,128]{1,0:T(8,128)S(1)}, f32[128,128]{1,0:T(8,128)S(1)}, u32[]{:S(2)}, u32[]{:S(2)}) collective-permute-start(f32[128,128]{1,0:T(8,128)S(1)} %collective-permute-done.16.refs_2_), channel_id=1, source_target_pairs={{0,8},{8,0},{1,9},{9,1},{2,10},{10,2},{3,11},{11,3},{4,12},{12,4},... | collective-permute-start | bytes 196616 | tf_op jit(solution)/shard_map/ppermute | solution.py:743
  87.6 1.6 collective-permute-start.19
  122.4 4.9 %collective-permute-start.22 = (f32[4,168,128]{2,1,0:T(8,128)S(1)}, f32[4,168,128]{2,1,0:T(8,128)S(1)}, u32[]{:S(2)}, u32[]{:S(2)}) collective-permute-start(f32[4,168,128]{2,1,0:T(8,128)S(1)} %get-tuple-element.124), channel_id=1, source_target_pairs={{0,8},{8,0},{1,9},{9,1},{2,10},{10,2},{3,11},{11,3},{4,12},{12,4},... | collective-permute-start | bytes 1032200 | tf_op jit(solution)/shard_map/ppermute | solution.py:743
  127.4 3.8 %collective-permute-start.23 = (f32[168,128]{1,0:T(8,128)S(1)}, f32[168,128]{1,0:T(8,128)S(1)}, u32[]{:S(2)}, u32[]{:S(2)}) collective-permute-start(f32[168,128]{1,0:T(8,128)S(1)} %get-tuple-element.126), channel_id=1, source_target_pairs={{0,3},{1,0},{2,1},{3,2},{4,7},{5,4},{6,5},{7,6},{8,11},{9,8},{10,9... | collective-permute-start | bytes 258056 | tf_op jit(solution)/shard_map/ppermute | solution.py:746
  128.3 4.8 %collective-permute-start.24 = (f32[168,128]{1,0:T(8,128)S(1)}, f32[168,128]{1,0:T(8,128)S(1)}, u32[]{:S(2)}, u32[]{:S(2)}) collective-permute-start(f32[168,128]{1,0:T(8,128)S(1)} %get-tuple-element.127), channel_id=1, source_target_pairs={{0,2},{1,3},{2,0},{3,1},{4,6},{5,7},{6,4},{7,5},{8,10},{9,11},{10,... | collective-permute-start | bytes 258056 | tf_op jit(solution)/shard_map/ppermute | solution.py:746
  129.6 5.9 %collective-permute-start.25 = (f32[168,128]{1,0:T(8,128)S(1)}, f32[168,128]{1,0:T(8,128)S(1)}, u32[]{:S(2)}, u32[]{:S(2)}) collective-permute-start(f32[168,128]{1,0:T(8,128)S(1)} %get-tuple-element.128), channel_id=1, source_target_pairs={{0,1},{1,2},{2,3},{3,0},{4,5},{5,6},{6,7},{7,4},{8,9},{9,10},{10,1... | collective-permute-start | bytes 258056 | tf_op jit(solution)/shard_map/ppermute | solution.py:746
  135.5 3.8 %collective-permute-start.26 = (f32[256,128]{1,0:T(8,128)S(1)}, f32[256,128]{1,0:T(8,128)S(1)}, u32[]{:S(2)}, u32[]{:S(2)}) collective-permute-start(f32[256,128]{1,0:T(8,128)S(1)} %get-tuple-element.140), channel_id=1, source_target_pairs={{0,1},{1,0},{2,3},{3,2},{4,5},{5,4},{6,7},{7,6},{8,9},{9,8},{10,11... | collective-permute-start | bytes 393224 | tf_op jit(solution)/shard_map/ppermute | solution.py:799
  139.4 12.4 %all-to-all-start.4 = ((f32[8,56,128]{2,1,0:T(8,128)}), f32[8,56,128]{2,1,0:T(8,128)S(1)}, u32[]{:S(2)}, u32[]{:S(2)}) async-start(f32[8,56,128]{2,1,0:T(8,128)} %get-tuple-element.141), calls=%async_computation.4 | async-start | bytes 458752 | tf_op jit(solution)/shard_map/all_to_all | solution.py:810
  142.8 17.1 %collective-permute-start.28 = (f32[512,128]{1,0:T(8,128)S(1)}, f32[512,128]{1,0:T(8,128)S(1)}, u32[]{:S(2)}, u32[]{:S(2)}) collective-permute-start(f32[512,128]{1,0:T(8,128)S(1)} %constant_dynamic-update-slice_fusion.refs_0_), channel_id=1, source_target_pairs={{0,2},{1,3},{2,0},{3,1},{4,6},{5,7},{6,4},{7,5},{8,10},{9,11},{10,... | collective-permute-start | bytes 786440 | tf_op jit(solution)/shard_map/ppermute | solution.py:809
  152.5 12.8 %all-to-all-start.5 = ((f32[16,56,128]{2,1,0:T(8,128)}), f32[16,56,128]{2,1,0:T(8,128)S(1)}, u32[]{:S(2)}, u32[]{:S(2)}) async-start(f32[16,56,128]{2,1,0:T(8,128)} %shard_map.193), calls=%async_computation.5 | async-start | bytes 917504 | tf_op jit(solution)/shard_map/all_to_all | solution.py:812
  156.7 13.0 %collective-permute-start.29 = (f32[512,128]{1,0:T(8,128)S(1)}, f32[512,128]{1,0:T(8,128)S(1)}, u32[]{:S(2)}, u32[]{:S(2)}) collective-permute-start(f32[512,128]{1,0:T(8,128)S(1)} %constant_dynamic-update-slice_fusion.refs_0_), channel_id=1, source_target_pairs={{0,8},{8,0},{1,9},{9,1},{2,10},{10,2},{3,11},{11,3},{4,12},{12,4},... | collective-permute-start | bytes 786440 | tf_op jit(solution)/shard_map/ppermute | solution.py:743
  159.9 9.8 %collective-permute-start.30 = (f32[512,128]{1,0:T(8,128)S(1)}, f32[512,128]{1,0:T(8,128)S(1)}, u32[]{:S(2)}, u32[]{:S(2)}) collective-permute-start(f32[512,128]{1,0:T(8,128)S(1)} %collective-permute-done.28.refs_1_), channel_id=1, source_target_pairs={{0,8},{8,0},{1,9},{9,1},{2,10},{10,2},{3,11},{11,3},{4,12},{12,4},... | collective-permute-start | bytes 786440 | tf_op jit(solution)/shard_map/ppermute | solution.py:743
  165.3 5.4 %collective-permute-start.27 = (f32[160,128]{1,0:T(8,128)S(1)}, f32[160,128]{1,0:T(8,128)S(1)}, u32[]{:S(2)}, u32[]{:S(2)}) collective-permute-start(f32[160,128]{1,0:T(8,128)S(1)} %get-tuple-element.143.own), channel_id=1, source_target_pairs={{0,8},{8,0},{1,9},{9,1},{2,10},{10,2},{3,11},{11,3},{4,12},{12,4},... | collective-permute-start | bytes 245768 | tf_op jit(solution)/shard_map/ppermute | solution.py:743

commit v6 on v5

--- a/solution.py
+++ b/solution.py
@@ -364,7 +364,7 @@
         for kind in range(KINDS)
     ]
 
-    def step(slot, carry):
+    def one(slot):
         row = pl.ds(slot, 1)
         kind_row = jnp.broadcast_to(edges[3, row, :], (BASIS, N))
         own_pull = list(pull[KINDS - 1])
@@ -384,20 +384,28 @@
         table = jnp.broadcast_to(places[0, row, :], (8, N)) == sub_table
         place = lane_rows == places[1, row, :]
         onehot = jnp.where(place, 1.0, 0.0).astype(jnp.bfloat16)
-        centre, pieces = [], []
+        parts, pieces = [], []
         for d in range(3):
             part = basis * own_pull[1 + d] + 2.0 * offset[d] * by_square
-            centre.append(carry[d] + part)
+            parts.append(part)
             whole = jnp.broadcast_to(jnp.sum(part, axis=0, keepdims=True), (8, N))
             high = whole.astype(jnp.bfloat16).astype(jnp.float32)
             pieces.append(jnp.where(table, jnp.where(high_rows, high, whole - high), 0.0))
-        rows = jnp.concatenate(pieces, axis=0).astype(jnp.bfloat16)
+        return parts, jnp.concatenate(pieces, axis=0).astype(jnp.bfloat16), onehot
+
+    def step(group, carry):
+        found = [one(group * 8 + number) for number in range(8)]
+        centre = list(carry[:3])
+        for parts, _, _ in found:
+            centre = [centre[d] + parts[d] for d in range(3)]
+        rows = jnp.concatenate([item[1] for item in found], axis=1)
+        onehot = jnp.concatenate([item[2] for item in found], axis=1)
         return (*centre, carry[3] + half_dot(rows, onehot, 1, 1))
 
     zero = jnp.zeros((8, N), jnp.float32)
-    out = lax.fori_loop(
-        0, SLOTS, step, (zero, zero, zero, jnp.zeros((24, N), jnp.float32)), unroll=16
-    )
+    out = (zero, zero, zero, jnp.zeros((24, N), jnp.float32))
+    for group in range(SLOTS // 8):
+        out = step(group, out)
     scattered = out[3]
     waves = total[N : N + 8, :]
     own_rows, one_rows, two_rows, three_rows = [], [], [], []
@@ -533,9 +541,7 @@
             out[place, :] = pair[half * SHARD : (half + 1) * SHARD, :]
 
 
-def structure_kernel(*refs):
-    tiles = refs[:MEMBERS]
-    kvec, embed, w_up, factor, wave_high, wave_low, feature_high, feature_low = refs[MEMBERS:]
+def structure_part(tiles, kvec, embed, w_up, wave_high, wave_low, feature_high, feature_low):
     me = lax.axis_index(GROUP)
     at = pl.multiple_of(me * SHARD, SHARD)
     rows = jnp.concatenate(
@@ -544,9 +550,8 @@
     turns = jnp.transpose(rows * (1.0 / (2.0 * math.pi)))
     table = jnp.concatenate([embed[...], jnp.zeros((2, N), jnp.float32)], axis=0)
     up = split(w_up[...])
-    for member in range(MEMBERS):
+    for member, tile in enumerate(tiles):
         part = slice(member * N, (member + 1) * N)
-        tile = tiles[member]
         tail = tile[N : N + 8, :]
         onehot = (row_of((8, N)).astype(jnp.float32) == tail[3:4, :]).astype(jnp.float32)
         feature = exact_dot(onehot, table, 0, 0) + dot_three(split(tile[0:N, :]), up)
@@ -576,24 +581,38 @@
             waves = slice(SHARD + chunk * 64, SHARD + chunk * 64 + 64)
             wave_high[waves, part] = high
             wave_low[waves, part] = low
-    project(wave_high, wave_low, feature_high[...], feature_low[...], factor)
+    return project(wave_high, wave_low, feature_high[...], feature_low[...])
+
+
+def structure_mine_kernel(*refs):
+    kvec, embed, w_up, factor, *part = refs[4:]
+    factor[...] = structure_part(refs[:4], kvec, embed, w_up, *part)
+
+
+def structure_other_kernel(*refs):
+    kvec, embed, w_up, mine, factor, *part = refs[4:]
+    total = mine[...] + structure_part(refs[:4], kvec, embed, w_up, *part)
+    factor[...] = total.reshape(CROSSES, 16, N)
 
 
 def whole(tiles):
     return jnp.concatenate([tile[0:N, :] for tile in tiles], axis=0)
 
 
-def project(wave_high, wave_low, high, low, out):
-    both = jnp.concatenate([high, low], axis=1)
-    wide = half_dot(wave_high[...], both)
-    total = wide[:, 0:N] + wide[:, N:] + half_dot(wave_low[...], high)
+def project(wave_high, wave_low, high, low):
+    wide = half_dot(wave_high[...], jnp.concatenate([high, low], axis=1))
+    return wide[:, 0:N] + wide[:, N:] + half_dot(wave_low[...], high)
+
+
+def projection_mine_kernel(*refs):
+    wave_high, wave_low, out = refs[4:]
+    out[...] = project(wave_high, wave_low, *split(whole(refs[:4])))
+
+
+def projection_other_kernel(*refs):
+    wave_high, wave_low, mine, out = refs[4:]
+    total = mine[...] + project(wave_high, wave_low, *split(whole(refs[:4])))
     out[...] = total.reshape(CROSSES, 16, N)
-
-
-def projection_kernel(*refs):
-    wave_high, wave_low, out = refs[MEMBERS:]
-    high, low = split(whole(refs[:MEMBERS]))
-    project(wave_high, wave_low, high, low, out)
 
 
 def sum_kernel(tiles, out):
@@ -612,22 +631,42 @@
         ref[...] = mine[number] + other[number]
 
 
-def waves_to_atoms(field, wave_high, wave_low):
-    high, low = split(jnp.transpose(field))
-    wide = half_dot(jnp.concatenate([high, low], axis=0), wave_high[...])
-    return wide[0:N] + wide[N:] + half_dot(high, wave_low[...])
-
-
-def potential_kernel(factor, w_charge, kfilter, wave_high, wave_low,
-                     mine, other, weighted, charge_factor):
+def core_sum_late_kernel(mine, late, other, *out):
+    for number, ref in enumerate(out):
+        ref[...] = mine[number] + other[number]
+        ref[N : N + 8, :] = mine[number, N : N + 8, :] + (
+            late[number] + other[number, N : N + 8, :]
+        )
+
+
+def field_rows(field):
+    return jnp.concatenate(split(jnp.transpose(field)), axis=0)
+
+
+def waves_to_atoms(rows, wave_high, wave_low):
+    wide = half_dot(rows, wave_high[...])
+    return wide[0:N] + wide[N:] + half_dot(rows[0:N], wave_low[...])
+
+
+def to_tiles(total, out):
+    for member in range(4):
+        out[member, 0:N, :] = total[:, member * N : (member + 1) * N]
+
+
+def potential_other_kernel(factor, w_charge, kfilter, wave_high, wave_low,
+                           other, weighted, charge_factor, rows_out):
     scaled = filter_of(kfilter)
     charged = dot(factor[...], w_charge[...])
     charge_factor[...] = charged
     field = charged * jnp.concatenate([scaled, scaled], axis=0)
     weighted[...] = field
-    total = waves_to_atoms(field, wave_high, wave_low)
-    for member in range(MEMBERS):
-        (mine, other)[member // 4][member % 4] = total[:, member * N : (member + 1) * N]
+    rows = field_rows(field)
+    rows_out[...] = rows
+    to_tiles(waves_to_atoms(rows, wave_high, wave_low), other)
+
+
+def potential_mine_kernel(rows, wave_high, wave_low, mine):
+    to_tiles(waves_to_atoms(rows[...], wave_high, wave_low), mine)
 
 
 def energy_kernel(tile_0, tile_1, tile_2, tile_3, feature_high, feature_low, read,
@@ -653,29 +692,10 @@
     return cosine, sine
 
 
-def wave_back_kernel(*refs):
-    grads, shared = refs[:MEMBERS], refs[MEMBERS : 2 * MEMBERS]
-    (
-        projected, factor, charge_factor, weighted, kfilter, kvec, wave_high, wave_low,
-        feature_high, feature_low, w_charge, up_part,
-        mine, other, grad_filter, up_grad, charge_grad,
-    ) = refs[2 * MEMBERS :]
-    scaled = filter_of(kfilter)
-    proj = projected[...]
-    mixed = charge_factor[...] * proj
-    grad_filter[...] = SCALE * (mixed[0:SHARD] + mixed[SHARD:])
-    field = proj * jnp.concatenate([scaled, scaled], axis=0)
-    pieces = split(field)
-    by_charge = waves_to_atoms(field, wave_high, wave_low)
-    charge_grad[...] = dot_three(split(factor[...]), pieces, 0, 0)
-    active = whole(shared)
-    mix = dot_three(split(by_charge), split(active))
-    weights = split(w_charge[...])
-    up_grad[...] = dot_three(split(mix), weights, 0, 1) + up_part[...]
-    by_feature = dot_three(pieces, weights, 1, 1)
+def by_position(left, grads, feature_high, feature_low, kvec, wave_high, wave_low):
     grad_high, grad_low = split(whole(grads))
     along = dot_three(
-        split(jnp.concatenate([weighted[...], by_feature], axis=1)),
+        left,
         (
             jnp.concatenate([grad_high, feature_high[...]], axis=1),
             jnp.concatenate([grad_low, feature_low[...]], axis=1),
@@ -692,18 +712,58 @@
         ],
         axis=0,
     )
-    by_pos = dot_three(split(rows), split(phase))
+    return dot_three(split(rows), split(phase))
+
+
+def wave_back_kernel(*refs):
+    grads, shared = refs[:4], refs[4:12]
+    (
+        projected, factor, weighted, kfilter, kvec, mine_high, mine_low, wave_high, wave_low,
+        feature_high, feature_low, w_charge, up_part,
+        mine, other, left_high, left_low, up_grad, charge_grad,
+    ) = refs[12:]
+    scaled = filter_of(kfilter)
+    field = projected[...] * jnp.concatenate([scaled, scaled], axis=0)
+    pieces = split(field)
+    rows = field_rows(field)
+    mine_charge = waves_to_atoms(rows, mine_high, mine_low)
+    other_charge = waves_to_atoms(rows, wave_high, wave_low)
+    charge_grad[...] = dot_three(split(factor[...]), pieces, 0, 0)
+    mix = dot(mine_charge, whole(shared[:4])) + dot(other_charge, whole(shared[4:]))
+    weights = split(w_charge[...])
+    up_grad[...] = dot_three(split(mix), weights, 0, 1) + up_part[...]
+    left = split(
+        jnp.concatenate([weighted[...], dot_three(pieces, weights, 1, 1)], axis=1)
+    )
+    left_high[...], left_low[...] = left
+    by_pos = by_position(left, grads, feature_high, feature_low, kvec, wave_high, wave_low)
+    to_tiles(mine_charge, mine)
+    to_tiles(other_charge, other)
     core, column = lax.axis_index("c"), lax.axis_index("x")
     for member in range(MEMBERS):
-        part = slice(member * N, (member + 1) * N)
-        out = (mine, other)[member // 4].at[member % 4]
-        place = jnp.where(core == member // 4, 0, 4) + (column + 4 - member % 4) % 4
-        place = place * 16
-        piece = pl.ds(pl.multiple_of(place, 16), 16)
-        out[0:N, :] = by_charge[:, part]
-        out[N : N + 8, :] = by_pos[:, part]
+        number = member % 4
+        out = (mine, other)[member // 4].at[number]
+        place = jnp.where(core == member // 4, 0, 4) + (column + 4 - number) % 4
+        piece = pl.ds(pl.multiple_of(place * 16, 16), 16)
+        if member < 4:
+            out[N : N + 8, :] = jnp.zeros((8, N), jnp.float32)
+        else:
+            out[N : N + 8, :] = by_pos[:, number * N : (number + 1) * N]
         out[N + 8 : N + 24, :] = up_grad[piece, :]
         out[N + 24 : N + 40, :] = charge_grad[piece, :]
+
+
+def wave_back_late_kernel(*refs):
+    (
+        left_high, left_low, projected, charge_factor, kvec, wave_high, wave_low,
+        feature_high, feature_low, late, grad_filter,
+    ) = refs[4:]
+    mixed = charge_factor[...] * projected[...]
+    grad_filter[...] = SCALE * (mixed[0:SHARD] + mixed[SHARD:])
+    left = (left_high[...], left_low[...])
+    by_pos = by_position(left, refs[:4], feature_high, feature_low, kvec, wave_high, wave_low)
+    for member in range(4):
+        late[member, :, :] = by_pos[:, member * N : (member + 1) * N]
 
 
 def body(
@@ -749,18 +809,25 @@
         values = [value] + [step_x(value, step) for step in (1, 2, 3)]
         return values + [other_core(item) for item in values]
 
-    def scatter(mine, other):
-        tiles = call(core_sum_kernel, (f32(*mine.shape[1:]),) * 4, mine, other_core(other))
+    def scatter(kernel, parts, other):
+        shape = f32(*other.shape[1:])
+        tiles = call(kernel, (shape,) * 4, *parts, other_core(other))
         return [tiles[0]] + [step_x(tiles[step], -step) for step in (1, 2, 3)]
 
     shared = gather(shared)
-    half = jax.ShapeDtypeStruct((2 * SHARD, MEMBERS * N), jnp.bfloat16)
-    feature = jax.ShapeDtypeStruct((MEMBERS * N, N), jnp.bfloat16)
-    factor, wave_high, wave_low, feature_high, feature_low = call(
-        structure_kernel,
-        (f32(CROSSES, 16, N), half, half, feature, feature),
-        *shared, kvec, embed, w_up,
-    )
+    half = jax.ShapeDtypeStruct((2 * SHARD, 4 * N), jnp.bfloat16)
+    feature = jax.ShapeDtypeStruct((4 * N, N), jnp.bfloat16)
+    part = (half, half, feature, feature)
+    both = f32(2 * SHARD, N)
+    factor, *mine_part = call(
+        structure_mine_kernel, (both,) + part, *shared[:4], kvec, embed, w_up
+    )
+    factor, *other_part = call(
+        structure_other_kernel, (f32(CROSSES, 16, N),) + part, *shared[4:], kvec, embed, w_up,
+        factor,
+    )
+    mine_waves, mine_features = mine_part[:2], mine_part[2:]
+    other_waves, other_features = other_part[:2], other_part[2:]
 
     def cross_sum(tiles):
         tiles = lax.all_to_all(tiles, CROSS, 0, 0)
@@ -768,33 +835,41 @@
         return lax.all_to_all(tiles, CROSS, 0, 0).reshape(2 * SHARD, N)
 
     factor = cross_sum(factor)
-    mine, other, weighted, charge_factor = call(
-        potential_kernel,
-        (f32(4, N, N), f32(4, N, N), f32(2 * SHARD, N), f32(2 * SHARD, N)),
-        factor, w_charge, kfilter, wave_high, wave_low,
-    )
+    rows = jax.ShapeDtypeStruct((2 * N, 2 * SHARD), jnp.bfloat16)
+    other, weighted, charge_factor, rows = call(
+        potential_other_kernel, (f32(4, N, N), both, both, rows),
+        factor, w_charge, kfilter, *other_waves,
+    )
+    mine = call(potential_mine_kernel, f32(4, N, N), rows, *mine_waves)
     grad_out, result = call(
-        energy_kernel, (f32(N, N),) * 2, *scatter(mine, other), feature_high, feature_low, read
+        energy_kernel, (f32(N, N),) * 2,
+        *scatter(core_sum_kernel, (mine,), other), *mine_features, read,
     )
     grads = gather(grad_out)
     energy, read_row, up_part = call(
         read_kernel, (f32(1, N), f32(1, N), f32(N, N)), result, grad_out, active, read
     )
-    *grads, energy, read_row, up_part = lax.optimization_barrier(
-        (*grads, energy, read_row, up_part)
+    projected = call(projection_mine_kernel, both, *grads[:4], *mine_waves)
+    *others, energy, read_row, up_part = lax.optimization_barrier(
+        (*grads[4:], energy, read_row, up_part)
     )
     projected = cross_sum(
-        call(projection_kernel, f32(CROSSES, 16, N), *grads, wave_high, wave_low)
+        call(projection_other_kernel, f32(CROSSES, 16, N), *others, *other_waves, projected)
     )
     square = pltpu.VMEM((N, N), jnp.float32)
-    mine, other, shard = call(
+    left = jax.ShapeDtypeStruct((2 * SHARD, 2 * N), jnp.bfloat16)
+    mine, other, *left = call(
         wave_back_kernel,
-        (f32(4, N + 40, N), f32(4, N + 40, N), f32(SHARD, N)),
-        *grads, *shared, projected, factor, charge_factor, weighted, kfilter, kvec,
-        wave_high, wave_low, feature_high, feature_low, w_charge, up_part,
+        (f32(4, N + 40, N), f32(4, N + 40, N), left, left),
+        *others, *shared, projected, factor, weighted, kfilter, kvec, *mine_waves,
+        *other_waves, *other_features, w_charge, up_part,
         scratch=(square, square),
     )
-    tiles = scatter(mine, other)
+    late, shard = call(
+        wave_back_late_kernel, (f32(4, 8, N), f32(SHARD, N)),
+        *grads[:4], *left, projected, charge_factor, kvec, *mine_waves, *mine_features,
+    )
+    tiles = scatter(core_sum_late_kernel, (mine, late), other)
     shard, *tiles = lax.optimization_barrier((shard, *tiles))
     next_shard = lax.ppermute(shard, "x", [(at, at ^ 1) for at in range(4)])
     payload, own_grad, charge_piece = call(

time: 172 us -> 172 us (level)
  starting transfers between devices: 62.8 us -> 59.7 us
  waiting for transfers between devices: 29.5 us -> 31.3 us
    ppermute x13, waiting for transfers between devices: 3.56 us -> 1.25 us  [other_core(): return lax.ppermute(value, 'c', swap)]
    all_to_all x1, waiting for transfers between devices: 6.99 us -> 8.94 us  [body(): payload = lax.all_to_all(payload, DEPTH, 0, 0)]
    ppermute x1, starting transfers between devices: 1.92 us -> 0.09 us  [body(): lax.ppermute(near_shards, 'x', [(at, at ^ 2) for at in range(4)])]
    pallas_call x18 -> x22, Pallas kernels: 16.5 us -> 16.7 us  [call(): pl.pallas_call(kernel, out_shape=out_shape, scratch_shapes=list(scratch),...]
  transfers between devices with their start and end apart: 33 -> 33, of which waited for: 16 -> 13; matrix products, arithmetic and copies ran while one was open for 0% -> 0% of each run, Pallas kernels for 4% -> 5%
where the time goes in v6:
time: 172 us; the launch traced here: 171 us
  blocking collectives  62.5 us (36%)
  starting transfers between devices  59.7 us (35%)
  waiting for transfers between devices  31.3 us (18%)
  Pallas kernels  16.7 us (10%)
    ppermute x13, starting transfers between devices, other_core(): return lax.ppermute(value, 'c', swap)  33.8 us
    all_to_all x2, blocking collectives, cross_sum(): return lax.all_to_all(tiles, CROSS, 0, 0).reshape(2 * SHARD, N)  32.1 us
    all_to_all x2, blocking collectives, cross_sum(): tiles = lax.all_to_all(tiles, CROSS, 0, 0)  30.4 us
    pallas_call x22, Pallas kernels, call(): pl.pallas_call(kernel, out_shape=out_shape, scratch_shapes=list(scratch),...  16.7 us
    ppermute x12, waiting for transfers between devices, step_x(): return lax.ppermute(value, 'x', [(at, (at + step) % 4) for at in range(4)])  11.6 us
    ppermute x4, starting transfers between devices, swapped(): return lax.ppermute(value, axes, places)  10.4 us
    all_to_all x1, waiting for transfers between devices, body(): payload = lax.all_to_all(payload, DEPTH, 0, 0)  8.94 us
    ppermute x12, starting transfers between devices, step_x(): return lax.ppermute(value, 'x', [(at, (at + step) % 4) for at in range(4)])  8.42 us
  transfers between devices with their start and end apart: 33, of which 13 were waited for; matrix products, arithmetic and copies ran while one was open for 0% of the time, Pallas kernels for 5%

profile of v6, /device:TPU:1, one launch (start us, length us, event | category | flops | bytes accessed | tf_op | source)
XLA Modules:
  0.0 171.1 jit_solution(2508221019362384639)
XLA Ops:
  0.6 1.1 shard_map.179
  1.7 2.1 %collective-permute-start = (f32[8,128]{1,0:T(8,128)S(1)}, f32[8,128]{1,0:T(8,128)S(1)}, u32[]{:S(2)}, u32[]{:S(2)}) collective-permute-start(f32[8,128]{1,0:T(8,128)S(1)} %get-tuple-element.89), channel_id=1, source_target_pairs={{0,1},{1,0},{2,3},{3,2},{4,5},{5,4},{6,7},{7,6},{8,9},{9,8},{10,11... | collective-permute-start | bytes 12296 | tf_op jit(solution)/shard_map/ppermute | solution.py:191
  3.9 3.2 %collective-permute-start.1 = (f32[8,128]{1,0:T(8,128)S(1)}, f32[8,128]{1,0:T(8,128)S(1)}, u32[]{:S(2)}, u32[]{:S(2)}) collective-permute-start(f32[8,128]{1,0:T(8,128)S(1)} %get-tuple-element.90), channel_id=1, source_target_pairs={{0,7},{1,2},{2,1},{3,4},{4,3},{5,6},{6,5},{7,0},{8,15},{9,10},{10,... | collective-permute-start | bytes 12296 | tf_op jit(solution)/shard_map/ppermute | solution.py:191
  7.0 1.4 collective-permute-done.1.far.far_y
  8.5 2.5 %collective-permute-start.2 = (f32[8,128]{1,0:T(8,128)S(1)}, f32[8,128]{1,0:T(8,128)S(1)}, u32[]{:S(2)}, u32[]{:S(2)}) collective-permute-start(f32[8,128]{1,0:T(8,128)S(1)} %get-tuple-element.91), channel_id=1, source_target_pairs={{0,8},{8,0},{16,24},{24,16},{32,40},{40,32},{48,56},{56,48},{64,72... | collective-permute-start | bytes 12296 | tf_op jit(solution)/shard_map/ppermute | solution.py:191
  11.0 2.6 %collective-permute-start.3 = (f32[8,128]{1,0:T(8,128)S(1)}, f32[8,128]{1,0:T(8,128)S(1)}, u32[]{:S(2)}, u32[]{:S(2)}) collective-permute-start(f32[8,128]{1,0:T(8,128)S(1)} %get-tuple-element.92), channel_id=1, source_target_pairs={{0,248},{8,16},{16,8},{24,32},{32,24},{40,48},{48,40},{56,64},{64,... | collective-permute-start | bytes 12296 | tf_op jit(solution)/shard_map/ppermute | solution.py:191
  13.6 1.3 collective-permute-done.3.far_x
  14.9 1.2 shard_map.181
  16.1 1.9 %collective-permute-start.9 = (f32[136,128]{1,0:T(8,128)S(1)}, f32[136,128]{1,0:T(8,128)S(1)}, u32[]{:S(2)}, u32[]{:S(2)}) collective-permute-start(f32[136,128]{1,0:T(8,128)S(1)} %get-tuple-element.95.refs_0_.refs_4_), channel_id=1, source_target_pairs={{0,3},{1,0},{2,1},{3,2},{4,7},{5,4},{6,5},{7,6},{8,11},{9,8},{10,9... | collective-permute-start | bytes 208904 | tf_op jit(solution)/shard_map/ppermute | solution.py:806
  18.0 0.7 collective-permute-start.5
  18.6 6.5 %collective-permute-start.4 = (f32[136,128]{1,0:T(8,128)S(1)}, f32[136,128]{1,0:T(8,128)S(1)}, u32[]{:S(2)}, u32[]{:S(2)}) collective-permute-start(f32[136,128]{1,0:T(8,128)S(1)} %get-tuple-element.95.refs_0_.refs_4_), channel_id=1, source_target_pairs={{0,8},{8,0},{1,9},{9,1},{2,10},{10,2},{3,11},{11,3},{4,12},{12,4},... | collective-permute-start | bytes 208904 | tf_op jit(solution)/shard_map/ppermute | solution.py:803
  25.1 1.6 collective-permute-start.10
  26.8 3.3 %collective-permute-start.8 = (f32[136,128]{1,0:T(8,128)S(1)}, f32[136,128]{1,0:T(8,128)S(1)}, u32[]{:S(2)}, u32[]{:S(2)}) collective-permute-start(f32[136,128]{1,0:T(8,128)S(1)} %collective-permute-done.7.refs_2_.refs_6_), channel_id=1, source_target_pairs={{0,8},{8,0},{1,9},{9,1},{2,10},{10,2},{3,11},{11,3},{4,12},{12,4},... | collective-permute-start | bytes 208904 | tf_op jit(solution)/shard_map/ppermute | solution.py:803
  30.1 0.3 collective-permute-start.6
  30.4 1.4 shard_map.182
  31.9 1.4 shard_map.183
  33.2 16.2 %all_to_all.30.tiles = f32[32,16,128]{2,1,0:T(8,128)S(1)} all-to-all(f32[32,16,128]{2,1,0:T(8,128)S(1)} %get-tuple-element.97), channel_id=1, replica_groups=mesh['y'=4,'zh'=4,'c'=2,'zl'=2,'x'=4] {'y','zh','zl'}, dimensions={0} | all-to-all | bytes 524288 | tf_op jit(solution)/shard_map/all_to_all | solution.py:833
  49.5 16.2 %all_to_all.31 = f32[32,16,128]{2,1,0:T(8,128)S(1)} all-to-all(f32[32,16,128]{2,1,0:T(8,128)S(1)} %shard_map.184), channel_id=1, replica_groups=mesh['y'=4,'zh'=4,'c'=2,'zl'=2,'x'=4] {'y','zh','zl'}, dimensions={0} | all-to-all | bytes 524288 | tf_op jit(solution)/shard_map/all_to_all | solution.py:835
  65.7 0.8 shard_map.185
  66.5 3.7 %collective-permute-start.11 = (f32[4,128,128]{2,1,0:T(8,128)S(1)}, f32[4,128,128]{2,1,0:T(8,128)S(1)}, u32[]{:S(2)}, u32[]{:S(2)}) collective-permute-start(f32[4,128,128]{2,1,0:T(8,128)S(1)} %get-tuple-element.103), channel_id=1, source_target_pairs={{0,8},{8,0},{1,9},{9,1},{2,10},{10,2},{3,11},{11,3},{4,12},{12,4},... | collective-permute-start | bytes 786440 | tf_op jit(solution)/shard_map/ppermute | solution.py:803
  70.2 0.4 shard_map.186.mine
  70.5 0.8 collective-permute-done.11.other
  71.4 0.8 collective-permute-start.12
  72.2 0.8 collective-permute-start.13
  73.0 0.8 collective-permute-start.14
  73.7 1.0 collective-permute-done.12.tile_1
  74.7 2.1 %collective-permute-done.13.tile_2 = f32[128,128]{1,0:T(8,128)S(1)} collective-permute-done((f32[128,128]{1,0:T(8,128)S(1)}, f32[128,128]{1,0:T(8,128)S(1)}, u32[]{:S(2)}, u32[]{:S(2)}) %collective-permute-start.13) | collective-permute-done | bytes 65568 | tf_op jit(solution)/shard_map/ppermute | solution.py:806
  76.8 1.9 %collective-permute-done.14.tile_3 = f32[128,128]{1,0:T(8,128)S(1)} collective-permute-done((f32[128,128]{1,0:T(8,128)S(1)}, f32[128,128]{1,0:T(8,128)S(1)}, u32[]{:S(2)}, u32[]{:S(2)}) %collective-permute-start.14) | collective-permute-done | bytes 65568 | tf_op jit(solution)/shard_map/ppermute | solution.py:806
  78.7 0.1 shard_map.188
  78.8 0.6 collective-permute-start.20
  79.4 0.3 collective-permute-start.18
  79.7 0.7 collective-permute-start.16
  80.4 2.0 %collective-permute-start.15 = (f32[128,128]{1,0:T(8,128)S(1)}, f32[128,128]{1,0:T(8,128)S(1)}, u32[]{:S(2)}, u32[]{:S(2)}) collective-permute-start(f32[128,128]{1,0:T(8,128)S(1)} %get-tuple-element.111.grad.refs_0_.grad_out), channel_id=1, source_target_pairs={{0,8},{8,0},{1,9},{9,1},{2,10},{10,2},{3,11},{11,3},{4,12},{12,4},... | collective-permute-start | bytes 196616 | tf_op jit(solution)/shard_map/ppermute | solution.py:803
  82.4 1.8 %collective-permute-start.21 = (f32[128,128]{1,0:T(8,128)S(1)}, f32[128,128]{1,0:T(8,128)S(1)}, u32[]{:S(2)}, u32[]{:S(2)}) collective-permute-start(f32[128,128]{1,0:T(8,128)S(1)} %collective-permute-done.20.refs_3_), channel_id=1, source_target_pairs={{0,8},{8,0},{1,9},{9,1},{2,10},{10,2},{3,11},{11,3},{4,12},{12,4},... | collective-permute-start | bytes 196616 | tf_op jit(solution)/shard_map/ppermute | solution.py:803
  84.1 2.9 %collective-permute-start.19 = (f32[128,128]{1,0:T(8,128)S(1)}, f32[128,128]{1,0:T(8,128)S(1)}, u32[]{:S(2)}, u32[]{:S(2)}) collective-permute-start(f32[128,128]{1,0:T(8,128)S(1)} %collective-permute-done.18.refs_2_), channel_id=1, source_target_pairs={{0,8},{8,0},{1,9},{9,1},{2,10},{10,2},{3,11},{11,3},{4,12},{12,4},... | collective-permute-start | bytes 196616 | tf_op jit(solution)/shard_map/ppermute | solution.py:803
  87.0 0.7 collective-permute-start.17
  87.7 0.7 shard_map.189
  88.4 0.4 shard_map.190.refs_6_
  88.9 0.4 shard_map.191
  89.3 14.3 %all_to_all.32.tiles = f32[32,16,128]{2,1,0:T(8,128)S(1)} all-to-all(f32[32,16,128]{2,1,0:T(8,128)S(1)} %shard_map.191), channel_id=1, replica_groups=mesh['y'=4,'zh'=4,'c'=2,'zl'=2,'x'=4] {'y','zh','zl'}, dimensions={0} | all-to-all | bytes 524288 | tf_op jit(solution)/shard_map/all_to_all | solution.py:833
  103.6 15.9 %all_to_all.33 = f32[32,16,128]{2,1,0:T(8,128)S(1)} all-to-all(f32[32,16,128]{2,1,0:T(8,128)S(1)} %shard_map.192), channel_id=1, replica_groups=mesh['y'=4,'zh'=4,'c'=2,'zl'=2,'x'=4] {'y','zh','zl'}, dimensions={0} | all-to-all | bytes 524288 | tf_op jit(solution)/shard_map/all_to_all | solution.py:835
  119.5 2.0 %shard_map.193 = (f32[4,168,128]{2,1,0:T(8,128)S(1)}, f32[4,168,128]{2,1,0:T(8,128)S(1)}, bf16[512,256]{1,0:T(8,128)(2,1)S(1)}, bf16[512,256]{1,0:T(8,128)(2,1)S(1)}) custom-call(f32[128,128]{1,0:T(8,128)S(1)} %collective-permute-done.15.refs_0_, f32[128,128]{1,0:T(8,128)S(1)} %collective-permute-done.17.refs_1_, ...), custom_call_target="tpu_custom_call" | custom-call | tf_op jit(solution)/shard_map/pallas_call | solution.py:112
  121.5 3.6 %collective-permute-start.22 = (f32[4,168,128]{2,1,0:T(8,128)S(1)}, f32[4,168,128]{2,1,0:T(8,128)S(1)}, u32[]{:S(2)}, u32[]{:S(2)}) collective-permute-start(f32[4,168,128]{2,1,0:T(8,128)S(1)} %get-tuple-element.132), channel_id=1, source_target_pairs={{0,8},{8,0},{1,9},{9,1},{2,10},{10,2},{3,11},{11,3},{4,12},{12,4},... | collective-permute-start | bytes 1032200 | tf_op jit(solution)/shard_map/ppermute | solution.py:803
  125.2 0.8 shard_map.194
  126.0 0.4 collective-permute-done.22.other
  126.5 0.9 collective-permute-start.23
  127.4 0.3 collective-permute-start.24
  127.7 0.8 collective-permute-start.25
  128.4 1.9 %collective-permute-done.23.tile_1 = f32[168,128]{1,0:T(8,128)S(1)} collective-permute-done((f32[168,128]{1,0:T(8,128)S(1)}, f32[168,128]{1,0:T(8,128)S(1)}, u32[]{:S(2)}, u32[]{:S(2)}) %collective-permute-start.23) | collective-permute-done | bytes 86048 | tf_op jit(solution)/shard_map/ppermute | solution.py:806
  130.3 2.0 %collective-permute-done.24.tile_2 = f32[168,128]{1,0:T(8,128)S(1)} collective-permute-done((f32[168,128]{1,0:T(8,128)S(1)}, f32[168,128]{1,0:T(8,128)S(1)}, u32[]{:S(2)}, u32[]{:S(2)}) %collective-permute-start.24) | collective-permute-done | bytes 86048 | tf_op jit(solution)/shard_map/ppermute | solution.py:806
  132.3 2.7 %collective-permute-done.25.tile_3 = f32[168,128]{1,0:T(8,128)S(1)} collective-permute-done((f32[168,128]{1,0:T(8,128)S(1)}, f32[168,128]{1,0:T(8,128)S(1)}, u32[]{:S(2)}, u32[]{:S(2)}) %collective-permute-start.25) | collective-permute-done | bytes 86048 | tf_op jit(solution)/shard_map/ppermute | solution.py:806
  135.1 3.0 %shard_map.196 = (f32[8,56,128]{2,1,0:T(8,128)}, f32[8,128]{1,0:T(8,128)S(1)}, f32[16,128]{1,0:T(8,128)S(1)}) custom-call(f32[168,128]{1,0:T(8,128)S(1)} %get-tuple-element.137.tile_0, f32[168,128]{1,0:T(8,128)S(1)} %collective-permute-done.23.tile_1, f32[168,128]{1,0:T(8,128)S(1)} %collective-permute-done.24.tile_2, ...), custom_call_target="tpu_custom_call" | custom-call | flops 1000000000 | bytes 10000000 | tf_op jit(solution)/shard_map/pallas_call | solution.py:112
  138.1 1.4 collective-permute-done.26
  139.5 3.4 %all-to-all-start.4 = ((f32[8,56,128]{2,1,0:T(8,128)}), f32[8,56,128]{2,1,0:T(8,128)S(1)}, u32[]{:S(2)}, u32[]{:S(2)}) async-start(f32[8,56,128]{2,1,0:T(8,128)} %get-tuple-element.149), calls=%async_computation.4 | async-start | bytes 458752 | tf_op jit(solution)/shard_map/all_to_all | solution.py:885
  142.9 0.1 collective-permute-start.28
  143.0 8.9 %all-to-all-done.4.tiles = f32[8,56,128]{2,1,0:T(8,128)S(1)} async-done(((f32[8,56,128]{2,1,0:T(8,128)}), f32[8,56,128]{2,1,0:T(8,128)S(1)}, u32[]{:S(2)}, u32[]{:S(2)}) %all-to-all-start.4) | async-done | bytes 229408 | tf_op jit(solution)/shard_map/all_to_all | solution.py:885
  152.0 0.8 shard_map.197
  152.8 3.6 %all-to-all-start.5 = ((f32[16,56,128]{2,1,0:T(8,128)}), f32[16,56,128]{2,1,0:T(8,128)S(1)}, u32[]{:S(2)}, u32[]{:S(2)}) async-start(f32[16,56,128]{2,1,0:T(8,128)} %shard_map.197), calls=%async_computation.5 | async-start | bytes 917504 | tf_op jit(solution)/shard_map/all_to_all | solution.py:887
  156.4 3.0 %collective-permute-start.29 = (f32[512,128]{1,0:T(8,128)S(1)}, f32[512,128]{1,0:T(8,128)S(1)}, u32[]{:S(2)}, u32[]{:S(2)}) collective-permute-start(f32[512,128]{1,0:T(8,128)S(1)} %constant_dynamic-update-slice_fusion.refs_0_), channel_id=1, source_target_pairs={{0,8},{8,0},{1,9},{9,1},{2,10},{10,2},{3,11},{11,3},{4,12},{12,4},... | collective-permute-start | bytes 786440 | tf_op jit(solution)/shard_map/ppermute | solution.py:803
  159.4 0.1 collective-permute-start.30
  159.5 5.4 %all-to-all-done.5.tiles = f32[16,56,128]{2,1,0:T(8,128)S(1)} async-done(((f32[16,56,128]{2,1,0:T(8,128)}), f32[16,56,128]{2,1,0:T(8,128)S(1)}, u32[]{:S(2)}, u32[]{:S(2)}) %all-to-all-start.5) | async-done | bytes 458784 | tf_op jit(solution)/shard_map/all_to_all | solution.py:887
  164.9 4.2 %collective-permute-start.27 = (f32[160,128]{1,0:T(8,128)S(1)}, f32[160,128]{1,0:T(8,128)S(1)}, u32[]{:S(2)}, u32[]{:S(2)}) collective-permute-start(f32[160,128]{1,0:T(8,128)S(1)} %get-tuple-element.151.own), channel_id=1, source_target_pairs={{0,8},{8,0},{1,9},{9,1},{2,10},{10,2},{3,11},{11,3},{4,12},{12,4},... | collective-permute-start | bytes 245768 | tf_op jit(solution)/shard_map/ppermute | solution.py:803
  169.2 1.1 shard_map.200
  170.2 0.9 shard_map.199
  (38 shorter events, 0.4 us)
Async XLA Ops:
  0.6 29.8 %copy-start.3 = (f32[128,128]{1,0:T(8,128)S(1)}, f32[128,128]{1,0:T(8,128)}, u32[]{:S(2)}) copy-start(f32[128,128]{1,0:T(8,128)} %w_up.1) | copy-start | bytes 196612
  1.7 5.3 %collective-permute-start = (f32[8,128]{1,0:T(8,128)S(1)}, f32[8,128]{1,0:T(8,128)S(1)}, u32[]{:S(2)}, u32[]{:S(2)}) collective-permute-start(f32[8,128]{1,0:T(8,128)S(1)} %get-tuple-element.89), channel_id=1, source_target_pairs={{0,1},{1,0},{2,3},{3,2},{4,5},{5,4},{6,7},{7,6},{8,9},{9,8},{10,11... | collective-permute-start | bytes 12296 | tf_op jit(solution)/shard_map/ppermute | solution.py:191
  3.9 4.6 %collective-permute-start.1 = (f32[8,128]{1,0:T(8,128)S(1)}, f32[8,128]{1,0:T(8,128)S(1)}, u32[]{:S(2)}, u32[]{:S(2)}) collective-permute-start(f32[8,128]{1,0:T(8,128)S(1)} %get-tuple-element.90), channel_id=1, source_target_pairs={{0,7},{1,2},{2,1},{3,4},{4,3},{5,6},{6,5},{7,0},{8,15},{9,10},{10,... | collective-permute-start | bytes 12296 | tf_op jit(solution)/shard_map/ppermute | solution.py:191
  8.5 5.1 %collective-permute-start.2 = (f32[8,128]{1,0:T(8,128)S(1)}, f32[8,128]{1,0:T(8,128)S(1)}, u32[]{:S(2)}, u32[]{:S(2)}) collective-permute-start(f32[8,128]{1,0:T(8,128)S(1)} %get-tuple-element.91), channel_id=1, source_target_pairs={{0,8},{8,0},{16,24},{24,16},{32,40},{40,32},{48,56},{56,48},{64,72... | collective-permute-start | bytes 12296 | tf_op jit(solution)/shard_map/ppermute | solution.py:191
  11.0 3.9 %collective-permute-start.3 = (f32[8,128]{1,0:T(8,128)S(1)}, f32[8,128]{1,0:T(8,128)S(1)}, u32[]{:S(2)}, u32[]{:S(2)}) collective-permute-start(f32[8,128]{1,0:T(8,128)S(1)} %get-tuple-element.92), channel_id=1, source_target_pairs={{0,248},{8,16},{16,8},{24,32},{32,24},{40,48},{48,40},{56,64},{64,... | collective-permute-start | bytes 12296 | tf_op jit(solution)/shard_map/ppermute | solution.py:191
  14.9 15.5 %copy-start.1 = (f32[3,2048]{1,0:T(4,128)S(1)}, f32[3,2048]{1,0:T(4,128)}, u32[]{:S(2)}) copy-start(f32[3,2048]{1,0:T(4,128)} %refs_8_.1) | copy-start | bytes 73732
  16.1 9.1 %collective-permute-start.9 = (f32[136,128]{1,0:T(8,128)S(1)}, f32[136,128]{1,0:T(8,128)S(1)}, u32[]{:S(2)}, u32[]{:S(2)}) collective-permute-start(f32[136,128]{1,0:T(8,128)S(1)} %get-tuple-element.95.refs_0_.refs_4_), channel_id=1, source_target_pairs={{0,3},{1,0},{2,1},{3,2},{4,7},{5,4},{6,5},{7,6},{8,11},{9,8},{10,9... | collective-permute-start | bytes 208904 | tf_op jit(solution)/shard_map/ppermute | solution.py:806
  18.0 8.8 %collective-permute-start.7 = (f32[136,128]{1,0:T(8,128)S(1)}, f32[136,128]{1,0:T(8,128)S(1)}, u32[]{:S(2)}, u32[]{:S(2)}) collective-permute-start(f32[136,128]{1,0:T(8,128)S(1)} %get-tuple-element.95.refs_0_.refs_4_), channel_id=1, source_target_pairs={{0,2},{1,3},{2,0},{3,1},{4,6},{5,7},{6,4},{7,5},{8,10},{9,11},{10,... | collective-permute-start | bytes 208904 | tf_op jit(solution)/shard_map/ppermute | solution.py:806
  18.0 12.1 %collective-permute-start.5 = (f32[136,128]{1,0:T(8,128)S(1)}, f32[136,128]{1,0:T(8,128)S(1)}, u32[]{:S(2)}, u32[]{:S(2)}) collective-permute-start(f32[136,128]{1,0:T(8,128)S(1)} %get-tuple-element.95.refs_0_.refs_4_), channel_id=1, source_target_pairs={{0,1},{1,2},{2,3},{3,0},{4,5},{5,6},{6,7},{7,4},{8,9},{9,10},{10,1... | collective-permute-start | bytes 208904 | tf_op jit(solution)/shard_map/ppermute | solution.py:806
  18.6 13.2 %collective-permute-start.4 = (f32[136,128]{1,0:T(8,128)S(1)}, f32[136,128]{1,0:T(8,128)S(1)}, u32[]{:S(2)}, u32[]{:S(2)}) collective-permute-start(f32[136,128]{1,0:T(8,128)S(1)} %get-tuple-element.95.refs_0_.refs_4_), channel_id=1, source_target_pairs={{0,8},{8,0},{1,9},{9,1},{2,10},{10,2},{3,11},{11,3},{4,12},{12,4},... | collective-permute-start | bytes 208904 | tf_op jit(solution)/shard_map/ppermute | solution.py:803
  25.1 6.7 %collective-permute-start.10 = (f32[136,128]{1,0:T(8,128)S(1)}, f32[136,128]{1,0:T(8,128)S(1)}, u32[]{:S(2)}, u32[]{:S(2)}) collective-permute-start(f32[136,128]{1,0:T(8,128)S(1)} %collective-permute-done.9.refs_3_.refs_7_), channel_id=1, source_target_pairs={{0,8},{8,0},{1,9},{9,1},{2,10},{10,2},{3,11},{11,3},{4,12},{12,4},... | collective-permute-start | bytes 208904 | tf_op jit(solution)/shard_map/ppermute | solution.py:803
  26.8 5.1 %collective-permute-start.8 = (f32[136,128]{1,0:T(8,128)S(1)}, f32[136,128]{1,0:T(8,128)S(1)}, u32[]{:S(2)}, u32[]{:S(2)}) collective-permute-start(f32[136,128]{1,0:T(8,128)S(1)} %collective-permute-done.7.refs_2_.refs_6_), channel_id=1, source_target_pairs={{0,8},{8,0},{1,9},{9,1},{2,10},{10,2},{3,11},{11,3},{4,12},{12,4},... | collective-permute-start | bytes 208904 | tf_op jit(solution)/shard_map/ppermute | solution.py:803
  30.1 1.8 %collective-permute-start.6 = (f32[136,128]{1,0:T(8,128)S(1)}, f32[136,128]{1,0:T(8,128)S(1)}, u32[]{:S(2)}, u32[]{:S(2)}) collective-permute-start(f32[136,128]{1,0:T(8,128)S(1)} %collective-permute-done.5.refs_1_.refs_5_), channel_id=1, source_target_pairs={{0,8},{8,0},{1,9},{9,1},{2,10},{10,2},{3,11},{11,3},{4,12},{12,4},... | collective-permute-start | bytes 208904 | tf_op jit(solution)/shard_map/ppermute | solution.py:803
  31.9 33.8 %copy-start = (f32[2048,128]{1,0:T(8,128)S(1)}, f32[2048,128]{1,0:T(8,128)}, u32[]{:S(2)}) copy-start(f32[2048,128]{1,0:T(8,128)} %refs_15_.1) | copy-start | bytes 3145732
  49.5 16.2 %copy-start.2 = (f32[128,128]{1,0:T(8,128)S(1)}, f32[128,128]{1,0:T(8,128)}, u32[]{:S(2)}) copy-start(f32[128,128]{1,0:T(8,128)} %w_charge.3) | copy-start | bytes 196612
  66.5 4.9 %collective-permute-start.11 = (f32[4,128,128]{2,1,0:T(8,128)S(1)}, f32[4,128,128]{2,1,0:T(8,128)S(1)}, u32[]{:S(2)}, u32[]{:S(2)}) collective-permute-start(f32[4,128,128]{2,1,0:T(8,128)S(1)} %get-tuple-element.103), channel_id=1, source_target_pairs={{0,8},{8,0},{1,9},{9,1},{2,10},{10,2},{3,11},{11,3},{4,12},{12,4},... | collective-permute-start | bytes 786440 | tf_op jit(solution)/shard_map/ppermute | solution.py:803
  71.4 3.4 %collective-permute-start.12 = (f32[128,128]{1,0:T(8,128)S(1)}, f32[128,128]{1,0:T(8,128)S(1)}, u32[]{:S(2)}, u32[]{:S(2)}) collective-permute-start(f32[128,128]{1,0:T(8,128)S(1)} %get-tuple-element.105), channel_id=1, source_target_pairs={{0,3},{1,0},{2,1},{3,2},{4,7},{5,4},{6,5},{7,6},{8,11},{9,8},{10,9... | collective-permute-start | bytes 196616 | tf_op jit(solution)/shard_map/ppermute | solution.py:806
  72.2 4.6 %collective-permute-start.13 = (f32[128,128]{1,0:T(8,128)S(1)}, f32[128,128]{1,0:T(8,128)S(1)}, u32[]{:S(2)}, u32[]{:S(2)}) collective-permute-start(f32[128,128]{1,0:T(8,128)S(1)} %get-tuple-element.106), channel_id=1, source_target_pairs={{0,2},{1,3},{2,0},{3,1},{4,6},{5,7},{6,4},{7,5},{8,10},{9,11},{10,... | collective-permute-start | bytes 196616 | tf_op jit(solution)/shard_map/ppermute | solution.py:806
  73.0 5.7 %collective-permute-start.14 = (f32[128,128]{1,0:T(8,128)S(1)}, f32[128,128]{1,0:T(8,128)S(1)}, u32[]{:S(2)}, u32[]{:S(2)}) collective-permute-start(f32[128,128]{1,0:T(8,128)S(1)} %get-tuple-element.107), channel_id=1, source_target_pairs={{0,1},{1,2},{2,3},{3,0},{4,5},{5,6},{6,7},{7,4},{8,9},{9,10},{10,1... | collective-permute-start | bytes 196616 | tf_op jit(solution)/shard_map/ppermute | solution.py:806
  78.8 3.5 %collective-permute-start.20 = (f32[128,128]{1,0:T(8,128)S(1)}, f32[128,128]{1,0:T(8,128)S(1)}, u32[]{:S(2)}, u32[]{:S(2)}) collective-permute-start(f32[128,128]{1,0:T(8,128)S(1)} %get-tuple-element.111.grad.refs_0_.grad_out), channel_id=1, source_target_pairs={{0,3},{1,0},{2,1},{3,2},{4,7},{5,4},{6,5},{7,6},{8,11},{9,8},{10,9... | collective-permute-start | bytes 196616 | tf_op jit(solution)/shard_map/ppermute | solution.py:806
  79.4 4.7 %collective-permute-start.18 = (f32[128,128]{1,0:T(8,128)S(1)}, f32[128,128]{1,0:T(8,128)S(1)}, u32[]{:S(2)}, u32[]{:S(2)}) collective-permute-start(f32[128,128]{1,0:T(8,128)S(1)} %get-tuple-element.111.grad.refs_0_.grad_out), channel_id=1, source_target_pairs={{0,2},{1,3},{2,0},{3,1},{4,6},{5,7},{6,4},{7,5},{8,10},{9,11},{10,... | collective-permute-start | bytes 196616 | tf_op jit(solution)/shard_map/ppermute | solution.py:806
  79.7 7.3 %collective-permute-start.16 = (f32[128,128]{1,0:T(8,128)S(1)}, f32[128,128]{1,0:T(8,128)S(1)}, u32[]{:S(2)}, u32[]{:S(2)}) collective-permute-start(f32[128,128]{1,0:T(8,128)S(1)} %get-tuple-element.111.grad.refs_0_.grad_out), channel_id=1, source_target_pairs={{0,1},{1,2},{2,3},{3,0},{4,5},{5,6},{6,7},{7,4},{8,9},{9,10},{10,1... | collective-permute-start | bytes 196616 | tf_op jit(solution)/shard_map/ppermute | solution.py:806
  80.4 8.5 %collective-permute-start.15 = (f32[128,128]{1,0:T(8,128)S(1)}, f32[128,128]{1,0:T(8,128)S(1)}, u32[]{:S(2)}, u32[]{:S(2)}) collective-permute-start(f32[128,128]{1,0:T(8,128)S(1)} %get-tuple-element.111.grad.refs_0_.grad_out), channel_id=1, source_target_pairs={{0,8},{8,0},{1,9},{9,1},{2,10},{10,2},{3,11},{11,3},{4,12},{12,4},... | collective-permute-start | bytes 196616 | tf_op jit(solution)/shard_map/ppermute | solution.py:803
  82.4 6.5 %collective-permute-start.21 = (f32[128,128]{1,0:T(8,128)S(1)}, f32[128,128]{1,0:T(8,128)S(1)}, u32[]{:S(2)}, u32[]{:S(2)}) collective-permute-start(f32[128,128]{1,0:T(8,128)S(1)} %collective-permute-done.20.refs_3_), channel_id=1, source_target_pairs={{0,8},{8,0},{1,9},{9,1},{2,10},{10,2},{3,11},{11,3},{4,12},{12,4},... | collective-permute-start | bytes 196616 | tf_op jit(solution)/shard_map/ppermute | solution.py:803
  84.1 4.7 %collective-permute-start.19 = (f32[128,128]{1,0:T(8,128)S(1)}, f32[128,128]{1,0:T(8,128)S(1)}, u32[]{:S(2)}, u32[]{:S(2)}) collective-permute-start(f32[128,128]{1,0:T(8,128)S(1)} %collective-permute-done.18.refs_2_), channel_id=1, source_target_pairs={{0,8},{8,0},{1,9},{9,1},{2,10},{10,2},{3,11},{11,3},{4,12},{12,4},... | collective-permute-start | bytes 196616 | tf_op jit(solution)/shard_map/ppermute | solution.py:803
  87.0 1.9 %collective-permute-start.17 = (f32[128,128]{1,0:T(8,128)S(1)}, f32[128,128]{1,0:T(8,128)S(1)}, u32[]{:S(2)}, u32[]{:S(2)}) collective-permute-start(f32[128,128]{1,0:T(8,128)S(1)} %collective-permute-done.16.refs_1_), channel_id=1, source_target_pairs={{0,8},{8,0},{1,9},{9,1},{2,10},{10,2},{3,11},{11,3},{4,12},{12,4},... | collective-permute-start | bytes 196616 | tf_op jit(solution)/shard_map/ppermute | solution.py:803
  121.5 4.9 %collective-permute-start.22 = (f32[4,168,128]{2,1,0:T(8,128)S(1)}, f32[4,168,128]{2,1,0:T(8,128)S(1)}, u32[]{:S(2)}, u32[]{:S(2)}) collective-permute-start(f32[4,168,128]{2,1,0:T(8,128)S(1)} %get-tuple-element.132), channel_id=1, source_target_pairs={{0,8},{8,0},{1,9},{9,1},{2,10},{10,2},{3,11},{11,3},{4,12},{12,4},... | collective-permute-start | bytes 1032200 | tf_op jit(solution)/shard_map/ppermute | solution.py:803
  126.5 3.8 %collective-permute-start.23 = (f32[168,128]{1,0:T(8,128)S(1)}, f32[168,128]{1,0:T(8,128)S(1)}, u32[]{:S(2)}, u32[]{:S(2)}) collective-permute-start(f32[168,128]{1,0:T(8,128)S(1)} %get-tuple-element.134), channel_id=1, source_target_pairs={{0,3},{1,0},{2,1},{3,2},{4,7},{5,4},{6,5},{7,6},{8,11},{9,8},{10,9... | collective-permute-start | bytes 258056 | tf_op jit(solution)/shard_map/ppermute | solution.py:806
  127.4 4.9 %collective-permute-start.24 = (f32[168,128]{1,0:T(8,128)S(1)}, f32[168,128]{1,0:T(8,128)S(1)}, u32[]{:S(2)}, u32[]{:S(2)}) collective-permute-start(f32[168,128]{1,0:T(8,128)S(1)} %get-tuple-element.135), channel_id=1, source_target_pairs={{0,2},{1,3},{2,0},{3,1},{4,6},{5,7},{6,4},{7,5},{8,10},{9,11},{10,... | collective-permute-start | bytes 258056 | tf_op jit(solution)/shard_map/ppermute | solution.py:806
  127.7 7.4 %collective-permute-start.25 = (f32[168,128]{1,0:T(8,128)S(1)}, f32[168,128]{1,0:T(8,128)S(1)}, u32[]{:S(2)}, u32[]{:S(2)}) collective-permute-start(f32[168,128]{1,0:T(8,128)S(1)} %get-tuple-element.136), channel_id=1, source_target_pairs={{0,1},{1,2},{2,3},{3,0},{4,5},{5,6},{6,7},{7,4},{8,9},{9,10},{10,1... | collective-permute-start | bytes 258056 | tf_op jit(solution)/shard_map/ppermute | solution.py:806
  135.1 4.4 %collective-permute-start.26 = (f32[256,128]{1,0:T(8,128)S(1)}, f32[256,128]{1,0:T(8,128)S(1)}, u32[]{:S(2)}, u32[]{:S(2)}) collective-permute-start(f32[256,128]{1,0:T(8,128)S(1)} %get-tuple-element.148), channel_id=1, source_target_pairs={{0,1},{1,0},{2,3},{3,2},{4,5},{5,4},{6,7},{7,6},{8,9},{9,8},{10,11... | collective-permute-start | bytes 393224 | tf_op jit(solution)/shard_map/ppermute | solution.py:874
  139.5 12.5 %all-to-all-start.4 = ((f32[8,56,128]{2,1,0:T(8,128)}), f32[8,56,128]{2,1,0:T(8,128)S(1)}, u32[]{:S(2)}, u32[]{:S(2)}) async-start(f32[8,56,128]{2,1,0:T(8,128)} %get-tuple-element.149), calls=%async_computation.4 | async-start | bytes 458752 | tf_op jit(solution)/shard_map/all_to_all | solution.py:885
  142.9 16.5 %collective-permute-start.28 = (f32[512,128]{1,0:T(8,128)S(1)}, f32[512,128]{1,0:T(8,128)S(1)}, u32[]{:S(2)}, u32[]{:S(2)}) collective-permute-start(f32[512,128]{1,0:T(8,128)S(1)} %constant_dynamic-update-slice_fusion.refs_0_), channel_id=1, source_target_pairs={{0,2},{1,3},{2,0},{3,1},{4,6},{5,7},{6,4},{7,5},{8,10},{9,11},{10,... | collective-permute-start | bytes 786440 | tf_op jit(solution)/shard_map/ppermute | solution.py:884
  152.8 12.1 %all-to-all-start.5 = ((f32[16,56,128]{2,1,0:T(8,128)}), f32[16,56,128]{2,1,0:T(8,128)S(1)}, u32[]{:S(2)}, u32[]{:S(2)}) async-start(f32[16,56,128]{2,1,0:T(8,128)} %shard_map.197), calls=%async_computation.5 | async-start | bytes 917504 | tf_op jit(solution)/shard_map/all_to_all | solution.py:887
  156.4 12.8 %collective-permute-start.29 = (f32[512,128]{1,0:T(8,128)S(1)}, f32[512,128]{1,0:T(8,128)S(1)}, u32[]{:S(2)}, u32[]{:S(2)}) collective-permute-start(f32[512,128]{1,0:T(8,128)S(1)} %constant_dynamic-update-slice_fusion.refs_0_), channel_id=1, source_target_pairs={{0,8},{8,0},{1,9},{9,1},{2,10},{10,2},{3,11},{11,3},{4,12},{12,4},... | collective-permute-start | bytes 786440 | tf_op jit(solution)/shard_map/ppermute | solution.py:803
  159.4 9.7 %collective-permute-start.30 = (f32[512,128]{1,0:T(8,128)S(1)}, f32[512,128]{1,0:T(8,128)S(1)}, u32[]{:S(2)}, u32[]{:S(2)}) collective-permute-start(f32[512,128]{1,0:T(8,128)S(1)} %collective-permute-done.28.refs_1_), channel_id=1, source_target_pairs={{0,8},{8,0},{1,9},{9,1},{2,10},{10,2},{3,11},{11,3},{4,12},{12,4},... | collective-permute-start | bytes 786440 | tf_op jit(solution)/shard_map/ppermute | solution.py:803
  164.9 5.3 %collective-permute-start.27 = (f32[160,128]{1,0:T(8,128)S(1)}, f32[160,128]{1,0:T(8,128)S(1)}, u32[]{:S(2)}, u32[]{:S(2)}) collective-permute-start(f32[160,128]{1,0:T(8,128)S(1)} %get-tuple-element.151.own), channel_id=1, source_target_pairs={{0,8},{8,0},{1,9},{9,1},{2,10},{10,2},{3,11},{11,3},{4,12},{12,4},... | collective-permute-start | bytes 245768 | tf_op jit(solution)/shard_map/ppermute | solution.py:803

commit v7 on v6

--- a/solution.py
+++ b/solution.py
@@ -33,24 +33,23 @@
 DEPTH = ("zh", "zl")
 PLANE = ("y", "x")
 
-COS_POLY = None
-SIN_POLY = None
-
-
-def _fit():
-    import numpy as np
-
-    points = (1.0 + np.cos(np.pi * (np.arange(200) + 0.5) / 200)) / 8.0
-    root = np.sqrt(points)
-    found = []
-    for count, value in ((7, np.cos(2 * np.pi * root)), (6, np.sin(2 * np.pi * root) / root)):
-        matrix = np.vander(points * 4.0, count, increasing=True)
-        terms = np.linalg.lstsq(matrix, value, rcond=None)[0] * 4.0 ** np.arange(count)
-        found.append([float(term) for term in terms])
-    return found
-
-
-COS_POLY, SIN_POLY = _fit()
+COS_POLY = (
+    0.999999989059021,
+    -19.73920449945393,
+    64.93911745989678,
+    -85.45013953089901,
+    60.16763095102345,
+    -25.96759924855853,
+    6.528658161204758,
+)
+SIN_POLY = (
+    6.283184916495438,
+    -41.34158923268875,
+    81.59994332978647,
+    -76.61447253128671,
+    41.34288235472546,
+    -12.471243535272281,
+)
 
 
 def dims(left, right):
@@ -805,16 +804,18 @@
     def step_x(value, step):
         return lax.ppermute(value, "x", [(at, (at + step) % 4) for at in range(4)])
 
-    def gather(value):
-        values = [value] + [step_x(value, step) for step in (1, 2, 3)]
-        return values + [other_core(item) for item in values]
+    def gather(value, beside=()):
+        one, two, three = (step_x(value, step) for step in (1, 2, 3))
+        two, *beside = lax.optimization_barrier((two, *beside))
+        values = [value, one, two, three]
+        return values + [other_core(item) for item in values], beside
 
     def scatter(kernel, parts, other):
         shape = f32(*other.shape[1:])
         tiles = call(kernel, (shape,) * 4, *parts, other_core(other))
         return [tiles[0]] + [step_x(tiles[step], -step) for step in (1, 2, 3)]
 
-    shared = gather(shared)
+    shared, _ = gather(shared)
     half = jax.ShapeDtypeStruct((2 * SHARD, 4 * N), jnp.bfloat16)
     feature = jax.ShapeDtypeStruct((4 * N, N), jnp.bfloat16)
     part = (half, half, feature, feature)
@@ -845,14 +846,10 @@
         energy_kernel, (f32(N, N),) * 2,
         *scatter(core_sum_kernel, (mine,), other), *mine_features, read,
     )
-    grads = gather(grad_out)
-    energy, read_row, up_part = call(
-        read_kernel, (f32(1, N), f32(1, N), f32(N, N)), result, grad_out, active, read
-    )
+    beside = call(read_kernel, (f32(1, N), f32(1, N), f32(N, N)), result, grad_out, active, read)
+    grads, (energy, read_row, up_part) = gather(grad_out, beside)
     projected = call(projection_mine_kernel, both, *grads[:4], *mine_waves)
-    *others, energy, read_row, up_part = lax.optimization_barrier(
-        (*grads[4:], energy, read_row, up_part)
-    )
+    others = grads[4:]
     projected = cross_sum(
         call(projection_other_kernel, f32(CROSSES, 16, N), *others, *other_waves, projected)
     )
@@ -870,7 +867,6 @@
         *grads[:4], *left, projected, charge_factor, kvec, *mine_waves, *mine_features,
     )
     tiles = scatter(core_sum_late_kernel, (mine, late), other)
-    shard, *tiles = lax.optimization_barrier((shard, *tiles))
     next_shard = lax.ppermute(shard, "x", [(at, at ^ 1) for at in range(4)])
     payload, own_grad, charge_piece = call(
         edge_back_kernel,
@@ -879,7 +875,6 @@
         w_charge, species, grad_out, read_row,
         cost=pl.CostEstimate(flops=10**9, bytes_accessed=10**7, transcendentals=10**5),
     )
-    payload, next_shard = lax.optimization_barrier((payload, next_shard))
     near_shards = jnp.concatenate([shard, next_shard], axis=0)
     far_shards = lax.ppermute(near_shards, "x", [(at, at ^ 2) for at in range(4)])
     payload = lax.all_to_all(payload, DEPTH, 0, 0)

time: 172 us -> 170 us (0.988)
  starting transfers between devices: 59.7 us -> 54.4 us
  waiting for transfers between devices: 31.3 us -> 35.4 us
    ppermute x13, starting transfers between devices: 33.8 us -> 28.3 us  [other_core(): return lax.ppermute(value, 'c', swap)]
    ppermute x1, waiting for transfers between devices: 1.41 us -> 4.54 us  [body(): next_shard = lax.ppermute(shard, 'x', [(at, at ^ 1) for at in range(4)])]
    all_to_all x1, waiting for transfers between devices: 5.4 us -> 8.45 us  [body(): payload = lax.all_to_all(payload, PLANE, 0, 0)]
    all_to_all x1, waiting for transfers between devices: 8.94 us -> 6.2 us  [body(): payload = lax.all_to_all(payload, DEPTH, 0, 0)]
  transfers between devices with their start and end apart: 33 -> 33, of which waited for: 13 -> 15; matrix products, arithmetic and copies ran while one was open for 0% -> 0% of each run, Pallas kernels for 5% -> 3%
where the time goes in v7:
time: 170 us
  blocking collectives  62.5 us (37%)
  starting transfers between devices  54.4 us (32%)
  waiting for transfers between devices  35.4 us (21%)
  Pallas kernels  16.7 us (10%)
    all_to_all x2, blocking collectives, cross_sum(): return lax.all_to_all(tiles, CROSS, 0, 0).reshape(2 * SHARD, N)  32 us
    all_to_all x2, blocking collectives, cross_sum(): tiles = lax.all_to_all(tiles, CROSS, 0, 0)  30.5 us
    ppermute x13, starting transfers between devices, other_core(): return lax.ppermute(value, 'c', swap)  28.3 us
    pallas_call x22, Pallas kernels, call(): pl.pallas_call(kernel, out_shape=out_shape, scratch_shapes=list(scratch),...  16.7 us
    ppermute x12, waiting for transfers between devices, step_x(): return lax.ppermute(value, 'x', [(at, (at + step) % 4) for at in range(4)])  11.5 us
    ppermute x4, starting transfers between devices, swapped(): return lax.ppermute(value, axes, places)  10.4 us
    ppermute x12, starting transfers between devices, step_x(): return lax.ppermute(value, 'x', [(at, (at + step) % 4) for at in range(4)])  8.48 us
    all_to_all x1, waiting for transfers between devices, body(): payload = lax.all_to_all(payload, PLANE, 0, 0)  8.45 us
  transfers between devices with their start and end apart: 33, of which 15 were waited for; matrix products, arithmetic and copies ran while one was open for 0% of the time, Pallas kernels for 3%

profile of v7, /device:TPU:1, one launch (start us, length us, event | category | flops | bytes accessed | tf_op | source)
XLA Modules:
  0.0 169.9 jit_solution(12469250575342620773)
XLA Ops:
  0.6 1.1 shard_map.179
  1.7 2.1 %collective-permute-start = (f32[8,128]{1,0:T(8,128)S(1)}, f32[8,128]{1,0:T(8,128)S(1)}, u32[]{:S(2)}, u32[]{:S(2)}) collective-permute-start(f32[8,128]{1,0:T(8,128)S(1)} %get-tuple-element.79), channel_id=1, source_target_pairs={{0,1},{1,0},{2,3},{3,2},{4,5},{5,4},{6,7},{7,6},{8,9},{9,8},{10,11... | collective-permute-start | bytes 12296 | tf_op jit(solution)/shard_map/ppermute | solution.py:190
  3.9 3.2 %collective-permute-start.1 = (f32[8,128]{1,0:T(8,128)S(1)}, f32[8,128]{1,0:T(8,128)S(1)}, u32[]{:S(2)}, u32[]{:S(2)}) collective-permute-start(f32[8,128]{1,0:T(8,128)S(1)} %get-tuple-element.80), channel_id=1, source_target_pairs={{0,7},{1,2},{2,1},{3,4},{4,3},{5,6},{6,5},{7,0},{8,15},{9,10},{10,... | collective-permute-start | bytes 12296 | tf_op jit(solution)/shard_map/ppermute | solution.py:190
  7.0 1.4 collective-permute-done.1.far.far_y
  8.5 2.5 %collective-permute-start.2 = (f32[8,128]{1,0:T(8,128)S(1)}, f32[8,128]{1,0:T(8,128)S(1)}, u32[]{:S(2)}, u32[]{:S(2)}) collective-permute-start(f32[8,128]{1,0:T(8,128)S(1)} %get-tuple-element.81), channel_id=1, source_target_pairs={{0,8},{8,0},{16,24},{24,16},{32,40},{40,32},{48,56},{56,48},{64,72... | collective-permute-start | bytes 12296 | tf_op jit(solution)/shard_map/ppermute | solution.py:190
  11.0 2.6 %collective-permute-start.3 = (f32[8,128]{1,0:T(8,128)S(1)}, f32[8,128]{1,0:T(8,128)S(1)}, u32[]{:S(2)}, u32[]{:S(2)}) collective-permute-start(f32[8,128]{1,0:T(8,128)S(1)} %get-tuple-element.82), channel_id=1, source_target_pairs={{0,248},{8,16},{16,8},{24,32},{32,24},{40,48},{48,40},{56,64},{64,... | collective-permute-start | bytes 12296 | tf_op jit(solution)/shard_map/ppermute | solution.py:190
  13.6 1.3 collective-permute-done.3.far_x
  14.9 1.2 shard_map.181
  16.1 0.4 collective-permute-start.7
  16.5 1.6 collective-permute-start.9
  18.1 0.5 collective-permute-start.5
  18.6 6.5 %collective-permute-start.4 = (f32[136,128]{1,0:T(8,128)S(1)}, f32[136,128]{1,0:T(8,128)S(1)}, u32[]{:S(2)}, u32[]{:S(2)}) collective-permute-start(f32[136,128]{1,0:T(8,128)S(1)} %get-tuple-element.85.refs_0_.refs_4_), channel_id=1, source_target_pairs={{0,8},{8,0},{1,9},{9,1},{2,10},{10,2},{3,11},{11,3},{4,12},{12,4},... | collective-permute-start | bytes 208904 | tf_op jit(solution)/shard_map/ppermute | solution.py:802
  25.0 2.9 %collective-permute-start.8 = (f32[136,128]{1,0:T(8,128)S(1)}, f32[136,128]{1,0:T(8,128)S(1)}, u32[]{:S(2)}, u32[]{:S(2)}) collective-permute-start(f32[136,128]{1,0:T(8,128)S(1)} %collective-permute-done.7.refs_2_.refs_6_), channel_id=1, source_target_pairs={{0,8},{8,0},{1,9},{9,1},{2,10},{10,2},{3,11},{11,3},{4,12},{12,4},... | collective-permute-start | bytes 208904 | tf_op jit(solution)/shard_map/ppermute | solution.py:802
  27.9 0.2 collective-permute-start.10
  28.1 1.7 %collective-permute-start.6 = (f32[136,128]{1,0:T(8,128)S(1)}, f32[136,128]{1,0:T(8,128)S(1)}, u32[]{:S(2)}, u32[]{:S(2)}) collective-permute-start(f32[136,128]{1,0:T(8,128)S(1)} %collective-permute-done.5.refs_1_.refs_5_), channel_id=1, source_target_pairs={{0,8},{8,0},{1,9},{9,1},{2,10},{10,2},{3,11},{11,3},{4,12},{12,4},... | collective-permute-start | bytes 208904 | tf_op jit(solution)/shard_map/ppermute | solution.py:802
  29.8 1.4 shard_map.182
  31.2 1.4 shard_map.183
  32.6 16.4 %all_to_all.30.tiles = f32[32,16,128]{2,1,0:T(8,128)S(1)} all-to-all(f32[32,16,128]{2,1,0:T(8,128)S(1)} %get-tuple-element.87), channel_id=1, replica_groups=mesh['y'=4,'zh'=4,'c'=2,'zl'=2,'x'=4] {'y','zh','zl'}, dimensions={0} | all-to-all | bytes 524288 | tf_op jit(solution)/shard_map/all_to_all | solution.py:834
  49.0 16.0 %all_to_all.31 = f32[32,16,128]{2,1,0:T(8,128)S(1)} all-to-all(f32[32,16,128]{2,1,0:T(8,128)S(1)} %shard_map.184), channel_id=1, replica_groups=mesh['y'=4,'zh'=4,'c'=2,'zl'=2,'x'=4] {'y','zh','zl'}, dimensions={0} | all-to-all | bytes 524288 | tf_op jit(solution)/shard_map/all_to_all | solution.py:836
  65.0 0.8 shard_map.185
  65.8 3.7 %collective-permute-start.11 = (f32[4,128,128]{2,1,0:T(8,128)S(1)}, f32[4,128,128]{2,1,0:T(8,128)S(1)}, u32[]{:S(2)}, u32[]{:S(2)}) collective-permute-start(f32[4,128,128]{2,1,0:T(8,128)S(1)} %get-tuple-element.93), channel_id=1, source_target_pairs={{0,8},{8,0},{1,9},{9,1},{2,10},{10,2},{3,11},{11,3},{4,12},{12,4},... | collective-permute-start | bytes 786440 | tf_op jit(solution)/shard_map/ppermute | solution.py:802
  69.5 0.4 shard_map.186.mine
  69.9 0.8 collective-permute-done.11.other
  70.7 1.0 collective-permute-start.12
  71.7 0.7 collective-permute-start.13
  72.4 0.8 collective-permute-start.14
  73.1 1.0 collective-permute-done.12.tile_1
  74.1 2.3 %collective-permute-done.13.tile_2 = f32[128,128]{1,0:T(8,128)S(1)} collective-permute-done((f32[128,128]{1,0:T(8,128)S(1)}, f32[128,128]{1,0:T(8,128)S(1)}, u32[]{:S(2)}, u32[]{:S(2)}) %collective-permute-start.13) | collective-permute-done | bytes 65568 | tf_op jit(solution)/shard_map/ppermute | solution.py:805
  76.4 1.9 %collective-permute-done.14.tile_3 = f32[128,128]{1,0:T(8,128)S(1)} collective-permute-done((f32[128,128]{1,0:T(8,128)S(1)}, f32[128,128]{1,0:T(8,128)S(1)}, u32[]{:S(2)}, u32[]{:S(2)}) %collective-permute-start.14) | collective-permute-done | bytes 65568 | tf_op jit(solution)/shard_map/ppermute | solution.py:805
  78.2 0.1 shard_map.188
  78.4 0.6 collective-permute-start.15
  78.9 0.7 collective-permute-start.20
  79.7 0.7 collective-permute-start.17
  80.4 2.0 %collective-permute-start.16 = (f32[128,128]{1,0:T(8,128)S(1)}, f32[128,128]{1,0:T(8,128)S(1)}, u32[]{:S(2)}, u32[]{:S(2)}) collective-permute-start(f32[128,128]{1,0:T(8,128)S(1)} %get-tuple-element.101.grad.refs_0_.grad_out), channel_id=1, source_target_pairs={{0,8},{8,0},{1,9},{9,1},{2,10},{10,2},{3,11},{11,3},{4,12},{12,4},... | collective-permute-start | bytes 196616 | tf_op jit(solution)/shard_map/ppermute | solution.py:802
  82.4 0.7 shard_map.189
  83.1 2.6 %collective-permute-start.21 = (f32[128,128]{1,0:T(8,128)S(1)}, f32[128,128]{1,0:T(8,128)S(1)}, u32[]{:S(2)}, u32[]{:S(2)}) collective-permute-start(f32[128,128]{1,0:T(8,128)S(1)} %collective-permute-done.20.refs_3_), channel_id=1, source_target_pairs={{0,8},{8,0},{1,9},{9,1},{2,10},{10,2},{3,11},{11,3},{4,12},{12,4},... | collective-permute-start | bytes 196616 | tf_op jit(solution)/shard_map/ppermute | solution.py:802
  85.7 1.8 %collective-permute-start.18 = (f32[128,128]{1,0:T(8,128)S(1)}, f32[128,128]{1,0:T(8,128)S(1)}, u32[]{:S(2)}, u32[]{:S(2)}) collective-permute-start(f32[128,128]{1,0:T(8,128)S(1)} %collective-permute-done.17.refs_1_), channel_id=1, source_target_pairs={{0,8},{8,0},{1,9},{9,1},{2,10},{10,2},{3,11},{11,3},{4,12},{12,4},... | collective-permute-start | bytes 196616 | tf_op jit(solution)/shard_map/ppermute | solution.py:802
  87.5 0.4 shard_map.190.refs_6_
  88.0 0.4 collective-permute-done.18.refs_1_
  88.4 0.4 collective-permute-done.19.refs_2_
  88.8 0.4 shard_map.191
  89.2 14.1 %all_to_all.32.tiles = f32[32,16,128]{2,1,0:T(8,128)S(1)} all-to-all(f32[32,16,128]{2,1,0:T(8,128)S(1)} %shard_map.191), channel_id=1, replica_groups=mesh['y'=4,'zh'=4,'c'=2,'zl'=2,'x'=4] {'y','zh','zl'}, dimensions={0} | all-to-all | bytes 524288 | tf_op jit(solution)/shard_map/all_to_all | solution.py:834
  103.4 16.0 %all_to_all.33 = f32[32,16,128]{2,1,0:T(8,128)S(1)} all-to-all(f32[32,16,128]{2,1,0:T(8,128)S(1)} %shard_map.192), channel_id=1, replica_groups=mesh['y'=4,'zh'=4,'c'=2,'zl'=2,'x'=4] {'y','zh','zl'}, dimensions={0} | all-to-all | bytes 524288 | tf_op jit(solution)/shard_map/all_to_all | solution.py:836
  119.4 2.0 %shard_map.193 = (f32[4,168,128]{2,1,0:T(8,128)S(1)}, f32[4,168,128]{2,1,0:T(8,128)S(1)}, bf16[512,256]{1,0:T(8,128)(2,1)S(1)}, bf16[512,256]{1,0:T(8,128)(2,1)S(1)}) custom-call(f32[128,128]{1,0:T(8,128)S(1)} %collective-permute-done.16.refs_0_, f32[128,128]{1,0:T(8,128)S(1)} %collective-permute-done.18.refs_1_, ...), custom_call_target="tpu_custom_call" | custom-call | tf_op jit(solution)/shard_map/pallas_call | solution.py:111
  121.4 3.6 %collective-permute-start.22 = (f32[4,168,128]{2,1,0:T(8,128)S(1)}, f32[4,168,128]{2,1,0:T(8,128)S(1)}, u32[]{:S(2)}, u32[]{:S(2)}) collective-permute-start(f32[4,168,128]{2,1,0:T(8,128)S(1)} %get-tuple-element.118), channel_id=1, source_target_pairs={{0,8},{8,0},{1,9},{9,1},{2,10},{10,2},{3,11},{11,3},{4,12},{12,4},... | collective-permute-start | bytes 1032200 | tf_op jit(solution)/shard_map/ppermute | solution.py:802
  125.1 0.8 shard_map.194
  125.9 0.4 collective-permute-done.22.other
  126.5 0.7 collective-permute-start.24
  127.2 0.8 collective-permute-start.25
  127.9 2.3 %collective-permute-done.23.tile_1 = f32[168,128]{1,0:T(8,128)S(1)} collective-permute-done((f32[168,128]{1,0:T(8,128)S(1)}, f32[168,128]{1,0:T(8,128)S(1)}, u32[]{:S(2)}, u32[]{:S(2)}) %collective-permute-start.23) | collective-permute-done | bytes 86048 | tf_op jit(solution)/shard_map/ppermute | solution.py:805
  130.2 1.6 collective-permute-done.24.tile_2
  131.8 2.5 %collective-permute-done.25.tile_3 = f32[168,128]{1,0:T(8,128)S(1)} collective-permute-done((f32[168,128]{1,0:T(8,128)S(1)}, f32[168,128]{1,0:T(8,128)S(1)}, u32[]{:S(2)}, u32[]{:S(2)}) %collective-permute-start.25) | collective-permute-done | bytes 86048 | tf_op jit(solution)/shard_map/ppermute | solution.py:805
  134.4 3.0 %shard_map.196 = (f32[8,56,128]{2,1,0:T(8,128)}, f32[8,128]{1,0:T(8,128)S(1)}, f32[16,128]{1,0:T(8,128)S(1)}) custom-call(f32[168,128]{1,0:T(8,128)S(1)} %get-tuple-element.119.tile_0, f32[168,128]{1,0:T(8,128)S(1)} %collective-permute-done.23.tile_1, f32[168,128]{1,0:T(8,128)S(1)} %collective-permute-done.24.tile_2, ...), custom_call_target="tpu_custom_call" | custom-call | flops 1000000000 | bytes 10000000 | tf_op jit(solution)/shard_map/pallas_call | solution.py:111
  137.4 3.4 %all-to-all-start.4 = ((f32[8,56,128]{2,1,0:T(8,128)}), f32[8,56,128]{2,1,0:T(8,128)S(1)}, u32[]{:S(2)}, u32[]{:S(2)}) async-start(f32[8,56,128]{2,1,0:T(8,128)} %get-tuple-element.129), calls=%async_computation.4 | async-start | bytes 458752 | tf_op jit(solution)/shard_map/all_to_all | solution.py:880
  140.9 4.5 %collective-permute-done.27 = f32[256,128]{1,0:T(8,128)S(1)} collective-permute-done((f32[256,128]{1,0:T(8,128)S(1)}, f32[256,128]{1,0:T(8,128)S(1)}, u32[]{:S(2)}, u32[]{:S(2)}) %collective-permute-start.27) | collective-permute-done | bytes 131104 | tf_op jit(solution)/shard_map/ppermute | solution.py:870
  145.6 6.2 %all-to-all-done.4.tiles = f32[8,56,128]{2,1,0:T(8,128)S(1)} async-done(((f32[8,56,128]{2,1,0:T(8,128)}), f32[8,56,128]{2,1,0:T(8,128)S(1)}, u32[]{:S(2)}, u32[]{:S(2)}) %all-to-all-start.4) | async-done | bytes 229408 | tf_op jit(solution)/shard_map/all_to_all | solution.py:880
  151.8 0.8 shard_map.197
  152.6 3.6 %all-to-all-start.5 = ((f32[16,56,128]{2,1,0:T(8,128)}), f32[16,56,128]{2,1,0:T(8,128)S(1)}, u32[]{:S(2)}, u32[]{:S(2)}) async-start(f32[16,56,128]{2,1,0:T(8,128)} %shard_map.197), calls=%async_computation.5 | async-start | bytes 917504 | tf_op jit(solution)/shard_map/all_to_all | solution.py:882
  156.1 1.2 collective-permute-start.29
  157.3 0.1 collective-permute-start.30
  157.4 8.4 %all-to-all-done.5.tiles = f32[16,56,128]{2,1,0:T(8,128)S(1)} async-done(((f32[16,56,128]{2,1,0:T(8,128)}), f32[16,56,128]{2,1,0:T(8,128)S(1)}, u32[]{:S(2)}, u32[]{:S(2)}) %all-to-all-start.5) | async-done | bytes 458784 | tf_op jit(solution)/shard_map/all_to_all | solution.py:882
  165.9 2.1 %collective-permute-start.26 = (f32[160,128]{1,0:T(8,128)S(1)}, f32[160,128]{1,0:T(8,128)S(1)}, u32[]{:S(2)}, u32[]{:S(2)}) collective-permute-start(f32[160,128]{1,0:T(8,128)S(1)} %get-tuple-element.131.own), channel_id=1, source_target_pairs={{0,8},{8,0},{1,9},{9,1},{2,10},{10,2},{3,11},{11,3},{4,12},{12,4},... | collective-permute-start | bytes 245768 | tf_op jit(solution)/shard_map/ppermute | solution.py:802
  168.0 1.1 shard_map.200
  169.0 0.9 shard_map.199
  (38 shorter events, 0.6 us)
Async XLA Ops:
  0.6 29.2 %copy-start.3 = (f32[128,128]{1,0:T(8,128)S(1)}, f32[128,128]{1,0:T(8,128)}, u32[]{:S(2)}) copy-start(f32[128,128]{1,0:T(8,128)} %w_up.1) | copy-start | bytes 196612
  1.7 5.3 %collective-permute-start = (f32[8,128]{1,0:T(8,128)S(1)}, f32[8,128]{1,0:T(8,128)S(1)}, u32[]{:S(2)}, u32[]{:S(2)}) collective-permute-start(f32[8,128]{1,0:T(8,128)S(1)} %get-tuple-element.79), channel_id=1, source_target_pairs={{0,1},{1,0},{2,3},{3,2},{4,5},{5,4},{6,7},{7,6},{8,9},{9,8},{10,11... | collective-permute-start | bytes 12296 | tf_op jit(solution)/shard_map/ppermute | solution.py:190
  3.9 4.6 %collective-permute-start.1 = (f32[8,128]{1,0:T(8,128)S(1)}, f32[8,128]{1,0:T(8,128)S(1)}, u32[]{:S(2)}, u32[]{:S(2)}) collective-permute-start(f32[8,128]{1,0:T(8,128)S(1)} %get-tuple-element.80), channel_id=1, source_target_pairs={{0,7},{1,2},{2,1},{3,4},{4,3},{5,6},{6,5},{7,0},{8,15},{9,10},{10,... | collective-permute-start | bytes 12296 | tf_op jit(solution)/shard_map/ppermute | solution.py:190
  8.5 5.1 %collective-permute-start.2 = (f32[8,128]{1,0:T(8,128)S(1)}, f32[8,128]{1,0:T(8,128)S(1)}, u32[]{:S(2)}, u32[]{:S(2)}) collective-permute-start(f32[8,128]{1,0:T(8,128)S(1)} %get-tuple-element.81), channel_id=1, source_target_pairs={{0,8},{8,0},{16,24},{24,16},{32,40},{40,32},{48,56},{56,48},{64,72... | collective-permute-start | bytes 12296 | tf_op jit(solution)/shard_map/ppermute | solution.py:190
  11.0 3.9 %collective-permute-start.3 = (f32[8,128]{1,0:T(8,128)S(1)}, f32[8,128]{1,0:T(8,128)S(1)}, u32[]{:S(2)}, u32[]{:S(2)}) collective-permute-start(f32[8,128]{1,0:T(8,128)S(1)} %get-tuple-element.82), channel_id=1, source_target_pairs={{0,248},{8,16},{16,8},{24,32},{32,24},{40,48},{48,40},{56,64},{64,... | collective-permute-start | bytes 12296 | tf_op jit(solution)/shard_map/ppermute | solution.py:190
  14.9 14.9 %copy-start.1 = (f32[3,2048]{1,0:T(4,128)S(1)}, f32[3,2048]{1,0:T(4,128)}, u32[]{:S(2)}) copy-start(f32[3,2048]{1,0:T(4,128)} %refs_8_.1) | copy-start | bytes 73732
  16.1 9.0 %collective-permute-start.7 = (f32[136,128]{1,0:T(8,128)S(1)}, f32[136,128]{1,0:T(8,128)S(1)}, u32[]{:S(2)}, u32[]{:S(2)}) collective-permute-start(f32[136,128]{1,0:T(8,128)S(1)} %get-tuple-element.85.refs_0_.refs_4_), channel_id=1, source_target_pairs={{0,2},{1,3},{2,0},{3,1},{4,6},{5,7},{6,4},{7,5},{8,10},{9,11},{10,... | collective-permute-start | bytes 208904 | tf_op jit(solution)/shard_map/ppermute | solution.py:805
  16.5 11.4 %collective-permute-start.9 = (f32[136,128]{1,0:T(8,128)S(1)}, f32[136,128]{1,0:T(8,128)S(1)}, u32[]{:S(2)}, u32[]{:S(2)}) collective-permute-start(f32[136,128]{1,0:T(8,128)S(1)} %get-tuple-element.85.refs_0_.refs_4_), channel_id=1, source_target_pairs={{0,3},{1,0},{2,1},{3,2},{4,7},{5,4},{6,5},{7,6},{8,11},{9,8},{10,9... | collective-permute-start | bytes 208904 | tf_op jit(solution)/shard_map/ppermute | solution.py:805
  18.1 10.0 %collective-permute-start.5 = (f32[136,128]{1,0:T(8,128)S(1)}, f32[136,128]{1,0:T(8,128)S(1)}, u32[]{:S(2)}, u32[]{:S(2)}) collective-permute-start(f32[136,128]{1,0:T(8,128)S(1)} %get-tuple-element.85.refs_0_.refs_4_), channel_id=1, source_target_pairs={{0,1},{1,2},{2,3},{3,0},{4,5},{5,6},{6,7},{7,4},{8,9},{9,10},{10,1... | collective-permute-start | bytes 208904 | tf_op jit(solution)/shard_map/ppermute | solution.py:805
  18.6 12.6 %collective-permute-start.4 = (f32[136,128]{1,0:T(8,128)S(1)}, f32[136,128]{1,0:T(8,128)S(1)}, u32[]{:S(2)}, u32[]{:S(2)}) collective-permute-start(f32[136,128]{1,0:T(8,128)S(1)} %get-tuple-element.85.refs_0_.refs_4_), channel_id=1, source_target_pairs={{0,8},{8,0},{1,9},{9,1},{2,10},{10,2},{3,11},{11,3},{4,12},{12,4},... | collective-permute-start | bytes 208904 | tf_op jit(solution)/shard_map/ppermute | solution.py:802
  25.0 6.1 %collective-permute-start.8 = (f32[136,128]{1,0:T(8,128)S(1)}, f32[136,128]{1,0:T(8,128)S(1)}, u32[]{:S(2)}, u32[]{:S(2)}) collective-permute-start(f32[136,128]{1,0:T(8,128)S(1)} %collective-permute-done.7.refs_2_.refs_6_), channel_id=1, source_target_pairs={{0,8},{8,0},{1,9},{9,1},{2,10},{10,2},{3,11},{11,3},{4,12},{12,4},... | collective-permute-start | bytes 208904 | tf_op jit(solution)/shard_map/ppermute | solution.py:802
  27.9 3.3 %collective-permute-start.10 = (f32[136,128]{1,0:T(8,128)S(1)}, f32[136,128]{1,0:T(8,128)S(1)}, u32[]{:S(2)}, u32[]{:S(2)}) collective-permute-start(f32[136,128]{1,0:T(8,128)S(1)} %collective-permute-done.9.refs_3_.refs_7_), channel_id=1, source_target_pairs={{0,8},{8,0},{1,9},{9,1},{2,10},{10,2},{3,11},{11,3},{4,12},{12,4},... | collective-permute-start | bytes 208904 | tf_op jit(solution)/shard_map/ppermute | solution.py:802
  28.1 3.1 %collective-permute-start.6 = (f32[136,128]{1,0:T(8,128)S(1)}, f32[136,128]{1,0:T(8,128)S(1)}, u32[]{:S(2)}, u32[]{:S(2)}) collective-permute-start(f32[136,128]{1,0:T(8,128)S(1)} %collective-permute-done.5.refs_1_.refs_5_), channel_id=1, source_target_pairs={{0,8},{8,0},{1,9},{9,1},{2,10},{10,2},{3,11},{11,3},{4,12},{12,4},... | collective-permute-start | bytes 208904 | tf_op jit(solution)/shard_map/ppermute | solution.py:802
  31.2 33.8 %copy-start = (f32[2048,128]{1,0:T(8,128)S(1)}, f32[2048,128]{1,0:T(8,128)}, u32[]{:S(2)}) copy-start(f32[2048,128]{1,0:T(8,128)} %refs_15_.1) | copy-start | bytes 3145732
  49.0 16.0 %copy-start.2 = (f32[128,128]{1,0:T(8,128)S(1)}, f32[128,128]{1,0:T(8,128)}, u32[]{:S(2)}) copy-start(f32[128,128]{1,0:T(8,128)} %w_charge.3) | copy-start | bytes 196612
  65.8 4.9 %collective-permute-start.11 = (f32[4,128,128]{2,1,0:T(8,128)S(1)}, f32[4,128,128]{2,1,0:T(8,128)S(1)}, u32[]{:S(2)}, u32[]{:S(2)}) collective-permute-start(f32[4,128,128]{2,1,0:T(8,128)S(1)} %get-tuple-element.93), channel_id=1, source_target_pairs={{0,8},{8,0},{1,9},{9,1},{2,10},{10,2},{3,11},{11,3},{4,12},{12,4},... | collective-permute-start | bytes 786440 | tf_op jit(solution)/shard_map/ppermute | solution.py:802
  70.7 3.4 %collective-permute-start.12 = (f32[128,128]{1,0:T(8,128)S(1)}, f32[128,128]{1,0:T(8,128)S(1)}, u32[]{:S(2)}, u32[]{:S(2)}) collective-permute-start(f32[128,128]{1,0:T(8,128)S(1)} %get-tuple-element.95), channel_id=1, source_target_pairs={{0,3},{1,0},{2,1},{3,2},{4,7},{5,4},{6,5},{7,6},{8,11},{9,8},{10,9... | collective-permute-start | bytes 196616 | tf_op jit(solution)/shard_map/ppermute | solution.py:805
  71.7 4.7 %collective-permute-start.13 = (f32[128,128]{1,0:T(8,128)S(1)}, f32[128,128]{1,0:T(8,128)S(1)}, u32[]{:S(2)}, u32[]{:S(2)}) collective-permute-start(f32[128,128]{1,0:T(8,128)S(1)} %get-tuple-element.96), channel_id=1, source_target_pairs={{0,2},{1,3},{2,0},{3,1},{4,6},{5,7},{6,4},{7,5},{8,10},{9,11},{10,... | collective-permute-start | bytes 196616 | tf_op jit(solution)/shard_map/ppermute | solution.py:805
  72.4 5.8 %collective-permute-start.14 = (f32[128,128]{1,0:T(8,128)S(1)}, f32[128,128]{1,0:T(8,128)S(1)}, u32[]{:S(2)}, u32[]{:S(2)}) collective-permute-start(f32[128,128]{1,0:T(8,128)S(1)} %get-tuple-element.97), channel_id=1, source_target_pairs={{0,1},{1,2},{2,3},{3,0},{4,5},{5,6},{6,7},{7,4},{8,9},{9,10},{10,1... | collective-permute-start | bytes 196616 | tf_op jit(solution)/shard_map/ppermute | solution.py:805
  78.4 4.7 %collective-permute-start.15 = (f32[128,128]{1,0:T(8,128)S(1)}, f32[128,128]{1,0:T(8,128)S(1)}, u32[]{:S(2)}, u32[]{:S(2)}) collective-permute-start(f32[128,128]{1,0:T(8,128)S(1)} %get-tuple-element.101.grad.refs_0_.grad_out), channel_id=1, source_target_pairs={{0,2},{1,3},{2,0},{3,1},{4,6},{5,7},{6,4},{7,5},{8,10},{9,11},{10,... | collective-permute-start | bytes 196616 | tf_op jit(solution)/shard_map/ppermute | solution.py:805
  78.9 4.2 %collective-permute-start.20 = (f32[128,128]{1,0:T(8,128)S(1)}, f32[128,128]{1,0:T(8,128)S(1)}, u32[]{:S(2)}, u32[]{:S(2)}) collective-permute-start(f32[128,128]{1,0:T(8,128)S(1)} %get-tuple-element.101.grad.refs_0_.grad_out), channel_id=1, source_target_pairs={{0,3},{1,0},{2,1},{3,2},{4,7},{5,4},{6,5},{7,6},{8,11},{9,8},{10,9... | collective-permute-start | bytes 196616 | tf_op jit(solution)/shard_map/ppermute | solution.py:805
  79.7 6.0 %collective-permute-start.17 = (f32[128,128]{1,0:T(8,128)S(1)}, f32[128,128]{1,0:T(8,128)S(1)}, u32[]{:S(2)}, u32[]{:S(2)}) collective-permute-start(f32[128,128]{1,0:T(8,128)S(1)} %get-tuple-element.101.grad.refs_0_.grad_out), channel_id=1, source_target_pairs={{0,1},{1,2},{2,3},{3,0},{4,5},{5,6},{6,7},{7,4},{8,9},{9,10},{10,1... | collective-permute-start | bytes 196616 | tf_op jit(solution)/shard_map/ppermute | solution.py:805
  80.4 7.6 %collective-permute-start.16 = (f32[128,128]{1,0:T(8,128)S(1)}, f32[128,128]{1,0:T(8,128)S(1)}, u32[]{:S(2)}, u32[]{:S(2)}) collective-permute-start(f32[128,128]{1,0:T(8,128)S(1)} %get-tuple-element.101.grad.refs_0_.grad_out), channel_id=1, source_target_pairs={{0,8},{8,0},{1,9},{9,1},{2,10},{10,2},{3,11},{11,3},{4,12},{12,4},... | collective-permute-start | bytes 196616 | tf_op jit(solution)/shard_map/ppermute | solution.py:802
  83.1 4.9 %collective-permute-start.21 = (f32[128,128]{1,0:T(8,128)S(1)}, f32[128,128]{1,0:T(8,128)S(1)}, u32[]{:S(2)}, u32[]{:S(2)}) collective-permute-start(f32[128,128]{1,0:T(8,128)S(1)} %collective-permute-done.20.refs_3_), channel_id=1, source_target_pairs={{0,8},{8,0},{1,9},{9,1},{2,10},{10,2},{3,11},{11,3},{4,12},{12,4},... | collective-permute-start | bytes 196616 | tf_op jit(solution)/shard_map/ppermute | solution.py:802
  85.7 2.7 %collective-permute-start.18 = (f32[128,128]{1,0:T(8,128)S(1)}, f32[128,128]{1,0:T(8,128)S(1)}, u32[]{:S(2)}, u32[]{:S(2)}) collective-permute-start(f32[128,128]{1,0:T(8,128)S(1)} %collective-permute-done.17.refs_1_), channel_id=1, source_target_pairs={{0,8},{8,0},{1,9},{9,1},{2,10},{10,2},{3,11},{11,3},{4,12},{12,4},... | collective-permute-start | bytes 196616 | tf_op jit(solution)/shard_map/ppermute | solution.py:802
  87.5 1.3 collective-permute-start.19
  121.4 4.9 %collective-permute-start.22 = (f32[4,168,128]{2,1,0:T(8,128)S(1)}, f32[4,168,128]{2,1,0:T(8,128)S(1)}, u32[]{:S(2)}, u32[]{:S(2)}) collective-permute-start(f32[4,168,128]{2,1,0:T(8,128)S(1)} %get-tuple-element.118), channel_id=1, source_target_pairs={{0,8},{8,0},{1,9},{9,1},{2,10},{10,2},{3,11},{11,3},{4,12},{12,4},... | collective-permute-start | bytes 1032200 | tf_op jit(solution)/shard_map/ppermute | solution.py:802
  126.4 3.8 %collective-permute-start.23 = (f32[168,128]{1,0:T(8,128)S(1)}, f32[168,128]{1,0:T(8,128)S(1)}, u32[]{:S(2)}, u32[]{:S(2)}) collective-permute-start(f32[168,128]{1,0:T(8,128)S(1)} %get-tuple-element.120), channel_id=1, source_target_pairs={{0,3},{1,0},{2,1},{3,2},{4,7},{5,4},{6,5},{7,6},{8,11},{9,8},{10,9... | collective-permute-start | bytes 258056 | tf_op jit(solution)/shard_map/ppermute | solution.py:805
  126.5 5.3 %collective-permute-start.24 = (f32[168,128]{1,0:T(8,128)S(1)}, f32[168,128]{1,0:T(8,128)S(1)}, u32[]{:S(2)}, u32[]{:S(2)}) collective-permute-start(f32[168,128]{1,0:T(8,128)S(1)} %get-tuple-element.121), channel_id=1, source_target_pairs={{0,2},{1,3},{2,0},{3,1},{4,6},{5,7},{6,4},{7,5},{8,10},{9,11},{10,... | collective-permute-start | bytes 258056 | tf_op jit(solution)/shard_map/ppermute | solution.py:805
  127.2 7.2 %collective-permute-start.25 = (f32[168,128]{1,0:T(8,128)S(1)}, f32[168,128]{1,0:T(8,128)S(1)}, u32[]{:S(2)}, u32[]{:S(2)}) collective-permute-start(f32[168,128]{1,0:T(8,128)S(1)} %get-tuple-element.122), channel_id=1, source_target_pairs={{0,1},{1,2},{2,3},{3,0},{4,5},{5,6},{6,7},{7,4},{8,9},{9,10},{10,1... | collective-permute-start | bytes 258056 | tf_op jit(solution)/shard_map/ppermute | solution.py:805
  137.4 14.4 %all-to-all-start.4 = ((f32[8,56,128]{2,1,0:T(8,128)}), f32[8,56,128]{2,1,0:T(8,128)S(1)}, u32[]{:S(2)}, u32[]{:S(2)}) async-start(f32[8,56,128]{2,1,0:T(8,128)} %get-tuple-element.129), calls=%async_computation.4 | async-start | bytes 458752 | tf_op jit(solution)/shard_map/all_to_all | solution.py:880
  140.8 4.7 %collective-permute-start.27 = (f32[256,128]{1,0:T(8,128)S(1)}, f32[256,128]{1,0:T(8,128)S(1)}, u32[]{:S(2)}, u32[]{:S(2)}) collective-permute-start(f32[256,128]{1,0:T(8,128)S(1)} %get-tuple-element.140), channel_id=1, source_target_pairs={{0,1},{1,0},{2,3},{3,2},{4,5},{5,4},{6,7},{7,6},{8,9},{9,8},{10,11... | collective-permute-start | bytes 393224 | tf_op jit(solution)/shard_map/ppermute | solution.py:870
  145.5 11.8 %collective-permute-start.28 = (f32[512,128]{1,0:T(8,128)S(1)}, f32[512,128]{1,0:T(8,128)S(1)}, u32[]{:S(2)}, u32[]{:S(2)}) collective-permute-start(f32[512,128]{1,0:T(8,128)S(1)} %constant_dynamic-update-slice_fusion.refs_0_), channel_id=1, source_target_pairs={{0,2},{1,3},{2,0},{3,1},{4,6},{5,7},{6,4},{7,5},{8,10},{9,11},{10,... | collective-permute-start | bytes 786440 | tf_op jit(solution)/shard_map/ppermute | solution.py:879
  152.6 13.3 %all-to-all-start.5 = ((f32[16,56,128]{2,1,0:T(8,128)}), f32[16,56,128]{2,1,0:T(8,128)S(1)}, u32[]{:S(2)}, u32[]{:S(2)}) async-start(f32[16,56,128]{2,1,0:T(8,128)} %shard_map.197), calls=%async_computation.5 | async-start | bytes 917504 | tf_op jit(solution)/shard_map/all_to_all | solution.py:882
  156.1 11.8 %collective-permute-start.29 = (f32[512,128]{1,0:T(8,128)S(1)}, f32[512,128]{1,0:T(8,128)S(1)}, u32[]{:S(2)}, u32[]{:S(2)}) collective-permute-start(f32[512,128]{1,0:T(8,128)S(1)} %constant_dynamic-update-slice_fusion.refs_0_), channel_id=1, source_target_pairs={{0,8},{8,0},{1,9},{9,1},{2,10},{10,2},{3,11},{11,3},{4,12},{12,4},... | collective-permute-start | bytes 786440 | tf_op jit(solution)/shard_map/ppermute | solution.py:802
  157.3 10.7 %collective-permute-start.30 = (f32[512,128]{1,0:T(8,128)S(1)}, f32[512,128]{1,0:T(8,128)S(1)}, u32[]{:S(2)}, u32[]{:S(2)}) collective-permute-start(f32[512,128]{1,0:T(8,128)S(1)} %collective-permute-done.28.refs_1_), channel_id=1, source_target_pairs={{0,8},{8,0},{1,9},{9,1},{2,10},{10,2},{3,11},{11,3},{4,12},{12,4},... | collective-permute-start | bytes 786440 | tf_op jit(solution)/shard_map/ppermute | solution.py:802
  165.9 3.1 %collective-permute-start.26 = (f32[160,128]{1,0:T(8,128)S(1)}, f32[160,128]{1,0:T(8,128)S(1)}, u32[]{:S(2)}, u32[]{:S(2)}) collective-permute-start(f32[160,128]{1,0:T(8,128)S(1)} %get-tuple-element.131.own), channel_id=1, source_target_pairs={{0,8},{8,0},{1,9},{9,1},{2,10},{10,2},{3,11},{11,3},{4,12},{12,4},... | collective-permute-start | bytes 245768 | tf_op jit(solution)/shard_map/ppermute | solution.py:802

commit v8 on v7

--- a/solution.py
+++ b/solution.py
@@ -150,7 +150,7 @@
     ]
     for copy in copies:
         copy.start()
-    for copy in copies:
+    for copy in copies[:4]:
         copy.wait()
     even = lax.axis_index("x") % 2 == 0
     rows = [pos[0:1, :], pos[1:2, :], pos[2:3, :], species[...].astype(jnp.float32)]
@@ -182,6 +182,8 @@
     near[4:8, :] = zero
     far[4:8, :] = zero
     own[4:8, :] = zero
+    for copy in copies[4:]:
+        copy.wait()
 
 
 def swapped(value, axes, odd):
@@ -742,7 +744,7 @@
     for member in range(MEMBERS):
         number = member % 4
         out = (mine, other)[member // 4].at[number]
-        place = jnp.where(core == member // 4, 0, 4) + (column + 4 - number) % 4
+        place = jnp.where(core == member // 4, 0, 4) + (column ^ number)
         piece = pl.ds(pl.multiple_of(place * 16, 16), 16)
         if member < 4:
             out[N : N + 8, :] = jnp.zeros((8, N), jnp.float32)
@@ -802,7 +804,7 @@
         return lax.ppermute(value, "c", swap)
 
     def step_x(value, step):
-        return lax.ppermute(value, "x", [(at, (at + step) % 4) for at in range(4)])
+        return lax.ppermute(value, "x", [(at, at ^ step) for at in range(4)])
 
     def gather(value, beside=()):
         one, two, three = (step_x(value, step) for step in (1, 2, 3))
@@ -813,7 +815,7 @@
     def scatter(kernel, parts, other):
         shape = f32(*other.shape[1:])
         tiles = call(kernel, (shape,) * 4, *parts, other_core(other))
-        return [tiles[0]] + [step_x(tiles[step], -step) for step in (1, 2, 3)]
+        return [tiles[0]] + [step_x(tiles[step], step) for step in (1, 2, 3)]
 
     shared, _ = gather(shared)
     half = jax.ShapeDtypeStruct((2 * SHARD, 4 * N), jnp.bfloat16)

time: 170 us -> 169 us (level)
  waiting for transfers between devices: 35.4 us -> 26.3 us
  starting transfers between devices: 54.4 us -> 62.6 us
    ppermute x12, starting transfers between devices: 8.48 us -> 13.8 us  [step_x(): return lax.ppermute(value, 'x', [(at, at ^ step) for at in range(4)])]
    ppermute x12, waiting for transfers between devices: 11.5 us -> 8.22 us  [step_x(): return lax.ppermute(value, 'x', [(at, at ^ step) for at in range(4)])]
    all_to_all x1, waiting for transfers between devices: 6.2 us -> 3.42 us  [body(): payload = lax.all_to_all(payload, DEPTH, 0, 0)]
    all_to_all x1, waiting for transfers between devices: 8.45 us -> 5.92 us  [body(): payload = lax.all_to_all(payload, PLANE, 0, 0)]
    ppermute x1, starting transfers between devices: 0.09 us -> 1.98 us  [body(): lax.ppermute(near_shards, 'x', [(at, at ^ 2) for at in range(4)])]
  transfers between devices with their start and end apart: 33 -> 33, of which waited for: 15 -> 13; matrix products, arithmetic and copies ran while one was open for 0% -> 0% of each run, Pallas kernels for 3% -> 3%
where the time goes in v8:
time: 169 us
  starting transfers between devices  62.6 us (37%)
  blocking collectives  62.5 us (37%)
  waiting for transfers between devices  26.3 us (16%)
  Pallas kernels  16.6 us (10%)
    all_to_all x2, blocking collectives, cross_sum(): return lax.all_to_all(tiles, CROSS, 0, 0).reshape(2 * SHARD, N)  32.3 us
    all_to_all x2, blocking collectives, cross_sum(): tiles = lax.all_to_all(tiles, CROSS, 0, 0)  30.1 us
    ppermute x13, starting transfers between devices, other_core(): return lax.ppermute(value, 'c', swap)  28.5 us
    pallas_call x22, Pallas kernels, call(): pl.pallas_call(kernel, out_shape=out_shape, scratch_shapes=list(scratch),...  16.6 us
    ppermute x12, starting transfers between devices, step_x(): return lax.ppermute(value, 'x', [(at, at ^ step) for at in range(4)])  13.8 us
    ppermute x4, starting transfers between devices, swapped(): return lax.ppermute(value, axes, places)  10.4 us
    ppermute x12, waiting for transfers between devices, step_x(): return lax.ppermute(value, 'x', [(at, at ^ step) for at in range(4)])  8.22 us
    all_to_all x1, waiting for transfers between devices, body(): payload = lax.all_to_all(payload, PLANE, 0, 0)  5.92 us
  transfers between devices with their start and end apart: 33, of which 13 were waited for; matrix products, arithmetic and copies ran while one was open for 0% of the time, Pallas kernels for 3%

profile of v8, /device:TPU:1, one launch (start us, length us, event | category | flops | bytes accessed | tf_op | source)
XLA Modules:
  0.0 168.8 jit_solution(3136116111742505524)
XLA Ops:
  0.6 1.0 shard_map.179
  1.6 2.1 %collective-permute-start = (f32[8,128]{1,0:T(8,128)S(1)}, f32[8,128]{1,0:T(8,128)S(1)}, u32[]{:S(2)}, u32[]{:S(2)}) collective-permute-start(f32[8,128]{1,0:T(8,128)S(1)} %get-tuple-element.79), channel_id=1, source_target_pairs={{0,1},{1,0},{2,3},{3,2},{4,5},{5,4},{6,7},{7,6},{8,9},{9,8},{10,11... | collective-permute-start | bytes 12296 | tf_op jit(solution)/shard_map/ppermute | solution.py:192
  3.8 3.2 %collective-permute-start.1 = (f32[8,128]{1,0:T(8,128)S(1)}, f32[8,128]{1,0:T(8,128)S(1)}, u32[]{:S(2)}, u32[]{:S(2)}) collective-permute-start(f32[8,128]{1,0:T(8,128)S(1)} %get-tuple-element.80), channel_id=1, source_target_pairs={{0,7},{1,2},{2,1},{3,4},{4,3},{5,6},{6,5},{7,0},{8,15},{9,10},{10,... | collective-permute-start | bytes 12296 | tf_op jit(solution)/shard_map/ppermute | solution.py:192
  6.9 1.4 collective-permute-done.1.far.far_y
  8.4 2.5 %collective-permute-start.2 = (f32[8,128]{1,0:T(8,128)S(1)}, f32[8,128]{1,0:T(8,128)S(1)}, u32[]{:S(2)}, u32[]{:S(2)}) collective-permute-start(f32[8,128]{1,0:T(8,128)S(1)} %get-tuple-element.81), channel_id=1, source_target_pairs={{0,8},{8,0},{16,24},{24,16},{32,40},{40,32},{48,56},{56,48},{64,72... | collective-permute-start | bytes 12296 | tf_op jit(solution)/shard_map/ppermute | solution.py:192
  10.9 2.6 %collective-permute-start.3 = (f32[8,128]{1,0:T(8,128)S(1)}, f32[8,128]{1,0:T(8,128)S(1)}, u32[]{:S(2)}, u32[]{:S(2)}) collective-permute-start(f32[8,128]{1,0:T(8,128)S(1)} %get-tuple-element.82), channel_id=1, source_target_pairs={{0,248},{8,16},{16,8},{24,32},{32,24},{40,48},{48,40},{56,64},{64,... | collective-permute-start | bytes 12296 | tf_op jit(solution)/shard_map/ppermute | solution.py:192
  13.5 1.3 collective-permute-done.3.far_x
  14.8 1.2 shard_map.181
  16.0 0.4 collective-permute-start.7
  16.4 1.6 collective-permute-start.9
  18.0 0.7 collective-permute-start.5
  18.7 6.8 %collective-permute-start.4 = (f32[136,128]{1,0:T(8,128)S(1)}, f32[136,128]{1,0:T(8,128)S(1)}, u32[]{:S(2)}, u32[]{:S(2)}) collective-permute-start(f32[136,128]{1,0:T(8,128)S(1)} %get-tuple-element.85.refs_0_.refs_4_), channel_id=1, source_target_pairs={{0,8},{8,0},{1,9},{9,1},{2,10},{10,2},{3,11},{11,3},{4,12},{12,4},... | collective-permute-start | bytes 208904 | tf_op jit(solution)/shard_map/ppermute | solution.py:804
  25.5 2.4 %collective-permute-start.8 = (f32[136,128]{1,0:T(8,128)S(1)}, f32[136,128]{1,0:T(8,128)S(1)}, u32[]{:S(2)}, u32[]{:S(2)}) collective-permute-start(f32[136,128]{1,0:T(8,128)S(1)} %collective-permute-done.7.refs_2_.refs_6_), channel_id=1, source_target_pairs={{0,8},{8,0},{1,9},{9,1},{2,10},{10,2},{3,11},{11,3},{4,12},{12,4},... | collective-permute-start | bytes 208904 | tf_op jit(solution)/shard_map/ppermute | solution.py:804
  27.9 0.7 collective-permute-start.10
  28.6 1.4 shard_map.182
  30.0 1.4 shard_map.183
  31.4 16.0 %all_to_all.30.tiles = f32[32,16,128]{2,1,0:T(8,128)S(1)} all-to-all(f32[32,16,128]{2,1,0:T(8,128)S(1)} %get-tuple-element.87), channel_id=1, replica_groups=mesh['y'=4,'zh'=4,'c'=2,'zl'=2,'x'=4] {'y','zh','zl'}, dimensions={0} | all-to-all | bytes 524288 | tf_op jit(solution)/shard_map/all_to_all | solution.py:836
  47.5 16.3 %all_to_all.31 = f32[32,16,128]{2,1,0:T(8,128)S(1)} all-to-all(f32[32,16,128]{2,1,0:T(8,128)S(1)} %shard_map.184), channel_id=1, replica_groups=mesh['y'=4,'zh'=4,'c'=2,'zl'=2,'x'=4] {'y','zh','zl'}, dimensions={0} | all-to-all | bytes 524288 | tf_op jit(solution)/shard_map/all_to_all | solution.py:838
  63.8 0.8 shard_map.185
  64.6 3.7 %collective-permute-start.11 = (f32[4,128,128]{2,1,0:T(8,128)S(1)}, f32[4,128,128]{2,1,0:T(8,128)S(1)}, u32[]{:S(2)}, u32[]{:S(2)}) collective-permute-start(f32[4,128,128]{2,1,0:T(8,128)S(1)} %get-tuple-element.93), channel_id=1, source_target_pairs={{0,8},{8,0},{1,9},{9,1},{2,10},{10,2},{3,11},{11,3},{4,12},{12,4},... | collective-permute-start | bytes 786440 | tf_op jit(solution)/shard_map/ppermute | solution.py:804
  68.3 0.4 shard_map.186.mine
  68.7 0.8 collective-permute-done.11.other
  69.5 1.0 collective-permute-start.12
  70.5 2.1 %collective-permute-start.13 = (f32[128,128]{1,0:T(8,128)S(1)}, f32[128,128]{1,0:T(8,128)S(1)}, u32[]{:S(2)}, u32[]{:S(2)}) collective-permute-start(f32[128,128]{1,0:T(8,128)S(1)} %get-tuple-element.96), channel_id=1, source_target_pairs={{0,2},{1,3},{2,0},{3,1},{4,6},{5,7},{6,4},{7,5},{8,10},{9,11},{10,... | collective-permute-start | bytes 196616 | tf_op jit(solution)/shard_map/ppermute | solution.py:807
  72.6 0.9 collective-permute-start.14
  73.4 2.7 %collective-permute-done.13.tile_2 = f32[128,128]{1,0:T(8,128)S(1)} collective-permute-done((f32[128,128]{1,0:T(8,128)S(1)}, f32[128,128]{1,0:T(8,128)S(1)}, u32[]{:S(2)}, u32[]{:S(2)}) %collective-permute-start.13) | collective-permute-done | bytes 65568 | tf_op jit(solution)/shard_map/ppermute | solution.py:807
  76.1 1.1 collective-permute-done.14.tile_3
  77.2 0.1 shard_map.188
  77.3 0.3 collective-permute-start.15
  77.6 2.9 %collective-permute-start.20 = (f32[128,128]{1,0:T(8,128)S(1)}, f32[128,128]{1,0:T(8,128)S(1)}, u32[]{:S(2)}, u32[]{:S(2)}) collective-permute-start(f32[128,128]{1,0:T(8,128)S(1)} %get-tuple-element.101.grad.refs_0_.grad_out), channel_id=1, source_target_pairs={{0,3},{1,2},{2,1},{3,0},{4,7},{5,6},{6,5},{7,4},{8,11},{9,10},{10,... | collective-permute-start | bytes 196616 | tf_op jit(solution)/shard_map/ppermute | solution.py:807
  80.5 2.2 %collective-permute-start.16 = (f32[128,128]{1,0:T(8,128)S(1)}, f32[128,128]{1,0:T(8,128)S(1)}, u32[]{:S(2)}, u32[]{:S(2)}) collective-permute-start(f32[128,128]{1,0:T(8,128)S(1)} %get-tuple-element.101.grad.refs_0_.grad_out), channel_id=1, source_target_pairs={{0,8},{8,0},{1,9},{9,1},{2,10},{10,2},{3,11},{11,3},{4,12},{12,4},... | collective-permute-start | bytes 196616 | tf_op jit(solution)/shard_map/ppermute | solution.py:804
  82.7 0.7 shard_map.189
  83.4 2.3 %collective-permute-start.21 = (f32[128,128]{1,0:T(8,128)S(1)}, f32[128,128]{1,0:T(8,128)S(1)}, u32[]{:S(2)}, u32[]{:S(2)}) collective-permute-start(f32[128,128]{1,0:T(8,128)S(1)} %collective-permute-done.20.refs_3_), channel_id=1, source_target_pairs={{0,8},{8,0},{1,9},{9,1},{2,10},{10,2},{3,11},{11,3},{4,12},{12,4},... | collective-permute-start | bytes 196616 | tf_op jit(solution)/shard_map/ppermute | solution.py:804
  85.7 0.4 collective-permute-start.18
  86.1 0.1 collective-permute-start.19
  86.2 0.4 shard_map.190.refs_6_
  86.7 0.3 collective-permute-done.18.refs_1_
  87.0 0.4 collective-permute-done.19.refs_2_
  87.3 0.4 shard_map.191
  87.8 14.1 %all_to_all.32.tiles = f32[32,16,128]{2,1,0:T(8,128)S(1)} all-to-all(f32[32,16,128]{2,1,0:T(8,128)S(1)} %shard_map.191), channel_id=1, replica_groups=mesh['y'=4,'zh'=4,'c'=2,'zl'=2,'x'=4] {'y','zh','zl'}, dimensions={0} | all-to-all | bytes 524288 | tf_op jit(solution)/shard_map/all_to_all | solution.py:836
  101.9 16.0 %all_to_all.33 = f32[32,16,128]{2,1,0:T(8,128)S(1)} all-to-all(f32[32,16,128]{2,1,0:T(8,128)S(1)} %shard_map.192), channel_id=1, replica_groups=mesh['y'=4,'zh'=4,'c'=2,'zl'=2,'x'=4] {'y','zh','zl'}, dimensions={0} | all-to-all | bytes 524288 | tf_op jit(solution)/shard_map/all_to_all | solution.py:838
  117.9 2.0 %shard_map.193 = (f32[4,168,128]{2,1,0:T(8,128)S(1)}, f32[4,168,128]{2,1,0:T(8,128)S(1)}, bf16[512,256]{1,0:T(8,128)(2,1)S(1)}, bf16[512,256]{1,0:T(8,128)(2,1)S(1)}) custom-call(f32[128,128]{1,0:T(8,128)S(1)} %collective-permute-done.16.refs_0_, f32[128,128]{1,0:T(8,128)S(1)} %collective-permute-done.18.refs_1_, ...), custom_call_target="tpu_custom_call" | custom-call | tf_op jit(solution)/shard_map/pallas_call | solution.py:111
  119.9 3.6 %collective-permute-start.22 = (f32[4,168,128]{2,1,0:T(8,128)S(1)}, f32[4,168,128]{2,1,0:T(8,128)S(1)}, u32[]{:S(2)}, u32[]{:S(2)}) collective-permute-start(f32[4,168,128]{2,1,0:T(8,128)S(1)} %get-tuple-element.118), channel_id=1, source_target_pairs={{0,8},{8,0},{1,9},{9,1},{2,10},{10,2},{3,11},{11,3},{4,12},{12,4},... | collective-permute-start | bytes 1032200 | tf_op jit(solution)/shard_map/ppermute | solution.py:804
  123.5 0.8 shard_map.194
  124.4 0.4 collective-permute-done.22.other
  124.9 0.8 collective-permute-start.23
  125.7 1.3 collective-permute-start.24
  127.0 1.8 %collective-permute-start.25 = (f32[168,128]{1,0:T(8,128)S(1)}, f32[168,128]{1,0:T(8,128)S(1)}, u32[]{:S(2)}, u32[]{:S(2)}) collective-permute-start(f32[168,128]{1,0:T(8,128)S(1)} %get-tuple-element.122), channel_id=1, source_target_pairs={{0,3},{1,2},{2,1},{3,0},{4,7},{5,6},{6,5},{7,4},{8,11},{9,10},{10,... | collective-permute-start | bytes 258056 | tf_op jit(solution)/shard_map/ppermute | solution.py:807
  128.8 1.9 %collective-permute-done.24.tile_2 = f32[168,128]{1,0:T(8,128)S(1)} collective-permute-done((f32[168,128]{1,0:T(8,128)S(1)}, f32[168,128]{1,0:T(8,128)S(1)}, u32[]{:S(2)}, u32[]{:S(2)}) %collective-permute-start.24) | collective-permute-done | bytes 86048 | tf_op jit(solution)/shard_map/ppermute | solution.py:807
  130.7 2.6 %collective-permute-done.25.tile_3 = f32[168,128]{1,0:T(8,128)S(1)} collective-permute-done((f32[168,128]{1,0:T(8,128)S(1)}, f32[168,128]{1,0:T(8,128)S(1)}, u32[]{:S(2)}, u32[]{:S(2)}) %collective-permute-start.25) | collective-permute-done | bytes 86048 | tf_op jit(solution)/shard_map/ppermute | solution.py:807
  133.3 3.0 %shard_map.196 = (f32[8,56,128]{2,1,0:T(8,128)}, f32[8,128]{1,0:T(8,128)S(1)}, f32[16,128]{1,0:T(8,128)S(1)}) custom-call(f32[168,128]{1,0:T(8,128)S(1)} %get-tuple-element.119.tile_0, f32[168,128]{1,0:T(8,128)S(1)} %collective-permute-done.23.tile_1, f32[168,128]{1,0:T(8,128)S(1)} %collective-permute-done.24.tile_2, ...), custom_call_target="tpu_custom_call" | custom-call | flops 1000000000 | bytes 10000000 | tf_op jit(solution)/shard_map/pallas_call | solution.py:111
  136.3 3.4 %all-to-all-start.4 = ((f32[8,56,128]{2,1,0:T(8,128)}), f32[8,56,128]{2,1,0:T(8,128)S(1)}, u32[]{:S(2)}, u32[]{:S(2)}) async-start(f32[8,56,128]{2,1,0:T(8,128)} %get-tuple-element.129), calls=%async_computation.4 | async-start | bytes 458752 | tf_op jit(solution)/shard_map/all_to_all | solution.py:882
  139.7 0.1 collective-permute-start.27
  139.8 4.1 %collective-permute-done.27 = f32[256,128]{1,0:T(8,128)S(1)} collective-permute-done((f32[256,128]{1,0:T(8,128)S(1)}, f32[256,128]{1,0:T(8,128)S(1)}, u32[]{:S(2)}, u32[]{:S(2)}) %collective-permute-start.27) | collective-permute-done | bytes 131104 | tf_op jit(solution)/shard_map/ppermute | solution.py:872
  144.0 2.0 %collective-permute-start.28 = (f32[512,128]{1,0:T(8,128)S(1)}, f32[512,128]{1,0:T(8,128)S(1)}, u32[]{:S(2)}, u32[]{:S(2)}) collective-permute-start(f32[512,128]{1,0:T(8,128)S(1)} %constant_dynamic-update-slice_fusion.refs_0_), channel_id=1, source_target_pairs={{0,2},{1,3},{2,0},{3,1},{4,6},{5,7},{6,4},{7,5},{8,10},{9,11},{10,... | collective-permute-start | bytes 786440 | tf_op jit(solution)/shard_map/ppermute | solution.py:881
  146.0 3.4 %all-to-all-done.4.tiles = f32[8,56,128]{2,1,0:T(8,128)S(1)} async-done(((f32[8,56,128]{2,1,0:T(8,128)}), f32[8,56,128]{2,1,0:T(8,128)S(1)}, u32[]{:S(2)}, u32[]{:S(2)}) %all-to-all-start.4) | async-done | bytes 229408 | tf_op jit(solution)/shard_map/all_to_all | solution.py:882
  149.4 0.8 shard_map.197
  150.2 4.3 %all-to-all-start.5 = ((f32[16,56,128]{2,1,0:T(8,128)}), f32[16,56,128]{2,1,0:T(8,128)S(1)}, u32[]{:S(2)}, u32[]{:S(2)}) async-start(f32[16,56,128]{2,1,0:T(8,128)} %shard_map.197), calls=%async_computation.5 | async-start | bytes 917504 | tf_op jit(solution)/shard_map/all_to_all | solution.py:884
  154.5 2.6 %collective-permute-start.29 = (f32[512,128]{1,0:T(8,128)S(1)}, f32[512,128]{1,0:T(8,128)S(1)}, u32[]{:S(2)}, u32[]{:S(2)}) collective-permute-start(f32[512,128]{1,0:T(8,128)S(1)} %constant_dynamic-update-slice_fusion.refs_0_), channel_id=1, source_target_pairs={{0,8},{8,0},{1,9},{9,1},{2,10},{10,2},{3,11},{11,3},{4,12},{12,4},... | collective-permute-start | bytes 786440 | tf_op jit(solution)/shard_map/ppermute | solution.py:804
  157.1 0.1 collective-permute-start.30
  157.2 5.9 %all-to-all-done.5.tiles = f32[16,56,128]{2,1,0:T(8,128)S(1)} async-done(((f32[16,56,128]{2,1,0:T(8,128)}), f32[16,56,128]{2,1,0:T(8,128)S(1)}, u32[]{:S(2)}, u32[]{:S(2)}) %all-to-all-start.5) | async-done | bytes 458784 | tf_op jit(solution)/shard_map/all_to_all | solution.py:884
  163.2 3.7 %collective-permute-start.26 = (f32[160,128]{1,0:T(8,128)S(1)}, f32[160,128]{1,0:T(8,128)S(1)}, u32[]{:S(2)}, u32[]{:S(2)}) collective-permute-start(f32[160,128]{1,0:T(8,128)S(1)} %get-tuple-element.131.own), channel_id=1, source_target_pairs={{0,8},{8,0},{1,9},{9,1},{2,10},{10,2},{3,11},{11,3},{4,12},{12,4},... | collective-permute-start | bytes 245768 | tf_op jit(solution)/shard_map/ppermute | solution.py:804
  166.9 1.1 shard_map.200
  168.0 0.9 shard_map.199
  (38 shorter events, 0.4 us)
Async XLA Ops:
  0.6 27.9 %copy-start.3 = (f32[128,128]{1,0:T(8,128)S(1)}, f32[128,128]{1,0:T(8,128)}, u32[]{:S(2)}) copy-start(f32[128,128]{1,0:T(8,128)} %w_up.1) | copy-start | bytes 196612
  1.6 5.3 %collective-permute-start = (f32[8,128]{1,0:T(8,128)S(1)}, f32[8,128]{1,0:T(8,128)S(1)}, u32[]{:S(2)}, u32[]{:S(2)}) collective-permute-start(f32[8,128]{1,0:T(8,128)S(1)} %get-tuple-element.79), channel_id=1, source_target_pairs={{0,1},{1,0},{2,3},{3,2},{4,5},{5,4},{6,7},{7,6},{8,9},{9,8},{10,11... | collective-permute-start | bytes 12296 | tf_op jit(solution)/shard_map/ppermute | solution.py:192
  3.8 4.6 %collective-permute-start.1 = (f32[8,128]{1,0:T(8,128)S(1)}, f32[8,128]{1,0:T(8,128)S(1)}, u32[]{:S(2)}, u32[]{:S(2)}) collective-permute-start(f32[8,128]{1,0:T(8,128)S(1)} %get-tuple-element.80), channel_id=1, source_target_pairs={{0,7},{1,2},{2,1},{3,4},{4,3},{5,6},{6,5},{7,0},{8,15},{9,10},{10,... | collective-permute-start | bytes 12296 | tf_op jit(solution)/shard_map/ppermute | solution.py:192
  8.4 5.1 %collective-permute-start.2 = (f32[8,128]{1,0:T(8,128)S(1)}, f32[8,128]{1,0:T(8,128)S(1)}, u32[]{:S(2)}, u32[]{:S(2)}) collective-permute-start(f32[8,128]{1,0:T(8,128)S(1)} %get-tuple-element.81), channel_id=1, source_target_pairs={{0,8},{8,0},{16,24},{24,16},{32,40},{40,32},{48,56},{56,48},{64,72... | collective-permute-start | bytes 12296 | tf_op jit(solution)/shard_map/ppermute | solution.py:192
  10.9 3.9 %collective-permute-start.3 = (f32[8,128]{1,0:T(8,128)S(1)}, f32[8,128]{1,0:T(8,128)S(1)}, u32[]{:S(2)}, u32[]{:S(2)}) collective-permute-start(f32[8,128]{1,0:T(8,128)S(1)} %get-tuple-element.82), channel_id=1, source_target_pairs={{0,248},{8,16},{16,8},{24,32},{32,24},{40,48},{48,40},{56,64},{64,... | collective-permute-start | bytes 12296 | tf_op jit(solution)/shard_map/ppermute | solution.py:192
  14.8 13.7 %copy-start.1 = (f32[3,2048]{1,0:T(4,128)S(1)}, f32[3,2048]{1,0:T(4,128)}, u32[]{:S(2)}) copy-start(f32[3,2048]{1,0:T(4,128)} %refs_8_.1) | copy-start | bytes 73732
  16.0 9.5 %collective-permute-start.7 = (f32[136,128]{1,0:T(8,128)S(1)}, f32[136,128]{1,0:T(8,128)S(1)}, u32[]{:S(2)}, u32[]{:S(2)}) collective-permute-start(f32[136,128]{1,0:T(8,128)S(1)} %get-tuple-element.85.refs_0_.refs_4_), channel_id=1, source_target_pairs={{0,2},{1,3},{2,0},{3,1},{4,6},{5,7},{6,4},{7,5},{8,10},{9,11},{10,... | collective-permute-start | bytes 208904 | tf_op jit(solution)/shard_map/ppermute | solution.py:807
  16.4 11.4 %collective-permute-start.9 = (f32[136,128]{1,0:T(8,128)S(1)}, f32[136,128]{1,0:T(8,128)S(1)}, u32[]{:S(2)}, u32[]{:S(2)}) collective-permute-start(f32[136,128]{1,0:T(8,128)S(1)} %get-tuple-element.85.refs_0_.refs_4_), channel_id=1, source_target_pairs={{0,3},{1,2},{2,1},{3,0},{4,7},{5,6},{6,5},{7,4},{8,11},{9,10},{10,... | collective-permute-start | bytes 208904 | tf_op jit(solution)/shard_map/ppermute | solution.py:807
  18.0 10.5 %collective-permute-start.5 = (f32[136,128]{1,0:T(8,128)S(1)}, f32[136,128]{1,0:T(8,128)S(1)}, u32[]{:S(2)}, u32[]{:S(2)}) collective-permute-start(f32[136,128]{1,0:T(8,128)S(1)} %get-tuple-element.85.refs_0_.refs_4_), channel_id=1, source_target_pairs={{0,1},{1,0},{2,3},{3,2},{4,5},{5,4},{6,7},{7,6},{8,9},{9,8},{10,11... | collective-permute-start | bytes 208904 | tf_op jit(solution)/shard_map/ppermute | solution.py:807
  18.7 11.2 %collective-permute-start.4 = (f32[136,128]{1,0:T(8,128)S(1)}, f32[136,128]{1,0:T(8,128)S(1)}, u32[]{:S(2)}, u32[]{:S(2)}) collective-permute-start(f32[136,128]{1,0:T(8,128)S(1)} %get-tuple-element.85.refs_0_.refs_4_), channel_id=1, source_target_pairs={{0,8},{8,0},{1,9},{9,1},{2,10},{10,2},{3,11},{11,3},{4,12},{12,4},... | collective-permute-start | bytes 208904 | tf_op jit(solution)/shard_map/ppermute | solution.py:804
  25.5 4.5 %collective-permute-start.8 = (f32[136,128]{1,0:T(8,128)S(1)}, f32[136,128]{1,0:T(8,128)S(1)}, u32[]{:S(2)}, u32[]{:S(2)}) collective-permute-start(f32[136,128]{1,0:T(8,128)S(1)} %collective-permute-done.7.refs_2_.refs_6_), channel_id=1, source_target_pairs={{0,8},{8,0},{1,9},{9,1},{2,10},{10,2},{3,11},{11,3},{4,12},{12,4},... | collective-permute-start | bytes 208904 | tf_op jit(solution)/shard_map/ppermute | solution.py:804
  27.9 2.1 %collective-permute-start.10 = (f32[136,128]{1,0:T(8,128)S(1)}, f32[136,128]{1,0:T(8,128)S(1)}, u32[]{:S(2)}, u32[]{:S(2)}) collective-permute-start(f32[136,128]{1,0:T(8,128)S(1)} %collective-permute-done.9.refs_3_.refs_7_), channel_id=1, source_target_pairs={{0,8},{8,0},{1,9},{9,1},{2,10},{10,2},{3,11},{11,3},{4,12},{12,4},... | collective-permute-start | bytes 208904 | tf_op jit(solution)/shard_map/ppermute | solution.py:804
  28.6 1.4 collective-permute-start.6
  30.0 33.8 %copy-start = (f32[2048,128]{1,0:T(8,128)S(1)}, f32[2048,128]{1,0:T(8,128)}, u32[]{:S(2)}) copy-start(f32[2048,128]{1,0:T(8,128)} %refs_15_.1) | copy-start | bytes 3145732
  47.5 16.4 %copy-start.2 = (f32[128,128]{1,0:T(8,128)S(1)}, f32[128,128]{1,0:T(8,128)}, u32[]{:S(2)}) copy-start(f32[128,128]{1,0:T(8,128)} %w_charge.3) | copy-start | bytes 196612
  64.6 4.8 %collective-permute-start.11 = (f32[4,128,128]{2,1,0:T(8,128)S(1)}, f32[4,128,128]{2,1,0:T(8,128)S(1)}, u32[]{:S(2)}, u32[]{:S(2)}) collective-permute-start(f32[4,128,128]{2,1,0:T(8,128)S(1)} %get-tuple-element.93), channel_id=1, source_target_pairs={{0,8},{8,0},{1,9},{9,1},{2,10},{10,2},{3,11},{11,3},{4,12},{12,4},... | collective-permute-start | bytes 786440 | tf_op jit(solution)/shard_map/ppermute | solution.py:804
  69.5 4.0 %collective-permute-start.12 = (f32[128,128]{1,0:T(8,128)S(1)}, f32[128,128]{1,0:T(8,128)S(1)}, u32[]{:S(2)}, u32[]{:S(2)}) collective-permute-start(f32[128,128]{1,0:T(8,128)S(1)} %get-tuple-element.95), channel_id=1, source_target_pairs={{0,1},{1,0},{2,3},{3,2},{4,5},{5,4},{6,7},{7,6},{8,9},{9,8},{10,11... | collective-permute-start | bytes 196616 | tf_op jit(solution)/shard_map/ppermute | solution.py:807
  70.5 5.6 %collective-permute-start.13 = (f32[128,128]{1,0:T(8,128)S(1)}, f32[128,128]{1,0:T(8,128)S(1)}, u32[]{:S(2)}, u32[]{:S(2)}) collective-permute-start(f32[128,128]{1,0:T(8,128)S(1)} %get-tuple-element.96), channel_id=1, source_target_pairs={{0,2},{1,3},{2,0},{3,1},{4,6},{5,7},{6,4},{7,5},{8,10},{9,11},{10,... | collective-permute-start | bytes 196616 | tf_op jit(solution)/shard_map/ppermute | solution.py:807
  72.6 4.6 %collective-permute-start.14 = (f32[128,128]{1,0:T(8,128)S(1)}, f32[128,128]{1,0:T(8,128)S(1)}, u32[]{:S(2)}, u32[]{:S(2)}) collective-permute-start(f32[128,128]{1,0:T(8,128)S(1)} %get-tuple-element.97), channel_id=1, source_target_pairs={{0,3},{1,2},{2,1},{3,0},{4,7},{5,6},{6,5},{7,4},{8,11},{9,10},{10,... | collective-permute-start | bytes 196616 | tf_op jit(solution)/shard_map/ppermute | solution.py:807
  77.3 6.1 %collective-permute-start.15 = (f32[128,128]{1,0:T(8,128)S(1)}, f32[128,128]{1,0:T(8,128)S(1)}, u32[]{:S(2)}, u32[]{:S(2)}) collective-permute-start(f32[128,128]{1,0:T(8,128)S(1)} %get-tuple-element.101.grad.refs_0_.grad_out), channel_id=1, source_target_pairs={{0,2},{1,3},{2,0},{3,1},{4,6},{5,7},{6,4},{7,5},{8,10},{9,11},{10,... | collective-permute-start | bytes 196616 | tf_op jit(solution)/shard_map/ppermute | solution.py:807
  77.6 5.8 %collective-permute-start.20 = (f32[128,128]{1,0:T(8,128)S(1)}, f32[128,128]{1,0:T(8,128)S(1)}, u32[]{:S(2)}, u32[]{:S(2)}) collective-permute-start(f32[128,128]{1,0:T(8,128)S(1)} %get-tuple-element.101.grad.refs_0_.grad_out), channel_id=1, source_target_pairs={{0,3},{1,2},{2,1},{3,0},{4,7},{5,6},{6,5},{7,4},{8,11},{9,10},{10,... | collective-permute-start | bytes 196616 | tf_op jit(solution)/shard_map/ppermute | solution.py:807
  80.5 5.2 %collective-permute-start.17 = (f32[128,128]{1,0:T(8,128)S(1)}, f32[128,128]{1,0:T(8,128)S(1)}, u32[]{:S(2)}, u32[]{:S(2)}) collective-permute-start(f32[128,128]{1,0:T(8,128)S(1)} %get-tuple-element.101.grad.refs_0_.grad_out), channel_id=1, source_target_pairs={{0,1},{1,0},{2,3},{3,2},{4,5},{5,4},{6,7},{7,6},{8,9},{9,8},{10,11... | collective-permute-start | bytes 196616 | tf_op jit(solution)/shard_map/ppermute | solution.py:807
  80.5 6.1 %collective-permute-start.16 = (f32[128,128]{1,0:T(8,128)S(1)}, f32[128,128]{1,0:T(8,128)S(1)}, u32[]{:S(2)}, u32[]{:S(2)}) collective-permute-start(f32[128,128]{1,0:T(8,128)S(1)} %get-tuple-element.101.grad.refs_0_.grad_out), channel_id=1, source_target_pairs={{0,8},{8,0},{1,9},{9,1},{2,10},{10,2},{3,11},{11,3},{4,12},{12,4},... | collective-permute-start | bytes 196616 | tf_op jit(solution)/shard_map/ppermute | solution.py:804
  83.4 3.3 %collective-permute-start.21 = (f32[128,128]{1,0:T(8,128)S(1)}, f32[128,128]{1,0:T(8,128)S(1)}, u32[]{:S(2)}, u32[]{:S(2)}) collective-permute-start(f32[128,128]{1,0:T(8,128)S(1)} %collective-permute-done.20.refs_3_), channel_id=1, source_target_pairs={{0,8},{8,0},{1,9},{9,1},{2,10},{10,2},{3,11},{11,3},{4,12},{12,4},... | collective-permute-start | bytes 196616 | tf_op jit(solution)/shard_map/ppermute | solution.py:804
  85.7 1.3 collective-permute-start.18
  86.1 1.3 collective-permute-start.19
  119.9 4.9 %collective-permute-start.22 = (f32[4,168,128]{2,1,0:T(8,128)S(1)}, f32[4,168,128]{2,1,0:T(8,128)S(1)}, u32[]{:S(2)}, u32[]{:S(2)}) collective-permute-start(f32[4,168,128]{2,1,0:T(8,128)S(1)} %get-tuple-element.118), channel_id=1, source_target_pairs={{0,8},{8,0},{1,9},{9,1},{2,10},{10,2},{3,11},{11,3},{4,12},{12,4},... | collective-permute-start | bytes 1032200 | tf_op jit(solution)/shard_map/ppermute | solution.py:804
  124.9 4.0 %collective-permute-start.23 = (f32[168,128]{1,0:T(8,128)S(1)}, f32[168,128]{1,0:T(8,128)S(1)}, u32[]{:S(2)}, u32[]{:S(2)}) collective-permute-start(f32[168,128]{1,0:T(8,128)S(1)} %get-tuple-element.120), channel_id=1, source_target_pairs={{0,1},{1,0},{2,3},{3,2},{4,5},{5,4},{6,7},{7,6},{8,9},{9,8},{10,11... | collective-permute-start | bytes 258056 | tf_op jit(solution)/shard_map/ppermute | solution.py:807
  125.7 5.0 %collective-permute-start.24 = (f32[168,128]{1,0:T(8,128)S(1)}, f32[168,128]{1,0:T(8,128)S(1)}, u32[]{:S(2)}, u32[]{:S(2)}) collective-permute-start(f32[168,128]{1,0:T(8,128)S(1)} %get-tuple-element.121), channel_id=1, source_target_pairs={{0,2},{1,3},{2,0},{3,1},{4,6},{5,7},{6,4},{7,5},{8,10},{9,11},{10,... | collective-permute-start | bytes 258056 | tf_op jit(solution)/shard_map/ppermute | solution.py:807
  127.0 6.3 %collective-permute-start.25 = (f32[168,128]{1,0:T(8,128)S(1)}, f32[168,128]{1,0:T(8,128)S(1)}, u32[]{:S(2)}, u32[]{:S(2)}) collective-permute-start(f32[168,128]{1,0:T(8,128)S(1)} %get-tuple-element.122), channel_id=1, source_target_pairs={{0,3},{1,2},{2,1},{3,0},{4,7},{5,6},{6,5},{7,4},{8,11},{9,10},{10,... | collective-permute-start | bytes 258056 | tf_op jit(solution)/shard_map/ppermute | solution.py:807
  136.3 13.1 %all-to-all-start.4 = ((f32[8,56,128]{2,1,0:T(8,128)}), f32[8,56,128]{2,1,0:T(8,128)S(1)}, u32[]{:S(2)}, u32[]{:S(2)}) async-start(f32[8,56,128]{2,1,0:T(8,128)} %get-tuple-element.129), calls=%async_computation.4 | async-start | bytes 458752 | tf_op jit(solution)/shard_map/all_to_all | solution.py:882
  139.7 4.3 %collective-permute-start.27 = (f32[256,128]{1,0:T(8,128)S(1)}, f32[256,128]{1,0:T(8,128)S(1)}, u32[]{:S(2)}, u32[]{:S(2)}) collective-permute-start(f32[256,128]{1,0:T(8,128)S(1)} %get-tuple-element.140), channel_id=1, source_target_pairs={{0,1},{1,0},{2,3},{3,2},{4,5},{5,4},{6,7},{7,6},{8,9},{9,8},{10,11... | collective-permute-start | bytes 393224 | tf_op jit(solution)/shard_map/ppermute | solution.py:872
  144.0 13.1 %collective-permute-start.28 = (f32[512,128]{1,0:T(8,128)S(1)}, f32[512,128]{1,0:T(8,128)S(1)}, u32[]{:S(2)}, u32[]{:S(2)}) collective-permute-start(f32[512,128]{1,0:T(8,128)S(1)} %constant_dynamic-update-slice_fusion.refs_0_), channel_id=1, source_target_pairs={{0,2},{1,3},{2,0},{3,1},{4,6},{5,7},{6,4},{7,5},{8,10},{9,11},{10,... | collective-permute-start | bytes 786440 | tf_op jit(solution)/shard_map/ppermute | solution.py:881
  150.2 12.9 %all-to-all-start.5 = ((f32[16,56,128]{2,1,0:T(8,128)}), f32[16,56,128]{2,1,0:T(8,128)S(1)}, u32[]{:S(2)}, u32[]{:S(2)}) async-start(f32[16,56,128]{2,1,0:T(8,128)} %shard_map.197), calls=%async_computation.5 | async-start | bytes 917504 | tf_op jit(solution)/shard_map/all_to_all | solution.py:884
  154.5 12.4 %collective-permute-start.29 = (f32[512,128]{1,0:T(8,128)S(1)}, f32[512,128]{1,0:T(8,128)S(1)}, u32[]{:S(2)}, u32[]{:S(2)}) collective-permute-start(f32[512,128]{1,0:T(8,128)S(1)} %constant_dynamic-update-slice_fusion.refs_0_), channel_id=1, source_target_pairs={{0,8},{8,0},{1,9},{9,1},{2,10},{10,2},{3,11},{11,3},{4,12},{12,4},... | collective-permute-start | bytes 786440 | tf_op jit(solution)/shard_map/ppermute | solution.py:804
  157.1 9.8 %collective-permute-start.30 = (f32[512,128]{1,0:T(8,128)S(1)}, f32[512,128]{1,0:T(8,128)S(1)}, u32[]{:S(2)}, u32[]{:S(2)}) collective-permute-start(f32[512,128]{1,0:T(8,128)S(1)} %collective-permute-done.28.refs_1_), channel_id=1, source_target_pairs={{0,8},{8,0},{1,9},{9,1},{2,10},{10,2},{3,11},{11,3},{4,12},{12,4},... | collective-permute-start | bytes 786440 | tf_op jit(solution)/shard_map/ppermute | solution.py:804
  163.2 4.8 %collective-permute-start.26 = (f32[160,128]{1,0:T(8,128)S(1)}, f32[160,128]{1,0:T(8,128)S(1)}, u32[]{:S(2)}, u32[]{:S(2)}) collective-permute-start(f32[160,128]{1,0:T(8,128)S(1)} %get-tuple-element.131.own), channel_id=1, source_target_pairs={{0,8},{8,0},{1,9},{9,1},{2,10},{10,2},{3,11},{11,3},{4,12},{12,4},... | collective-permute-start | bytes 245768 | tf_op jit(solution)/shard_map/ppermute | solution.py:804

commit v9 on v8

--- a/solution.py
+++ b/solution.py
@@ -807,7 +807,7 @@
         return lax.ppermute(value, "x", [(at, at ^ step) for at in range(4)])
 
     def gather(value, beside=()):
-        one, two, three = (step_x(value, step) for step in (1, 2, 3))
+        one, three, two = (step_x(value, step) for step in (1, 3, 2))
         two, *beside = lax.optimization_barrier((two, *beside))
         values = [value, one, two, three]
         return values + [other_core(item) for item in values], beside
@@ -815,7 +815,8 @@
     def scatter(kernel, parts, other):
         shape = f32(*other.shape[1:])
         tiles = call(kernel, (shape,) * 4, *parts, other_core(other))
-        return [tiles[0]] + [step_x(tiles[step], step) for step in (1, 2, 3)]
+        two, one, three = (step_x(tiles[step], step) for step in (2, 1, 3))
+        return [tiles[0], one, two, three]
 
     shared, _ = gather(shared)
     half = jax.ShapeDtypeStruct((2 * SHARD, 4 * N), jnp.bfloat16)

time: 169 us -> 169 us (level)
  no operation moved by 1% of the time
where the time goes in v9:
time: 169 us
  starting transfers between devices  62.6 us (37%)
  blocking collectives  62.5 us (37%)
  waiting for transfers between devices  26.3 us (16%)
  Pallas kernels  16.6 us (10%)
    all_to_all x2, blocking collectives, cross_sum(): return lax.all_to_all(tiles, CROSS, 0, 0).reshape(2 * SHARD, N)  32.3 us
    all_to_all x2, blocking collectives, cross_sum(): tiles = lax.all_to_all(tiles, CROSS, 0, 0)  30.1 us
    ppermute x13, starting transfers between devices, other_core(): return lax.ppermute(value, 'c', swap)  28.5 us
    pallas_call x22, Pallas kernels, call(): pl.pallas_call(kernel, out_shape=out_shape, scratch_shapes=list(scratch),...  16.6 us
    ppermute x12, starting transfers between devices, step_x(): return lax.ppermute(value, 'x', [(at, at ^ step) for at in range(4)])  13.8 us
    ppermute x4, starting transfers between devices, swapped(): return lax.ppermute(value, axes, places)  10.4 us
    ppermute x12, waiting for transfers between devices, step_x(): return lax.ppermute(value, 'x', [(at, at ^ step) for at in range(4)])  8.22 us
    all_to_all x1, waiting for transfers between devices, body(): payload = lax.all_to_all(payload, PLANE, 0, 0)  5.92 us
  transfers between devices with their start and end apart: 33, of which 13 were waited for; matrix products, arithmetic and copies ran while one was open for 0% of the time, Pallas kernels for 3%

profile of v9, /device:TPU:1, one launch (start us, length us, event | category | flops | bytes accessed | tf_op | source)
XLA Modules:
  0.0 168.8 jit_solution(3136116111742505524)
XLA Ops:
  0.6 1.0 shard_map.179
  1.6 2.1 %collective-permute-start = (f32[8,128]{1,0:T(8,128)S(1)}, f32[8,128]{1,0:T(8,128)S(1)}, u32[]{:S(2)}, u32[]{:S(2)}) collective-permute-start(f32[8,128]{1,0:T(8,128)S(1)} %get-tuple-element.79), channel_id=1, source_target_pairs={{0,1},{1,0},{2,3},{3,2},{4,5},{5,4},{6,7},{7,6},{8,9},{9,8},{10,11... | collective-permute-start | bytes 12296 | tf_op jit(solution)/shard_map/ppermute | solution.py:192
  3.8 3.2 %collective-permute-start.1 = (f32[8,128]{1,0:T(8,128)S(1)}, f32[8,128]{1,0:T(8,128)S(1)}, u32[]{:S(2)}, u32[]{:S(2)}) collective-permute-start(f32[8,128]{1,0:T(8,128)S(1)} %get-tuple-element.80), channel_id=1, source_target_pairs={{0,7},{1,2},{2,1},{3,4},{4,3},{5,6},{6,5},{7,0},{8,15},{9,10},{10,... | collective-permute-start | bytes 12296 | tf_op jit(solution)/shard_map/ppermute | solution.py:192
  6.9 1.4 collective-permute-done.1.far.far_y
  8.4 2.5 %collective-permute-start.2 = (f32[8,128]{1,0:T(8,128)S(1)}, f32[8,128]{1,0:T(8,128)S(1)}, u32[]{:S(2)}, u32[]{:S(2)}) collective-permute-start(f32[8,128]{1,0:T(8,128)S(1)} %get-tuple-element.81), channel_id=1, source_target_pairs={{0,8},{8,0},{16,24},{24,16},{32,40},{40,32},{48,56},{56,48},{64,72... | collective-permute-start | bytes 12296 | tf_op jit(solution)/shard_map/ppermute | solution.py:192
  10.9 2.6 %collective-permute-start.3 = (f32[8,128]{1,0:T(8,128)S(1)}, f32[8,128]{1,0:T(8,128)S(1)}, u32[]{:S(2)}, u32[]{:S(2)}) collective-permute-start(f32[8,128]{1,0:T(8,128)S(1)} %get-tuple-element.82), channel_id=1, source_target_pairs={{0,248},{8,16},{16,8},{24,32},{32,24},{40,48},{48,40},{56,64},{64,... | collective-permute-start | bytes 12296 | tf_op jit(solution)/shard_map/ppermute | solution.py:192
  13.5 1.3 collective-permute-done.3.far_x
  14.8 1.2 shard_map.181
  16.0 0.4 collective-permute-start.7
  16.4 1.6 collective-permute-start.9
  18.0 0.7 collective-permute-start.5
  18.7 6.8 %collective-permute-start.4 = (f32[136,128]{1,0:T(8,128)S(1)}, f32[136,128]{1,0:T(8,128)S(1)}, u32[]{:S(2)}, u32[]{:S(2)}) collective-permute-start(f32[136,128]{1,0:T(8,128)S(1)} %get-tuple-element.85.refs_0_.refs_4_), channel_id=1, source_target_pairs={{0,8},{8,0},{1,9},{9,1},{2,10},{10,2},{3,11},{11,3},{4,12},{12,4},... | collective-permute-start | bytes 208904 | tf_op jit(solution)/shard_map/ppermute | solution.py:804
  25.5 2.4 %collective-permute-start.8 = (f32[136,128]{1,0:T(8,128)S(1)}, f32[136,128]{1,0:T(8,128)S(1)}, u32[]{:S(2)}, u32[]{:S(2)}) collective-permute-start(f32[136,128]{1,0:T(8,128)S(1)} %collective-permute-done.7.refs_2_.refs_6_), channel_id=1, source_target_pairs={{0,8},{8,0},{1,9},{9,1},{2,10},{10,2},{3,11},{11,3},{4,12},{12,4},... | collective-permute-start | bytes 208904 | tf_op jit(solution)/shard_map/ppermute | solution.py:804
  27.9 0.7 collective-permute-start.10
  28.6 1.4 shard_map.182
  30.0 1.4 shard_map.183
  31.4 16.0 %all_to_all.30.tiles = f32[32,16,128]{2,1,0:T(8,128)S(1)} all-to-all(f32[32,16,128]{2,1,0:T(8,128)S(1)} %get-tuple-element.87), channel_id=1, replica_groups=mesh['y'=4,'zh'=4,'c'=2,'zl'=2,'x'=4] {'y','zh','zl'}, dimensions={0} | all-to-all | bytes 524288 | tf_op jit(solution)/shard_map/all_to_all | solution.py:837
  47.5 16.3 %all_to_all.31 = f32[32,16,128]{2,1,0:T(8,128)S(1)} all-to-all(f32[32,16,128]{2,1,0:T(8,128)S(1)} %shard_map.184), channel_id=1, replica_groups=mesh['y'=4,'zh'=4,'c'=2,'zl'=2,'x'=4] {'y','zh','zl'}, dimensions={0} | all-to-all | bytes 524288 | tf_op jit(solution)/shard_map/all_to_all | solution.py:839
  63.8 0.8 shard_map.185
  64.6 3.7 %collective-permute-start.11 = (f32[4,128,128]{2,1,0:T(8,128)S(1)}, f32[4,128,128]{2,1,0:T(8,128)S(1)}, u32[]{:S(2)}, u32[]{:S(2)}) collective-permute-start(f32[4,128,128]{2,1,0:T(8,128)S(1)} %get-tuple-element.93), channel_id=1, source_target_pairs={{0,8},{8,0},{1,9},{9,1},{2,10},{10,2},{3,11},{11,3},{4,12},{12,4},... | collective-permute-start | bytes 786440 | tf_op jit(solution)/shard_map/ppermute | solution.py:804
  68.3 0.4 shard_map.186.mine
  68.7 0.8 collective-permute-done.11.other
  69.5 1.0 collective-permute-start.12
  70.5 2.1 %collective-permute-start.13 = (f32[128,128]{1,0:T(8,128)S(1)}, f32[128,128]{1,0:T(8,128)S(1)}, u32[]{:S(2)}, u32[]{:S(2)}) collective-permute-start(f32[128,128]{1,0:T(8,128)S(1)} %get-tuple-element.96), channel_id=1, source_target_pairs={{0,2},{1,3},{2,0},{3,1},{4,6},{5,7},{6,4},{7,5},{8,10},{9,11},{10,... | collective-permute-start | bytes 196616 | tf_op jit(solution)/shard_map/ppermute | solution.py:807
  72.6 0.9 collective-permute-start.14
  73.4 2.7 %collective-permute-done.13.tile_2 = f32[128,128]{1,0:T(8,128)S(1)} collective-permute-done((f32[128,128]{1,0:T(8,128)S(1)}, f32[128,128]{1,0:T(8,128)S(1)}, u32[]{:S(2)}, u32[]{:S(2)}) %collective-permute-start.13) | collective-permute-done | bytes 65568 | tf_op jit(solution)/shard_map/ppermute | solution.py:807
  76.1 1.1 collective-permute-done.14.tile_3
  77.2 0.1 shard_map.188
  77.3 0.3 collective-permute-start.15
  77.6 2.9 %collective-permute-start.20 = (f32[128,128]{1,0:T(8,128)S(1)}, f32[128,128]{1,0:T(8,128)S(1)}, u32[]{:S(2)}, u32[]{:S(2)}) collective-permute-start(f32[128,128]{1,0:T(8,128)S(1)} %get-tuple-element.101.grad.refs_0_.grad_out), channel_id=1, source_target_pairs={{0,3},{1,2},{2,1},{3,0},{4,7},{5,6},{6,5},{7,4},{8,11},{9,10},{10,... | collective-permute-start | bytes 196616 | tf_op jit(solution)/shard_map/ppermute | solution.py:807
  80.5 2.2 %collective-permute-start.16 = (f32[128,128]{1,0:T(8,128)S(1)}, f32[128,128]{1,0:T(8,128)S(1)}, u32[]{:S(2)}, u32[]{:S(2)}) collective-permute-start(f32[128,128]{1,0:T(8,128)S(1)} %get-tuple-element.101.grad.refs_0_.grad_out), channel_id=1, source_target_pairs={{0,8},{8,0},{1,9},{9,1},{2,10},{10,2},{3,11},{11,3},{4,12},{12,4},... | collective-permute-start | bytes 196616 | tf_op jit(solution)/shard_map/ppermute | solution.py:804
  82.7 0.7 shard_map.189
  83.4 2.3 %collective-permute-start.21 = (f32[128,128]{1,0:T(8,128)S(1)}, f32[128,128]{1,0:T(8,128)S(1)}, u32[]{:S(2)}, u32[]{:S(2)}) collective-permute-start(f32[128,128]{1,0:T(8,128)S(1)} %collective-permute-done.20.refs_3_), channel_id=1, source_target_pairs={{0,8},{8,0},{1,9},{9,1},{2,10},{10,2},{3,11},{11,3},{4,12},{12,4},... | collective-permute-start | bytes 196616 | tf_op jit(solution)/shard_map/ppermute | solution.py:804
  85.7 0.4 collective-permute-start.18
  86.1 0.1 collective-permute-start.19
  86.2 0.4 shard_map.190.refs_6_
  86.7 0.3 collective-permute-done.18.refs_1_
  87.0 0.4 collective-permute-done.19.refs_2_
  87.3 0.4 shard_map.191
  87.8 14.1 %all_to_all.32.tiles = f32[32,16,128]{2,1,0:T(8,128)S(1)} all-to-all(f32[32,16,128]{2,1,0:T(8,128)S(1)} %shard_map.191), channel_id=1, replica_groups=mesh['y'=4,'zh'=4,'c'=2,'zl'=2,'x'=4] {'y','zh','zl'}, dimensions={0} | all-to-all | bytes 524288 | tf_op jit(solution)/shard_map/all_to_all | solution.py:837
  101.9 16.0 %all_to_all.33 = f32[32,16,128]{2,1,0:T(8,128)S(1)} all-to-all(f32[32,16,128]{2,1,0:T(8,128)S(1)} %shard_map.192), channel_id=1, replica_groups=mesh['y'=4,'zh'=4,'c'=2,'zl'=2,'x'=4] {'y','zh','zl'}, dimensions={0} | all-to-all | bytes 524288 | tf_op jit(solution)/shard_map/all_to_all | solution.py:839
  117.9 2.0 %shard_map.193 = (f32[4,168,128]{2,1,0:T(8,128)S(1)}, f32[4,168,128]{2,1,0:T(8,128)S(1)}, bf16[512,256]{1,0:T(8,128)(2,1)S(1)}, bf16[512,256]{1,0:T(8,128)(2,1)S(1)}) custom-call(f32[128,128]{1,0:T(8,128)S(1)} %collective-permute-done.16.refs_0_, f32[128,128]{1,0:T(8,128)S(1)} %collective-permute-done.18.refs_1_, ...), custom_call_target="tpu_custom_call" | custom-call | tf_op jit(solution)/shard_map/pallas_call | solution.py:111
  119.9 3.6 %collective-permute-start.22 = (f32[4,168,128]{2,1,0:T(8,128)S(1)}, f32[4,168,128]{2,1,0:T(8,128)S(1)}, u32[]{:S(2)}, u32[]{:S(2)}) collective-permute-start(f32[4,168,128]{2,1,0:T(8,128)S(1)} %get-tuple-element.118), channel_id=1, source_target_pairs={{0,8},{8,0},{1,9},{9,1},{2,10},{10,2},{3,11},{11,3},{4,12},{12,4},... | collective-permute-start | bytes 1032200 | tf_op jit(solution)/shard_map/ppermute | solution.py:804
  123.5 0.8 shard_map.194
  124.4 0.4 collective-permute-done.22.other
  124.9 0.8 collective-permute-start.23
  125.7 1.3 collective-permute-start.24
  127.0 1.8 %collective-permute-start.25 = (f32[168,128]{1,0:T(8,128)S(1)}, f32[168,128]{1,0:T(8,128)S(1)}, u32[]{:S(2)}, u32[]{:S(2)}) collective-permute-start(f32[168,128]{1,0:T(8,128)S(1)} %get-tuple-element.122), channel_id=1, source_target_pairs={{0,3},{1,2},{2,1},{3,0},{4,7},{5,6},{6,5},{7,4},{8,11},{9,10},{10,... | collective-permute-start | bytes 258056 | tf_op jit(solution)/shard_map/ppermute | solution.py:807
  128.8 1.9 %collective-permute-done.24.tile_2 = f32[168,128]{1,0:T(8,128)S(1)} collective-permute-done((f32[168,128]{1,0:T(8,128)S(1)}, f32[168,128]{1,0:T(8,128)S(1)}, u32[]{:S(2)}, u32[]{:S(2)}) %collective-permute-start.24) | collective-permute-done | bytes 86048 | tf_op jit(solution)/shard_map/ppermute | solution.py:807
  130.7 2.6 %collective-permute-done.25.tile_3 = f32[168,128]{1,0:T(8,128)S(1)} collective-permute-done((f32[168,128]{1,0:T(8,128)S(1)}, f32[168,128]{1,0:T(8,128)S(1)}, u32[]{:S(2)}, u32[]{:S(2)}) %collective-permute-start.25) | collective-permute-done | bytes 86048 | tf_op jit(solution)/shard_map/ppermute | solution.py:807
  133.3 3.0 %shard_map.196 = (f32[8,56,128]{2,1,0:T(8,128)}, f32[8,128]{1,0:T(8,128)S(1)}, f32[16,128]{1,0:T(8,128)S(1)}) custom-call(f32[168,128]{1,0:T(8,128)S(1)} %get-tuple-element.119.tile_0, f32[168,128]{1,0:T(8,128)S(1)} %collective-permute-done.23.tile_1, f32[168,128]{1,0:T(8,128)S(1)} %collective-permute-done.24.tile_2, ...), custom_call_target="tpu_custom_call" | custom-call | flops 1000000000 | bytes 10000000 | tf_op jit(solution)/shard_map/pallas_call | solution.py:111
  136.3 3.4 %all-to-all-start.4 = ((f32[8,56,128]{2,1,0:T(8,128)}), f32[8,56,128]{2,1,0:T(8,128)S(1)}, u32[]{:S(2)}, u32[]{:S(2)}) async-start(f32[8,56,128]{2,1,0:T(8,128)} %get-tuple-element.129), calls=%async_computation.4 | async-start | bytes 458752 | tf_op jit(solution)/shard_map/all_to_all | solution.py:883
  139.7 0.1 collective-permute-start.27
  139.8 4.1 %collective-permute-done.27 = f32[256,128]{1,0:T(8,128)S(1)} collective-permute-done((f32[256,128]{1,0:T(8,128)S(1)}, f32[256,128]{1,0:T(8,128)S(1)}, u32[]{:S(2)}, u32[]{:S(2)}) %collective-permute-start.27) | collective-permute-done | bytes 131104 | tf_op jit(solution)/shard_map/ppermute | solution.py:873
  144.0 2.0 %collective-permute-start.28 = (f32[512,128]{1,0:T(8,128)S(1)}, f32[512,128]{1,0:T(8,128)S(1)}, u32[]{:S(2)}, u32[]{:S(2)}) collective-permute-start(f32[512,128]{1,0:T(8,128)S(1)} %constant_dynamic-update-slice_fusion.refs_0_), channel_id=1, source_target_pairs={{0,2},{1,3},{2,0},{3,1},{4,6},{5,7},{6,4},{7,5},{8,10},{9,11},{10,... | collective-permute-start | bytes 786440 | tf_op jit(solution)/shard_map/ppermute | solution.py:882
  146.0 3.4 %all-to-all-done.4.tiles = f32[8,56,128]{2,1,0:T(8,128)S(1)} async-done(((f32[8,56,128]{2,1,0:T(8,128)}), f32[8,56,128]{2,1,0:T(8,128)S(1)}, u32[]{:S(2)}, u32[]{:S(2)}) %all-to-all-start.4) | async-done | bytes 229408 | tf_op jit(solution)/shard_map/all_to_all | solution.py:883
  149.4 0.8 shard_map.197
  150.2 4.3 %all-to-all-start.5 = ((f32[16,56,128]{2,1,0:T(8,128)}), f32[16,56,128]{2,1,0:T(8,128)S(1)}, u32[]{:S(2)}, u32[]{:S(2)}) async-start(f32[16,56,128]{2,1,0:T(8,128)} %shard_map.197), calls=%async_computation.5 | async-start | bytes 917504 | tf_op jit(solution)/shard_map/all_to_all | solution.py:885
  154.5 2.6 %collective-permute-start.29 = (f32[512,128]{1,0:T(8,128)S(1)}, f32[512,128]{1,0:T(8,128)S(1)}, u32[]{:S(2)}, u32[]{:S(2)}) collective-permute-start(f32[512,128]{1,0:T(8,128)S(1)} %constant_dynamic-update-slice_fusion.refs_0_), channel_id=1, source_target_pairs={{0,8},{8,0},{1,9},{9,1},{2,10},{10,2},{3,11},{11,3},{4,12},{12,4},... | collective-permute-start | bytes 786440 | tf_op jit(solution)/shard_map/ppermute | solution.py:804
  157.1 0.1 collective-permute-start.30
  157.2 5.9 %all-to-all-done.5.tiles = f32[16,56,128]{2,1,0:T(8,128)S(1)} async-done(((f32[16,56,128]{2,1,0:T(8,128)}), f32[16,56,128]{2,1,0:T(8,128)S(1)}, u32[]{:S(2)}, u32[]{:S(2)}) %all-to-all-start.5) | async-done | bytes 458784 | tf_op jit(solution)/shard_map/all_to_all | solution.py:885
  163.2 3.7 %collective-permute-start.26 = (f32[160,128]{1,0:T(8,128)S(1)}, f32[160,128]{1,0:T(8,128)S(1)}, u32[]{:S(2)}, u32[]{:S(2)}) collective-permute-start(f32[160,128]{1,0:T(8,128)S(1)} %get-tuple-element.131.own), channel_id=1, source_target_pairs={{0,8},{8,0},{1,9},{9,1},{2,10},{10,2},{3,11},{11,3},{4,12},{12,4},... | collective-permute-start | bytes 245768 | tf_op jit(solution)/shard_map/ppermute | solution.py:804
  166.9 1.1 shard_map.200
  168.0 0.9 shard_map.199
  (38 shorter events, 0.4 us)
Async XLA Ops:
  0.6 27.9 %copy-start.3 = (f32[128,128]{1,0:T(8,128)S(1)}, f32[128,128]{1,0:T(8,128)}, u32[]{:S(2)}) copy-start(f32[128,128]{1,0:T(8,128)} %w_up.1) | copy-start | bytes 196612
  1.6 5.3 %collective-permute-start = (f32[8,128]{1,0:T(8,128)S(1)}, f32[8,128]{1,0:T(8,128)S(1)}, u32[]{:S(2)}, u32[]{:S(2)}) collective-permute-start(f32[8,128]{1,0:T(8,128)S(1)} %get-tuple-element.79), channel_id=1, source_target_pairs={{0,1},{1,0},{2,3},{3,2},{4,5},{5,4},{6,7},{7,6},{8,9},{9,8},{10,11... | collective-permute-start | bytes 12296 | tf_op jit(solution)/shard_map/ppermute | solution.py:192
  3.8 4.6 %collective-permute-start.1 = (f32[8,128]{1,0:T(8,128)S(1)}, f32[8,128]{1,0:T(8,128)S(1)}, u32[]{:S(2)}, u32[]{:S(2)}) collective-permute-start(f32[8,128]{1,0:T(8,128)S(1)} %get-tuple-element.80), channel_id=1, source_target_pairs={{0,7},{1,2},{2,1},{3,4},{4,3},{5,6},{6,5},{7,0},{8,15},{9,10},{10,... | collective-permute-start | bytes 12296 | tf_op jit(solution)/shard_map/ppermute | solution.py:192
  8.4 5.1 %collective-permute-start.2 = (f32[8,128]{1,0:T(8,128)S(1)}, f32[8,128]{1,0:T(8,128)S(1)}, u32[]{:S(2)}, u32[]{:S(2)}) collective-permute-start(f32[8,128]{1,0:T(8,128)S(1)} %get-tuple-element.81), channel_id=1, source_target_pairs={{0,8},{8,0},{16,24},{24,16},{32,40},{40,32},{48,56},{56,48},{64,72... | collective-permute-start | bytes 12296 | tf_op jit(solution)/shard_map/ppermute | solution.py:192
  10.9 3.9 %collective-permute-start.3 = (f32[8,128]{1,0:T(8,128)S(1)}, f32[8,128]{1,0:T(8,128)S(1)}, u32[]{:S(2)}, u32[]{:S(2)}) collective-permute-start(f32[8,128]{1,0:T(8,128)S(1)} %get-tuple-element.82), channel_id=1, source_target_pairs={{0,248},{8,16},{16,8},{24,32},{32,24},{40,48},{48,40},{56,64},{64,... | collective-permute-start | bytes 12296 | tf_op jit(solution)/shard_map/ppermute | solution.py:192
  14.8 13.7 %copy-start.1 = (f32[3,2048]{1,0:T(4,128)S(1)}, f32[3,2048]{1,0:T(4,128)}, u32[]{:S(2)}) copy-start(f32[3,2048]{1,0:T(4,128)} %refs_8_.1) | copy-start | bytes 73732
  16.0 9.5 %collective-permute-start.7 = (f32[136,128]{1,0:T(8,128)S(1)}, f32[136,128]{1,0:T(8,128)S(1)}, u32[]{:S(2)}, u32[]{:S(2)}) collective-permute-start(f32[136,128]{1,0:T(8,128)S(1)} %get-tuple-element.85.refs_0_.refs_4_), channel_id=1, source_target_pairs={{0,2},{1,3},{2,0},{3,1},{4,6},{5,7},{6,4},{7,5},{8,10},{9,11},{10,... | collective-permute-start | bytes 208904 | tf_op jit(solution)/shard_map/ppermute | solution.py:807
  16.4 11.4 %collective-permute-start.9 = (f32[136,128]{1,0:T(8,128)S(1)}, f32[136,128]{1,0:T(8,128)S(1)}, u32[]{:S(2)}, u32[]{:S(2)}) collective-permute-start(f32[136,128]{1,0:T(8,128)S(1)} %get-tuple-element.85.refs_0_.refs_4_), channel_id=1, source_target_pairs={{0,3},{1,2},{2,1},{3,0},{4,7},{5,6},{6,5},{7,4},{8,11},{9,10},{10,... | collective-permute-start | bytes 208904 | tf_op jit(solution)/shard_map/ppermute | solution.py:807
  18.0 10.5 %collective-permute-start.5 = (f32[136,128]{1,0:T(8,128)S(1)}, f32[136,128]{1,0:T(8,128)S(1)}, u32[]{:S(2)}, u32[]{:S(2)}) collective-permute-start(f32[136,128]{1,0:T(8,128)S(1)} %get-tuple-element.85.refs_0_.refs_4_), channel_id=1, source_target_pairs={{0,1},{1,0},{2,3},{3,2},{4,5},{5,4},{6,7},{7,6},{8,9},{9,8},{10,11... | collective-permute-start | bytes 208904 | tf_op jit(solution)/shard_map/ppermute | solution.py:807
  18.7 11.2 %collective-permute-start.4 = (f32[136,128]{1,0:T(8,128)S(1)}, f32[136,128]{1,0:T(8,128)S(1)}, u32[]{:S(2)}, u32[]{:S(2)}) collective-permute-start(f32[136,128]{1,0:T(8,128)S(1)} %get-tuple-element.85.refs_0_.refs_4_), channel_id=1, source_target_pairs={{0,8},{8,0},{1,9},{9,1},{2,10},{10,2},{3,11},{11,3},{4,12},{12,4},... | collective-permute-start | bytes 208904 | tf_op jit(solution)/shard_map/ppermute | solution.py:804
  25.5 4.5 %collective-permute-start.8 = (f32[136,128]{1,0:T(8,128)S(1)}, f32[136,128]{1,0:T(8,128)S(1)}, u32[]{:S(2)}, u32[]{:S(2)}) collective-permute-start(f32[136,128]{1,0:T(8,128)S(1)} %collective-permute-done.7.refs_2_.refs_6_), channel_id=1, source_target_pairs={{0,8},{8,0},{1,9},{9,1},{2,10},{10,2},{3,11},{11,3},{4,12},{12,4},... | collective-permute-start | bytes 208904 | tf_op jit(solution)/shard_map/ppermute | solution.py:804
  27.9 2.1 %collective-permute-start.10 = (f32[136,128]{1,0:T(8,128)S(1)}, f32[136,128]{1,0:T(8,128)S(1)}, u32[]{:S(2)}, u32[]{:S(2)}) collective-permute-start(f32[136,128]{1,0:T(8,128)S(1)} %collective-permute-done.9.refs_3_.refs_7_), channel_id=1, source_target_pairs={{0,8},{8,0},{1,9},{9,1},{2,10},{10,2},{3,11},{11,3},{4,12},{12,4},... | collective-permute-start | bytes 208904 | tf_op jit(solution)/shard_map/ppermute | solution.py:804
  28.6 1.4 collective-permute-start.6
  30.0 33.8 %copy-start = (f32[2048,128]{1,0:T(8,128)S(1)}, f32[2048,128]{1,0:T(8,128)}, u32[]{:S(2)}) copy-start(f32[2048,128]{1,0:T(8,128)} %refs_15_.1) | copy-start | bytes 3145732
  47.5 16.4 %copy-start.2 = (f32[128,128]{1,0:T(8,128)S(1)}, f32[128,128]{1,0:T(8,128)}, u32[]{:S(2)}) copy-start(f32[128,128]{1,0:T(8,128)} %w_charge.3) | copy-start | bytes 196612
  64.6 4.8 %collective-permute-start.11 = (f32[4,128,128]{2,1,0:T(8,128)S(1)}, f32[4,128,128]{2,1,0:T(8,128)S(1)}, u32[]{:S(2)}, u32[]{:S(2)}) collective-permute-start(f32[4,128,128]{2,1,0:T(8,128)S(1)} %get-tuple-element.93), channel_id=1, source_target_pairs={{0,8},{8,0},{1,9},{9,1},{2,10},{10,2},{3,11},{11,3},{4,12},{12,4},... | collective-permute-start | bytes 786440 | tf_op jit(solution)/shard_map/ppermute | solution.py:804
  69.5 4.0 %collective-permute-start.12 = (f32[128,128]{1,0:T(8,128)S(1)}, f32[128,128]{1,0:T(8,128)S(1)}, u32[]{:S(2)}, u32[]{:S(2)}) collective-permute-start(f32[128,128]{1,0:T(8,128)S(1)} %get-tuple-element.95), channel_id=1, source_target_pairs={{0,1},{1,0},{2,3},{3,2},{4,5},{5,4},{6,7},{7,6},{8,9},{9,8},{10,11... | collective-permute-start | bytes 196616 | tf_op jit(solution)/shard_map/ppermute | solution.py:807
  70.5 5.6 %collective-permute-start.13 = (f32[128,128]{1,0:T(8,128)S(1)}, f32[128,128]{1,0:T(8,128)S(1)}, u32[]{:S(2)}, u32[]{:S(2)}) collective-permute-start(f32[128,128]{1,0:T(8,128)S(1)} %get-tuple-element.96), channel_id=1, source_target_pairs={{0,2},{1,3},{2,0},{3,1},{4,6},{5,7},{6,4},{7,5},{8,10},{9,11},{10,... | collective-permute-start | bytes 196616 | tf_op jit(solution)/shard_map/ppermute | solution.py:807
  72.6 4.6 %collective-permute-start.14 = (f32[128,128]{1,0:T(8,128)S(1)}, f32[128,128]{1,0:T(8,128)S(1)}, u32[]{:S(2)}, u32[]{:S(2)}) collective-permute-start(f32[128,128]{1,0:T(8,128)S(1)} %get-tuple-element.97), channel_id=1, source_target_pairs={{0,3},{1,2},{2,1},{3,0},{4,7},{5,6},{6,5},{7,4},{8,11},{9,10},{10,... | collective-permute-start | bytes 196616 | tf_op jit(solution)/shard_map/ppermute | solution.py:807
  77.3 6.1 %collective-permute-start.15 = (f32[128,128]{1,0:T(8,128)S(1)}, f32[128,128]{1,0:T(8,128)S(1)}, u32[]{:S(2)}, u32[]{:S(2)}) collective-permute-start(f32[128,128]{1,0:T(8,128)S(1)} %get-tuple-element.101.grad.refs_0_.grad_out), channel_id=1, source_target_pairs={{0,2},{1,3},{2,0},{3,1},{4,6},{5,7},{6,4},{7,5},{8,10},{9,11},{10,... | collective-permute-start | bytes 196616 | tf_op jit(solution)/shard_map/ppermute | solution.py:807
  77.6 5.8 %collective-permute-start.20 = (f32[128,128]{1,0:T(8,128)S(1)}, f32[128,128]{1,0:T(8,128)S(1)}, u32[]{:S(2)}, u32[]{:S(2)}) collective-permute-start(f32[128,128]{1,0:T(8,128)S(1)} %get-tuple-element.101.grad.refs_0_.grad_out), channel_id=1, source_target_pairs={{0,3},{1,2},{2,1},{3,0},{4,7},{5,6},{6,5},{7,4},{8,11},{9,10},{10,... | collective-permute-start | bytes 196616 | tf_op jit(solution)/shard_map/ppermute | solution.py:807
  80.5 5.2 %collective-permute-start.17 = (f32[128,128]{1,0:T(8,128)S(1)}, f32[128,128]{1,0:T(8,128)S(1)}, u32[]{:S(2)}, u32[]{:S(2)}) collective-permute-start(f32[128,128]{1,0:T(8,128)S(1)} %get-tuple-element.101.grad.refs_0_.grad_out), channel_id=1, source_target_pairs={{0,1},{1,0},{2,3},{3,2},{4,5},{5,4},{6,7},{7,6},{8,9},{9,8},{10,11... | collective-permute-start | bytes 196616 | tf_op jit(solution)/shard_map/ppermute | solution.py:807
  80.5 6.1 %collective-permute-start.16 = (f32[128,128]{1,0:T(8,128)S(1)}, f32[128,128]{1,0:T(8,128)S(1)}, u32[]{:S(2)}, u32[]{:S(2)}) collective-permute-start(f32[128,128]{1,0:T(8,128)S(1)} %get-tuple-element.101.grad.refs_0_.grad_out), channel_id=1, source_target_pairs={{0,8},{8,0},{1,9},{9,1},{2,10},{10,2},{3,11},{11,3},{4,12},{12,4},... | collective-permute-start | bytes 196616 | tf_op jit(solution)/shard_map/ppermute | solution.py:804
  83.4 3.3 %collective-permute-start.21 = (f32[128,128]{1,0:T(8,128)S(1)}, f32[128,128]{1,0:T(8,128)S(1)}, u32[]{:S(2)}, u32[]{:S(2)}) collective-permute-start(f32[128,128]{1,0:T(8,128)S(1)} %collective-permute-done.20.refs_3_), channel_id=1, source_target_pairs={{0,8},{8,0},{1,9},{9,1},{2,10},{10,2},{3,11},{11,3},{4,12},{12,4},... | collective-permute-start | bytes 196616 | tf_op jit(solution)/shard_map/ppermute | solution.py:804
  85.7 1.3 collective-permute-start.18
  86.1 1.3 collective-permute-start.19
  119.9 4.9 %collective-permute-start.22 = (f32[4,168,128]{2,1,0:T(8,128)S(1)}, f32[4,168,128]{2,1,0:T(8,128)S(1)}, u32[]{:S(2)}, u32[]{:S(2)}) collective-permute-start(f32[4,168,128]{2,1,0:T(8,128)S(1)} %get-tuple-element.118), channel_id=1, source_target_pairs={{0,8},{8,0},{1,9},{9,1},{2,10},{10,2},{3,11},{11,3},{4,12},{12,4},... | collective-permute-start | bytes 1032200 | tf_op jit(solution)/shard_map/ppermute | solution.py:804
  124.9 4.0 %collective-permute-start.23 = (f32[168,128]{1,0:T(8,128)S(1)}, f32[168,128]{1,0:T(8,128)S(1)}, u32[]{:S(2)}, u32[]{:S(2)}) collective-permute-start(f32[168,128]{1,0:T(8,128)S(1)} %get-tuple-element.120), channel_id=1, source_target_pairs={{0,1},{1,0},{2,3},{3,2},{4,5},{5,4},{6,7},{7,6},{8,9},{9,8},{10,11... | collective-permute-start | bytes 258056 | tf_op jit(solution)/shard_map/ppermute | solution.py:807
  125.7 5.0 %collective-permute-start.24 = (f32[168,128]{1,0:T(8,128)S(1)}, f32[168,128]{1,0:T(8,128)S(1)}, u32[]{:S(2)}, u32[]{:S(2)}) collective-permute-start(f32[168,128]{1,0:T(8,128)S(1)} %get-tuple-element.121), channel_id=1, source_target_pairs={{0,2},{1,3},{2,0},{3,1},{4,6},{5,7},{6,4},{7,5},{8,10},{9,11},{10,... | collective-permute-start | bytes 258056 | tf_op jit(solution)/shard_map/ppermute | solution.py:807
  127.0 6.3 %collective-permute-start.25 = (f32[168,128]{1,0:T(8,128)S(1)}, f32[168,128]{1,0:T(8,128)S(1)}, u32[]{:S(2)}, u32[]{:S(2)}) collective-permute-start(f32[168,128]{1,0:T(8,128)S(1)} %get-tuple-element.122), channel_id=1, source_target_pairs={{0,3},{1,2},{2,1},{3,0},{4,7},{5,6},{6,5},{7,4},{8,11},{9,10},{10,... | collective-permute-start | bytes 258056 | tf_op jit(solution)/shard_map/ppermute | solution.py:807
  136.3 13.1 %all-to-all-start.4 = ((f32[8,56,128]{2,1,0:T(8,128)}), f32[8,56,128]{2,1,0:T(8,128)S(1)}, u32[]{:S(2)}, u32[]{:S(2)}) async-start(f32[8,56,128]{2,1,0:T(8,128)} %get-tuple-element.129), calls=%async_computation.4 | async-start | bytes 458752 | tf_op jit(solution)/shard_map/all_to_all | solution.py:883
  139.7 4.3 %collective-permute-start.27 = (f32[256,128]{1,0:T(8,128)S(1)}, f32[256,128]{1,0:T(8,128)S(1)}, u32[]{:S(2)}, u32[]{:S(2)}) collective-permute-start(f32[256,128]{1,0:T(8,128)S(1)} %get-tuple-element.140), channel_id=1, source_target_pairs={{0,1},{1,0},{2,3},{3,2},{4,5},{5,4},{6,7},{7,6},{8,9},{9,8},{10,11... | collective-permute-start | bytes 393224 | tf_op jit(solution)/shard_map/ppermute | solution.py:873
  144.0 13.1 %collective-permute-start.28 = (f32[512,128]{1,0:T(8,128)S(1)}, f32[512,128]{1,0:T(8,128)S(1)}, u32[]{:S(2)}, u32[]{:S(2)}) collective-permute-start(f32[512,128]{1,0:T(8,128)S(1)} %constant_dynamic-update-slice_fusion.refs_0_), channel_id=1, source_target_pairs={{0,2},{1,3},{2,0},{3,1},{4,6},{5,7},{6,4},{7,5},{8,10},{9,11},{10,... | collective-permute-start | bytes 786440 | tf_op jit(solution)/shard_map/ppermute | solution.py:882
  150.2 12.9 %all-to-all-start.5 = ((f32[16,56,128]{2,1,0:T(8,128)}), f32[16,56,128]{2,1,0:T(8,128)S(1)}, u32[]{:S(2)}, u32[]{:S(2)}) async-start(f32[16,56,128]{2,1,0:T(8,128)} %shard_map.197), calls=%async_computation.5 | async-start | bytes 917504 | tf_op jit(solution)/shard_map/all_to_all | solution.py:885
  154.5 12.4 %collective-permute-start.29 = (f32[512,128]{1,0:T(8,128)S(1)}, f32[512,128]{1,0:T(8,128)S(1)}, u32[]{:S(2)}, u32[]{:S(2)}) collective-permute-start(f32[512,128]{1,0:T(8,128)S(1)} %constant_dynamic-update-slice_fusion.refs_0_), channel_id=1, source_target_pairs={{0,8},{8,0},{1,9},{9,1},{2,10},{10,2},{3,11},{11,3},{4,12},{12,4},... | collective-permute-start | bytes 786440 | tf_op jit(solution)/shard_map/ppermute | solution.py:804
  157.1 9.8 %collective-permute-start.30 = (f32[512,128]{1,0:T(8,128)S(1)}, f32[512,128]{1,0:T(8,128)S(1)}, u32[]{:S(2)}, u32[]{:S(2)}) collective-permute-start(f32[512,128]{1,0:T(8,128)S(1)} %collective-permute-done.28.refs_1_), channel_id=1, source_target_pairs={{0,8},{8,0},{1,9},{9,1},{2,10},{10,2},{3,11},{11,3},{4,12},{12,4},... | collective-permute-start | bytes 786440 | tf_op jit(solution)/shard_map/ppermute | solution.py:804
  163.2 4.8 %collective-permute-start.26 = (f32[160,128]{1,0:T(8,128)S(1)}, f32[160,128]{1,0:T(8,128)S(1)}, u32[]{:S(2)}, u32[]{:S(2)}) collective-permute-start(f32[160,128]{1,0:T(8,128)S(1)} %get-tuple-element.131.own), channel_id=1, source_target_pairs={{0,8},{8,0},{1,9},{9,1},{2,10},{10,2},{3,11},{11,3},{4,12},{12,4},... | collective-permute-start | bytes 245768 | tf_op jit(solution)/shard_map/ppermute | solution.py:804
